TPU v7x, 32 devices: a whole 2x2x4 slice. The times are simulated.
32 devices in a mesh: seq: 8 (over y, x, core), feat: 4 (over z).
Axes of the slice: x: 2, y: 2, z: 4, core: 2. Of those that a mesh axis runs over, the one named last changes fastest.
Arguments:
- tokens: bfloat16 [2, 6144, 2048], P(None, 'seq'), may hold values from -6 to 6
- cotangent: bfloat16 [2, 6144, 2048], P(None, 'seq'), may hold values from -6 to 6
- lengths: int32 [2, 3], replicated, may hold values from 96 to 5760, as said below
- w_query: bfloat16 [2048, 256], P('seq', 'feat'), may hold values from -0.125 to 0.125
- w_key: bfloat16 [2048, 256], P('seq', 'feat'), may hold values from -0.125 to 0.125
- w_value: bfloat16 [2048, 2048], P('seq', 'feat'), may hold values from -0.125 to 0.125
- w_output: bfloat16 [2048, 2048], P('seq', 'feat'), may hold values from -6 to 6
- w_gate: bfloat16 [2048, 5504], P('seq', 'feat'), may hold values from -0.125 to 0.125
- w_up: bfloat16 [2048, 5504], P('seq', 'feat'), may hold values from -0.125 to 0.125
- w_down: bfloat16 [5504, 2048], P('feat', 'seq'), may hold values from -0.078125 to 0.078125
- gain_mixer: bfloat16 [2048], P('seq'), may hold values from 0.099609375 to 1.8984375
- gain_mlp: bfloat16 [2048], P('seq'), may hold values from 0.099609375 to 1.8984375
Outputs:
- mixed: bfloat16 [2, 6144, 2048], P(None, 'seq', 'feat')
- input_grad: float32 [2, 6144, 2048], P(None, 'seq')
- grad_query: float32 [2048, 256], P('seq', 'feat')
- grad_key: float32 [2048, 256], P('seq', 'feat')
- grad_value: float32 [2048, 2048], P('seq', 'feat')
- grad_output: float32 [2048, 2048], P('seq', 'feat')
- grad_gate: float32 [2048, 5504], P('seq', 'feat')
- grad_up: float32 [2048, 5504], P('seq', 'feat')
- grad_down: float32 [5504, 2048], P('feat', 'seq')
- grad_gain_mixer: float32 [2048], P('seq')
- grad_gain_mlp: float32 [2048], P('seq')
Inputs may be any that keep to these rules, and one draw needn't show every extreme that they name: `lengths`: in each micro-batch the first document lies within the first 768 slots, the second reaches into the last 768 slots, and the slots after the three documents are padding, at least one and fewer than 768.
All inputs are finite; a program needn't handle non-finite values.
Results may differ from a plain program's by a relative error of at most 0.03.
Values may be sent and summed in bfloat16 or wider, within the bound.
No kernel may reach another device: no remote copies, remote signals or barrier semaphores. Data moves between devices by JAX's collectives and lax.ppermute only.
A program may use at most 256 MiB of HBM per device.

v0:
```python
import jax
import jax.numpy as jnp
import numpy as np
from jax import lax
from jax.sharding import PartitionSpec as P

HEADS = 16
HEAD_V = 128
QK = 16
FEATS = 288


EPS = 1e-05
HIGH = lax.Precision.HIGHEST


def prefix(value, axis, combine, identity, reverse):
    length, index = (lax.axis_size(axis), lax.axis_index(axis))
    everything = jax.tree.map(
        lambda part, kind: lax.all_gather(part.astype(kind), axis),
        value,
        (jnp.bfloat16, jnp.bfloat16, jnp.bfloat16),
    )
    start = jax.tree.map(
        lambda part, zero: jnp.broadcast_to(jnp.asarray(zero, part.dtype), part.shape),
        value,
        identity,
    )

    def step(k, before):
        at = length - 1 - k if reverse else k
        reached = at > index if reverse else at < index
        new = combine(
            before, jax.tree.map(lambda part, own: part[at].astype(own.dtype), everything, value)
        )
        return jax.tree.map(lambda a, b: jnp.where(reached, a, b), new, before)

    return lax.fori_loop(0, length, step, start)


def feature_tables():
    left_list = (
        [0]
        + list(range(1, QK + 1))
        + [left_idx + 1 for left_idx in range(QK) for right_idx in range(QK)]
    )
    right_list = [0] * (QK + 1) + [
        right_idx + 1 for left_idx in range(QK) for right_idx in range(QK)
    ]
    scale_list = [1.0] * (QK + 1) + [0.7071067811865476] * (QK * QK)
    padding = FEATS - len(left_list)
    left_list = left_list + [0] * padding
    right_list = right_list + [0] * padding
    scale_list = scale_list + [0.0] * padding
    pick_left = (np.arange(QK + 1)[:, None] == np.array(left_list)[None, :]).astype(np.float32)
    pick_right = (np.arange(QK + 1)[:, None] == np.array(right_list)[None, :]).astype(np.float32)
    return (pick_left, pick_right, np.array(scale_list, np.float32))


def feature_slice(heads_in, pick_left, pick_right, scale_row):
    extended = jnp.concatenate(
        [jnp.ones(heads_in.shape[:-1] + (1,), jnp.float32), 0.5 * heads_in], axis=-1
    )
    left_part = jnp.einsum("thi,ij->thj", extended, pick_left, precision=HIGH)
    right_part = jnp.einsum("thi,ij->thj", extended, pick_right, precision=HIGH)
    return scale_row * left_part * right_part


def combine_states(earlier, later):
    keep = 1.0 - later[2]
    return (
        later[0] + keep * earlier[0],
        later[1] + keep * earlier[1],
        jnp.maximum(earlier[2], later[2]),
    )


def times_transposed(left, right):
    return lax.dot_general(
        left, right, (((1,), (1,)), ((), ())), preferred_element_type=jnp.float32
    )


def transposed_times(left, right):
    return lax.dot_general(
        left, right, (((0,), (0,)), ((), ())), preferred_element_type=jnp.float32
    )


def norm_backward(grad_normed, inputs_f, inv_root, gain_f):
    scaled_in = inputs_f * inv_root
    weighted = grad_normed * gain_f
    inner = jnp.mean(weighted * scaled_in, axis=-1, keepdims=True)
    return (inv_root * (weighted - scaled_in * inner), jnp.sum(grad_normed * scaled_in, axis=0))


def on_device(
    tokens,
    cotangent,
    lengths,
    w_query,
    w_key,
    w_value,
    w_output,
    w_gate,
    w_up,
    w_down,
    gain_mixer,
    gain_mlp,
):
    micro = tokens.shape[0]
    rows = tokens.shape[1]
    width = tokens.shape[2]
    feat_count = lax.axis_size("feat")
    feat_rank = lax.axis_index("feat")
    seq_rank = lax.axis_index("seq")
    column_width = width // feat_count
    left_np, right_np, scale_np = feature_tables()
    piece = FEATS // feat_count
    head_count = HEADS
    pick_left = lax.dynamic_slice_in_dim(jnp.asarray(left_np), feat_rank * piece, piece, 1)
    pick_right = lax.dynamic_slice_in_dim(jnp.asarray(right_np), feat_rank * piece, piece, 1)
    scale_row = lax.dynamic_slice_in_dim(jnp.asarray(scale_np), feat_rank * piece, piece, 0)

    def features(heads_in):
        return feature_slice(heads_in, pick_left, pick_right, scale_row)

    outputs = []
    input_grads = []
    totals = None
    order = jnp.arange(rows)
    for batch_number in range(micro):
        full_weights = (
            lax.all_gather(w_query, "seq", axis=0, tiled=True),
            lax.all_gather(w_key, "seq", axis=0, tiled=True),
            lax.all_gather(w_value, "seq", axis=0, tiled=True),
            lax.all_gather(w_output, "seq", axis=0, tiled=True),
            lax.all_gather(w_gate, "seq", axis=0, tiled=True),
            lax.all_gather(w_up, "seq", axis=0, tiled=True),
            lax.all_gather(w_down, "seq", axis=1, tiled=True),
            lax.all_gather(gain_mixer, "seq", axis=0, tiled=True),
            lax.all_gather(gain_mlp, "seq", axis=0, tiled=True),
        )
        (
            query_full,
            key_full,
            value_full,
            output_full,
            gate_full,
            up_full,
            down_full,
            mixer_gain,
            mlp_gain,
        ) = full_weights
        mixer_gain_f = mixer_gain.astype(jnp.float32)
        mlp_gain_f = mlp_gain.astype(jnp.float32)
        start = seq_rank * rows
        positions = start + jnp.arange(rows, dtype=jnp.int32)
        bounds = jnp.cumsum(lengths[batch_number])
        segment = jnp.sum((positions[:, None] >= bounds[None, :]).astype(jnp.int32), axis=1)
        valid = segment < 3
        valid_f = valid.astype(jnp.float32)
        before = jnp.sum((start - 1 >= bounds).astype(jnp.int32))
        before = jnp.where(start == 0, -1, before)
        use = (valid & (segment == before)).astype(jnp.float32)
        tail = (valid & (segment == segment[-1])).astype(jnp.float32)
        flag = (segment[-1] != before).astype(jnp.float32)
        mask = (
            (order[None, :] <= order[:, None])
            & (segment[None, :] == segment[:, None])
            & valid[None, :]
        ).astype(jnp.float32)
        tokens_b = tokens[batch_number]
        tokens_f = tokens_b.astype(jnp.float32)
        inv_one = lax.rsqrt(jnp.mean(tokens_f * tokens_f, axis=-1, keepdims=True) + EPS)
        normed = (tokens_f * inv_one * mixer_gain_f).astype(jnp.bfloat16)
        query_part = jnp.dot(normed, query_full, preferred_element_type=jnp.float32).astype(
            jnp.bfloat16
        )
        key_part = jnp.dot(normed, key_full, preferred_element_type=jnp.float32).astype(
            jnp.bfloat16
        )
        value_part = jnp.dot(normed, value_full, preferred_element_type=jnp.float32).astype(
            jnp.bfloat16
        )
        query, keys, values = (
            lax.all_gather(query_part, "feat", axis=1, tiled=True),
            lax.all_gather(key_part, "feat", axis=1, tiled=True),
            lax.all_gather(value_part, "feat", axis=1, tiled=True),
        )
        query_heads = query.reshape(rows, head_count, QK).astype(jnp.float32)
        key_heads = keys.reshape(rows, head_count, QK).astype(jnp.float32)
        values_h = values.reshape(rows, head_count, HEAD_V)
        feat_q = features(query_heads).astype(jnp.bfloat16)
        feat_k = features(key_heads).astype(jnp.bfloat16)
        scores = jnp.einsum("thf,shf->hts", feat_q, feat_k, preferred_element_type=jnp.float32)
        scores_b = (scores * mask[None]).astype(jnp.bfloat16)
        tail_keys = feat_k * tail.astype(jnp.bfloat16)[:, None, None]
        local_state = jnp.einsum(
            "shf,shc->hfc", tail_keys, values_h, preferred_element_type=jnp.float32
        )
        local_sum = jnp.sum(tail_keys, axis=0, dtype=jnp.float32)
        identity = (jnp.zeros_like(local_state), jnp.zeros_like(local_sum), jnp.float32(0.0))
        prefix_state, prefix_sum, ignored_flag = prefix(
            (local_state, local_sum, flag), "seq", combine_states, identity, False
        )
        state_b = prefix_state.astype(jnp.bfloat16)
        feat_q_f = feat_q.astype(jnp.float32)
        pre_num = (
            jnp.einsum("thf,hfc->thc", feat_q, state_b, preferred_element_type=jnp.float32)
            * use[:, None, None]
        )
        pre_den = jnp.einsum("thf,hf->th", feat_q_f, prefix_sum, precision=HIGH) * use[:, None]
        num_part = (
            jnp.einsum("hts,shc->thc", scores_b, values_h, preferred_element_type=jnp.float32)
            + pre_num
        )
        den_part = jnp.sum(scores_b, axis=2, dtype=jnp.float32).T + pre_den
        numer, denom = (
            lax.psum(num_part.astype(jnp.bfloat16), "feat").astype(jnp.float32),
            lax.psum(den_part.astype(jnp.bfloat16), "feat").astype(jnp.float32),
        )
        safe = denom + (1.0 - valid_f)[:, None]
        mixer_own = (
            (numer / safe[:, :, None]).astype(jnp.bfloat16).reshape(rows, head_count * HEAD_V)
        )
        branch_part = jnp.dot(mixer_own, output_full, preferred_element_type=jnp.float32).astype(
            jnp.bfloat16
        )
        branch = lax.all_gather(branch_part, "feat", axis=1, tiled=True)
        hidden_state = tokens_f + branch.astype(jnp.float32)
        inv_two = lax.rsqrt(jnp.mean(hidden_state * hidden_state, axis=-1, keepdims=True) + EPS)
        normed_two = (hidden_state * inv_two * mlp_gain_f).astype(jnp.bfloat16)
        gate = jnp.dot(normed_two, gate_full, preferred_element_type=jnp.float32)
        upward = jnp.dot(normed_two, up_full, preferred_element_type=jnp.float32)
        logistic = jax.nn.sigmoid(gate)
        activated = gate * logistic
        hidden = (activated * upward).astype(jnp.bfloat16)
        mlp_piece = lax.psum_scatter(
            jnp.dot(hidden, down_full, preferred_element_type=jnp.float32).astype(jnp.bfloat16),
            "feat",
            scatter_dimension=1,
            tiled=True,
        ).astype(jnp.float32)
        own_columns = lax.dynamic_slice_in_dim(
            hidden_state, feat_rank * column_width, column_width, 1
        )
        outputs.append((own_columns + mlp_piece).astype(jnp.bfloat16))
        grad_out = cotangent[batch_number]
        grad_down = transposed_times(hidden, grad_out)
        grad_hidden = times_transposed(grad_out, down_full)
        grad_gate_b = (grad_hidden * upward * logistic * (1.0 + gate * (1.0 - logistic))).astype(
            jnp.bfloat16
        )
        grad_up_b = (grad_hidden * activated).astype(jnp.bfloat16)
        grad_gate = transposed_times(normed_two, grad_gate_b)
        grad_up = transposed_times(normed_two, grad_up_b)
        normed_grad_part = times_transposed(grad_gate_b, gate_full) + times_transposed(
            grad_up_b, up_full
        )
        normed_grad = lax.psum(normed_grad_part.astype(jnp.bfloat16), "feat").astype(jnp.float32)
        hidden_grad_norm, grad_gain_mlp = norm_backward(
            normed_grad, hidden_state, inv_two, mlp_gain_f
        )
        hidden_grad = grad_out.astype(jnp.float32) + hidden_grad_norm
        branch_grad = lax.dynamic_slice_in_dim(
            hidden_grad, feat_rank * column_width, column_width, 1
        ).astype(jnp.bfloat16)
        grad_output = transposed_times(mixer_own, branch_grad)
        mixer_grad_part = times_transposed(branch_grad, output_full)
        mixer_grad = lax.psum(mixer_grad_part.astype(jnp.bfloat16), "feat").astype(jnp.float32)
        mixer_grad = mixer_grad.reshape(rows, head_count, HEAD_V)
        grad_numer = (mixer_grad / safe[:, :, None]).astype(jnp.bfloat16)
        grad_denom = -jnp.sum(mixer_grad * numer, axis=2) / (safe * safe)
        grad_scores = (
            jnp.einsum("thc,shc->hts", grad_numer, values_h, preferred_element_type=jnp.float32)
            + grad_denom.T[:, :, None]
        )
        grad_scores = (grad_scores * mask[None]).astype(jnp.bfloat16)
        use_b = use.astype(jnp.bfloat16)
        grad_state = jnp.einsum(
            "thf,thc->hfc",
            feat_q * use_b[:, None, None],
            grad_numer,
            preferred_element_type=jnp.float32,
        )
        grad_sum = jnp.einsum(
            "thf,th->hf", feat_q_f * use[:, None, None], grad_denom, precision=HIGH
        )
        carried, carried_sum, ignored_back = prefix(
            (grad_state, grad_sum, flag), "seq", combine_states, identity, True
        )
        carried_b = carried.astype(jnp.bfloat16)
        grad_fq = jnp.einsum(
            "hts,shf->thf", grad_scores, feat_k, preferred_element_type=jnp.float32
        )
        grad_fq = grad_fq + use[:, None, None] * (
            jnp.einsum("thc,hfc->thf", grad_numer, state_b, preferred_element_type=jnp.float32)
            + grad_denom[:, :, None] * prefix_sum[None]
        )
        grad_fk = jnp.einsum(
            "hts,thf->shf", grad_scores, feat_q, preferred_element_type=jnp.float32
        )
        grad_fk = grad_fk + tail[:, None, None] * (
            jnp.einsum("shc,hfc->shf", values_h, carried_b, preferred_element_type=jnp.float32)
            + carried_sum[None]
        )
        grad_values = jnp.einsum(
            "hts,thc->shc", scores_b, grad_numer, preferred_element_type=jnp.float32
        )
        grad_values = grad_values + tail[:, None, None] * jnp.einsum(
            "shf,hfc->shc", feat_k, carried_b, preferred_element_type=jnp.float32
        )
        ignored_q, query_pull = jax.vjp(features, query_heads)
        ignored_k, key_pull = jax.vjp(features, key_heads)
        grad_query_part = query_pull(grad_fq)[0].reshape(rows, head_count * QK)
        grad_key_part = key_pull(grad_fk)[0].reshape(rows, head_count * QK)
        grad_value_part = grad_values.reshape(rows, head_count * HEAD_V)
        grad_q_own, grad_k_own, grad_v_own = (
            lax.psum_scatter(
                grad_query_part.astype(jnp.bfloat16), "feat", scatter_dimension=1, tiled=True
            ).astype(jnp.float32),
            lax.psum_scatter(
                grad_key_part.astype(jnp.bfloat16), "feat", scatter_dimension=1, tiled=True
            ).astype(jnp.float32),
            lax.psum_scatter(
                grad_value_part.astype(jnp.bfloat16), "feat", scatter_dimension=1, tiled=True
            ).astype(jnp.float32),
        )
        grad_q_b = grad_q_own.astype(jnp.bfloat16)
        grad_k_b = grad_k_own.astype(jnp.bfloat16)
        grad_v_b = grad_v_own.astype(jnp.bfloat16)
        grad_query = transposed_times(normed, grad_q_b)
        grad_key = transposed_times(normed, grad_k_b)
        grad_value = transposed_times(normed, grad_v_b)
        input_normed_part = (
            times_transposed(grad_q_b, query_full)
            + times_transposed(grad_k_b, key_full)
            + times_transposed(grad_v_b, value_full)
        )
        input_normed = lax.psum(input_normed_part.astype(jnp.bfloat16), "feat").astype(jnp.float32)
        input_grad_norm, grad_gain_mixer = norm_backward(
            input_normed, tokens_f, inv_one, mixer_gain_f
        )
        input_grads.append(hidden_grad + input_grad_norm)
        step_grads = (
            grad_query,
            grad_key,
            grad_value,
            grad_output,
            grad_gate,
            grad_up,
            grad_down,
            grad_gain_mixer,
            grad_gain_mlp,
        )
        step_grads = (
            lax.psum_scatter(
                grad_query.astype(jnp.bfloat16), "seq", scatter_dimension=0, tiled=True
            ).astype(jnp.float32),
            lax.psum_scatter(
                grad_key.astype(jnp.bfloat16), "seq", scatter_dimension=0, tiled=True
            ).astype(jnp.float32),
            lax.psum_scatter(
                grad_value.astype(jnp.bfloat16), "seq", scatter_dimension=0, tiled=True
            ).astype(jnp.float32),
            lax.psum_scatter(
                grad_output.astype(jnp.bfloat16), "seq", scatter_dimension=0, tiled=True
            ).astype(jnp.float32),
            lax.psum_scatter(
                grad_gate.astype(jnp.bfloat16), "seq", scatter_dimension=0, tiled=True
            ).astype(jnp.float32),
            lax.psum_scatter(
                grad_up.astype(jnp.bfloat16), "seq", scatter_dimension=0, tiled=True
            ).astype(jnp.float32),
            lax.psum_scatter(
                grad_down.astype(jnp.bfloat16), "seq", scatter_dimension=1, tiled=True
            ).astype(jnp.float32),
            lax.psum_scatter(
                grad_gain_mixer.astype(jnp.bfloat16), "seq", scatter_dimension=0, tiled=True
            ).astype(jnp.float32),
            lax.psum_scatter(
                grad_gain_mlp.astype(jnp.bfloat16), "seq", scatter_dimension=0, tiled=True
            ).astype(jnp.float32),
        )
        if batch_number == 0:
            totals = step_grads
        else:
            totals = jax.tree.map(jnp.add, totals, step_grads)
    return (
        jnp.stack(outputs),
        jnp.stack(input_grads),
        totals[0],
        totals[1],
        totals[2],
        totals[3],
        totals[4],
        totals[5],
        totals[6],
        totals[7],
        totals[8],
    )


def solution(mesh):
    in_specs = (
        P(None, "seq", None),
        P(None, "seq", None),
        P(),
        P("seq", "feat"),
        P("seq", "feat"),
        P("seq", "feat"),
        P("seq", "feat"),
        P("seq", "feat"),
        P("seq", "feat"),
        P("feat", "seq"),
        P("seq"),
        P("seq"),
    )
    out_specs = (
        P(None, "seq", "feat"),
        P(None, "seq", None),
        P("seq", "feat"),
        P("seq", "feat"),
        P("seq", "feat"),
        P("seq", "feat"),
        P("seq", "feat"),
        P("seq", "feat"),
        P("feat", "seq"),
        P("seq"),
        P("seq"),
    )
    return jax.shard_map(
        on_device, mesh=mesh, in_specs=in_specs, out_specs=out_specs, check_vma=False
    )
```

profile of v0, /device:TPU:7, one launch (start us, length us, event | category | flops | bytes accessed | tf_op | source)
XLA Modules:
  0.0 2935.2 jit_solution(6121585874645820839)
XLA Ops:
  24.6 14.0 all-gather.24.cloned.1.call-done
  52.3 9.9 all_gather.127
  72.1 17.7 all_gather.128
  90.9 17.8 all_gather.130
  109.8 15.3 all_gather.144
  130.6 12.8 all_gather.145
  156.9 15.3 fusion.150
  198.3 19.9 all-reduce.11
  218.2 11.9 all-gather.3
  230.2 9.8 all-gather.1
  242.6 11.6 convert_reduce_fusion
  254.2 11.8 convert_reduce_fusion.1
  270.7 13.2 fusion.86
  283.9 12.3 fusion.93
  296.2 36.6 %while.69 = (s32[]{:T(128)}, f32[16,72,128]{2,1,0:T(8,128)}, f32[16,72]{1,0:T(8,128)S(1)}, s32[]{:T(128)}, bf16[8,16,72,128]{3,2,1,0:T(8,128)(2,1)}, /*index=5*/...) while((s32[]{:T(128)}, f32[16,72,128]{2,1,0:T(8,128)}, ...), condition=%wide.region_18.19_spmd.clone, body=%wide.region_17.18_spmd.clone.sunk | while | flops 743045 | bytes 1486245 | solution.py:38
  332.7 36.5 %while.68 = (s32[]{:T(128)}, f32[16,72,128]{2,1,0:T(8,128)}, f32[16,72]{1,0:T(8,128)S(1)}, s32[]{:T(128)}, bf16[8,16,72,128]{3,2,1,0:T(8,128)(2,1)}, /*index=5*/...) while((s32[]{:T(128)}, f32[16,72,128]{2,1,0:T(8,128)}, ...), condition=%wide.region_6.7_spmd.clone, body=%wide.region_5.6_spmd.clone.sunk | while | flops 743045 | bytes 1486245 | solution.py:38
  383.7 20.8 all-reduce.12
  405.8 194.5 %all-reduce.28.cloned.1.call-done = (bf16[768,16,128]{0,2,1:T(8,128)(2,1)}, bf16[768,16,128]{0,2,1:T(8,128)(2,1)}) async-done(((bf16[768,16,128]{0,2,1:T(8,128)(2,1)}, bf16[768,16,128]{0,2,1:T(8,128)(2,1)}), (bf16[768,16,128]{0,2,1:T(8,128)(2,1)}, bf16[768,16,128]{0,2,1:T(8,128)(2,1)})) %all-reduce.28.cloned.1.call-update) | async-done | bytes 6291472 | tf_op jit(solution)/shard_map/psum | solution.py:220
  604.6 24.0 all-gather.28.cloned.1.call-done
  653.5 44.5 %all-gather.30.cloned.1.call-done = bf16[768,2048]{1,0:T(8,128)(2,1)} async-done(((bf16[768,512]{1,0:T(8,128)(2,1)}), bf16[768,2048]{1,0:T(8,128)(2,1)}) %all-gather.30.cloned.1.call-update) | async-done | bytes 3145744 | tf_op jit(solution)/shard_map/all_gather | solution.py:230
  698.0 64.3 %all-gather.40.cloned.1.call-done = bf16[768,2048]{1,0:T(8,128)(2,1)} async-done(((bf16[768,512]{1,0:T(8,128)(2,1)}), bf16[768,2048]{1,0:T(8,128)(2,1)}) %all-gather.40.cloned.1.call-update) | async-done | bytes 3145744 | tf_op jit(solution)/shard_map/all_gather | solution.py:230
  776.6 29.4 %all-gather.34.cloned.1.call-done = bf16[2048,1376]{0,1:T(8,128)(2,1)} async-done(((bf16[256,1376]{0,1:T(8,128)(2,1)}), bf16[2048,1376]{0,1:T(8,128)(2,1)}) %all-gather.34.cloned.1.call-update) | async-done | bytes 5636112 | tf_op jit(solution)/shard_map/all_gather | solution.py:139
  806.0 10.1 fusion.277
  816.2 35.6 %all-gather.32.cloned.1.call-done = bf16[2048,1376]{0,1:T(8,128)(2,1)} async-done(((bf16[256,1376]{0,1:T(8,128)(2,1)}), bf16[2048,1376]{0,1:T(8,128)(2,1)}) %all-gather.32.cloned.1.call-update) | async-done | bytes 5636112 | tf_op jit(solution)/shard_map/all_gather | solution.py:138
  851.7 10.4 fusion.276
  874.6 22.7 all-gather.36.cloned.1.call-done
  897.3 14.8 multiply_convert_fusion.6
  920.1 11.4 multiply_convert_fusion.8
  953.1 223.8 %all-reduce.26.cloned.1.call-done = (bf16[768,2048]{1,0:T(8,128)(2,1)}, bf16[768,2048]{1,0:T(8,128)(2,1)}) async-done(((bf16[768,2048]{1,0:T(8,128)(2,1)}, bf16[768,2048]{1,0:T(8,128)(2,1)}), (bf16[768,2048]{1,0:T(8,128)(2,1)}, bf16[768,2048]{1,0:T(8,128)(2,1)})) %all-reduce.26.cloned.1.call-update) | async-done | bytes 6291472 | tf_op jit(solution)/shard_map/psum | solution.py:261
  1176.9 9.7 fusion.39
  1187.0 14.1 fusion.33
  1224.1 222.0 %all-reduce.24.cloned.1.call-done = (bf16[768,16,128]{0,2,1:T(8,128)(2,1)}, bf16[768,16,128]{0,2,1:T(8,128)(2,1)}) async-done(((bf16[768,16,128]{0,2,1:T(8,128)(2,1)}, bf16[768,16,128]{0,2,1:T(8,128)(2,1)}), (bf16[768,16,128]{0,2,1:T(8,128)(2,1)}, bf16[768,16,128]{0,2,1:T(8,128)(2,1)})) %all-reduce.24.cloned.1.call-update) | async-done | bytes 6291472 | tf_op jit(solution)/shard_map/psum | solution.py:271
  1470.1 12.2 multiply_convert_fusion
  1482.3 11.0 fusion.57
  1501.7 11.4 reduce-scatter.33.cloned.1.call-start
  1515.7 12.3 multiply_convert_fusion.1
  1541.0 9.9 all-gather.5
  1550.9 10.8 fusion.63
  1570.1 13.3 fusion.288
  1586.5 13.4 fusion.283
  1600.0 26.1 while.70
  1626.2 26.1 while.71
  1674.7 11.6 fusion.289
  1694.3 11.7 fusion.284
  1815.7 12.0 reduce-scatter.31.cloned.1.call-done
  1845.0 45.3 %reduce-scatter.25.cloned.1.call-done = bf16[768,512]{1,0:T(8,128)(2,1)} async-done(((bf16[768,2048]{1,0:T(8,128)(2,1)}), bf16[768,512]{1,0:T(8,128)(2,1)}) %reduce-scatter.25.cloned.1.call-update) | async-done | bytes 786448 | tf_op jit(solution)/shard_map/reduce_scatter | solution.py:239
  1892.3 60.6 %reduce-scatter.23.cloned.1.call-done = bf16[768,512]{1,0:T(8,128)(2,1)} async-done(((bf16[768,2048]{1,0:T(8,128)(2,1)}), bf16[768,512]{1,0:T(8,128)(2,1)}) %reduce-scatter.23.cloned.1.call-update) | async-done | bytes 786448 | tf_op jit(solution)/shard_map/reduce_scatter | solution.py:239
  1956.0 58.0 %reduce-scatter.61.cloned.1.call-done = bf16[256,1376]{0,1:T(8,128)(2,1)} async-done(((bf16[2048,1376]{0,1:T(8,128)(2,1)}), bf16[256,1376]{0,1:T(8,128)(2,1)}) %reduce-scatter.61.cloned.1.call-update) | async-done | bytes 704528 | tf_op jit(solution)/shard_map/reduce_scatter | solution.py:373
  2014.0 61.8 %reduce-scatter.59.cloned.1.call-done = bf16[256,1376]{0,1:T(8,128)(2,1)} async-done(((bf16[2048,1376]{0,1:T(8,128)(2,1)}), bf16[256,1376]{0,1:T(8,128)(2,1)}) %reduce-scatter.59.cloned.1.call-update) | async-done | bytes 704528 | tf_op jit(solution)/shard_map/reduce_scatter | solution.py:373
  2078.3 59.2 %reduce-scatter.57.cloned.1.call-done = bf16[256,1376]{0,1:T(8,128)(2,1)} async-done(((bf16[2048,1376]{0,1:T(8,128)(2,1)}), bf16[256,1376]{0,1:T(8,128)(2,1)}) %reduce-scatter.57.cloned.1.call-update) | async-done | bytes 704528 | tf_op jit(solution)/shard_map/reduce_scatter | solution.py:370
  2137.6 61.9 %reduce-scatter.55.cloned.1.call-done = bf16[256,1376]{0,1:T(8,128)(2,1)} async-done(((bf16[2048,1376]{0,1:T(8,128)(2,1)}), bf16[256,1376]{0,1:T(8,128)(2,1)}) %reduce-scatter.55.cloned.1.call-update) | async-done | bytes 704528 | tf_op jit(solution)/shard_map/reduce_scatter | solution.py:370
  2202.0 59.4 %reduce-scatter.63.cloned.1.call-done = bf16[1376,256]{1,0:T(8,128)(2,1)} async-done(((bf16[1376,2048]{1,0:T(8,128)(2,1)}), bf16[1376,256]{1,0:T(8,128)(2,1)}) %reduce-scatter.63.cloned.1.call-update) | async-done | bytes 704528 | tf_op jit(solution)/shard_map/reduce_scatter | solution.py:376
  2261.4 61.8 %reduce-scatter.65.cloned.1.call-done = bf16[1376,256]{1,0:T(8,128)(2,1)} async-done(((bf16[1376,2048]{1,0:T(8,128)(2,1)}), bf16[1376,256]{1,0:T(8,128)(2,1)}) %reduce-scatter.65.cloned.1.call-update) | async-done | bytes 704528 | tf_op jit(solution)/shard_map/reduce_scatter | solution.py:376
  2325.8 42.0 %reduce-scatter.51.cloned.1.call-done = bf16[256,512]{1,0:T(8,128)(2,1)} async-done(((bf16[2048,512]{1,0:T(8,128)(2,1)}), bf16[256,512]{1,0:T(8,128)(2,1)}) %reduce-scatter.51.cloned.1.call-update) | async-done | bytes 262160 | tf_op jit(solution)/shard_map/reduce_scatter | solution.py:367
  2367.7 44.9 %reduce-scatter.53.cloned.1.call-done = bf16[256,512]{1,0:T(8,128)(2,1)} async-done(((bf16[2048,512]{1,0:T(8,128)(2,1)}), bf16[256,512]{1,0:T(8,128)(2,1)}) %reduce-scatter.53.cloned.1.call-update) | async-done | bytes 262160 | tf_op jit(solution)/shard_map/reduce_scatter | solution.py:367
  2414.5 34.2 %reduce-scatter.41.cloned.1.call-done = bf16[256,64]{0,1:T(8,128)(2,1)} async-done(((bf16[2048,64]{0,1:T(8,128)(2,1)}), bf16[256,64]{0,1:T(8,128)(2,1)}) %reduce-scatter.41.cloned.1.call-update) | async-done | bytes 32784 | tf_op jit(solution)/shard_map/reduce_scatter | solution.py:358
  2448.7 37.0 %reduce-scatter.39.cloned.1.call-done = bf16[256,64]{0,1:T(8,128)(2,1)} async-done(((bf16[2048,64]{0,1:T(8,128)(2,1)}), bf16[256,64]{0,1:T(8,128)(2,1)}) %reduce-scatter.39.cloned.1.call-update) | async-done | bytes 32784 | tf_op jit(solution)/shard_map/reduce_scatter | solution.py:358
  2487.1 35.8 %reduce-scatter.45.cloned.1.call-done = bf16[256,64]{0,1:T(8,128)(2,1)} async-done(((bf16[2048,64]{0,1:T(8,128)(2,1)}), bf16[256,64]{0,1:T(8,128)(2,1)}) %reduce-scatter.45.cloned.1.call-update) | async-done | bytes 32784 | tf_op jit(solution)/shard_map/reduce_scatter | solution.py:361
  2522.9 36.8 %reduce-scatter.43.cloned.1.call-done = bf16[256,64]{0,1:T(8,128)(2,1)} async-done(((bf16[2048,64]{0,1:T(8,128)(2,1)}), bf16[256,64]{0,1:T(8,128)(2,1)}) %reduce-scatter.43.cloned.1.call-update) | async-done | bytes 32784 | tf_op jit(solution)/shard_map/reduce_scatter | solution.py:361
  2561.1 43.4 %reduce-scatter.49.cloned.1.call-done = bf16[256,512]{1,0:T(8,128)(2,1)} async-done(((bf16[2048,512]{1,0:T(8,128)(2,1)}), bf16[256,512]{1,0:T(8,128)(2,1)}) %reduce-scatter.49.cloned.1.call-update) | async-done | bytes 262160 | tf_op jit(solution)/shard_map/reduce_scatter | solution.py:364
  2604.6 44.9 %reduce-scatter.47.cloned.1.call-done = bf16[256,512]{1,0:T(8,128)(2,1)} async-done(((bf16[2048,512]{1,0:T(8,128)(2,1)}), bf16[256,512]{1,0:T(8,128)(2,1)}) %reduce-scatter.47.cloned.1.call-update) | async-done | bytes 262160 | tf_op jit(solution)/shard_map/reduce_scatter | solution.py:364
  2651.3 224.5 %all-reduce.22.cloned.1.call-done = (bf16[768,2048]{1,0:T(8,128)(2,1)}, bf16[768,2048]{1,0:T(8,128)(2,1)}) async-done(((bf16[768,2048]{1,0:T(8,128)(2,1)}, bf16[768,2048]{1,0:T(8,128)(2,1)}), (bf16[768,2048]{1,0:T(8,128)(2,1)}, bf16[768,2048]{1,0:T(8,128)(2,1)})) %all-reduce.22.cloned.1.call-update) | async-done | bytes 6291472 | tf_op jit(solution)/shard_map/psum | solution.py:341
  2882.8 22.1 all-reduce.10
  2906.1 12.7 fusion.30
  (608 shorter events, 572.7 us)
Async XLA Ops:
  7.2 31.3 %all-gather.24.cloned.1.call-start = ((), (), s32[]{:S(2)}) async-start(), calls=%async_computation.22 | async-start | bytes 2359296 | tf_op jit(solution)/shard_map/all_gather | solution.py:136
  7.9 184.4 %all-gather.38.cloned.1.call-start = ((), (), s32[]{:S(2)}) async-start(), calls=%async_computation.30 | async-start | bytes 3932160 | tf_op jit(solution)/shard_map/all_gather | solution.py:189
  24.6 103.3 %copy-start.1 = (bf16[768,2048]{1,0:T(8,128)(2,1)}, bf16[768,2048]{1,0:T(8,128)(2,1)S(1)}, u32[]{:S(2)}) copy-start(bf16[768,2048]{1,0:T(8,128)(2,1)S(1)} %get-tuple-element.838) | copy-start | bytes 9437188
  38.5 23.6 copy-start.103
  43.8 222.2 %all-gather.26.cloned.1.call-start = ((), (), s32[]{:S(2)}) async-start(), calls=%async_computation.23 | async-start | bytes 3932160 | tf_op jit(solution)/shard_map/all_gather | solution.py:189
  46.3 130.8 %copy-start.86 = (s32[768]{0:T(1024)}, s32[768]{0:T(1024)S(1)}, u32[]{:S(2)}) copy-start(s32[768]{0:T(1024)S(1)} %get-tuple-element.735) | copy-start | bytes 9220
  49.5 135.6 %copy-start.93 = (f32[72]{0:T(128)}, f32[72]{0:T(128)S(1)}, u32[]{:S(2)}) copy-start(f32[72]{0:T(128)S(1)} %dynamic_slice.123) | copy-start | bytes 868
  52.3 38.6 %copy-start.119 = (bf16[8]{0:T(256)(128)(2,1)}, bf16[8]{0:T(256)(128)(2,1)S(1)}, u32[]{:S(2)}) copy-start(bf16[8]{0:T(256)(128)(2,1)S(1)} %dynamic-update-slice) | copy-start | bytes 52
  62.1 46.6 %copy-start.48 = (bf16[2048,64]{0,1:T(8,128)(2,1)}, bf16[2048,64]{0,1:T(8,128)(2,1)S(1)}, u32[]{:S(2)}) copy-start(bf16[2048,64]{0,1:T(8,128)(2,1)S(1)} %all_gather.127) | copy-start | bytes 786436
  71.0 55.1 %copy-start.46 = (bf16[2048,64]{0,1:T(8,128)(2,1)}, bf16[2048,64]{0,1:T(8,128)(2,1)S(1)}, u32[]{:S(2)}) copy-start(bf16[2048,64]{0,1:T(8,128)(2,1)S(1)} %all_gather.129) | copy-start | bytes 786436
  72.1 36.6 %copy-start.3 = (bf16[768,2048]{1,0:T(8,128)(2,1)S(1)}, bf16[768,2048]{1,0:T(8,128)(2,1)}, u32[]{:S(2)}) copy-start(bf16[768,2048]{1,0:T(8,128)(2,1)} %get-tuple-element.837) | copy-start | bytes 9437188
  130.5 165.6 %all-gather.44.cloned.1.call-start = ((), (), s32[]{:S(2)}) async-start(), calls=%async_computation.54 | async-start | bytes 2654208 | tf_op jit(solution)/shard_map/all_gather | solution.py:20
  147.6 31.9 %copy-start.22 = (f32[768,16,72]{0,2,1:T(8,128)}, f32[768,16,72]{0,2,1:T(8,128)S(1)}, u32[]{:S(2)}) copy-start(f32[768,16,72]{0,2,1:T(8,128)S(1)} %fusion.156) | copy-start | bytes 10616836
  150.7 28.9 copy-start.20
  153.8 31.4 %copy-start.16 = (f32[768,16,72]{0,2,1:T(8,128)}, f32[768,16,72]{0,2,1:T(8,128)S(1)}, u32[]{:S(2)}) copy-start(f32[768,16,72]{0,2,1:T(8,128)S(1)} %fusion.152) | copy-start | bytes 10616836
  156.8 28.3 copy-start.14
  196.5 136.2 %all-gather.42.cloned.1.call-start = ((), (), s32[]{:S(2)}) async-start(), calls=%async_computation.53 | async-start | bytes 2654208 | tf_op jit(solution)/shard_map/all_gather | solution.py:20
  270.2 330.1 %all-reduce.28.cloned.1.call-start = ((), (), s32[]{:S(2)}) async-start(), calls=%async_computation.60 | async-start | bytes 12582912 | tf_op jit(solution)/shard_map/psum | solution.py:220
  332.7 47.2 %copy-start.67 = (f32[16,72]{1,0:T(8,128)}, f32[16,72]{1,0:T(8,128)S(1)}, u32[]{:S(2)}) copy-start(f32[16,72]{1,0:T(8,128)S(1)} %get-tuple-element.618) | copy-start | bytes 13828
  377.8 250.8 %all-gather.28.cloned.1.call-start = ((), (), s32[]{:S(2)}) async-start(), calls=%async_computation.24 | async-start | bytes 2359296 | tf_op jit(solution)/shard_map/all_gather | solution.py:137
  378.5 319.4 %all-gather.30.cloned.1.call-start = ((), (), s32[]{:S(2)}) async-start(), calls=%async_computation.25 | async-start | bytes 3932160 | tf_op jit(solution)/shard_map/all_gather | solution.py:230
  604.6 29.4 copy-start.107
  633.9 128.5 %all-gather.40.cloned.1.call-start = ((), (), s32[]{:S(2)}) async-start(), calls=%async_computation.31 | async-start | bytes 3932160 | tf_op jit(solution)/shard_map/all_gather | solution.py:230
  642.4 163.6 %all-gather.34.cloned.1.call-start = ((), (), s32[]{:S(2)}) async-start(), calls=%async_computation.27 | async-start | bytes 6340608 | tf_op jit(solution)/shard_map/all_gather | solution.py:139
  643.0 208.7 %all-gather.32.cloned.1.call-start = ((), (), s32[]{:S(2)}) async-start(), calls=%async_computation.26 | async-start | bytes 6340608 | tf_op jit(solution)/shard_map/all_gather | solution.py:138
  643.7 253.5 %all-gather.36.cloned.1.call-start = ((), (), s32[]{:S(2)}) async-start(), calls=%async_computation.28 | async-start | bytes 6340608 | tf_op jit(solution)/shard_map/all_gather | solution.py:140
  644.3 532.6 %all-reduce.26.cloned.1.call-start = ((), (), s32[]{:S(2)}) async-start(), calls=%async_computation.59 | async-start | bytes 12582912 | tf_op jit(solution)/shard_map/psum | solution.py:261
  912.1 27.4 slice-start.4
  953.0 493.1 %all-reduce.24.cloned.1.call-start = ((), (), s32[]{:S(2)}) async-start(), calls=%async_computation.58 | async-start | bytes 12582912 | tf_op jit(solution)/shard_map/psum | solution.py:271
  1223.8 376.2 %all-gather.46.cloned.1.call-start = ((), (), s32[]{:S(2)}) async-start(), calls=%async_computation.55 | async-start | bytes 2654208 | tf_op jit(solution)/shard_map/all_gather | solution.py:20
  1463.2 162.9 %all-gather.48.cloned.1.call-start = ((), (), s32[]{:S(2)}) async-start(), calls=%async_computation.56 | async-start | bytes 2654208 | tf_op jit(solution)/shard_map/all_gather | solution.py:20
  1501.7 296.8 %reduce-scatter.33.cloned.1.call-start = ((), (), s32[]{:S(2)}) async-start(), calls=%async_computation.36 | async-start | bytes 491520 | tf_op jit(solution)/shard_map/reduce_scatter | solution.py:320
  1515.6 35.3 %copy-start.58 = (f32[768,16]{0,1:T(8,128)S(1)}, f32[768,16]{0,1:T(8,128)}, u32[]{:S(2)}) copy-start(f32[768,16]{0,1:T(8,128)} %copy-done.57) | copy-start | bytes 147460
  1515.6 35.3 %copy-start.66 = (f32[16,72]{1,0:T(8,128)S(1)}, f32[16,72]{1,0:T(8,128)}, u32[]{:S(2)}) copy-start(f32[16,72]{1,0:T(8,128)} %copy-done.65) | copy-start | bytes 13828
  1515.7 35.3 %copy-start.83 = (f32[768]{0:T(1024)S(1)}, f32[768]{0:T(1024)}, u32[]{:S(2)}) copy-start(f32[768]{0:T(1024)} %get-tuple-element.810) | copy-start | bytes 9220
  1583.5 218.7 %reduce-scatter.27.cloned.1.call-start = ((), (), s32[]{:S(2)}) async-start(), calls=%async_computation.33 | async-start | bytes 491520 | tf_op jit(solution)/shard_map/reduce_scatter | solution.py:320
  1599.9 204.7 %reduce-scatter.35.cloned.1.call-start = ((), (), s32[]{:S(2)}) async-start(), calls=%async_computation.37 | async-start | bytes 491520 | tf_op jit(solution)/shard_map/reduce_scatter | solution.py:323
  1600.0 26.2 copy-start.26
  1600.0 26.2 copy-start.117
  1626.1 37.6 %copy-start.30 = (f32[16,72,128]{2,1,0:T(8,128)}, f32[16,72,128]{2,1,0:T(8,128)S(1)}, u32[]{:S(2)}) copy-start(f32[16,72,128]{2,1,0:T(8,128)S(1)} %get-tuple-element.619) | copy-start | bytes 1769476
  1626.2 26.2 copy-start.98
  1663.5 144.5 %reduce-scatter.29.cloned.1.call-start = ((), (), s32[]{:S(2)}) async-start(), calls=%async_computation.34 | async-start | bytes 491520 | tf_op jit(solution)/shard_map/reduce_scatter | solution.py:323
  1674.7 135.7 %reduce-scatter.37.cloned.1.call-start = ((), (), s32[]{:S(2)}) async-start(), calls=%async_computation.38 | async-start | bytes 3932160 | tf_op jit(solution)/shard_map/reduce_scatter | solution.py:326
  1692.4 135.3 %reduce-scatter.31.cloned.1.call-start = ((), (), s32[]{:S(2)}) async-start(), calls=%async_computation.35 | async-start | bytes 3932160 | tf_op jit(solution)/shard_map/reduce_scatter | solution.py:326
  1712.2 178.2 %reduce-scatter.25.cloned.1.call-start = ((), (), s32[]{:S(2)}) async-start(), calls=%async_computation.32 | async-start | bytes 3932160 | tf_op jit(solution)/shard_map/reduce_scatter | solution.py:239
  1721.8 231.0 %reduce-scatter.23.cloned.1.call-start = ((), (), s32[]{:S(2)}) async-start(), calls=%async_computation.29 | async-start | bytes 3932160 | tf_op jit(solution)/shard_map/reduce_scatter | solution.py:239
  1731.0 283.0 %reduce-scatter.61.cloned.1.call-start = ((), (), s32[]{:S(2)}) async-start(), calls=%async_computation.50 | async-start | bytes 6340608 | tf_op jit(solution)/shard_map/reduce_scatter | solution.py:373
  1739.1 336.7 %reduce-scatter.59.cloned.1.call-start = ((), (), s32[]{:S(2)}) async-start(), calls=%async_computation.49 | async-start | bytes 6340608 | tf_op jit(solution)/shard_map/reduce_scatter | solution.py:373
  1748.9 388.6 %reduce-scatter.57.cloned.1.call-start = ((), (), s32[]{:S(2)}) async-start(), calls=%async_computation.48 | async-start | bytes 6340608 | tf_op jit(solution)/shard_map/reduce_scatter | solution.py:370
  1758.6 440.9 %reduce-scatter.55.cloned.1.call-start = ((), (), s32[]{:S(2)}) async-start(), calls=%async_computation.47 | async-start | bytes 6340608 | tf_op jit(solution)/shard_map/reduce_scatter | solution.py:370
  1766.8 494.7 %reduce-scatter.63.cloned.1.call-start = ((), (), s32[]{:S(2)}) async-start(), calls=%async_computation.51 | async-start | bytes 6340608 | tf_op jit(solution)/shard_map/reduce_scatter | solution.py:376
  1776.7 546.5 %reduce-scatter.65.cloned.1.call-start = ((), (), s32[]{:S(2)}) async-start(), calls=%async_computation.52 | async-start | bytes 6340608 | tf_op jit(solution)/shard_map/reduce_scatter | solution.py:376
  1786.4 581.3 %reduce-scatter.51.cloned.1.call-start = ((), (), s32[]{:S(2)}) async-start(), calls=%async_computation.45 | async-start | bytes 2359296 | tf_op jit(solution)/shard_map/reduce_scatter | solution.py:367
  1792.9 619.7 %reduce-scatter.53.cloned.1.call-start = ((), (), s32[]{:S(2)}) async-start(), calls=%async_computation.46 | async-start | bytes 2359296 | tf_op jit(solution)/shard_map/reduce_scatter | solution.py:367
  1798.5 650.3 %reduce-scatter.41.cloned.1.call-start = ((), (), s32[]{:S(2)}) async-start(), calls=%async_computation.40 | async-start | bytes 294912 | tf_op jit(solution)/shard_map/reduce_scatter | solution.py:358
  1802.1 683.6 %reduce-scatter.39.cloned.1.call-start = ((), (), s32[]{:S(2)}) async-start(), calls=%async_computation.39 | async-start | bytes 294912 | tf_op jit(solution)/shard_map/reduce_scatter | solution.py:358
  1804.4 718.5 %reduce-scatter.45.cloned.1.call-start = ((), (), s32[]{:S(2)}) async-start(), calls=%async_computation.42 | async-start | bytes 294912 | tf_op jit(solution)/shard_map/reduce_scatter | solution.py:361
  1807.9 751.8 %reduce-scatter.43.cloned.1.call-start = ((), (), s32[]{:S(2)}) async-start(), calls=%async_computation.41 | async-start | bytes 294912 | tf_op jit(solution)/shard_map/reduce_scatter | solution.py:361
  1810.2 794.3 %reduce-scatter.49.cloned.1.call-start = ((), (), s32[]{:S(2)}) async-start(), calls=%async_computation.44 | async-start | bytes 2359296 | tf_op jit(solution)/shard_map/reduce_scatter | solution.py:364
  1815.7 833.8 %reduce-scatter.47.cloned.1.call-start = ((), (), s32[]{:S(2)}) async-start(), calls=%async_computation.43 | async-start | bytes 2359296 | tf_op jit(solution)/shard_map/reduce_scatter | solution.py:364
  1832.1 1043.8 %all-reduce.22.cloned.1.call-start = ((), (), s32[]{:S(2)}) async-start(), calls=%async_computation.57 | async-start | bytes 12582912 | tf_op jit(solution)/shard_map/psum | solution.py:341
  2078.3 797.6 %copy-start.79 = (f32[8,1,256]{2,1,0:T(1,128)S(1)}, f32[8,1,256]{2,1,0:T(1,128)}, u32[]{:S(2)}) copy-start(f32[8,1,256]{2,1,0:T(1,128)} %copy-done.78) | copy-start | bytes 24580
  2078.3 797.6 %copy-start.90 = (f32[768]{0:T(1024)S(1)}, f32[768]{0:T(1024)}, u32[]{:S(2)}) copy-start(f32[768]{0:T(1024)} %copy-done.89) | copy-start | bytes 9220
  2078.3 797.6 %copy-start.92 = (f32[768]{0:T(1024)S(1)}, f32[768]{0:T(1024)}, u32[]{:S(2)}) copy-start(f32[768]{0:T(1024)} %copy-done.91) | copy-start | bytes 9220
  (108 other events, 794.4 us)
Sparse Core Ops, SparseCore 0:
  9.9 28.5 all-gather.23
  43.9 79.9 all-gather.37
  130.7 68.6 all-gather.25
  201.7 32.1 all-gather.43
  270.3 26.7 all-gather.41
  377.9 222.3 all-reduce.27
  602.2 26.3 all-gather.27
  634.0 63.9 all-gather.29
  700.1 62.1 all-gather.39
  764.0 41.9 all-gather.33
  807.9 43.7 all-gather.31
  853.5 43.7 all-gather.35
  953.1 223.6 all-reduce.25
  1223.9 222.1 all-reduce.23
  1463.3 27.4 all-gather.45
  1501.8 27.5 all-gather.47
  1583.6 17.8 reduce-scatter.32
  1604.3 18.8 reduce-scatter.26
  1663.6 17.8 reduce-scatter.34
  1684.3 18.8 reduce-scatter.28
  1705.5 59.5 reduce-scatter.36
  1767.4 60.2 reduce-scatter.30
  1830.0 60.2 reduce-scatter.24
  1892.5 60.2 reduce-scatter.22
  1956.3 57.6 reduce-scatter.60
  2017.3 58.3 reduce-scatter.58
  2079.1 58.4 reduce-scatter.56
  2141.0 58.4 reduce-scatter.54
  2203.0 58.4 reduce-scatter.62
  2264.8 58.3 reduce-scatter.64
  2326.5 41.1 reduce-scatter.50
  2371.4 41.2 reduce-scatter.52
  2415.5 33.1 reduce-scatter.40
  2452.0 33.5 reduce-scatter.38
  2489.3 33.6 reduce-scatter.44
  2526.1 33.5 reduce-scatter.42
  2562.8 41.6 reduce-scatter.48
  2608.2 41.2 reduce-scatter.46
  2651.7 224.1 all-reduce.21
where the time goes:
time: 2950 us; the launch traced here: 2940 us
  waiting for transfers between devices  1900 us (64%)
  matrix products  505 us (17%)
  other arithmetic  207 us (7%)
  blocking collectives  204 us (7%)
  local copies, waits for them, and re-layouts  60.1 us (2%)
    psum x1, waiting for transfers between devices, on_device(): lax.psum(input_normed_part.astype(jnp.bfloat16), 'feat').astype(jnp.float32)  225 us
    psum x1, waiting for transfers between devices, on_device(): lax.psum(normed_grad_part.astype(jnp.bfloat16), 'feat').astype(jnp.float32)  224 us
    psum x1, waiting for transfers between devices, on_device(): lax.psum(mixer_grad_part.astype(jnp.bfloat16), 'feat').astype(jnp.float32)  222 us
    psum x1, waiting for transfers between devices, on_device(): lax.psum(num_part.astype(jnp.bfloat16), 'feat').astype(jnp.float32)  194 us
    reduce_scatter x2, waiting for transfers between devices, on_device(): lax.psum_scatter(grad_gate.astype(jnp.bfloat16), 'seq', scatter_dimension...  121 us
    reduce_scatter x2, waiting for transfers between devices, on_device(): lax.psum_scatter(grad_down.astype(jnp.bfloat16), 'seq', scatter_dimension...  121 us
    reduce_scatter x2, waiting for transfers between devices, on_device(): lax.psum_scatter(grad_up.astype(jnp.bfloat16), 'seq', scatter_dimension=0...  120 us
    all_gather x2, waiting for transfers between devices, on_device(): branch = lax.all_gather(branch_part, 'feat', axis=1, tiled=True)  109 us
  transfers between devices with their start and end apart: 39, of which 28 were waited for; matrix products, arithmetic and copies ran while one was open for 19% of the time, Pallas kernels for 0%

commit v1 on v0

v1 whole, which is shorter than its diff:
```python
import jax
import jax.numpy as jnp
import numpy as np
from jax import lax
from jax.sharding import PartitionSpec as P

HEADS = 16
HEAD_V = 128
QK = 16
NFEAT = 160
CORES = 2
EPS = 1e-05
BF = jnp.bfloat16
F32 = jnp.float32


def feature_tables():
    left, right, scale = [-1], [-1], [1.0]
    for i in range(QK):
        left.append(i), right.append(-1), scale.append(1.0)
    for i in range(QK):
        for j in range(i, QK):
            left.append(i), right.append(j), scale.append(1.0 if i < j else 0.7071067811865476)
    padding = NFEAT - len(left)
    left, right, scale = left + [-2] * padding, right + [-2] * padding, scale + [0.0] * padding
    table = []
    for side in (left, right):
        side = np.array(side)
        table.append((0.5 * (np.arange(QK)[:, None] == side[None, :])).astype(np.float32))
        table.append((side == -1).astype(np.float32))
    return (*table, np.array(scale, np.float32))


def dot(a, b, ca=1, cb=0):
    return lax.dot_general(a, b, (((ca,), (cb,)), ((), ())), preferred_element_type=F32)


def ein(spec, *args):
    return jnp.einsum(spec, *args, preferred_element_type=F32)


def on_device(
    tokens,
    cotangent,
    lengths,
    w_query,
    w_key,
    w_value,
    w_output,
    w_gate,
    w_up,
    w_down,
    gain_mixer,
    gain_mlp,
):
    micro, block, width = tokens.shape
    seq_count, feat_count = lax.axis_size("seq"), lax.axis_size("feat")
    seq_rank, feat_rank = lax.axis_index("seq"), lax.axis_index("feat")
    group = feat_count // micro
    ranks = CORES * group
    chips = seq_count // CORES
    chip, core = seq_rank // CORES, seq_rank % CORES
    batch, part = feat_rank // group, feat_rank % group
    rank = core * group + part
    rows = CORES * block
    piece = width // ranks
    heads = HEADS // ranks

    def move(value, target):
        pairs = []
        for s in range(seq_count):
            for f in range(feat_count):
                there = target(s // CORES, s % CORES, f // group, f % group)
                if there is not None:
                    c2, k2, m2, l2 = there
                    pairs.append(
                        (s * feat_count + f, (c2 * CORES + k2) * feat_count + m2 * group + l2)
                    )
        return lax.ppermute(value, ("seq", "feat"), pairs)

    def to_core(value):
        return move(value, lambda c, k, m, l: (c, 1 - k, m, l))

    def to_part(value, d):
        return move(value, lambda c, k, m, l: (c, k, m, l ^ d))

    def to_chip(value, mask):
        return move(value, lambda c, k, m, l: (c ^ mask, k, m, l))

    def shift_chip(value, d):
        return move(value, lambda c, k, m, l: (c + d, k, m, l) if 0 <= c + d < chips else None)

    def spread(value):
        return (
            move(value, lambda c, k, m, l: (c, m, k, l)),
            move(value, lambda c, k, m, l: (c, m, 1 - k, l)),
        )

    def unspread(same, other):
        return (
            move(same, lambda c, k, m, l: (c, m, k, l)),
            move(other, lambda c, k, m, l: (c, 1 - m, k, l)),
        )

    def ordered(first_if_zero, second_if_zero, bit, axis):
        return jnp.where(
            bit == 0,
            jnp.concatenate([first_if_zero, second_if_zero], axis),
            jnp.concatenate([second_if_zero, first_if_zero], axis),
        )

    def gather_chips(value):
        size = value.shape[0]
        bits = [1 << i for i in range(chips.bit_length() - 1)]
        full = jnp.zeros((size * seq_count, value.shape[1]), value.dtype)
        for own, order, k in zip(spread(value), (bits, bits[::-1]), (batch, 1 - batch)):
            held = {0: own}
            for bit in order:
                for mask in list(held):
                    held[mask | bit] = to_chip(held[mask], bit)
            for mask, got in held.items():
                at = ((chip ^ mask) * CORES + k) * size
                full = lax.dynamic_update_slice_in_dim(full, got, at, 0)
        return full

    chip_groups = [[c * CORES + k for c in range(chips)] for k in range(CORES)]

    def gather_chips_bulk(value, axis):
        same, other = spread(value)
        return lax.all_gather(
            ordered(same, other, batch, axis),
            "seq",
            axis=axis,
            tiled=True,
            axis_index_groups=chip_groups,
        )

    def scatter_chips(value, axis):
        mine = lax.psum_scatter(
            value.astype(BF),
            "seq",
            scatter_dimension=axis,
            tiled=True,
            axis_index_groups=chip_groups,
        )
        size = mine.shape[axis] // CORES
        same = lax.dynamic_slice_in_dim(mine, batch * size, size, axis)
        other = lax.dynamic_slice_in_dim(mine, (1 - batch) * size, size, axis)
        a, b = unspread(same, other)
        return a.astype(F32) + b.astype(F32)

    def gather_ranks(own):
        found = []
        for d in range(group):
            here = own if d == 0 else to_part(own, d)
            found.append((core * group + (part ^ d), here))
            found.append(((1 - core) * group + (part ^ d), to_core(here)))
        return found

    def reduce_ranks(partial):
        arrived = []
        for d in range(group - 1, -1, -1):
            away = to_core(partial((1 - core) * group + (part ^ d)).astype(BF))
            total = partial(core * group + (part ^ d)) + away.astype(F32)
            arrived.append(to_part(total.astype(BF), d).astype(F32) if d else total)
        return sum(arrived[:-1], arrived[-1])

    def sum_ranks(value):
        for d in [1 << i for i in range(group.bit_length() - 1)]:
            value = value + to_part(value, d)
        return value + to_core(value)

    def row_piece(value, r):
        return lax.dynamic_slice_in_dim(value, r * piece, piece, 0)

    def column_piece(value, r):
        return lax.dynamic_slice_in_dim(value, r * piece, piece, 1)

    qkv_full = gather_chips(jnp.concatenate([w_query, w_key, w_value], 1))
    qk_width, v_width = heads * QK, heads * HEAD_V
    gains = lax.all_gather(jnp.stack([gain_mixer, gain_mlp]), "seq", axis=1, tiled=True)
    gains = gains.astype(F32)
    mixer_gain, mlp_gain = gains[0], gains[1]
    output_full = gather_chips(w_output)
    gate_full = gather_chips_bulk(w_gate, 0)
    up_full = gather_chips_bulk(w_up, 0)
    down_full = gather_chips_bulk(w_down, 1)

    def chip_tokens(value):
        own = lax.dynamic_index_in_dim(value, batch, 0, False)
        return ordered(own, to_core(own), core, 0)

    tokens_c = chip_tokens(tokens)
    grad_out = chip_tokens(cotangent)

    bounds = jnp.cumsum(lax.dynamic_index_in_dim(lengths, batch, 0, False))

    def segment_of(p):
        return jnp.sum((p[..., None] >= bounds).astype(jnp.int32), axis=-1)

    start = chip * rows
    segment = segment_of(start + jnp.arange(rows, dtype=jnp.int32))
    valid = segment < 3
    valid_f = valid.astype(F32)
    edges = segment_of(start - 1 + block * jnp.arange(CORES + 1, dtype=jnp.int32))
    edges = jnp.where((jnp.arange(CORES + 1) == 0) & (start == 0), -1, edges)
    before, last = jnp.repeat(edges[:-1], block), jnp.repeat(edges[1:], block)
    use = (valid & (segment == before)).astype(F32)
    tail = (valid & (segment == last)).astype(F32)
    keep = (edges[1:] == edges[:-1]).astype(F32)
    segment_b, valid_b = segment.reshape(CORES, block), valid.reshape(CORES, block)
    order = jnp.arange(block)
    mask = (
        (order[None, None, :] <= order[None, :, None])
        & (segment_b[:, None, :] == segment_b[:, :, None])
        & valid_b[:, None, :]
    )[:, None]

    tokens_f = tokens_c.astype(F32)
    inv_one = lax.rsqrt(jnp.mean(tokens_f * tokens_f, axis=-1, keepdims=True) + EPS)
    normed = (tokens_f * inv_one * mixer_gain).astype(BF)
    qkv = dot(normed, qkv_full).astype(BF)

    def by_head(value, size):
        return value.reshape(CORES, block, heads, size).transpose(0, 2, 1, 3)

    def from_head(value):
        return value.transpose(0, 2, 1, 3).reshape(rows, -1)

    query = by_head(qkv[:, :qk_width], QK)
    keys = by_head(qkv[:, qk_width : 2 * qk_width], QK)
    values = by_head(qkv[:, 2 * qk_width :], HEAD_V)
    pick_l, one_l, pick_r, one_r, scale = feature_tables()
    pick_l, pick_r = jnp.asarray(pick_l, BF), jnp.asarray(pick_r, BF)

    def sides(x):
        return ein("bhti,ij->bhtj", x, pick_l) + one_l, ein("bhti,ij->bhtj", x, pick_r) + one_r

    def features(x):
        left, right = sides(x)
        return (left * right * scale).astype(BF)

    def features_back(x, grad):
        left, right = sides(x)
        grad = grad * scale
        return ein("bhtj,ij->bhti", (grad * right).astype(BF), pick_l) + ein(
            "bhtj,ij->bhti", (grad * left).astype(BF), pick_r
        )

    feat_q, feat_k = features(query), features(keys)
    use_b, tail_b = use.reshape(CORES, 1, block, 1), tail.reshape(CORES, 1, block, 1)
    tail_k = feat_k * tail_b.astype(BF)
    local_state = ein("bhsf,bhsc->bhfc", tail_k, values)
    local_sum = jnp.sum(tail_k, axis=2, dtype=F32)

    def pack(state, total):
        total = jnp.pad(total, ((0, 0), (0, -NFEAT % HEAD_V))).reshape(-1, HEAD_V)
        return jnp.concatenate([state.reshape(-1, HEAD_V), total], 0).astype(BF)

    def unpack(flat):
        flat = flat.astype(F32)
        cut = heads * NFEAT
        return (
            flat[:cut].reshape(heads, NFEAT, HEAD_V),
            flat[cut:].reshape(heads, -1)[:, :NFEAT],
        )

    def scan_blocks(state, total, blocks_order, step):
        at_end = (state[blocks_order[0]], total[blocks_order[0]])
        for i in blocks_order[1:]:
            carry_keep = keep[i]
            at_end = (
                state[i] + carry_keep * at_end[0],
                total[i] + carry_keep * at_end[1],
            )
        message = pack(*at_end)
        run = None
        for d in range(1, chips):
            got = unpack(shift_chip(message, step * d))
            other = chip - step * d
            if step > 0:
                same = edges[0] == segment_of((other + 1) * rows - 1)
            else:
                same = edges[CORES] == segment_of(other * rows - 1)
            weight = (same & (other >= 0) & (other < chips)).astype(F32)
            term = (weight * got[0], weight * got[1])
            run = term if run is None else (run[0] + term[0], run[1] + term[1])
        found = {}
        for i in blocks_order:
            found[i] = run
            run = (state[i] + keep[i] * run[0], total[i] + keep[i] * run[1])
        return tuple(jnp.stack([found[i][j] for i in range(CORES)]) for j in range(2))

    state, total = scan_blocks(local_state, local_sum, list(range(CORES)), 1)
    state_b = state.astype(BF)
    total_high = total.astype(BF)
    total_low = (total - total_high.astype(F32)).astype(BF)
    total_two = jnp.stack([total_high, total_low], -1)

    products = ein("bhti,bhsi->bhts", query, keys) * 0.25
    scores = jnp.where(mask, 1.0 + products + 0.5 * products * products, 0.0).astype(BF)
    numer = ein("bhts,bhsc->bhtc", scores, values)
    numer = numer + use_b * ein("bhtf,bhfc->bhtc", feat_q, state_b)
    denom = jnp.sum(scores, axis=3, dtype=F32)[..., None]
    denom = denom + use_b * jnp.sum(
        ein("bhtf,bhfe->bhte", feat_q, total_two), axis=3, keepdims=True
    )
    safe = denom + (1.0 - valid_f.reshape(CORES, 1, block, 1))
    mixer_own = from_head((numer / safe).astype(BF))

    mixer_parts = gather_ranks(mixer_own)
    branch_own = sum(dot(got, row_piece(output_full, r)) for r, got in mixer_parts).astype(BF)
    branch = jnp.zeros((rows, width), BF)
    for r, got in gather_ranks(branch_own):
        branch = lax.dynamic_update_slice_in_dim(branch, got, r * piece, 1)
    hidden_state = tokens_f + branch.astype(F32)
    inv_two = lax.rsqrt(jnp.mean(hidden_state * hidden_state, axis=-1, keepdims=True) + EPS)
    normed_two = (hidden_state * inv_two * mlp_gain).astype(BF)

    grad_hidden = dot(grad_out, down_full, 1, 1).astype(BF).astype(F32)
    gate = dot(normed_two, gate_full).astype(BF).astype(F32)
    upward = dot(normed_two, up_full).astype(BF).astype(F32)
    logistic = jax.nn.sigmoid(gate)
    activated = gate * logistic
    hidden = (activated * upward).astype(BF)
    grad_gate_f = grad_hidden * upward * logistic * (1.0 + gate * (1.0 - logistic))
    grad_up_f = grad_hidden * activated
    grad_gate_b, grad_up_b = grad_gate_f.astype(BF), grad_up_f.astype(BF)
    inner_two = sum_ranks(jnp.sum(grad_gate_f * gate + grad_up_f * upward, axis=1)) / width
    normed_grad = reduce_ranks(
        lambda r: dot(grad_gate_b, row_piece(gate_full, r), 1, 1)
        + dot(grad_up_b, row_piece(up_full, r), 1, 1)
    )
    tokens_own = column_piece(tokens_c, rank).astype(F32)
    hidden_own = tokens_own + branch_own.astype(F32)
    scaled_two = hidden_own * inv_two
    mlp_gain_own = lax.dynamic_slice_in_dim(mlp_gain, rank * piece, piece, 0)
    hidden_grad = column_piece(grad_out, rank).astype(F32) + inv_two * (
        normed_grad * mlp_gain_own - scaled_two * inner_two[:, None]
    )
    grad_gain_mlp = jnp.sum(normed_grad * scaled_two, axis=0)
    branch_grad = hidden_grad.astype(BF)

    mixer_grad = reduce_ranks(lambda r: dot(branch_grad, row_piece(output_full, r), 1, 1))
    mixer_grad = by_head(mixer_grad, HEAD_V)
    mixer_f = by_head(mixer_own, HEAD_V).astype(F32)
    grad_numer = (mixer_grad / safe).astype(BF)
    grad_denom = -jnp.sum(mixer_grad * mixer_f, axis=3, keepdims=True) / safe
    use_q = feat_q * use_b.astype(BF)
    grad_state = ein("bhtf,bhtc->bhfc", use_q, grad_numer)
    grad_sum = jnp.sum(use_q.astype(F32) * grad_denom, axis=2)
    carried, carried_sum = scan_blocks(grad_state, grad_sum, list(range(CORES))[::-1], -1)
    carried_b = carried.astype(BF)
    grad_scores = jnp.where(
        mask, ein("bhtc,bhsc->bhts", grad_numer, values) + grad_denom, 0.0
    ).astype(BF)
    grad_products = (grad_scores.astype(F32) * (0.25 + 0.25 * products)).astype(BF)
    grad_fq = use_b * (
        ein("bhtc,bhfc->bhtf", grad_numer, state_b) + grad_denom * total[:, :, None, :]
    )
    grad_fk = tail_b * (
        ein("bhsc,bhfc->bhsf", values, carried_b) + carried_sum[:, :, None, :]
    )
    grad_query = ein("bhts,bhsi->bhti", grad_products, keys) + features_back(query, grad_fq)
    grad_keys = ein("bhts,bhti->bhsi", grad_products, query) + features_back(keys, grad_fk)
    grad_values = ein("bhts,bhtc->bhsc", scores, grad_numer) + tail_b * ein(
        "bhsf,bhfc->bhsc", feat_k, carried_b
    )
    grad_qkv = jnp.concatenate(
        [from_head(g.astype(BF)) for g in (grad_query, grad_keys, grad_values)], 1
    )
    inner_one = jnp.sum(grad_qkv.astype(F32) * qkv.astype(F32), axis=1)
    inner_one = sum_ranks(inner_one) / width
    input_normed = reduce_ranks(lambda r: dot(grad_qkv, row_piece(qkv_full, r), 1, 1))
    scaled_one = tokens_own * inv_one
    mixer_gain_own = lax.dynamic_slice_in_dim(mixer_gain, rank * piece, piece, 0)
    grad_gain_mixer = jnp.sum(input_normed * scaled_one, axis=0)
    input_own = (
        hidden_grad
        + inv_one * (input_normed * mixer_gain_own - scaled_one * inner_one[:, None])
    ).astype(BF)

    def half(value, k):
        return lax.dynamic_slice_in_dim(value, k * block, block, 0)

    input_pair = ordered(
        half(input_own, core)[None], to_core(half(input_own, 1 - core))[None], core, 0
    )
    input_grad = lax.all_gather(input_pair, "feat", axis=0)
    input_grad = input_grad.reshape(micro, group, CORES, block, piece)
    input_grad = input_grad.transpose(0, 3, 2, 1, 4).reshape(micro, block, width).astype(F32)

    mlp_own = reduce_ranks(lambda r: dot(hidden, column_piece(down_full, r)))
    mixed_own = (hidden_own + mlp_own).astype(BF)
    same, other = unspread(half(mixed_own, batch), half(mixed_own, 1 - batch))
    mixed = ordered(same[None], other[None], core, 0)

    grad_gate = scatter_chips(dot(normed_two, grad_gate_b, 0, 0), 0)
    grad_up = scatter_chips(dot(normed_two, grad_up_b, 0, 0), 0)
    grad_down = scatter_chips(dot(hidden, grad_out, 0, 0), 1)
    grad_output = jnp.zeros((width, piece), BF)
    for r, got in mixer_parts:
        grad_output = lax.dynamic_update_slice_in_dim(
            grad_output, dot(got, branch_grad, 0, 0).astype(BF), r * piece, 0
        )
    grad_output = scatter_chips(grad_output, 0)
    grad_qkv_w = scatter_chips(dot(normed, grad_qkv, 0, 0), 0)

    gain_grads = lax.dynamic_update_slice_in_dim(
        jnp.zeros((2, width), F32), jnp.stack([grad_gain_mixer, grad_gain_mlp]), rank * piece, 1
    )
    gain_grads = lax.psum(gain_grads, ("seq", "feat"))
    shard = width // seq_count
    gain_grads = lax.dynamic_slice_in_dim(gain_grads, seq_rank * shard, shard, 1)
    return (
        mixed,
        input_grad,
        grad_qkv_w[:, :qk_width],
        grad_qkv_w[:, qk_width : 2 * qk_width],
        grad_qkv_w[:, 2 * qk_width :],
        grad_output,
        grad_gate,
        grad_up,
        grad_down,
        gain_grads[0],
        gain_grads[1],
    )


def solution(mesh):
    in_specs = (
        P(None, "seq", None),
        P(None, "seq", None),
        P(),
        P("seq", "feat"),
        P("seq", "feat"),
        P("seq", "feat"),
        P("seq", "feat"),
        P("seq", "feat"),
        P("seq", "feat"),
        P("feat", "seq"),
        P("seq"),
        P("seq"),
    )
    out_specs = (
        P(None, "seq", "feat"),
        P(None, "seq", None),
        P("seq", "feat"),
        P("seq", "feat"),
        P("seq", "feat"),
        P("seq", "feat"),
        P("seq", "feat"),
        P("seq", "feat"),
        P("feat", "seq"),
        P("seq"),
        P("seq"),
    )
    return jax.shard_map(
        on_device, mesh=mesh, in_specs=in_specs, out_specs=out_specs, check_vma=False
    )
```

time: 2950 us -> 1100 us (0.37)
  waiting for transfers between devices: 1900 us -> 341 us
  matrix products: 505 us -> 273 us
  other arithmetic: 207 us -> 75.1 us
  starting transfers between devices: 15.3 us -> 139 us
  blocking collectives: 204 us -> 117 us
  local copies, waits for them, and re-layouts: 60.1 us -> 129 us
    psum x4 -> x0, waiting for transfers between devices: 865 us -> none  [the longest x1 225 us: on_device(): lax.psum(input_normed_part.astype(jnp.bfloat16), 'feat').astype(jnp.float32)]
    reduce_scatter x22 -> x5, waiting for transfers between devices: 799 us -> 0.06 us  [scatter_chips(): lax.psum_scatter(value.astype(BF), 'seq', scatter_dimension=axis, tiled=T...]
    ppermute x0 -> x65, waiting for transfers between devices: none -> 341 us  [move(): return lax.ppermute(value, ('seq', 'feat'), pairs)]
    all_gather x13 -> x4, waiting for transfers between devices: 234 us -> 0.01 us  [the longest x3 0.01 us: gather_chips_bulk(): lax.all_gather(ordered(same, other, batch, axis), 'seq', axis=axis, tiled...]
    dot_general x86 -> x57, matrix products: 505 us -> 273 us  [the longest x36 210 us: dot(): lax.dot_general(a, b, (((ca,), (cb,)), ((), ())), preferred_element_type=...]
    ppermute x0 -> x65, starting transfers between devices: none -> 137 us  [move(): return lax.ppermute(value, ('seq', 'feat'), pairs)]
    all_gather x12 -> x1, blocking collectives: 141 us -> 7.78 us  [on_device(): lax.all_gather(jnp.stack([gain_mixer, gain_mlp]), 'seq', axis=1, tiled=True)]
    psum x1, blocking collectives: 20.8 us -> 109 us  [on_device(): gain_grads = lax.psum(gain_grads, ('seq', 'feat'))]
  transfers between devices with their start and end apart: 39 -> 74, of which waited for: 28 -> 22; matrix products, arithmetic and copies ran while one was open for 19% -> 34% of each run, Pallas kernels for 0% -> 0%
where the time goes in v1:
time: 1100 us
  waiting for transfers between devices  341 us (31%)
  matrix products  273 us (25%)
  starting transfers between devices  139 us (13%)
  local copies, waits for them, and re-layouts  129 us (12%)
  blocking collectives  117 us (11%)
  other arithmetic  75.1 us (7%)
  between operations  24 us (2%)
    ppermute x65, waiting for transfers between devices, move(): return lax.ppermute(value, ('seq', 'feat'), pairs)  341 us
    dot_general x36, matrix products, dot(): lax.dot_general(a, b, (((ca,), (cb,)), ((), ())), preferred_element_type=...  210 us
    ppermute x65, starting transfers between devices, move(): return lax.ppermute(value, ('seq', 'feat'), pairs)  137 us
    psum x1, blocking collectives, on_device(): gain_grads = lax.psum(gain_grads, ('seq', 'feat'))  109 us
    dot_general x21, matrix products, ein(): return jnp.einsum(spec, *args, preferred_element_type=F32)  62.4 us
    convert_element_type x2, local copies, waits for them, and re-layouts, on_device(): input_grad.transpose(0, 3, 2, 1, 4).reshape(micro, block, width).astype(F32)  36.3 us
  transfers between devices with their start and end apart: 74, of which 22 were waited for; matrix products, arithmetic and copies ran while one was open for 34% of the time, Pallas kernels for 0%

profile of v1, /device:TPU:7, one launch (start us, length us, event | category | flops | bytes accessed | tf_op | source)
XLA Modules:
  0.0 1097.3 jit_solution(12352814480450119286)
XLA Ops:
  8.0 4.1 collective-permute-start.30
  12.1 27.7 %collective-permute-done.31 = bf16[1376,256]{1,0:T(8,128)(2,1)S(1)} collective-permute-done((bf16[1376,256]{1,0:T(8,128)(2,1)}, bf16[1376,256]{1,0:T(8,128)(2,1)S(1)}, u32[]{:S(2)}, u32[]{:S(2)}) %collective-permute-start.31) | collective-permute-done | bytes 704544 | tf_op jit(solution)/shard_map/ppermute | solution.py:79
  52.1 5.2 collective-permute-start
  58.6 7.8 all_gather.16
  79.0 15.2 %collective-permute-done.2 = bf16[256,640]{1,0:T(8,128)(2,1)} collective-permute-done((bf16[256,640]{1,0:T(8,128)(2,1)}, bf16[256,640]{1,0:T(8,128)(2,1)}, u32[]{:S(2)}, u32[]{:S(2)}) %collective-permute-start.2) | collective-permute-done | bytes 327712 | tf_op jit(solution)/shard_map/ppermute | solution.py:79
  101.7 9.5 collective-permute-done.6
  116.5 8.3 collective-permute-done.4
  132.5 4.9 fusion
  137.5 8.7 convolution_convert_fusion.7
  150.7 4.1 convert_reduce_fusion.1
  168.0 10.2 convert_reduce_fusion
  178.2 3.7 fusion.43
  196.0 6.8 collective-permute-start.12
  202.9 30.7 %collective-permute-done.12 = bf16[256,512]{1,0:T(8,128)(2,1)} collective-permute-done((bf16[256,512]{1,0:T(8,128)(2,1)}, bf16[256,512]{1,0:T(8,128)(2,1)}, u32[]{:S(2)}, u32[]{:S(2)}) %collective-permute-start.12) | collective-permute-done | bytes 262176 | tf_op jit(solution)/shard_map/ppermute | solution.py:79
  238.4 4.0 dynamic-slice_bitcast_fusion
  249.8 5.6 collective-permute-done.15
  261.9 8.7 collective-permute-start.26
  283.4 4.4 collective-permute-done.27
  287.9 4.5 collective-permute-done.26
  294.2 8.2 maximum_select_fusion.1
  302.4 24.0 %collective-permute-done.24 = bf16[1536,512]{1,0:T(8,128)(2,1)} collective-permute-done((bf16[1536,512]{1,0:T(8,128)(2,1)S(1)}, bf16[1536,512]{1,0:T(8,128)(2,1)}, u32[]{:S(2)}, u32[]{:S(2)}) %collective-permute-start.24) | collective-permute-done | bytes 1572896 | tf_op jit(solution)/shard_map/ppermute | solution.py:79
  332.0 14.5 %convolution_convert_fusion.3 = bf16[1536,1376]{0,1:T(8,128)(2,1)} fusion(bf16[1536,2048]{1,0:T(8,128)(2,1)} %maximum_select_fusion.1, bf16[1376,2048]{1,0:T(8,128)(2,1)} %all-gather.9.cloned.1.call-done), kind=kOutput, calls=%fused_computation.33 | convolution fusion | flops 8659156992 | bytes 16154624 | tf_op jit(solution)/shard_map/dot_general | solution.py:35
  349.3 6.8 multiply_reduce_fusion
  356.2 8.0 multiply_convert_fusion.1
  364.3 14.1 %convolution_convert_fusion.4 = bf16[1536,1376]{0,1:T(8,128)(2,1)} fusion(bf16[1536,2048]{1,0:T(8,128)(2,1)} %multiply_convert_fusion.1, bf16[2048,1376]{0,1:T(8,128)(2,1)} %all-gather.7.cloned.1.call-done), kind=kOutput, calls=%fused_computation.34 | convolution fusion | flops 8659156992 | bytes 16154624 | tf_op jit(solution)/shard_map/dot_general | solution.py:35
  378.3 22.0 %fusion.18 = (bf16[1536,1376]{0,1:T(8,128)(2,1)}, f32[1536]{0:T(1024)S(1)}, bf16[1536,1376]{0,1:T(8,128)(2,1)S(1)}, bf16[1536,1376]{0,1:T(8,128)(2,1)}) fusion(bf16[1536,1376]{0,1:T(8,128)(2,1)} %convolution_convert_fusion.4, bf16[1536,1376]{0,1:T(8,128)(2,1)} %convolution_convert_fusion.3, bf16[1536,2048]{1,0:T(8,128)(2,1)} %multiply_convert_fusion.1, ...), kind=kOutput, calls=%fused_computation.70 | convolution fusion | flops 8705652736 | bytes 33069056 | tf_op jit(solution)/shard_map/dot_general | solution.py:35
  400.4 6.2 fusion.51
  422.8 34.6 %collective-permute-done.41 = f32[1536]{0:T(1024)S(1)} collective-permute-done((f32[1536]{0:T(1024)S(1)}, f32[1536]{0:T(1024)S(1)}, u32[]{:S(2)}, u32[]{:S(2)}) %collective-permute-start.41) | collective-permute-done | bytes 6176 | tf_op jit(solution)/shard_map/ppermute | solution.py:79
  461.3 11.0 %fusion.180 = (bf16[1536,512]{1,0:T(8,128)(2,1)S(1)}, f32[1536,512]{1,0:T(8,128)}, f32[1536,512]{1,0:T(8,128)}) fusion(f32[1536]{0:T(1024)S(1)} %add_multiply_fusion.1, bf16[1536,512]{1,0:T(8,128)(2,1)S(1)} %copy-done.32, bf16[1536,2048]{1,0:T(8,128)(2,1)} %copy-done.2, s32[]{:T(128)S(6)} %select_n.202, f32[512]{0:T(512)S(1)} %bitcast.275, ...), kind=kOutput, calls=%fused_computation.362 | convolution fusion | flops 2176843776 | bytes 24529920 | tf_op jit(solution)/shard_map/dot_general | solution.py:35
  482.7 13.9 %convolution_convert_fusion.1 = bf16[2048,1376]{0,1:T(8,128)(2,1)} fusion(bf16[1536,1376]{0,1:T(8,128)(2,1)} %get-tuple-element.83, bf16[1536,2048]{1,0:T(8,128)(2,1)} %multiply_convert_fusion.1), kind=kOutput, calls=%fused_computation.31 | convolution fusion | flops 8659861504 | bytes 16154624 | tf_op jit(solution)/shard_map/dot_general | solution.py:35
  496.7 14.5 %convolution_convert_fusion = bf16[2048,1376]{0,1:T(8,128)(2,1)} fusion(bf16[1536,1376]{0,1:T(8,128)(2,1)} %copy-done.107, bf16[1536,2048]{1,0:T(8,128)(2,1)} %multiply_convert_fusion.1), kind=kOutput, calls=%fused_computation.30 | convolution fusion | flops 8659861504 | bytes 16154624 | tf_op jit(solution)/shard_map/dot_general | solution.py:35
  517.6 6.7 convolution_convert_fusion.12
  524.6 5.3 convolution_convert_fusion.13
  534.9 10.6 convolution_convert_fusion.2
  545.7 25.4 %collective-permute-done.45 = bf16[1536,512]{1,0:T(8,128)(2,1)} collective-permute-done((bf16[1536,512]{1,0:T(8,128)(2,1)}, bf16[1536,512]{1,0:T(8,128)(2,1)}, u32[]{:S(2)}, u32[]{:S(2)}) %collective-permute-start.45) | collective-permute-done | bytes 1572896 | tf_op jit(solution)/shard_map/ppermute | solution.py:79
  571.1 4.5 fusion.15
  581.6 3.6 fusion.25
  603.5 11.5 %multiply_convert_fusion = bf16[2,4,768,768]{2,3,1,0:T(8,128)(2,1)} fusion(f32[2,4,768,768]{2,3,1,0:T(8,128)} %get-tuple-element.125, f32[2,4,768]{2,1,0:T(4,128)S(1)} %bitcast.259, pred[2,768,768]{1,2,0:T(8,128)(4,1)S(1)} %copy-done.51, bf16[2,4,768,128]{2,3,1,0:T(8,128)(2,1)S(1)} %get-tuple-element.90, bf16[2,768,4,128]{1,0,3,2:T(2,128)(2,1)S(1)} %copy-done.11), kind=kOutput, calls=%fused_computation.3 | convolution fusion | flops 1245708288 | bytes 32661504 | tf_op jit(solution)/shard_map/bhtc,bhsc->bhts/dot_general | solution.py:39
  615.0 5.2 fusion.80
  620.5 8.1 fusion.193
  653.6 4.3 copy.122
  659.0 4.0 convolution_convert_fusion.10
  663.8 7.2 convolution_convert_fusion.6
  671.0 7.6 add_convert_fusion.3
  679.0 3.8 convolution_convert_fusion.11
  682.8 4.4 fusion.31
  690.0 59.1 %collective-permute-done.52 = f32[1536]{0:T(1024)} collective-permute-done((f32[1536]{0:T(1024)S(1)}, f32[1536]{0:T(1024)}, u32[]{:S(2)}, u32[]{:S(2)}) %collective-permute-start.52) | collective-permute-done | bytes 6176 | tf_op jit(solution)/shard_map/ppermute | solution.py:79
  750.4 5.6 fusion.70
  757.3 7.0 fusion.23
  770.1 4.8 collective-permute-start.58
  777.0 4.5 collective-permute-start.35
  781.5 40.2 %collective-permute-done.57 = bf16[256,512]{1,0:T(8,128)(2,1)} collective-permute-done((bf16[256,512]{1,0:T(8,128)(2,1)S(1)}, bf16[256,512]{1,0:T(8,128)(2,1)}, u32[]{:S(2)}, u32[]{:S(2)}) %collective-permute-start.57) | collective-permute-done | bytes 262176 | tf_op jit(solution)/shard_map/ppermute | solution.py:79
  823.6 109.4 %psum.7 = f32[2,2048]{1,0:T(2,128)S(1)} all-reduce(f32[2,2048]{1,0:T(2,128)S(1)} %constant_dynamic-update-slice_fusion), channel_id=1, replica_groups=mesh['seq'=8,'feat'=4] {'seq','feat'}, use_global_device_ids=true, to_apply=%region_25.26 | all-reduce | flops 4096 | bytes 32768 | tf_op jit(solution)/shard_map/psum | solution.py:412
  938.5 4.6 collective-permute-start.59
  945.9 4.8 collective-permute-start.62
  955.5 34.3 %collective-permute-start.63 = (bf16[1376,256]{1,0:T(8,128)(2,1)S(1)}, bf16[1376,256]{1,0:T(8,128)(2,1)S(1)}, u32[]{:S(2)}, u32[]{:S(2)}) collective-permute-start(bf16[1376,256]{1,0:T(8,128)(2,1)S(1)} %get-tuple-element.97), channel_id=1, source_target_pairs={{0,0},{1,1},{2,4},{3,5},{4,2},{5,3},{6,6},{7,7},{8,8},{9,9},{10,12... | collective-permute-start | bytes 2113544 | tf_op jit(solution)/shard_map/ppermute | solution.py:79
  989.8 13.4 %collective-permute-done.59 = bf16[256,1376]{0,1:T(8,128)(2,1)} collective-permute-done((bf16[256,1376]{0,1:T(8,128)(2,1)}, bf16[256,1376]{0,1:T(8,128)(2,1)}, u32[]{:S(2)}, u32[]{:S(2)}) %collective-permute-start.59) | collective-permute-done | bytes 704544 | tf_op jit(solution)/shard_map/ppermute | solution.py:79
  1005.7 10.1 collective-permute-start.55
  1015.9 9.4 collective-permute-done.61
  1027.6 12.7 %collective-permute-done.63 = bf16[1376,256]{1,0:T(8,128)(2,1)S(1)} collective-permute-done((bf16[1376,256]{1,0:T(8,128)(2,1)S(1)}, bf16[1376,256]{1,0:T(8,128)(2,1)S(1)}, u32[]{:S(2)}, u32[]{:S(2)}) %collective-permute-start.63) | collective-permute-done | bytes 704544 | tf_op jit(solution)/shard_map/ppermute | solution.py:79
  1042.6 4.7 collective-permute-done.55
  1049.7 4.5 convert_bitcast_fusion
  1054.3 19.3 %copy.123 = f32[2,768,2,2,512]{4,3,2,1,0:T(2,128)} copy(f32[2,768,2,2,512]{4,1,2,3,0:T(8,128)S(1)} %convert_bitcast_fusion) | data formatting | bytes 25165824 | tf_op jit(solution)/shard_map/convert_element_type | solution.py:391
  1073.6 17.0 %reshape.581 = f32[2,768,2048]{2,1,0:T(8,128)} reshape(f32[2,768,2,2,512]{4,3,2,1,0:T(2,128)} %copy.123) | data formatting | bytes 25165824 | tf_op jit(solution)/shard_map/convert_element_type | solution.py:391
  (552 shorter events, 243.9 us)
Async XLA Ops:
  7.2 324.8 %all-gather.9.cloned.1.call-start = ((), (), s32[]{:S(2)}) async-start(), calls=%async_computation.7 | async-start | bytes 7045120 | tf_op jit(solution)/shard_map/all_gather | solution.py:130
  7.3 32.6 %collective-permute-start.31 = (bf16[1376,256]{1,0:T(8,128)(2,1)}, bf16[1376,256]{1,0:T(8,128)(2,1)S(1)}, u32[]{:S(2)}, u32[]{:S(2)}) collective-permute-start(bf16[1376,256]{1,0:T(8,128)(2,1)} %param.26), channel_id=1, source_target_pairs={{0,2},{1,3},{2,6},{3,7},{4,0},{5,1},{6,4},{7,5},{8,10},{9,11},{10,... | collective-permute-start | bytes 2113544 | tf_op jit(solution)/shard_map/ppermute | solution.py:79
  8.0 33.0 %collective-permute-start.30 = (bf16[1376,256]{1,0:T(8,128)(2,1)}, bf16[1376,256]{1,0:T(8,128)(2,1)S(1)}, u32[]{:S(2)}, u32[]{:S(2)}) collective-permute-start(bf16[1376,256]{1,0:T(8,128)(2,1)} %param.26), channel_id=1, source_target_pairs={{0,0},{1,1},{2,4},{3,5},{4,2},{5,3},{6,6},{7,7},{8,8},{9,9},{10,12... | collective-permute-start | bytes 2113544 | tf_op jit(solution)/shard_map/ppermute | solution.py:79
  42.5 321.7 %all-gather.7.cloned.1.call-start = ((), (), s32[]{:S(2)}) async-start(), calls=%async_computation.6 | async-start | bytes 7045120 | tf_op jit(solution)/shard_map/all_gather | solution.py:130
  43.0 35.0 %collective-permute-start.1 = (bf16[256,640]{1,0:T(8,128)(2,1)S(1)}, bf16[256,640]{1,0:T(8,128)(2,1)}, u32[]{:S(2)}, u32[]{:S(2)}) collective-permute-start(bf16[256,640]{1,0:T(8,128)(2,1)S(1)} %pad_maximum_fusion), channel_id=1, source_target_pairs={{0,0},{1,1},{2,4},{3,5},{4,2},{5,3},{6,6},{7,7},{8,8},{9,9},{10,12... | collective-permute-start | bytes 983048 | tf_op jit(solution)/shard_map/ppermute | solution.py:79
  44.9 33.4 %collective-permute-start.5 = (bf16[256,640]{1,0:T(8,128)(2,1)S(1)}, bf16[256,640]{1,0:T(8,128)(2,1)}, u32[]{:S(2)}, u32[]{:S(2)}) collective-permute-start(bf16[256,640]{1,0:T(8,128)(2,1)S(1)} %pad_maximum_fusion), channel_id=1, source_target_pairs={{0,2},{1,3},{2,6},{3,7},{4,0},{5,1},{6,4},{7,5},{8,10},{9,11},{10,... | collective-permute-start | bytes 983048 | tf_op jit(solution)/shard_map/ppermute | solution.py:79
  45.0 66.7 %collective-permute-start.29 = (bf16[256,1376]{0,1:T(8,128)(2,1)}, bf16[256,1376]{0,1:T(8,128)(2,1)}, u32[]{:S(2)}, u32[]{:S(2)}) collective-permute-start(bf16[256,1376]{0,1:T(8,128)(2,1)} %param.25), channel_id=1, source_target_pairs={{0,2},{1,3},{2,6},{3,7},{4,0},{5,1},{6,4},{7,5},{8,10},{9,11},{10,... | collective-permute-start | bytes 2113544 | tf_op jit(solution)/shard_map/ppermute | solution.py:79
  48.0 64.7 %collective-permute-start.28 = (bf16[256,1376]{0,1:T(8,128)(2,1)}, bf16[256,1376]{0,1:T(8,128)(2,1)}, u32[]{:S(2)}, u32[]{:S(2)}) collective-permute-start(bf16[256,1376]{0,1:T(8,128)(2,1)} %param.25), channel_id=1, source_target_pairs={{0,0},{1,1},{2,4},{3,5},{4,2},{5,3},{6,6},{7,7},{8,8},{9,9},{10,12... | collective-permute-start | bytes 2113544 | tf_op jit(solution)/shard_map/ppermute | solution.py:79
  52.1 80.4 %collective-permute-start = (bf16[768,2048]{1,0:T(8,128)(2,1)S(1)}, bf16[768,2048]{1,0:T(8,128)(2,1)}, u32[]{:S(2)}, u32[]{:S(2)}) collective-permute-start(bf16[768,2048]{1,0:T(8,128)(2,1)S(1)} %dynamic-slice_bitcast_fusion.1), channel_id=1, source_target_pairs={{0,4},{1,5},{2,6},{3,7},{4,0},{5,1},{6,2},{7,3},{8,12},{9,13},{10,... | collective-permute-start | bytes 9437192 | tf_op jit(solution)/shard_map/ppermute | solution.py:79
  77.9 16.3 %collective-permute-start.2 = (bf16[256,640]{1,0:T(8,128)(2,1)}, bf16[256,640]{1,0:T(8,128)(2,1)}, u32[]{:S(2)}, u32[]{:S(2)}) collective-permute-start(bf16[256,640]{1,0:T(8,128)(2,1)} %collective-permute-done.1), channel_id=1, source_target_pairs={{0,8},{1,9},{2,10},{3,11},{4,12},{5,13},{6,14},{7,15},{8,0},{9,1},... | collective-permute-start | bytes 983048 | tf_op jit(solution)/shard_map/ppermute | solution.py:79
  78.3 21.8 %collective-permute-start.3 = (bf16[256,640]{1,0:T(8,128)(2,1)}, bf16[256,640]{1,0:T(8,128)(2,1)S(1)}, u32[]{:S(2)}, u32[]{:S(2)}) collective-permute-start(bf16[256,640]{1,0:T(8,128)(2,1)} %collective-permute-done.1), channel_id=1, source_target_pairs={{0,16},{1,17},{2,18},{3,19},{4,20},{5,21},{6,22},{7,23},{8,24},{9,... | collective-permute-start | bytes 983048 | tf_op jit(solution)/shard_map/ppermute | solution.py:79
  94.2 17.0 %collective-permute-start.6 = (bf16[256,640]{1,0:T(8,128)(2,1)}, bf16[256,640]{1,0:T(8,128)(2,1)S(1)}, u32[]{:S(2)}, u32[]{:S(2)}) collective-permute-start(bf16[256,640]{1,0:T(8,128)(2,1)} %collective-permute-done.5), channel_id=1, source_target_pairs={{0,16},{1,17},{2,18},{3,19},{4,20},{5,21},{6,22},{7,23},{8,24},{9,... | collective-permute-start | bytes 983048 | tf_op jit(solution)/shard_map/ppermute | solution.py:79
  100.0 24.8 %collective-permute-start.4 = (bf16[256,640]{1,0:T(8,128)(2,1)}, bf16[256,640]{1,0:T(8,128)(2,1)}, u32[]{:S(2)}, u32[]{:S(2)}) collective-permute-start(bf16[256,640]{1,0:T(8,128)(2,1)} %collective-permute-done.2), channel_id=1, source_target_pairs={{0,16},{1,17},{2,18},{3,19},{4,20},{5,21},{6,22},{7,23},{8,24},{9,... | collective-permute-start | bytes 983048 | tf_op jit(solution)/shard_map/ppermute | solution.py:79
  111.2 17.8 %collective-permute-start.7 = (bf16[256,640]{1,0:T(8,128)(2,1)}, bf16[256,640]{1,0:T(8,128)(2,1)}, u32[]{:S(2)}, u32[]{:S(2)}) collective-permute-start(bf16[256,640]{1,0:T(8,128)(2,1)} %collective-permute-done.5), channel_id=1, source_target_pairs={{0,8},{1,9},{2,10},{3,11},{4,12},{5,13},{6,14},{7,15},{8,0},{9,1},... | collective-permute-start | bytes 983048 | tf_op jit(solution)/shard_map/ppermute | solution.py:79
  111.6 19.1 %collective-permute-start.8 = (bf16[256,640]{1,0:T(8,128)(2,1)S(1)}, bf16[256,640]{1,0:T(8,128)(2,1)}, u32[]{:S(2)}, u32[]{:S(2)}) collective-permute-start(bf16[256,640]{1,0:T(8,128)(2,1)S(1)} %collective-permute-done.6), channel_id=1, source_target_pairs={{0,8},{1,9},{2,10},{3,11},{4,12},{5,13},{6,14},{7,15},{8,0},{9,1},... | collective-permute-start | bytes 983048 | tf_op jit(solution)/shard_map/ppermute | solution.py:79
  115.9 262.4 %all-gather.5.cloned.1.call-start = ((), (), s32[]{:S(2)}) async-start(), calls=%async_computation.5 | async-start | bytes 7045120 | tf_op jit(solution)/shard_map/all_gather | solution.py:130
  163.9 18.9 %collective-permute-start.11 = (bf16[648,128]{1,0:T(8,128)(2,1)}, bf16[648,128]{1,0:T(8,128)(2,1)S(1)}, u32[]{:S(2)}, u32[]{:S(2)}) collective-permute-start(bf16[648,128]{1,0:T(8,128)(2,1)} %pad_maximum_fusion.7), channel_id=1, source_target_pairs={{0,24},{1,25},{2,26},{3,27},{4,28},{5,29},{6,30},{7,31}} | collective-permute-start | bytes 497672 | tf_op jit(solution)/shard_map/ppermute | solution.py:79
  165.2 18.3 %collective-permute-start.10 = (bf16[648,128]{1,0:T(8,128)(2,1)}, bf16[648,128]{1,0:T(8,128)(2,1)}, u32[]{:S(2)}, u32[]{:S(2)}) collective-permute-start(bf16[648,128]{1,0:T(8,128)(2,1)} %pad_maximum_fusion.7), channel_id=1, source_target_pairs={{0,16},{1,17},{2,18},{3,19},{4,20},{5,21},{6,22},{7,23},{8,24},{9,... | collective-permute-start | bytes 497672 | tf_op jit(solution)/shard_map/ppermute | solution.py:79
  166.5 17.7 %collective-permute-start.9 = (bf16[648,128]{1,0:T(8,128)(2,1)}, bf16[648,128]{1,0:T(8,128)(2,1)}, u32[]{:S(2)}, u32[]{:S(2)}) collective-permute-start(bf16[648,128]{1,0:T(8,128)(2,1)} %pad_maximum_fusion.7), channel_id=1, source_target_pairs={{0,8},{1,9},{2,10},{3,11},{4,12},{5,13},{6,14},{7,15},{8,16},{9,17... | collective-permute-start | bytes 497672 | tf_op jit(solution)/shard_map/ppermute | solution.py:79
  196.0 59.5 %collective-permute-start.21 = (bf16[1536,512]{1,0:T(8,128)(2,1)}, bf16[1536,512]{1,0:T(8,128)(2,1)S(1)}, u32[]{:S(2)}, u32[]{:S(2)}) collective-permute-start(bf16[1536,512]{1,0:T(8,128)(2,1)} %bitcast.223), channel_id=1, source_target_pairs={{0,1},{1,0},{2,3},{3,2},{4,5},{5,4},{6,7},{7,6},{8,9},{9,8},{10,11... | collective-permute-start | bytes 4718600 | tf_op jit(solution)/shard_map/ppermute | solution.py:79
  196.0 37.5 %collective-permute-start.12 = (bf16[256,512]{1,0:T(8,128)(2,1)}, bf16[256,512]{1,0:T(8,128)(2,1)}, u32[]{:S(2)}, u32[]{:S(2)}) collective-permute-start(bf16[256,512]{1,0:T(8,128)(2,1)} %param.23), channel_id=1, source_target_pairs={{0,0},{1,1},{2,4},{3,5},{4,2},{5,3},{6,6},{7,7},{8,8},{9,9},{10,12... | collective-permute-start | bytes 786440 | tf_op jit(solution)/shard_map/ppermute | solution.py:79
  202.8 39.7 %collective-permute-start.16 = (bf16[256,512]{1,0:T(8,128)(2,1)}, bf16[256,512]{1,0:T(8,128)(2,1)S(1)}, u32[]{:S(2)}, u32[]{:S(2)}) collective-permute-start(bf16[256,512]{1,0:T(8,128)(2,1)} %param.23), channel_id=1, source_target_pairs={{0,2},{1,3},{2,6},{3,7},{4,0},{5,1},{6,4},{7,5},{8,10},{9,11},{10,... | collective-permute-start | bytes 786440 | tf_op jit(solution)/shard_map/ppermute | solution.py:79
  238.4 33.2 %collective-permute-start.20 = (bf16[1536,512]{1,0:T(8,128)(2,1)}, bf16[1536,512]{1,0:T(8,128)(2,1)}, u32[]{:S(2)}, u32[]{:S(2)}) collective-permute-start(bf16[1536,512]{1,0:T(8,128)(2,1)} %bitcast.223), channel_id=1, source_target_pairs={{0,4},{1,5},{2,6},{3,7},{4,0},{5,1},{6,2},{7,3},{8,12},{9,13},{10,... | collective-permute-start | bytes 4718600 | tf_op jit(solution)/shard_map/ppermute | solution.py:79
  242.5 13.0 %collective-permute-start.15 = (bf16[256,512]{1,0:T(8,128)(2,1)}, bf16[256,512]{1,0:T(8,128)(2,1)S(1)}, u32[]{:S(2)}, u32[]{:S(2)}) collective-permute-start(bf16[256,512]{1,0:T(8,128)(2,1)} %collective-permute-done.13), channel_id=1, source_target_pairs={{0,16},{1,17},{2,18},{3,19},{4,20},{5,21},{6,22},{7,23},{8,24},{9,... | collective-permute-start | bytes 786440 | tf_op jit(solution)/shard_map/ppermute | solution.py:79
  245.1 49.1 %collective-permute-start.37 = (bf16[768,2048]{1,0:T(8,128)(2,1)}, bf16[768,2048]{1,0:T(8,128)(2,1)}, u32[]{:S(2)}, u32[]{:S(2)}) collective-permute-start(bf16[768,2048]{1,0:T(8,128)(2,1)} %dynamic-slice_bitcast_fusion), channel_id=1, source_target_pairs={{0,4},{1,5},{2,6},{3,7},{4,0},{5,1},{6,2},{7,3},{8,12},{9,13},{10,... | collective-permute-start | bytes 9437192 | tf_op jit(solution)/shard_map/ppermute | solution.py:79
  255.5 19.7 %collective-permute-start.22 = (bf16[1536,512]{1,0:T(8,128)(2,1)S(1)}, bf16[1536,512]{1,0:T(8,128)(2,1)S(1)}, u32[]{:S(2)}, u32[]{:S(2)}) collective-permute-start(bf16[1536,512]{1,0:T(8,128)(2,1)S(1)} %collective-permute-done.21), channel_id=1, source_target_pairs={{0,4},{1,5},{2,6},{3,7},{4,0},{5,1},{6,2},{7,3},{8,12},{9,13},{10,... | collective-permute-start | bytes 4718600 | tf_op jit(solution)/shard_map/ppermute | solution.py:79
  257.3 30.6 %collective-permute-start.27 = (bf16[256,1376]{0,1:T(8,128)(2,1)S(1)}, bf16[256,1376]{0,1:T(8,128)(2,1)S(1)}, u32[]{:S(2)}, u32[]{:S(2)}) collective-permute-start(bf16[256,1376]{0,1:T(8,128)(2,1)S(1)} %copy-done.104), channel_id=1, source_target_pairs={{0,2},{1,3},{2,6},{3,7},{4,0},{5,1},{6,4},{7,5},{8,10},{9,11},{10,... | collective-permute-start | bytes 2113544 | tf_op jit(solution)/shard_map/ppermute | solution.py:79
  261.9 30.5 %collective-permute-start.26 = (bf16[256,1376]{0,1:T(8,128)(2,1)S(1)}, bf16[256,1376]{0,1:T(8,128)(2,1)S(1)}, u32[]{:S(2)}, u32[]{:S(2)}) collective-permute-start(bf16[256,1376]{0,1:T(8,128)(2,1)S(1)} %copy-done.104), channel_id=1, source_target_pairs={{0,0},{1,1},{2,4},{3,5},{4,2},{5,3},{6,6},{7,7},{8,8},{9,9},{10,12... | collective-permute-start | bytes 2113544 | tf_op jit(solution)/shard_map/ppermute | solution.py:79
  280.9 45.4 %collective-permute-start.24 = (bf16[1536,512]{1,0:T(8,128)(2,1)S(1)}, bf16[1536,512]{1,0:T(8,128)(2,1)}, u32[]{:S(2)}, u32[]{:S(2)}) collective-permute-start(bf16[1536,512]{1,0:T(8,128)(2,1)S(1)} %get-tuple-element.130), channel_id=1, source_target_pairs={{0,1},{1,0},{2,3},{3,2},{4,5},{5,4},{6,7},{7,6},{8,9},{9,8},{10,11... | collective-permute-start | bytes 4718600 | tf_op jit(solution)/shard_map/ppermute | solution.py:79
  283.4 43.3 %collective-permute-start.23 = (bf16[1536,512]{1,0:T(8,128)(2,1)S(1)}, bf16[1536,512]{1,0:T(8,128)(2,1)}, u32[]{:S(2)}, u32[]{:S(2)}) collective-permute-start(bf16[1536,512]{1,0:T(8,128)(2,1)S(1)} %get-tuple-element.130), channel_id=1, source_target_pairs={{0,4},{1,5},{2,6},{3,7},{4,0},{5,1},{6,2},{7,3},{8,12},{9,13},{10,... | collective-permute-start | bytes 4718600 | tf_op jit(solution)/shard_map/ppermute | solution.py:79
  293.9 474.4 %reduce-scatter.8.cloned.1.call-start = ((), (), s32[]{:S(2)}) async-start(), calls=%async_computation.10 | async-start | bytes 2621440 | tf_op jit(solution)/shard_map/reduce_scatter | solution.py:139
  326.3 20.2 %collective-permute-start.25 = (bf16[1536,512]{1,0:T(8,128)(2,1)}, bf16[1536,512]{1,0:T(8,128)(2,1)}, u32[]{:S(2)}, u32[]{:S(2)}) collective-permute-start(bf16[1536,512]{1,0:T(8,128)(2,1)} %collective-permute-done.24), channel_id=1, source_target_pairs={{0,4},{1,5},{2,6},{3,7},{4,0},{5,1},{6,2},{7,3},{8,12},{9,13},{10,... | collective-permute-start | bytes 4718600 | tf_op jit(solution)/shard_map/ppermute | solution.py:79
  415.1 46.2 %collective-permute-start.38 = (bf16[1536,512]{1,0:T(8,128)(2,1)S(1)}, bf16[1536,512]{1,0:T(8,128)(2,1)S(1)}, u32[]{:S(2)}, u32[]{:S(2)}) collective-permute-start(bf16[1536,512]{1,0:T(8,128)(2,1)S(1)} %fusion.27), channel_id=1, source_target_pairs={{0,4},{1,5},{2,6},{3,7},{4,0},{5,1},{6,2},{7,3},{8,12},{9,13},{10,... | collective-permute-start | bytes 4718600 | tf_op jit(solution)/shard_map/ppermute | solution.py:79
  421.2 40.1 %collective-permute-start.40 = (bf16[1536,512]{1,0:T(8,128)(2,1)S(1)}, bf16[1536,512]{1,0:T(8,128)(2,1)S(1)}, u32[]{:S(2)}, u32[]{:S(2)}) collective-permute-start(bf16[1536,512]{1,0:T(8,128)(2,1)S(1)} %add_convert_fusion.1), channel_id=1, source_target_pairs={{0,1},{1,0},{2,3},{3,2},{4,5},{5,4},{6,7},{7,6},{8,9},{9,8},{10,11... | collective-permute-start | bytes 4718600 | tf_op jit(solution)/shard_map/ppermute | solution.py:79
  421.3 36.1 %collective-permute-start.41 = (f32[1536]{0:T(1024)S(1)}, f32[1536]{0:T(1024)S(1)}, u32[]{:S(2)}, u32[]{:S(2)}) collective-permute-start(f32[1536]{0:T(1024)S(1)} %get-tuple-element.84), channel_id=1, source_target_pairs={{0,1},{1,0},{2,3},{3,2},{4,5},{5,4},{6,7},{7,6},{8,9},{9,8},{10,11... | collective-permute-start | bytes 18440 | tf_op jit(solution)/shard_map/ppermute | solution.py:79
  482.7 451.0 %reduce-scatter.10.cloned.1.call-start = ((), (), s32[]{:S(2)}) async-start(), calls=%async_computation.11 | async-start | bytes 7045120 | tf_op jit(solution)/shard_map/reduce_scatter | solution.py:139
  496.7 447.9 %reduce-scatter.12.cloned.1.call-start = ((), (), s32[]{:S(2)}) async-start(), calls=%async_computation.12 | async-start | bytes 7045120 | tf_op jit(solution)/shard_map/reduce_scatter | solution.py:139
  511.3 441.5 %reduce-scatter.14.cloned.1.call-start = ((), (), s32[]{:S(2)}) async-start(), calls=%async_computation.13 | async-start | bytes 7045120 | tf_op jit(solution)/shard_map/reduce_scatter | solution.py:139
  517.4 15.2 %collective-permute-start.44 = (bf16[1536,512]{1,0:T(8,128)(2,1)S(1)}, bf16[1536,512]{1,0:T(8,128)(2,1)S(1)}, u32[]{:S(2)}, u32[]{:S(2)}) collective-permute-start(bf16[1536,512]{1,0:T(8,128)(2,1)S(1)} %convolution_convert_fusion.8), channel_id=1, source_target_pairs={{0,4},{1,5},{2,6},{3,7},{4,0},{5,1},{6,2},{7,3},{8,12},{9,13},{10,... | collective-permute-start | bytes 4718600 | tf_op jit(solution)/shard_map/ppermute | solution.py:79
  524.2 146.8 %collective-permute-start.33 = (bf16[1536,512]{1,0:T(8,128)(2,1)}, bf16[1536,512]{1,0:T(8,128)(2,1)}, u32[]{:S(2)}, u32[]{:S(2)}) collective-permute-start(bf16[1536,512]{1,0:T(8,128)(2,1)} %convolution_convert_fusion.12), channel_id=1, source_target_pairs={{0,4},{1,5},{2,6},{3,7},{4,0},{5,1},{6,2},{7,3},{8,12},{9,13},{10,... | collective-permute-start | bytes 4718600 | tf_op jit(solution)/shard_map/ppermute | solution.py:79
  529.9 226.1 %collective-permute-start.32 = (bf16[1536,512]{1,0:T(8,128)(2,1)}, bf16[1536,512]{1,0:T(8,128)(2,1)}, u32[]{:S(2)}, u32[]{:S(2)}) collective-permute-start(bf16[1536,512]{1,0:T(8,128)(2,1)} %convolution_convert_fusion.13), channel_id=1, source_target_pairs={{0,4},{1,5},{2,6},{3,7},{4,0},{5,1},{6,2},{7,3},{8,12},{9,13},{10,... | collective-permute-start | bytes 4718600 | tf_op jit(solution)/shard_map/ppermute | solution.py:79
  532.2 13.6 %collective-permute-start.43 = (bf16[1536,512]{1,0:T(8,128)(2,1)}, bf16[1536,512]{1,0:T(8,128)(2,1)S(1)}, u32[]{:S(2)}, u32[]{:S(2)}) collective-permute-start(bf16[1536,512]{1,0:T(8,128)(2,1)} %convolution_convert_fusion.9), channel_id=1, source_target_pairs={{0,4},{1,5},{2,6},{3,7},{4,0},{5,1},{6,2},{7,3},{8,12},{9,13},{10,... | collective-permute-start | bytes 4718600 | tf_op jit(solution)/shard_map/ppermute | solution.py:79
  534.9 36.3 %collective-permute-start.45 = (bf16[1536,512]{1,0:T(8,128)(2,1)}, bf16[1536,512]{1,0:T(8,128)(2,1)}, u32[]{:S(2)}, u32[]{:S(2)}) collective-permute-start(bf16[1536,512]{1,0:T(8,128)(2,1)} %fusion.30), channel_id=1, source_target_pairs={{0,1},{1,0},{2,3},{3,2},{4,5},{5,4},{6,7},{7,6},{8,9},{9,8},{10,11... | collective-permute-start | bytes 4718600 | tf_op jit(solution)/shard_map/ppermute | solution.py:79
  545.5 408.8 %reduce-scatter.6.cloned.1.call-start = ((), (), s32[]{:S(2)}) async-start(), calls=%async_computation.9 | async-start | bytes 3276800 | tf_op jit(solution)/shard_map/reduce_scatter | solution.py:139
  591.3 37.3 %collective-permute-start.48 = (bf16[648,128]{1,0:T(8,128)(2,1)}, bf16[648,128]{1,0:T(8,128)(2,1)S(1)}, u32[]{:S(2)}, u32[]{:S(2)}) collective-permute-start(bf16[648,128]{1,0:T(8,128)(2,1)} %pad_maximum_fusion.8), channel_id=1, source_target_pairs={{24,0},{25,1},{26,2},{27,3},{28,4},{29,5},{30,6},{31,7}} | collective-permute-start | bytes 497672 | tf_op jit(solution)/shard_map/ppermute | solution.py:79
  593.4 37.8 %collective-permute-start.47 = (bf16[648,128]{1,0:T(8,128)(2,1)}, bf16[648,128]{1,0:T(8,128)(2,1)}, u32[]{:S(2)}, u32[]{:S(2)}) collective-permute-start(bf16[648,128]{1,0:T(8,128)(2,1)} %pad_maximum_fusion.8), channel_id=1, source_target_pairs={{16,0},{17,1},{18,2},{19,3},{20,4},{21,5},{22,6},{23,7},{24,8},{25... | collective-permute-start | bytes 497672 | tf_op jit(solution)/shard_map/ppermute | solution.py:79
  595.4 38.3 %collective-permute-start.46 = (bf16[648,128]{1,0:T(8,128)(2,1)}, bf16[648,128]{1,0:T(8,128)(2,1)}, u32[]{:S(2)}, u32[]{:S(2)}) collective-permute-start(bf16[648,128]{1,0:T(8,128)(2,1)} %pad_maximum_fusion.8), channel_id=1, source_target_pairs={{8,0},{9,1},{10,2},{11,3},{12,4},{13,5},{14,6},{15,7},{16,8},{17,9... | collective-permute-start | bytes 497672 | tf_op jit(solution)/shard_map/ppermute | solution.py:79
  663.0 19.8 %collective-permute-start.50 = (bf16[1536,512]{1,0:T(8,128)(2,1)}, bf16[1536,512]{1,0:T(8,128)(2,1)}, u32[]{:S(2)}, u32[]{:S(2)}) collective-permute-start(bf16[1536,512]{1,0:T(8,128)(2,1)} %convolution_convert_fusion.10), channel_id=1, source_target_pairs={{0,4},{1,5},{2,6},{3,7},{4,0},{5,1},{6,2},{7,3},{8,12},{9,13},{10,... | collective-permute-start | bytes 4718600 | tf_op jit(solution)/shard_map/ppermute | solution.py:79
  671.0 378.8 %all-gather.11.cloned.1.call-start = ((), (), s32[]{:S(2)}) async-start(), calls=%async_computation.8 | async-start | bytes 7864320 | tf_op jit(solution)/shard_map/all_gather | solution.py:389
  678.6 77.5 %collective-permute-start.34 = (bf16[1536,512]{1,0:T(8,128)(2,1)}, bf16[1536,512]{1,0:T(8,128)(2,1)S(1)}, u32[]{:S(2)}, u32[]{:S(2)}) collective-permute-start(bf16[1536,512]{1,0:T(8,128)(2,1)} %add_convert_fusion.3), channel_id=1, source_target_pairs={{0,1},{1,0},{2,3},{3,2},{4,5},{5,4},{6,7},{7,6},{8,9},{9,8},{10,11... | collective-permute-start | bytes 4718600 | tf_op jit(solution)/shard_map/ppermute | solution.py:79
  682.8 73.3 %collective-permute-start.49 = (bf16[1536,512]{1,0:T(8,128)(2,1)}, bf16[1536,512]{1,0:T(8,128)(2,1)}, u32[]{:S(2)}, u32[]{:S(2)}) collective-permute-start(bf16[1536,512]{1,0:T(8,128)(2,1)} %convolution_convert_fusion.11), channel_id=1, source_target_pairs={{0,4},{1,5},{2,6},{3,7},{4,0},{5,1},{6,2},{7,3},{8,12},{9,13},{10,... | collective-permute-start | bytes 4718600 | tf_op jit(solution)/shard_map/ppermute | solution.py:79
  687.3 68.9 %collective-permute-start.51 = (bf16[1536,512]{1,0:T(8,128)(2,1)}, bf16[1536,512]{1,0:T(8,128)(2,1)}, u32[]{:S(2)}, u32[]{:S(2)}) collective-permute-start(bf16[1536,512]{1,0:T(8,128)(2,1)} %fusion.31), channel_id=1, source_target_pairs={{0,1},{1,0},{2,3},{3,2},{4,5},{5,4},{6,7},{7,6},{8,9},{9,8},{10,11... | collective-permute-start | bytes 4718600 | tf_op jit(solution)/shard_map/ppermute | solution.py:79
  688.9 60.1 %collective-permute-start.52 = (f32[1536]{0:T(1024)S(1)}, f32[1536]{0:T(1024)}, u32[]{:S(2)}, u32[]{:S(2)}) collective-permute-start(f32[1536]{0:T(1024)S(1)} %multiply_reduce_fusion.1), channel_id=1, source_target_pairs={{0,1},{1,0},{2,3},{3,2},{4,5},{5,4},{6,7},{7,6},{8,9},{9,8},{10,11... | collective-permute-start | bytes 18440 | tf_op jit(solution)/shard_map/ppermute | solution.py:79
  774.8 46.8 %collective-permute-start.57 = (bf16[256,512]{1,0:T(8,128)(2,1)S(1)}, bf16[256,512]{1,0:T(8,128)(2,1)}, u32[]{:S(2)}, u32[]{:S(2)}) collective-permute-start(bf16[256,512]{1,0:T(8,128)(2,1)S(1)} %get-tuple-element.107), channel_id=1, source_target_pairs={{0,0},{1,1},{2,4},{3,5},{4,2},{5,3},{6,6},{7,7},{8,8},{9,9},{10,12... | collective-permute-start | bytes 786440 | tf_op jit(solution)/shard_map/ppermute | solution.py:79
  776.9 166.2 %collective-permute-start.36 = (bf16[768,512]{1,0:T(8,128)(2,1)S(1)}, bf16[768,512]{1,0:T(8,128)(2,1)S(1)}, u32[]{:S(2)}, u32[]{:S(2)}) collective-permute-start(bf16[768,512]{1,0:T(8,128)(2,1)S(1)} %get-tuple-element.96), channel_id=1, source_target_pairs={{0,4},{1,5},{2,0},{3,1},{4,6},{5,7},{6,2},{7,3},{8,12},{9,13},{10,... | collective-permute-start | bytes 2359304 | tf_op jit(solution)/shard_map/ppermute | solution.py:79
  777.0 166.1 %collective-permute-start.35 = (bf16[768,512]{1,0:T(8,128)(2,1)S(1)}, bf16[768,512]{1,0:T(8,128)(2,1)S(1)}, u32[]{:S(2)}, u32[]{:S(2)}) collective-permute-start(bf16[768,512]{1,0:T(8,128)(2,1)S(1)} %get-tuple-element.95), channel_id=1, source_target_pairs={{0,0},{1,1},{2,4},{3,5},{4,2},{5,3},{6,6},{7,7},{8,8},{9,9},{10,12... | collective-permute-start | bytes 2359304 | tf_op jit(solution)/shard_map/ppermute | solution.py:79
  936.2 19.3 %collective-permute-start.60 = (bf16[256,1376]{0,1:T(8,128)(2,1)}, bf16[256,1376]{0,1:T(8,128)(2,1)}, u32[]{:S(2)}, u32[]{:S(2)}) collective-permute-start(bf16[256,1376]{0,1:T(8,128)(2,1)} %get-tuple-element.102), channel_id=1, source_target_pairs={{0,4},{1,5},{2,0},{3,1},{4,6},{5,7},{6,2},{7,3},{8,12},{9,13},{10,... | collective-permute-start | bytes 2113544 | tf_op jit(solution)/shard_map/ppermute | solution.py:79
  938.5 64.6 %collective-permute-start.59 = (bf16[256,1376]{0,1:T(8,128)(2,1)}, bf16[256,1376]{0,1:T(8,128)(2,1)}, u32[]{:S(2)}, u32[]{:S(2)}) collective-permute-start(bf16[256,1376]{0,1:T(8,128)(2,1)} %get-tuple-element.101), channel_id=1, source_target_pairs={{0,0},{1,1},{2,4},{3,5},{4,2},{5,3},{6,6},{7,7},{8,8},{9,9},{10,12... | collective-permute-start | bytes 2113544 | tf_op jit(solution)/shard_map/ppermute | solution.py:79
  945.9 59.8 %collective-permute-start.62 = (bf16[256,1376]{0,1:T(8,128)(2,1)S(1)}, bf16[256,1376]{0,1:T(8,128)(2,1)S(1)}, u32[]{:S(2)}, u32[]{:S(2)}) collective-permute-start(bf16[256,1376]{0,1:T(8,128)(2,1)S(1)} %get-tuple-element.100), channel_id=1, source_target_pairs={{0,4},{1,5},{2,0},{3,1},{4,6},{5,7},{6,2},{7,3},{8,12},{9,13},{10,... | collective-permute-start | bytes 2113544 | tf_op jit(solution)/shard_map/ppermute | solution.py:79
  950.7 74.6 %collective-permute-start.61 = (bf16[256,1376]{0,1:T(8,128)(2,1)S(1)}, bf16[256,1376]{0,1:T(8,128)(2,1)}, u32[]{:S(2)}, u32[]{:S(2)}) collective-permute-start(bf16[256,1376]{0,1:T(8,128)(2,1)S(1)} %get-tuple-element.99), channel_id=1, source_target_pairs={{0,0},{1,1},{2,4},{3,5},{4,2},{5,3},{6,6},{7,7},{8,8},{9,9},{10,12... | collective-permute-start | bytes 2113544 | tf_op jit(solution)/shard_map/ppermute | solution.py:79
  954.2 73.4 %collective-permute-start.64 = (bf16[1376,256]{1,0:T(8,128)(2,1)S(1)}, bf16[1376,256]{1,0:T(8,128)(2,1)}, u32[]{:S(2)}, u32[]{:S(2)}) collective-permute-start(bf16[1376,256]{1,0:T(8,128)(2,1)S(1)} %get-tuple-element.98), channel_id=1, source_target_pairs={{0,4},{1,5},{2,0},{3,1},{4,6},{5,7},{6,2},{7,3},{8,12},{9,13},{10,... | collective-permute-start | bytes 2113544 | tf_op jit(solution)/shard_map/ppermute | solution.py:79
  955.5 84.8 %collective-permute-start.63 = (bf16[1376,256]{1,0:T(8,128)(2,1)S(1)}, bf16[1376,256]{1,0:T(8,128)(2,1)S(1)}, u32[]{:S(2)}, u32[]{:S(2)}) collective-permute-start(bf16[1376,256]{1,0:T(8,128)(2,1)S(1)} %get-tuple-element.97), channel_id=1, source_target_pairs={{0,0},{1,1},{2,4},{3,5},{4,2},{5,3},{6,6},{7,7},{8,8},{9,9},{10,12... | collective-permute-start | bytes 2113544 | tf_op jit(solution)/shard_map/ppermute | solution.py:79
  1003.2 39.4 %collective-permute-start.56 = (bf16[256,640]{1,0:T(8,128)(2,1)S(1)}, bf16[256,640]{1,0:T(8,128)(2,1)S(1)}, u32[]{:S(2)}, u32[]{:S(2)}) collective-permute-start(bf16[256,640]{1,0:T(8,128)(2,1)S(1)} %get-tuple-element.106), channel_id=1, source_target_pairs={{0,4},{1,5},{2,0},{3,1},{4,6},{5,7},{6,2},{7,3},{8,12},{9,13},{10,... | collective-permute-start | bytes 983048 | tf_op jit(solution)/shard_map/ppermute | solution.py:79
  1005.7 41.6 %collective-permute-start.55 = (bf16[256,640]{1,0:T(8,128)(2,1)S(1)}, bf16[256,640]{1,0:T(8,128)(2,1)S(1)}, u32[]{:S(2)}, u32[]{:S(2)}) collective-permute-start(bf16[256,640]{1,0:T(8,128)(2,1)S(1)} %get-tuple-element.105), channel_id=1, source_target_pairs={{0,0},{1,1},{2,4},{3,5},{4,2},{5,3},{6,6},{7,7},{8,8},{9,9},{10,12... | collective-permute-start | bytes 983048 | tf_op jit(solution)/shard_map/ppermute | solution.py:79
  (132 other events, 1229.7 us)
Sparse Core Ops, SparseCore 0:
  42.7 86.9 all-gather.8
  132.0 71.6 all-gather.6
  294.0 67.2 all-gather.4
  482.8 37.2 reduce-scatter.7
  523.4 64.6 reduce-scatter.9
  591.3 70.5 reduce-scatter.11
  665.3 64.6 reduce-scatter.13
  733.9 39.5 reduce-scatter.5
  775.1 148.6 all-gather.10

commit v2 on v1

v2 whole, which is shorter than its diff:
```python
import functools

import jax
import jax.numpy as jnp
import numpy as np
from jax import lax
from jax.experimental import pallas as pl
from jax.experimental.pallas import tpu as pltpu
from jax.sharding import PartitionSpec as P

HEADS = 16
HEAD_V = 128
QK = 16
NFEAT = 160
CORES = 2
EPS = 1e-05
BF = jnp.bfloat16
F32 = jnp.float32


LANES = 256
TILE = 256


def feature_tables(heads):
    left, right, scale = [-1], [-1], [1.0]
    for i in range(QK):
        left.append(i), right.append(-1), scale.append(1.0)
    for i in range(QK):
        for j in range(i, QK):
            left.append(i), right.append(j), scale.append(1.0 if i < j else 0.7071067811865476)
    padding = LANES - len(left)
    left, right, scale = left + [-2] * padding, right + [-2] * padding, scale + [0.0] * padding
    both = np.array(left + right)
    pick = np.zeros((heads * QK, heads, 2 * LANES), np.float32)
    for h in range(heads):
        pick[h * QK : (h + 1) * QK, h] = 0.5 * (np.arange(QK)[:, None] == both[None, :])
    ones = (both == -1).astype(np.float32)[None]
    own = np.zeros((8, heads * QK), np.float32)
    for h in range(heads):
        own[h, h * QK : (h + 1) * QK] = 0.25
    return (
        jnp.asarray(pick.reshape(heads * QK, -1), BF),
        jnp.asarray(ones),
        jnp.asarray(np.array(scale, np.float32)[None]),
        jnp.asarray(own, BF),
    )


def nt(a, b):
    return lax.dot_general(a, b, (((1,), (1,)), ((), ())), preferred_element_type=F32)


def tn(a, b):
    return lax.dot_general(a, b, (((0,), (0,)), ((), ())), preferred_element_type=F32)


def nn(a, b):
    return lax.dot_general(a, b, (((1,), (0,)), ((), ())), preferred_element_type=F32)


class Marks:
    def __init__(self, marks, b, block):
        t = lax.broadcasted_iota(jnp.int32, (block, 1), 0)
        first, second, third = marks[b, 0], marks[b, 1], marks[b, 2]
        low = jnp.where(t >= first, first, 0)
        low = jnp.where(t >= second, second, low)
        self.low = jnp.where(t >= third, block, low)
        self.padding = jnp.where(t >= third, 1.0, 0.0).astype(F32)
        self.use = jnp.where(t < marks[b, 3], 1.0, 0.0).astype(F32)
        self.tail = jnp.where(t >= marks[b, 4], 1.0, 0.0).astype(F32)

    def mask(self, at, count):
        t = lax.broadcasted_iota(jnp.int32, (TILE, count), 0) + at
        s = lax.broadcasted_iota(jnp.int32, (TILE, count), 1)
        return (s <= t) & (s >= self.low[at : at + TILE])


def sides(x, pick, ones, h):
    both = nn(x, pick[:, 2 * LANES * h : 2 * LANES * (h + 1)]) + ones
    return both[:, :LANES], both[:, LANES:]


def head_cols(ref, h):
    return ref[:, HEAD_V * h : HEAD_V * (h + 1)]


def output_grads(do_ref, o_ref, den_ref, h):
    do, o, den = head_cols(do_ref, h), head_cols(o_ref, h).astype(F32), head_cols(den_ref, h)
    do = do.astype(F32)
    inverse = 1.0 / den
    dnum = (do * inverse).astype(BF)
    dden = -jnp.sum(do * o, axis=1, keepdims=True) * inverse
    return dnum, dden


def state_kernel(marks, k_ref, v_ref, pick, ones, scale, out_ref, *, heads, block):
    m = Marks(marks, pl.program_id(0), block)
    k = k_ref[...]
    for h in range(heads):
        left, right = sides(k, pick, ones[...], h)
        feat = (left * right * (scale[...] * m.tail)).astype(BF)
        v = head_cols(v_ref, h)
        out_ref[0, h] = tn(feat, jnp.concatenate([v, jnp.ones_like(v)], 1))[:NFEAT]


def grad_state_kernel(
    marks, q_ref, do_ref, o_ref, den_ref, pick, ones, scale, out_ref, *, heads, block
):
    m = Marks(marks, pl.program_id(0), block)
    q = q_ref[...]
    for h in range(heads):
        left, right = sides(q, pick, ones[...], h)
        feat = (left * right * (scale[...] * m.use)).astype(BF)
        dnum, dden = output_grads(do_ref, o_ref, den_ref, h)
        out_ref[0, h] = tn(feat, jnp.concatenate([dnum, dden.astype(BF)], 1))[:NFEAT]


def mixer_kernel(
    marks, q_ref, k_ref, v_ref, s_ref, pick, ones, scale, own, o_ref, den_ref, *, heads, block
):
    m = Marks(marks, pl.program_id(0), block)
    q, k = q_ref[...], k_ref[...]
    for h in range(heads):
        q_own = q * own[h : h + 1, :]
        left, right = sides(q, pick, ones[...], h)
        feat = (left * right * scale[...]).astype(BF)
        before = nn(feat, s_ref[0, h]) * m.use
        v = head_cols(v_ref, h)
        v_one = jnp.concatenate([v, jnp.ones_like(v)], 1)
        for at in range(0, block, TILE):
            count = at + TILE
            prod = nt(q_own[at:count], k[:count])
            score = 1.0 + prod + 0.5 * prod * prod
            score = jnp.where(m.mask(at, count), score, 0.0).astype(BF)
            both = nn(score, v_one[:count]) + before[at:count]
            den = both[:, HEAD_V:] + m.padding[at:count]
            here = (slice(at, count), slice(HEAD_V * h, HEAD_V * (h + 1)))
            o_ref[here] = (both[:, :HEAD_V] / den).astype(BF)
            den_ref[here] = den


def mixer_back_kernel(
    marks,
    q_ref,
    k_ref,
    v_ref,
    do_ref,
    o_ref,
    den_ref,
    s_ref,
    g_ref,
    pick,
    ones,
    scale,
    own,
    dq_ref,
    dk_ref,
    dv_ref,
    dq,
    dk,
    dv,
    *,
    heads,
    block,
):
    m = Marks(marks, pl.program_id(0), block)
    q, k = q_ref[...], k_ref[...]
    first_lane = lax.broadcasted_iota(jnp.int32, (block, HEAD_V), 1) == 0
    dq[...] = jnp.zeros_like(dq)
    dk[...] = jnp.zeros_like(dk)
    for h in range(heads):
        table = pick[:, 2 * LANES * h : 2 * LANES * (h + 1)]
        q_own, k_own = q * own[h : h + 1, :], k * own[h : h + 1, :]
        v = head_cols(v_ref, h)
        dnum, dden = output_grads(do_ref, o_ref, den_ref, h)
        state, carried = s_ref[0, h], g_ref[0, h]

        left, right = sides(q, pick, ones[...], h)
        wide = jnp.concatenate([dnum, jnp.where(first_lane, dden, 0.0).astype(BF)], 1)
        dfeat = nt(wide, state) * (scale[...] * m.use)
        pulled = jnp.concatenate([(dfeat * right).astype(BF), (dfeat * left).astype(BF)], 1)
        dq[...] += nt(pulled, table)

        left, right = sides(k, pick, ones[...], h)
        wide = jnp.concatenate([v, jnp.where(first_lane, 1.0, 0.0).astype(BF)], 1)
        dfeat = nt(wide, carried) * (scale[...] * m.tail)
        pulled = jnp.concatenate([(dfeat * right).astype(BF), (dfeat * left).astype(BF)], 1)
        dk[...] += nt(pulled, table)
        feat = (left * right * (scale[...] * m.tail)).astype(BF)
        dv[...] = nn(feat, carried[:, :HEAD_V])

        for at in range(0, block, TILE):
            count = at + TILE
            prod = nt(q_own[at:count], k[:count])
            one = 1.0 + prod
            mask = m.mask(at, count)
            score = jnp.where(mask, one + 0.5 * prod * prod, 0.0).astype(BF)
            dscore = nt(dnum[at:count], v[:count]) + dden[at:count, :1]
            dprod = jnp.where(mask, dscore * one, 0.0).astype(BF)
            dq[at:count] += nn(dprod, k_own[:count])
            dk[:count] += tn(dprod, q_own[at:count])
            dv[:count] += tn(score, dnum[at:count])
        dv_ref[:, HEAD_V * h : HEAD_V * (h + 1)] = dv[...].astype(BF)
    dq_ref[...] = dq[...].astype(BF)
    dk_ref[...] = dk[...].astype(BF)


def mixer_calls(heads, block, blocks):
    tables = feature_tables(heads)
    narrow = pl.BlockSpec((block, heads * QK), lambda b, marks: (b, 0))
    wide = pl.BlockSpec((block, heads * HEAD_V), lambda b, marks: (b, 0))
    local = pl.BlockSpec((1, heads, NFEAT, 2 * HEAD_V), lambda b, marks: (b, 0, 0, 0))
    state = pl.BlockSpec((1, heads, LANES, 2 * HEAD_V), lambda b, marks: (b, 0, 0, 0))
    fixed = [pl.BlockSpec(t.shape, lambda b, marks: (0, 0)) for t in tables]
    rows = block * blocks

    def call(kernel, specs, used, outs, scratch, cost):
        def run(marks, *args):
            return pl.pallas_call(
                functools.partial(kernel, heads=heads, block=block),
                grid_spec=pltpu.PrefetchScalarGridSpec(
                    num_scalar_prefetch=1,
                    grid=(blocks,),
                    in_specs=specs + fixed[:used],
                    out_specs=[o[0] for o in outs],
                    scratch_shapes=scratch,
                ),
                out_shape=[jax.ShapeDtypeStruct(*o[1:]) for o in outs],
                cost_estimate=pl.CostEstimate(
                    flops=cost * rows * heads, bytes_accessed=rows * heads * 1500, transcendentals=0
                ),
                compiler_params=pltpu.CompilerParams(vmem_limit_bytes=48 * 2**20),
            )(marks, *args, *tables[:used])

        return run

    local_out = (local, (blocks, heads, NFEAT, 2 * HEAD_V), F32)
    wide_b, wide_f = (wide, (rows, heads * HEAD_V), BF), (wide, (rows, heads * HEAD_V), F32)
    narrow_b = (narrow, (rows, heads * QK), BF)
    scratch = [
        pltpu.VMEM((block, heads * QK), F32),
        pltpu.VMEM((block, heads * QK), F32),
        pltpu.VMEM((block, HEAD_V), F32),
    ]
    return (
        call(state_kernel, [narrow, wide], 3, [local_out], [], 500000),
        call(mixer_kernel, [narrow, narrow, wide, state], 4, [wide_b, wide_f], [], 1000000),
        call(grad_state_kernel, [narrow, wide, wide, wide], 3, [local_out], [], 500000),
        call(
            mixer_back_kernel,
            [narrow, narrow, wide, wide, wide, wide, state, state],
            4,
            [narrow_b, narrow_b, wide_b],
            scratch,
            2500000,
        ),
    )


def dot(a, b, ca=1, cb=0):
    return lax.dot_general(a, b, (((ca,), (cb,)), ((), ())), preferred_element_type=F32)


def after(value, *others):
    return lax.optimization_barrier((value, *others))[0]


def place_kernel(offsets, *refs, axis):
    *pieces, out, sems = refs
    copies = []
    for i, piece in enumerate(pieces):
        size = piece.shape[axis]
        span = pl.ds(pl.multiple_of(offsets[i], size), size)
        target = out.at[span] if axis == 0 else out.at[:, span]
        copies.append(pltpu.make_async_copy(piece, target, sems.at[i]))
    for copy in copies:
        copy.start()
    for copy in copies:
        copy.wait()


def place(pieces, offsets, axis):
    shape = list(pieces[0].shape)
    shape[axis] = sum(p.shape[axis] for p in pieces)
    size = int(np.prod(shape)) * pieces[0].dtype.itemsize
    return pl.pallas_call(
        functools.partial(place_kernel, axis=axis),
        grid_spec=pltpu.PrefetchScalarGridSpec(
            num_scalar_prefetch=1,
            grid=(),
            in_specs=[pl.BlockSpec(memory_space=pl.ANY)] * len(pieces),
            out_specs=pl.BlockSpec(memory_space=pl.ANY),
            scratch_shapes=[pltpu.SemaphoreType.DMA((len(pieces),))],
        ),
        out_shape=jax.ShapeDtypeStruct(tuple(shape), pieces[0].dtype),
        cost_estimate=pl.CostEstimate(flops=0, bytes_accessed=2 * size, transcendentals=0),
    )(jnp.stack(offsets).astype(jnp.int32), *pieces)


def widen_kernel(where, *refs, group):
    *shares, out = refs
    count, core = (len(shares) + 1) // 2, where[1]
    piece = shares[0].shape[2]
    for d in range(count):
        plane = lax.rem(where[0] + count - d, count)
        batch, part = plane // group, lax.rem(plane, group)
        for j in range(CORES):
            got = shares[d][j].astype(F32)
            if d:
                got = got + shares[2 * count - 1 - d][j].astype(F32)
            k = core if j == 0 else 1 - core
            at = pl.multiple_of((k * group + part) * piece, piece)
            out[batch, :, pl.ds(at, piece)] = got


def widen(shares, feat_rank, core, micro, group, width):
    _, block, piece = shares[0].shape
    tile = 128
    return pl.pallas_call(
        functools.partial(widen_kernel, group=group),
        grid_spec=pltpu.PrefetchScalarGridSpec(
            num_scalar_prefetch=1,
            grid=(block // tile,),
            in_specs=[pl.BlockSpec((CORES, tile, piece), lambda i, w: (0, i, 0))] * len(shares),
            out_specs=pl.BlockSpec((micro, tile, width), lambda i, w: (0, i, 0)),
        ),
        out_shape=jax.ShapeDtypeStruct((micro, block, width), F32),
        compiler_params=pltpu.CompilerParams(vmem_limit_bytes=48 * 2**20),
    )(jnp.stack([feat_rank, core]).astype(jnp.int32), *shares)


def on_device(
    tokens,
    cotangent,
    lengths,
    w_query,
    w_key,
    w_value,
    w_output,
    w_gate,
    w_up,
    w_down,
    gain_mixer,
    gain_mlp,
):
    micro, block, width = tokens.shape
    seq_count, feat_count = lax.axis_size("seq"), lax.axis_size("feat")
    seq_rank, feat_rank = lax.axis_index("seq"), lax.axis_index("feat")
    group = feat_count // micro
    ranks = CORES * group
    chips = seq_count // CORES
    chip, core = seq_rank // CORES, seq_rank % CORES
    batch, part = feat_rank // group, feat_rank % group
    rank = core * group + part
    rows = CORES * block
    piece = width // ranks
    heads = HEADS // ranks

    def move(value, target):
        pairs = []
        for s in range(seq_count):
            for f in range(feat_count):
                there = target(s // CORES, s % CORES, f // group, f % group)
                if there is not None:
                    c2, k2, m2, l2 = there
                    pairs.append(
                        (s * feat_count + f, (c2 * CORES + k2) * feat_count + m2 * group + l2)
                    )
        return lax.ppermute(value, ("seq", "feat"), pairs)

    def to_core(value):
        return move(value, lambda c, k, m, l: (c, 1 - k, m, l))

    def to_part(value, d):
        return move(value, lambda c, k, m, l: (c, k, m, l ^ d))

    def to_chip(value, mask):
        return move(value, lambda c, k, m, l: (c ^ mask, k, m, l))

    def shift_chip(value, d):
        return move(value, lambda c, k, m, l: (c + d, k, m, l) if 0 <= c + d < chips else None)

    def spread(value):
        return (
            move(value, lambda c, k, m, l: (c, m, k, l)),
            move(value, lambda c, k, m, l: (c, m, 1 - k, l)),
        )

    def unspread(same, other):
        return (
            move(same, lambda c, k, m, l: (c, m, k, l)),
            move(other, lambda c, k, m, l: (c, 1 - m, k, l)),
        )

    def ordered(first_if_zero, second_if_zero, bit, axis):
        return jnp.where(
            bit == 0,
            jnp.concatenate([first_if_zero, second_if_zero], axis),
            jnp.concatenate([second_if_zero, first_if_zero], axis),
        )

    def gather_chips(value, axis=0, needs=()):
        size = value.shape[axis]
        bits = [1 << i for i in range(chips.bit_length() - 1)]
        pieces, offsets = [], []
        owns = spread(after(value, *needs) if needs else value)
        for own, order, k in zip(owns, (bits, bits[::-1]), (batch, 1 - batch)):
            held = {0: own}
            for bit in order:
                for mask in list(held):
                    held[mask | bit] = to_chip(held[mask], bit)
            for mask, got in held.items():
                pieces.append(got)
                offsets.append(((chip ^ mask) * CORES + k) * size)
        return place(pieces, offsets, axis), owns

    chip_groups = [[c * CORES + k for c in range(chips)] for k in range(CORES)]

    def scatter_chips(value, axis):
        mine = lax.psum_scatter(
            value.astype(BF),
            "seq",
            scatter_dimension=axis,
            tiled=True,
            axis_index_groups=chip_groups,
        )
        size = mine.shape[axis] // CORES
        same = lax.dynamic_slice_in_dim(mine, batch * size, size, axis)
        other = lax.dynamic_slice_in_dim(mine, (1 - batch) * size, size, axis)
        a, b = unspread(same, other)
        return a.astype(F32) + b.astype(F32)

    def gather_ranks(own):
        found = []
        for d in range(group):
            here = own if d == 0 else to_part(own, d)
            found.append((core * group + (part ^ d), here))
            found.append(((1 - core) * group + (part ^ d), to_core(here)))
        return found

    def reduce_ranks(partial, needs=()):
        arrived = []
        for d in range(group - 1, -1, -1):
            away = to_core(partial((1 - core) * group + (part ^ d)).astype(BF))
            total = partial(core * group + (part ^ d)) + away.astype(F32)
            if d:
                total = total.astype(BF)
                total = after(total, *needs) if needs else total
                total = to_part(total, d).astype(F32)
            arrived.append(total)
        return sum(arrived[:-1], arrived[-1])

    def sum_ranks(value):
        for d in [1 << i for i in range(group.bit_length() - 1)]:
            value = value + to_part(value, d)
        return value + to_core(value)

    def row_piece(value, r):
        return lax.dynamic_slice_in_dim(value, r * piece, piece, 0)

    def column_piece(value, r):
        return lax.dynamic_slice_in_dim(value, r * piece, piece, 1)

    def chip_tokens(value):
        own = lax.dynamic_index_in_dim(value, batch, 0, False)
        return place([own, to_core(own)], [core * block, (1 - core) * block], 0)

    tokens_c = chip_tokens(tokens)
    grad_out = chip_tokens(cotangent)

    qk_width, v_width = heads * QK, heads * HEAD_V
    qkv_full, first = gather_chips(jnp.concatenate([w_query, w_key, w_value], 1))
    gains = lax.all_gather(jnp.stack([gain_mixer, gain_mlp]), "seq", axis=1, tiled=True)
    gains = gains.astype(F32)
    mixer_gain, mlp_gain = gains[0], gains[1]
    output_full, first = gather_chips(w_output, 0, first)
    gate_full, first = gather_chips(w_gate, 0, first)
    up_full, first = gather_chips(w_up, 0, first)
    down_full, first = gather_chips(w_down, 1, first)

    bounds = jnp.cumsum(lax.dynamic_index_in_dim(lengths, batch, 0, False))

    def segment_of(p):
        return jnp.sum((p[..., None] >= bounds).astype(jnp.int32), axis=-1)

    start = chip * rows
    base = start + block * jnp.arange(CORES + 1, dtype=jnp.int32)
    edges = jnp.where(base == 0, -1, segment_of(base - 1))
    keep = (edges[1:] == edges[:-1]).astype(F32)
    base = base[:-1]
    ends = jnp.concatenate([jnp.zeros((1,), jnp.int32), bounds])
    open_end = jnp.where((edges[:-1] < 0) | (edges[:-1] > 2), 0, ends[edges[:-1] + 1] - base)
    tail_start = jnp.where(edges[1:] > 2, block, ends[edges[1:]] - base)
    marks = jnp.concatenate(
        [bounds[None, :] - base[:, None], open_end[:, None], tail_start[:, None]], 1
    ).astype(jnp.int32)

    tokens_f = tokens_c.astype(F32)
    inv_one = lax.rsqrt(jnp.mean(tokens_f * tokens_f, axis=-1, keepdims=True) + EPS)
    normed = (tokens_f * inv_one * mixer_gain).astype(BF)
    qkv = dot(normed, qkv_full).astype(BF)

    query, keys = qkv[:, :qk_width], qkv[:, qk_width : 2 * qk_width]
    values = qkv[:, 2 * qk_width :]
    local_states, mixer, grad_states, mixer_back = mixer_calls(heads, block, CORES)

    def pack(state, total):
        total = jnp.pad(total, ((0, 0), (0, -NFEAT % HEAD_V))).reshape(-1, HEAD_V)
        return jnp.concatenate([state.reshape(-1, HEAD_V), total], 0).astype(BF)

    def unpack(flat):
        flat = flat.astype(F32)
        cut = heads * NFEAT
        return (
            flat[:cut].reshape(heads, NFEAT, HEAD_V),
            flat[cut:].reshape(heads, -1)[:, :NFEAT],
        )

    def scan_blocks(both, blocks_order, step):
        state, total = both[..., :HEAD_V], both[..., HEAD_V]
        at_end = (state[blocks_order[0]], total[blocks_order[0]])
        for i in blocks_order[1:]:
            carry_keep = keep[i]
            at_end = (
                state[i] + carry_keep * at_end[0],
                total[i] + carry_keep * at_end[1],
            )
        message = pack(*at_end)
        run = None
        for d in range(1, chips):
            got = unpack(shift_chip(message, step * d))
            other = chip - step * d
            if step > 0:
                same = edges[0] == segment_of((other + 1) * rows - 1)
            else:
                same = edges[CORES] == segment_of(other * rows - 1)
            weight = (same & (other >= 0) & (other < chips)).astype(F32)
            term = (weight * got[0], weight * got[1])
            run = term if run is None else (run[0] + term[0], run[1] + term[1])
        found = {}
        for i in blocks_order:
            found[i] = run
            run = (state[i] + keep[i] * run[0], total[i] + keep[i] * run[1])
        state, total = (jnp.stack([found[i][j] for i in range(CORES)]) for j in range(2))
        total = jnp.broadcast_to(total[..., None], state.shape)
        both = jnp.concatenate([state, total], -1).astype(BF)
        return jnp.pad(both, ((0, 0), (0, 0), (0, LANES - NFEAT), (0, 0)))

    (local,) = local_states(marks, keys, values)
    states = scan_blocks(local, list(range(CORES)), 1)
    mixer_own, denom = mixer(marks, query, keys, values, states)

    mixer_parts = gather_ranks(mixer_own)
    branch_own = sum(dot(got, row_piece(output_full, r)) for r, got in mixer_parts).astype(BF)
    branch_parts = gather_ranks(branch_own)
    branch = place([got for _, got in branch_parts], [r * piece for r, _ in branch_parts], 1)
    hidden_state = tokens_f + branch.astype(F32)
    inv_two = lax.rsqrt(jnp.mean(hidden_state * hidden_state, axis=-1, keepdims=True) + EPS)
    normed_two = (hidden_state * inv_two * mlp_gain).astype(BF)

    grad_hidden = dot(grad_out, down_full, 1, 1).astype(BF).astype(F32)
    gate = dot(normed_two, gate_full).astype(BF).astype(F32)
    upward = dot(normed_two, up_full).astype(BF).astype(F32)
    logistic = jax.nn.sigmoid(gate)
    activated = gate * logistic
    hidden = (activated * upward).astype(BF)
    grad_gate_f = grad_hidden * upward * logistic * (1.0 + gate * (1.0 - logistic))
    grad_up_f = grad_hidden * activated
    grad_gate_b, grad_up_b = grad_gate_f.astype(BF), grad_up_f.astype(BF)
    inner_two = sum_ranks(jnp.sum(grad_gate_f * gate + grad_up_f * upward, axis=1)) / width
    normed_grad = reduce_ranks(
        lambda r: dot(grad_gate_b, row_piece(gate_full, r), 1, 1)
        + dot(grad_up_b, row_piece(up_full, r), 1, 1),
        (inner_two,),
    )
    tokens_own = column_piece(tokens_c, rank).astype(F32)
    hidden_own = tokens_own + branch_own.astype(F32)
    scaled_two = hidden_own * inv_two
    mlp_gain_own = lax.dynamic_slice_in_dim(mlp_gain, rank * piece, piece, 0)
    hidden_grad = column_piece(grad_out, rank).astype(F32) + inv_two * (
        normed_grad * mlp_gain_own - scaled_two * inner_two[:, None]
    )
    grad_gain_mlp = jnp.sum(normed_grad * scaled_two, axis=0)
    branch_grad = hidden_grad.astype(BF)

    mixer_grad = reduce_ranks(lambda r: dot(branch_grad, row_piece(output_full, r), 1, 1))
    (grad_local,) = grad_states(marks, query, mixer_grad, mixer_own, denom)
    carried = scan_blocks(grad_local, list(range(CORES))[::-1], -1)
    grad_qkv = jnp.concatenate(
        mixer_back(
            marks, query, keys, values, mixer_grad, mixer_own, denom, states, carried
        ),
        1,
    )
    inner_one = jnp.sum(grad_qkv.astype(F32) * qkv.astype(F32), axis=1)
    inner_one = sum_ranks(inner_one) / width
    input_normed = reduce_ranks(
        lambda r: dot(grad_qkv, row_piece(qkv_full, r), 1, 1), (inner_one,)
    )
    scaled_one = tokens_own * inv_one
    mixer_gain_own = lax.dynamic_slice_in_dim(mixer_gain, rank * piece, piece, 0)
    grad_gain_mixer = jnp.sum(input_normed * scaled_one, axis=0)
    input_own = (
        hidden_grad
        + inv_one * (input_normed * mixer_gain_own - scaled_one * inner_one[:, None])
    ).astype(BF)

    def half(value, k):
        return lax.dynamic_slice_in_dim(value, k * block, block, 0)

    gain_grads = lax.dynamic_update_slice_in_dim(
        jnp.zeros((2, width), F32), jnp.stack([grad_gain_mixer, grad_gain_mlp]), rank * piece, 1
    )
    planes = [
        move(gain_grads, lambda c, k, m, l: (c, k, *divmod((m * group + l) ^ d, group)))
        for d in range(1, feat_count)
    ]
    input_own = after(input_own, gain_grads)
    input_pair = jnp.stack([half(input_own, core), to_core(half(input_own, 1 - core))])

    def step_plane(value, step, first):
        def target(c, k, m, l):
            here = m * group + l
            behind = here if step > 0 else feat_count - 1 - here
            if behind < first or behind == feat_count - 1:
                return None
            return (c, k, *divmod(here + step, group))

        return move(value, target)

    ups, downs = [input_pair], [input_pair]
    for d in range(feat_count - 1):
        ups.append(step_plane(ups[-1], 1, d))
        downs.append(step_plane(downs[-1], -1, d))
    input_grad = widen(ups + downs[1:], feat_rank, core, micro, group, width)

    gain_grads = sum(planes, gain_grads)
    gain_grads = gain_grads + to_core(gain_grads)
    for bit in [1 << i for i in range(chips.bit_length() - 1)]:
        gain_grads = gain_grads + to_chip(gain_grads, bit)
    shard = width // seq_count
    gain_grads = lax.dynamic_slice_in_dim(gain_grads, seq_rank * shard, shard, 1)

    mlp_own = reduce_ranks(lambda r: dot(hidden, column_piece(down_full, r)), (mixer_grad,))
    mixed_own = (hidden_own + mlp_own).astype(BF)
    same, other = unspread(half(mixed_own, batch), half(mixed_own, 1 - batch))
    mixed = ordered(same[None], other[None], core, 0)

    grad_gate = scatter_chips(dot(normed_two, grad_gate_b, 0, 0), 0)
    grad_up = scatter_chips(dot(normed_two, grad_up_b, 0, 0), 0)
    grad_down = scatter_chips(dot(hidden, grad_out, 0, 0), 1)
    grad_output = place(
        [dot(got, branch_grad, 0, 0).astype(BF) for _, got in mixer_parts],
        [r * piece for r, _ in mixer_parts],
        0,
    )
    grad_output = scatter_chips(grad_output, 0)
    grad_qkv_w = scatter_chips(dot(normed, grad_qkv, 0, 0), 0)

    return (
        mixed,
        input_grad,
        grad_qkv_w[:, :qk_width],
        grad_qkv_w[:, qk_width : 2 * qk_width],
        grad_qkv_w[:, 2 * qk_width :],
        grad_output,
        grad_gate,
        grad_up,
        grad_down,
        gain_grads[0],
        gain_grads[1],
    )


def solution(mesh):
    in_specs = (
        P(None, "seq", None),
        P(None, "seq", None),
        P(),
        P("seq", "feat"),
        P("seq", "feat"),
        P("seq", "feat"),
        P("seq", "feat"),
        P("seq", "feat"),
        P("seq", "feat"),
        P("feat", "seq"),
        P("seq"),
        P("seq"),
    )
    out_specs = (
        P(None, "seq", "feat"),
        P(None, "seq", None),
        P("seq", "feat"),
        P("seq", "feat"),
        P("seq", "feat"),
        P("seq", "feat"),
        P("seq", "feat"),
        P("seq", "feat"),
        P("feat", "seq"),
        P("seq"),
        P("seq"),
    )
    return jax.shard_map(
        on_device, mesh=mesh, in_specs=in_specs, out_specs=out_specs, check_vma=False
    )
```

time: 1100 us -> 2320 us (2.11)
  Pallas kernels: 0 us -> 1370 us
  blocking collectives: 117 us -> 8.2 us
  matrix products: 273 us -> 209 us
  waiting for transfers between devices: 341 us -> 397 us
  local copies, waits for them, and re-layouts: 129 us -> 74.9 us
  starting transfers between devices: 139 us -> 179 us
  other arithmetic: 75.1 us -> 41.2 us
    pallas_call x0 -> x14, Pallas kernels: none -> 1370 us  [the longest x9 1310 us: place(): pl.pallas_call(functools.partial(place_kernel, axis=axis), grid_spec=pltp...]
    psum x1 -> x0, blocking collectives: 109 us -> none  [on_device(): gain_grads = lax.psum(gain_grads, ('seq', 'feat'))]
    dot_general x21 -> x0, matrix products: 62.4 us -> none  [ein(): return jnp.einsum(spec, *args, preferred_element_type=F32)]
    ppermute x65 -> x95, waiting for transfers between devices: 341 us -> 397 us  [move(): return lax.ppermute(value, ('seq', 'feat'), pairs)]
    convert_element_type x6 -> x0, local copies, waits for them, and re-layouts: 42 us -> none  [the longest x2 36.3 us: on_device(): input_grad.transpose(0, 3, 2, 1, 4).reshape(micro, block, width).astype(F32)]
    ppermute x65 -> x95, starting transfers between devices: 137 us -> 179 us  [move(): return lax.ppermute(value, ('seq', 'feat'), pairs)]
    ppermute x0 -> x16, local copies, waits for them, and re-layouts: none -> 36 us  [move(): return lax.ppermute(value, ('seq', 'feat'), pairs)]
  transfers between devices with their start and end apart: 74 -> 100, of which waited for: 22 -> 31; matrix products, arithmetic and copies ran while one was open for 34% -> 10% of each run, Pallas kernels for 0% -> 48%
where the time goes in v2:
time: 2320 us; the launch traced here: 2300 us
  Pallas kernels  1370 us (59%)
  waiting for transfers between devices  397 us (17%)
  matrix products  209 us (9%)
  starting transfers between devices  179 us (8%)
  local copies, waits for them, and re-layouts  74.9 us (3%)
  other arithmetic  41.2 us (2%)
  between operations  23.4 us (1%)
    pallas_call x9, Pallas kernels, place(): pl.pallas_call(functools.partial(place_kernel, axis=axis), grid_spec=pltp...  1310 us
    ppermute x95, waiting for transfers between devices, move(): return lax.ppermute(value, ('seq', 'feat'), pairs)  397 us
    dot_general x36, matrix products, dot(): lax.dot_general(a, b, (((ca,), (cb,)), ((), ())), preferred_element_type=...  209 us
    ppermute x95, starting transfers between devices, move(): return lax.ppermute(value, ('seq', 'feat'), pairs)  179 us
    pallas_call x4, Pallas kernels, run(): pl.pallas_call(functools.partial(kernel, heads=heads, block=block), grid_...  46.5 us
  transfers between devices with their start and end apart: 100, of which 31 were waited for; matrix products, arithmetic and copies ran while one was open for 10% of the time, Pallas kernels for 48%

profile of v2, /device:TPU:7, one launch (start us, length us, event | category | flops | bytes accessed | tf_op | source)
XLA Modules:
  0.0 2302.9 jit_solution(3227577012821517217)
XLA Ops:
  12.2 4.4 collective-permute-start.1
  19.5 8.2 all_gather.3
  34.5 6.4 collective-permute-done.2.refs_1_
  43.0 6.2 collective-permute-done.3.refs_2_
  55.1 81.2 %shard_map.240 = bf16[2048,640]{1,0:T(8,128)(2,1)} custom-call(s32[8]{0:T(128)} %stack.175.offsets, bf16[256,640]{1,0:T(8,128)(2,1)} %collective-permute-done.1.refs_0_, bf16[256,640]{1,0:T(8,128)(2,1)} %copy-done.47, bf16[256,640]{1,0:T(8,128)(2,1)} %copy-done.49, bf16[256,640]{1,0:T(8,128)(2,1)} %copy-done.51, ...), custom_call_target="tpu_custom_call" | custom-call | bytes 5242880 | tf_op jit(solution)/shard_map/pallas_call | solution.py:287
  136.3 192.5 %shard_map.239 = bf16[1536,2048]{1,0:T(8,128)(2,1)} custom-call(s32[2]{0:T(128)} %pad_add_fusion.1.offsets, bf16[768,2048]{1,0:T(8,128)(2,1)} %copy-done.20, bf16[768,2048]{1,0:T(8,128)(2,1)} %collective-permute-done.refs_1_), custom_call_target="tpu_custom_call" | custom-call | bytes 12582912 | tf_op jit(solution)/shard_map/pallas_call | solution.py:287
  328.9 4.2 fusion
  333.5 5.4 convolution_convert_fusion.7
  340.3 4.3 shard_map.241
  375.1 9.2 shard_map.242
  384.4 7.4 collective-permute-done.26
  407.9 16.4 collective-permute-done.19.refs_7_
  424.3 4.4 collective-permute-start.28
  428.7 8.7 collective-permute-done.34
  444.3 12.7 collective-permute-done.31
  459.2 13.4 collective-permute-done.35
  477.9 65.4 %shard_map.243 = bf16[2048,512]{1,0:T(8,128)(2,1)} custom-call(s32[8]{0:T(128)} %stack.175.offsets, bf16[256,512]{1,0:T(8,128)(2,1)} %collective-permute-done.12.refs_0_, bf16[256,512]{1,0:T(8,128)(2,1)} %collective-permute-done.13.refs_1_, bf16[256,512]{1,0:T(8,128)(2,1)} %collective-permute-done.14.refs_2_, bf16[256,512]{1,0:T(8,128)(2,1)} %copy-done.52, ...), custom_call_target="tpu_custom_call" | custom-call | bytes 4194304 | tf_op jit(solution)/shard_map/pallas_call | solution.py:287
  546.7 11.6 collective-permute-start.42
  563.4 25.8 %collective-permute-done.42.refs_0_ = bf16[1376,256]{1,0:T(8,128)(2,1)} collective-permute-done((bf16[1376,256]{1,0:T(8,128)(2,1)S(1)}, bf16[1376,256]{1,0:T(8,128)(2,1)}, u32[]{:S(2)}, u32[]{:S(2)}) %collective-permute-start.42) | collective-permute-done | bytes 704544 | tf_op jit(solution)/shard_map/ppermute | solution.py:370
  592.8 15.0 collective-permute-done.37
  609.6 14.2 collective-permute-done.43.refs_1_
  648.1 176.5 %shard_map.245 = bf16[2048,1376]{1,0:T(8,128)(2,1)} custom-call(s32[8]{0:T(128)} %stack.175.offsets, bf16[256,1376]{1,0:T(8,128)(2,1)} %copy.116.refs_0_, bf16[256,1376]{1,0:T(8,128)(2,1)} %copy.117.refs_1_, bf16[256,1376]{1,0:T(8,128)(2,1)} %copy.118.refs_2_, bf16[256,1376]{1,0:T(8,128)(2,1)} %copy.119.refs_3_, bf16[256,1376]{1,0:T(8,128)(2,1)} %copy.120.refs_4_, ...), custom_call_target="tpu_custom_call" | custom-call | bytes 11272192 | tf_op jit(solution)/shard_map/pallas_call | solution.py:287
  833.8 192.4 %shard_map.248 = bf16[1536,2048]{1,0:T(8,128)(2,1)} custom-call(s32[2]{0:T(128)} %pad_add_fusion.1.offsets, bf16[768,2048]{1,0:T(8,128)(2,1)} %dynamic-slice_bitcast_fusion.refs_0_, bf16[768,2048]{1,0:T(8,128)(2,1)} %collective-permute-done.52.refs_1_), custom_call_target="tpu_custom_call" | custom-call | bytes 12582912 | tf_op jit(solution)/shard_map/pallas_call | solution.py:287
  1030.6 176.5 %shard_map.246 = bf16[2048,1376]{1,0:T(8,128)(2,1)} custom-call(s32[8]{0:T(128)} %stack.175.offsets, bf16[256,1376]{1,0:T(8,128)(2,1)} %copy.124.refs_0_, bf16[256,1376]{1,0:T(8,128)(2,1)} %copy.125.refs_1_, bf16[256,1376]{1,0:T(8,128)(2,1)} %copy.126.refs_2_, bf16[256,1376]{1,0:T(8,128)(2,1)} %copy.127.refs_3_, bf16[256,1376]{1,0:T(8,128)(2,1)} %copy.128.refs_4_, ...), custom_call_target="tpu_custom_call" | custom-call | bytes 11272192 | tf_op jit(solution)/shard_map/pallas_call | solution.py:287
  1207.2 172.6 %shard_map.247 = bf16[1376,2048]{1,0:T(8,128)(2,1)} custom-call(s32[8]{0:T(128)} %stack.175.offsets, bf16[1376,256]{1,0:T(8,128)(2,1)} %collective-permute-done.42.refs_0_, bf16[1376,256]{1,0:T(8,128)(2,1)} %collective-permute-done.43.refs_1_, bf16[1376,256]{1,0:T(8,128)(2,1)} %collective-permute-done.44.refs_2_, ...), custom_call_target="tpu_custom_call" | custom-call | bytes 11272192 | tf_op jit(solution)/shard_map/pallas_call | solution.py:287
  1380.4 14.3 convolution_convert_fusion.3
  1395.8 192.4 %shard_map.244 = bf16[1536,2048]{1,0:T(8,128)(2,1)} custom-call(s32[4]{0:T(128)} %pad_add_fusion.3.offsets, bf16[1536,512]{1,0:T(8,128)(2,1)} %copy-done.29, bf16[1536,512]{1,0:T(8,128)(2,1)} %copy-done.34, bf16[1536,512]{1,0:T(8,128)(2,1)} %collective-permute-done.24.refs_2_, bf16[1536,512]{1,0:T(8,128)(2,1)} %collective-permute-done.25.refs_3_), custom_call_target="tpu_custom_call" | custom-call | bytes 12582912 | tf_op jit(solution)/shard_map/pallas_call | solution.py:287
  1588.2 6.9 multiply_reduce_fusion
  1595.1 5.7 multiply_convert_fusion
  1603.5 13.3 convolution_convert_fusion.4
  1616.8 22.7 fusion.23
  1639.5 5.5 fusion.46
  1645.0 5.0 fusion.30
  1666.7 32.2 %collective-permute-done.57 = bf16[1536,512]{1,0:T(8,128)(2,1)S(1)} collective-permute-done((bf16[1536,512]{1,0:T(8,128)(2,1)S(1)}, bf16[1536,512]{1,0:T(8,128)(2,1)S(1)}, u32[]{:S(2)}, u32[]{:S(2)}) %collective-permute-start.57) | collective-permute-done | bytes 1572896 | tf_op jit(solution)/shard_map/ppermute | solution.py:370
  1699.0 7.4 fusion.127
  1715.2 65.3 %shard_map.252 = bf16[2048,512]{1,0:T(8,128)(2,1)} custom-call(s32[4]{0:T(128)} %pad_add_fusion.3.offsets, bf16[512,512]{1,0:T(8,128)(2,1)} %convolution_convert_fusion.17.refs_0_, bf16[512,512]{1,0:T(8,128)(2,1)} %convolution_convert_fusion.16.refs_1_, bf16[512,512]{1,0:T(8,128)(2,1)} %convolution_convert_fusion.15.refs_2_, ...), custom_call_target="tpu_custom_call" | custom-call | bytes 4194304 | tf_op jit(solution)/shard_map/pallas_call | solution.py:287
  1780.6 13.9 convolution_convert_fusion.1
  1794.5 14.6 convolution_convert_fusion
  1813.7 13.9 convolution_convert_fusion.2
  1840.2 30.3 %collective-permute-done.60 = bf16[1536,512]{1,0:T(8,128)(2,1)} collective-permute-done((bf16[1536,512]{1,0:T(8,128)(2,1)}, bf16[1536,512]{1,0:T(8,128)(2,1)}, u32[]{:S(2)}, u32[]{:S(2)}) %collective-permute-start.60) | collective-permute-done | bytes 1572896 | tf_op jit(solution)/shard_map/ppermute | solution.py:370
  1870.5 5.2 fusion.15.do_ref
  1875.7 6.6 shard_map.249
  1891.5 6.4 convolution_convert_fusion.12
  1904.2 26.3 %shard_map.250 = (bf16[1536,64]{1,0:T(8,128)(2,1)S(1)}, bf16[1536,64]{1,0:T(8,128)(2,1)S(1)}, bf16[1536,512]{1,0:T(8,128)(2,1)S(1)}) custom-call(s32[2,5]{1,0:T(2,128)S(1)} %pad_add_fusion.marks, bf16[1536,64]{1,0:T(8,128)(2,1)S(1)} %copy-done.8, bf16[1536,64]{1,0:T(8,128)(2,1)S(1)} %get-tuple-element.141.k_ref, bf16[1536,512]{1,0:T(8,128)(2,1)} %copy-done.3, ...), custom_call_target="tpu_custom_call" | custom-call | flops 15360000000 | bytes 9216000 | tf_op jit(solution)/shard_map/pallas_call | solution.py:220
  1932.3 6.7 convolution_convert_fusion.13
  1940.5 5.5 fusion.34
  1953.6 7.4 convolution_convert_fusion.6
  1961.1 54.5 %collective-permute-done.71 = bf16[1536,512]{1,0:T(8,128)(2,1)} collective-permute-done((bf16[1536,512]{1,0:T(8,128)(2,1)}, bf16[1536,512]{1,0:T(8,128)(2,1)}, u32[]{:S(2)}, u32[]{:S(2)}) %collective-permute-start.71) | collective-permute-done | bytes 1572896 | tf_op jit(solution)/shard_map/ppermute | solution.py:370
  2015.5 7.8 fusion.28
  2026.0 4.9 collective-permute-start.82
  2034.9 7.8 fusion.32
  2047.6 24.7 %collective-permute-done.89 = f32[2,2048]{1,0:T(2,128)S(1)} collective-permute-done((f32[2,2048]{1,0:T(2,128)S(1)}, f32[2,2048]{1,0:T(2,128)S(1)}, u32[]{:S(2)}, u32[]{:S(2)}) %collective-permute-start.89) | collective-permute-done | bytes 16416 | tf_op jit(solution)/shard_map/ppermute | solution.py:370
  2072.2 4.7 collective-permute-start.81
  2079.8 20.4 collective-permute-done.81
  2104.0 20.7 collective-permute-done.62
  2136.2 5.4 collective-permute-start.86
  2149.9 21.5 collective-permute-done.83
  2171.4 43.1 %collective-permute-start.87 = (bf16[1376,256]{1,0:T(8,128)(2,1)}, bf16[1376,256]{1,0:T(8,128)(2,1)S(1)}, u32[]{:S(2)}, u32[]{:S(2)}) collective-permute-start(bf16[1376,256]{1,0:T(8,128)(2,1)} %get-tuple-element.147), channel_id=1, source_target_pairs={{0,0},{1,1},{2,4},{3,5},{4,2},{5,3},{6,6},{7,7},{8,8},{9,9},{10,12... | collective-permute-start | bytes 2113544 | tf_op jit(solution)/shard_map/ppermute | solution.py:370
  2217.1 10.8 collective-permute-done.85
  2233.6 7.1 collective-permute-start.79
  2240.7 9.3 collective-permute-done.87
  2251.2 5.8 collective-permute-done.79
  2259.5 27.1 %collective-permute-done.78.refs_6_ = bf16[2,768,512]{2,1,0:T(8,128)(2,1)} collective-permute-done((bf16[2,768,512]{2,1,0:T(8,128)(2,1)}, bf16[2,768,512]{2,1,0:T(8,128)(2,1)}, u32[]{:S(2)}, u32[]{:S(2)}) %collective-permute-start.78) | collective-permute-done | bytes 1572896 | tf_op jit(solution)/shard_map/ppermute | solution.py:370
  2286.6 9.4 shard_map.251
  (494 shorter events, 252.1 us)
Async XLA Ops:
  7.2 2017.8 %reduce-scatter.8.cloned.1.call-start = ((), (), s32[]{:S(2)}) async-start(), calls=%async_computation.6 | async-start | bytes 2621440 | tf_op jit(solution)/shard_map/reduce_scatter | solution.py:421
  9.5 126.9 %collective-permute-start = (bf16[768,2048]{1,0:T(8,128)(2,1)S(1)}, bf16[768,2048]{1,0:T(8,128)(2,1)}, u32[]{:S(2)}, u32[]{:S(2)}) collective-permute-start(bf16[768,2048]{1,0:T(8,128)(2,1)S(1)} %dynamic-slice_bitcast_fusion.1.refs_0_), channel_id=1, source_target_pairs={{0,4},{1,5},{2,6},{3,7},{4,0},{5,1},{6,2},{7,3},{8,12},{9,13},{10,... | collective-permute-start | bytes 9437192 | tf_op jit(solution)/shard_map/ppermute | solution.py:370
  12.2 18.8 collective-permute-start.1
  49.3 307.5 %collective-permute-start.12 = (bf16[256,512]{1,0:T(8,128)(2,1)}, bf16[256,512]{1,0:T(8,128)(2,1)}, u32[]{:S(2)}, u32[]{:S(2)}) collective-permute-start(bf16[256,512]{1,0:T(8,128)(2,1)} %param.22), channel_id=1, source_target_pairs={{0,0},{1,1},{2,4},{3,5},{4,2},{5,3},{6,6},{7,7},{8,8},{9,9},{10,12... | collective-permute-start | bytes 786440 | tf_op jit(solution)/shard_map/ppermute | solution.py:370
  51.2 305.6 %collective-permute-start.16 = (bf16[256,512]{1,0:T(8,128)(2,1)}, bf16[256,512]{1,0:T(8,128)(2,1)}, u32[]{:S(2)}, u32[]{:S(2)}) collective-permute-start(bf16[256,512]{1,0:T(8,128)(2,1)} %param.22), channel_id=1, source_target_pairs={{0,2},{1,3},{2,6},{3,7},{4,0},{5,1},{6,4},{7,5},{8,10},{9,11},{10,... | collective-permute-start | bytes 786440 | tf_op jit(solution)/shard_map/ppermute | solution.py:370
  349.6 21.0 collective-permute-start.9
  356.8 35.0 %collective-permute-start.26 = (bf16[256,1376]{0,1:T(8,128)(2,1)}, bf16[256,1376]{0,1:T(8,128)(2,1)}, u32[]{:S(2)}, u32[]{:S(2)}) collective-permute-start(bf16[256,1376]{0,1:T(8,128)(2,1)} %param.23), channel_id=1, source_target_pairs={{0,0},{1,1},{2,4},{3,5},{4,2},{5,3},{6,6},{7,7},{8,8},{9,9},{10,12... | collective-permute-start | bytes 2113544 | tf_op jit(solution)/shard_map/ppermute | solution.py:370
  360.2 33.0 %collective-permute-start.30 = (bf16[256,1376]{0,1:T(8,128)(2,1)}, bf16[256,1376]{0,1:T(8,128)(2,1)}, u32[]{:S(2)}, u32[]{:S(2)}) collective-permute-start(bf16[256,1376]{0,1:T(8,128)(2,1)} %param.23), channel_id=1, source_target_pairs={{0,2},{1,3},{2,6},{3,7},{4,0},{5,1},{6,4},{7,5},{8,10},{9,11},{10,... | collective-permute-start | bytes 2113544 | tf_op jit(solution)/shard_map/ppermute | solution.py:370
  363.8 32.2 %collective-permute-start.13 = (bf16[256,512]{1,0:T(8,128)(2,1)}, bf16[256,512]{1,0:T(8,128)(2,1)}, u32[]{:S(2)}, u32[]{:S(2)}) collective-permute-start(bf16[256,512]{1,0:T(8,128)(2,1)} %collective-permute-done.12.refs_0_), channel_id=1, source_target_pairs={{0,8},{1,9},{2,10},{3,11},{4,12},{5,13},{6,14},{7,15},{8,0},{9,1},... | collective-permute-start | bytes 786440 | tf_op jit(solution)/shard_map/ppermute | solution.py:370
  366.2 29.9 %collective-permute-start.14 = (bf16[256,512]{1,0:T(8,128)(2,1)}, bf16[256,512]{1,0:T(8,128)(2,1)}, u32[]{:S(2)}, u32[]{:S(2)}) collective-permute-start(bf16[256,512]{1,0:T(8,128)(2,1)} %collective-permute-done.12.refs_0_), channel_id=1, source_target_pairs={{0,16},{1,17},{2,18},{3,19},{4,20},{5,21},{6,22},{7,23},{8,24},{9,... | collective-permute-start | bytes 786440 | tf_op jit(solution)/shard_map/ppermute | solution.py:370
  370.6 27.9 %collective-permute-start.17 = (bf16[256,512]{1,0:T(8,128)(2,1)}, bf16[256,512]{1,0:T(8,128)(2,1)}, u32[]{:S(2)}, u32[]{:S(2)}) collective-permute-start(bf16[256,512]{1,0:T(8,128)(2,1)} %collective-permute-done.16.refs_4_), channel_id=1, source_target_pairs={{0,16},{1,17},{2,18},{3,19},{4,20},{5,21},{6,22},{7,23},{8,24},{9,... | collective-permute-start | bytes 786440 | tf_op jit(solution)/shard_map/ppermute | solution.py:370
  391.8 50.3 %collective-permute-start.21 = (bf16[1536,512]{1,0:T(8,128)(2,1)S(1)}, bf16[1536,512]{1,0:T(8,128)(2,1)S(1)}, u32[]{:S(2)}, u32[]{:S(2)}) collective-permute-start(bf16[1536,512]{1,0:T(8,128)(2,1)S(1)} %get-tuple-element.24.o_ref), channel_id=1, source_target_pairs={{0,1},{1,0},{2,3},{3,2},{4,5},{5,4},{6,7},{7,6},{8,9},{9,8},{10,11... | collective-permute-start | bytes 4718600 | tf_op jit(solution)/shard_map/ppermute | solution.py:370
  393.2 44.2 %collective-permute-start.34 = (bf16[256,1376]{0,1:T(8,128)(2,1)S(1)}, bf16[256,1376]{0,1:T(8,128)(2,1)}, u32[]{:S(2)}, u32[]{:S(2)}) collective-permute-start(bf16[256,1376]{0,1:T(8,128)(2,1)S(1)} %copy-done.65), channel_id=1, source_target_pairs={{0,0},{1,1},{2,4},{3,5},{4,2},{5,3},{6,6},{7,7},{8,8},{9,9},{10,12... | collective-permute-start | bytes 2113544 | tf_op jit(solution)/shard_map/ppermute | solution.py:370
  396.0 43.2 %collective-permute-start.38 = (bf16[256,1376]{0,1:T(8,128)(2,1)S(1)}, bf16[256,1376]{0,1:T(8,128)(2,1)}, u32[]{:S(2)}, u32[]{:S(2)}) collective-permute-start(bf16[256,1376]{0,1:T(8,128)(2,1)S(1)} %copy-done.65), channel_id=1, source_target_pairs={{0,2},{1,3},{2,6},{3,7},{4,0},{5,1},{6,4},{7,5},{8,10},{9,11},{10,... | collective-permute-start | bytes 2113544 | tf_op jit(solution)/shard_map/ppermute | solution.py:370
  403.6 37.6 %collective-permute-start.27 = (bf16[256,1376]{0,1:T(8,128)(2,1)}, bf16[256,1376]{0,1:T(8,128)(2,1)S(1)}, u32[]{:S(2)}, u32[]{:S(2)}) collective-permute-start(bf16[256,1376]{0,1:T(8,128)(2,1)} %collective-permute-done.26), channel_id=1, source_target_pairs={{0,8},{1,9},{2,10},{3,11},{4,12},{5,13},{6,14},{7,15},{8,0},{9,1},... | collective-permute-start | bytes 2113544 | tf_op jit(solution)/shard_map/ppermute | solution.py:370
  437.4 19.6 collective-permute-start.31
  439.2 37.2 %collective-permute-start.20 = (bf16[1536,512]{1,0:T(8,128)(2,1)S(1)}, bf16[1536,512]{1,0:T(8,128)(2,1)S(1)}, u32[]{:S(2)}, u32[]{:S(2)}) collective-permute-start(bf16[1536,512]{1,0:T(8,128)(2,1)S(1)} %get-tuple-element.24.o_ref), channel_id=1, source_target_pairs={{0,4},{1,5},{2,6},{3,7},{4,0},{5,1},{6,2},{7,3},{8,12},{9,13},{10,... | collective-permute-start | bytes 4718600 | tf_op jit(solution)/shard_map/ppermute | solution.py:370
  441.2 150.7 %collective-permute-start.52 = (bf16[768,2048]{1,0:T(8,128)(2,1)}, bf16[768,2048]{1,0:T(8,128)(2,1)}, u32[]{:S(2)}, u32[]{:S(2)}) collective-permute-start(bf16[768,2048]{1,0:T(8,128)(2,1)} %dynamic-slice_bitcast_fusion.refs_0_), channel_id=1, source_target_pairs={{0,4},{1,5},{2,6},{3,7},{4,0},{5,1},{6,2},{7,3},{8,12},{9,13},{10,... | collective-permute-start | bytes 9437192 | tf_op jit(solution)/shard_map/ppermute | solution.py:370
  442.1 117.3 %collective-permute-start.22 = (bf16[1536,512]{1,0:T(8,128)(2,1)S(1)}, bf16[1536,512]{1,0:T(8,128)(2,1)}, u32[]{:S(2)}, u32[]{:S(2)}) collective-permute-start(bf16[1536,512]{1,0:T(8,128)(2,1)S(1)} %collective-permute-done.21), channel_id=1, source_target_pairs={{0,4},{1,5},{2,6},{3,7},{4,0},{5,1},{6,2},{7,3},{8,12},{9,13},{10,... | collective-permute-start | bytes 4718600 | tf_op jit(solution)/shard_map/ppermute | solution.py:370
  457.4 89.2 %collective-permute-start.36 = (bf16[256,1376]{0,1:T(8,128)(2,1)}, bf16[256,1376]{0,1:T(8,128)(2,1)}, u32[]{:S(2)}, u32[]{:S(2)}) collective-permute-start(bf16[256,1376]{0,1:T(8,128)(2,1)} %collective-permute-done.34), channel_id=1, source_target_pairs={{0,16},{1,17},{2,18},{3,19},{4,20},{5,21},{6,22},{7,23},{8,24},{9,... | collective-permute-start | bytes 2113544 | tf_op jit(solution)/shard_map/ppermute | solution.py:370
  472.7 85.6 %collective-permute-start.39 = (bf16[256,1376]{0,1:T(8,128)(2,1)}, bf16[256,1376]{0,1:T(8,128)(2,1)}, u32[]{:S(2)}, u32[]{:S(2)}) collective-permute-start(bf16[256,1376]{0,1:T(8,128)(2,1)} %collective-permute-done.38), channel_id=1, source_target_pairs={{0,16},{1,17},{2,18},{3,19},{4,20},{5,21},{6,22},{7,23},{8,24},{9,... | collective-permute-start | bytes 2113544 | tf_op jit(solution)/shard_map/ppermute | solution.py:370
  477.6 81.2 %collective-permute-start.40 = (bf16[256,1376]{0,1:T(8,128)(2,1)}, bf16[256,1376]{0,1:T(8,128)(2,1)}, u32[]{:S(2)}, u32[]{:S(2)}) collective-permute-start(bf16[256,1376]{0,1:T(8,128)(2,1)} %collective-permute-done.38), channel_id=1, source_target_pairs={{0,8},{1,9},{2,10},{3,11},{4,12},{5,13},{6,14},{7,15},{8,0},{9,1},... | collective-permute-start | bytes 2113544 | tf_op jit(solution)/shard_map/ppermute | solution.py:370
  546.7 42.5 %collective-permute-start.42 = (bf16[1376,256]{1,0:T(8,128)(2,1)S(1)}, bf16[1376,256]{1,0:T(8,128)(2,1)}, u32[]{:S(2)}, u32[]{:S(2)}) collective-permute-start(bf16[1376,256]{1,0:T(8,128)(2,1)S(1)} %copy-done.66), channel_id=1, source_target_pairs={{0,0},{1,1},{2,4},{3,5},{4,2},{5,3},{6,6},{7,7},{8,8},{9,9},{10,12... | collective-permute-start | bytes 2113544 | tf_op jit(solution)/shard_map/ppermute | solution.py:370
  558.3 31.6 %collective-permute-start.46 = (bf16[1376,256]{1,0:T(8,128)(2,1)S(1)}, bf16[1376,256]{1,0:T(8,128)(2,1)}, u32[]{:S(2)}, u32[]{:S(2)}) collective-permute-start(bf16[1376,256]{1,0:T(8,128)(2,1)S(1)} %copy-done.66), channel_id=1, source_target_pairs={{0,2},{1,3},{2,6},{3,7},{4,0},{5,1},{6,4},{7,5},{8,10},{9,11},{10,... | collective-permute-start | bytes 2113544 | tf_op jit(solution)/shard_map/ppermute | solution.py:370
  558.8 31.7 %collective-permute-start.29 = (bf16[256,1376]{0,1:T(8,128)(2,1)S(1)}, bf16[256,1376]{0,1:T(8,128)(2,1)S(1)}, u32[]{:S(2)}, u32[]{:S(2)}) collective-permute-start(bf16[256,1376]{0,1:T(8,128)(2,1)S(1)} %copy-done.36), channel_id=1, source_target_pairs={{0,16},{1,17},{2,18},{3,19},{4,20},{5,21},{6,22},{7,23},{8,24},{9,... | collective-permute-start | bytes 2113544 | tf_op jit(solution)/shard_map/ppermute | solution.py:370
  559.4 31.5 %collective-permute-start.33 = (bf16[256,1376]{0,1:T(8,128)(2,1)S(1)}, bf16[256,1376]{0,1:T(8,128)(2,1)S(1)}, u32[]{:S(2)}, u32[]{:S(2)}) collective-permute-start(bf16[256,1376]{0,1:T(8,128)(2,1)S(1)} %copy-done.39), channel_id=1, source_target_pairs={{0,8},{1,9},{2,10},{3,11},{4,12},{5,13},{6,14},{7,15},{8,0},{9,1},... | collective-permute-start | bytes 2113544 | tf_op jit(solution)/shard_map/ppermute | solution.py:370
  589.2 790.7 %collective-permute-start.24 = (bf16[1536,512]{1,0:T(8,128)(2,1)S(1)}, bf16[1536,512]{1,0:T(8,128)(2,1)}, u32[]{:S(2)}, u32[]{:S(2)}) collective-permute-start(bf16[1536,512]{1,0:T(8,128)(2,1)S(1)} %fusion.33.refs_0_), channel_id=1, source_target_pairs={{0,1},{1,0},{2,3},{3,2},{4,5},{5,4},{6,7},{7,6},{8,9},{9,8},{10,11... | collective-permute-start | bytes 4718600 | tf_op jit(solution)/shard_map/ppermute | solution.py:370
  590.9 32.9 %collective-permute-start.43 = (bf16[1376,256]{1,0:T(8,128)(2,1)}, bf16[1376,256]{1,0:T(8,128)(2,1)}, u32[]{:S(2)}, u32[]{:S(2)}) collective-permute-start(bf16[1376,256]{1,0:T(8,128)(2,1)} %collective-permute-done.42.refs_0_), channel_id=1, source_target_pairs={{0,8},{1,9},{2,10},{3,11},{4,12},{5,13},{6,14},{7,15},{8,0},{9,1},... | collective-permute-start | bytes 2113544 | tf_op jit(solution)/shard_map/ppermute | solution.py:370
  592.0 32.7 %collective-permute-start.47 = (bf16[1376,256]{1,0:T(8,128)(2,1)}, bf16[1376,256]{1,0:T(8,128)(2,1)}, u32[]{:S(2)}, u32[]{:S(2)}) collective-permute-start(bf16[1376,256]{1,0:T(8,128)(2,1)} %collective-permute-done.46.refs_4_), channel_id=1, source_target_pairs={{0,16},{1,17},{2,18},{3,19},{4,20},{5,21},{6,22},{7,23},{8,24},{9,... | collective-permute-start | bytes 2113544 | tf_op jit(solution)/shard_map/ppermute | solution.py:370
  607.9 599.3 %collective-permute-start.44 = (bf16[1376,256]{1,0:T(8,128)(2,1)}, bf16[1376,256]{1,0:T(8,128)(2,1)}, u32[]{:S(2)}, u32[]{:S(2)}) collective-permute-start(bf16[1376,256]{1,0:T(8,128)(2,1)} %collective-permute-done.42.refs_0_), channel_id=1, source_target_pairs={{0,16},{1,17},{2,18},{3,19},{4,20},{5,21},{6,22},{7,23},{8,24},{9,... | collective-permute-start | bytes 2113544 | tf_op jit(solution)/shard_map/ppermute | solution.py:370
  608.7 598.4 %collective-permute-start.48 = (bf16[1376,256]{1,0:T(8,128)(2,1)}, bf16[1376,256]{1,0:T(8,128)(2,1)}, u32[]{:S(2)}, u32[]{:S(2)}) collective-permute-start(bf16[1376,256]{1,0:T(8,128)(2,1)} %collective-permute-done.46.refs_4_), channel_id=1, source_target_pairs={{0,8},{1,9},{2,10},{3,11},{4,12},{5,13},{6,14},{7,15},{8,0},{9,1},... | collective-permute-start | bytes 2113544 | tf_op jit(solution)/shard_map/ppermute | solution.py:370
  623.8 583.4 %collective-permute-start.45 = (bf16[1376,256]{1,0:T(8,128)(2,1)}, bf16[1376,256]{1,0:T(8,128)(2,1)}, u32[]{:S(2)}, u32[]{:S(2)}) collective-permute-start(bf16[1376,256]{1,0:T(8,128)(2,1)} %collective-permute-done.43.refs_1_), channel_id=1, source_target_pairs={{0,16},{1,17},{2,18},{3,19},{4,20},{5,21},{6,22},{7,23},{8,24},{9,... | collective-permute-start | bytes 2113544 | tf_op jit(solution)/shard_map/ppermute | solution.py:370
  624.7 582.5 %collective-permute-start.49 = (bf16[1376,256]{1,0:T(8,128)(2,1)}, bf16[1376,256]{1,0:T(8,128)(2,1)}, u32[]{:S(2)}, u32[]{:S(2)}) collective-permute-start(bf16[1376,256]{1,0:T(8,128)(2,1)} %collective-permute-done.47.refs_5_), channel_id=1, source_target_pairs={{0,8},{1,9},{2,10},{3,11},{4,12},{5,13},{6,14},{7,15},{8,0},{9,1},... | collective-permute-start | bytes 2113544 | tf_op jit(solution)/shard_map/ppermute | solution.py:370
  1663.4 35.6 %collective-permute-start.57 = (bf16[1536,512]{1,0:T(8,128)(2,1)S(1)}, bf16[1536,512]{1,0:T(8,128)(2,1)S(1)}, u32[]{:S(2)}, u32[]{:S(2)}) collective-permute-start(bf16[1536,512]{1,0:T(8,128)(2,1)S(1)} %fusion.31), channel_id=1, source_target_pairs={{0,1},{1,0},{2,3},{3,2},{4,5},{5,4},{6,7},{7,6},{8,9},{9,8},{10,11... | collective-permute-start | bytes 4718600 | tf_op jit(solution)/shard_map/ppermute | solution.py:370
  1780.5 321.0 %reduce-scatter.10.cloned.1.call-start = ((), (), s32[]{:S(2)}) async-start(), calls=%async_computation.7 | async-start | bytes 7045120 | tf_op jit(solution)/shard_map/reduce_scatter | solution.py:421
  1794.5 339.2 %reduce-scatter.12.cloned.1.call-start = ((), (), s32[]{:S(2)}) async-start(), calls=%async_computation.8 | async-start | bytes 7045120 | tf_op jit(solution)/shard_map/reduce_scatter | solution.py:421
  1809.1 337.1 %reduce-scatter.14.cloned.1.call-start = ((), (), s32[]{:S(2)}) async-start(), calls=%async_computation.9 | async-start | bytes 7045120 | tf_op jit(solution)/shard_map/reduce_scatter | solution.py:421
  1827.6 321.2 %reduce-scatter.6.cloned.1.call-start = ((), (), s32[]{:S(2)}) async-start(), calls=%async_computation.5 | async-start | bytes 3276800 | tf_op jit(solution)/shard_map/reduce_scatter | solution.py:421
  1834.7 35.8 %collective-permute-start.60 = (bf16[1536,512]{1,0:T(8,128)(2,1)}, bf16[1536,512]{1,0:T(8,128)(2,1)}, u32[]{:S(2)}, u32[]{:S(2)}) collective-permute-start(bf16[1536,512]{1,0:T(8,128)(2,1)} %fusion.35), channel_id=1, source_target_pairs={{0,1},{1,0},{2,3},{3,2},{4,5},{5,4},{6,7},{7,6},{8,9},{9,8},{10,11... | collective-permute-start | bytes 4718600 | tf_op jit(solution)/shard_map/ppermute | solution.py:370
  1897.9 42.5 %collective-permute-start.51 = (bf16[1536,512]{1,0:T(8,128)(2,1)}, bf16[1536,512]{1,0:T(8,128)(2,1)}, u32[]{:S(2)}, u32[]{:S(2)}) collective-permute-start(bf16[1536,512]{1,0:T(8,128)(2,1)} %convolution_convert_fusion.12), channel_id=1, source_target_pairs={{0,4},{1,5},{2,6},{3,7},{4,0},{5,1},{6,2},{7,3},{8,12},{9,13},{10,... | collective-permute-start | bytes 4718600 | tf_op jit(solution)/shard_map/ppermute | solution.py:370
  1938.9 95.9 %collective-permute-start.50 = (bf16[1536,512]{1,0:T(8,128)(2,1)}, bf16[1536,512]{1,0:T(8,128)(2,1)}, u32[]{:S(2)}, u32[]{:S(2)}) collective-permute-start(bf16[1536,512]{1,0:T(8,128)(2,1)} %convolution_convert_fusion.13), channel_id=1, source_target_pairs={{0,4},{1,5},{2,6},{3,7},{4,0},{5,1},{6,2},{7,3},{8,12},{9,13},{10,... | collective-permute-start | bytes 4718600 | tf_op jit(solution)/shard_map/ppermute | solution.py:370
  1946.0 88.9 %collective-permute-start.61 = (bf16[1536,512]{1,0:T(8,128)(2,1)}, bf16[1536,512]{1,0:T(8,128)(2,1)}, u32[]{:S(2)}, u32[]{:S(2)}) collective-permute-start(bf16[1536,512]{1,0:T(8,128)(2,1)} %fusion.34), channel_id=1, source_target_pairs={{0,1},{1,0},{2,3},{3,2},{4,5},{5,4},{6,7},{7,6},{8,9},{9,8},{10,11... | collective-permute-start | bytes 4718600 | tf_op jit(solution)/shard_map/ppermute | solution.py:370
  1953.5 62.1 %collective-permute-start.71 = (bf16[1536,512]{1,0:T(8,128)(2,1)}, bf16[1536,512]{1,0:T(8,128)(2,1)}, u32[]{:S(2)}, u32[]{:S(2)}) collective-permute-start(bf16[1536,512]{1,0:T(8,128)(2,1)} %fusion.36), channel_id=1, source_target_pairs={{0,1},{1,0},{2,3},{3,2},{4,5},{5,4},{6,7},{7,6},{8,9},{9,8},{10,11... | collective-permute-start | bytes 4718600 | tf_op jit(solution)/shard_map/ppermute | solution.py:370
  2026.0 46.2 %collective-permute-start.82 = (bf16[256,512]{1,0:T(8,128)(2,1)S(1)}, bf16[256,512]{1,0:T(8,128)(2,1)S(1)}, u32[]{:S(2)}, u32[]{:S(2)}) collective-permute-start(bf16[256,512]{1,0:T(8,128)(2,1)S(1)} %get-tuple-element.158), channel_id=1, source_target_pairs={{0,4},{1,5},{2,0},{3,1},{4,6},{5,7},{6,2},{7,3},{8,12},{9,13},{10,... | collective-permute-start | bytes 786440 | tf_op jit(solution)/shard_map/ppermute | solution.py:370
  2031.0 99.6 %collective-permute-start.73 = (bf16[2,768,512]{2,1,0:T(8,128)(2,1)S(1)}, bf16[2,768,512]{2,1,0:T(8,128)(2,1)S(1)}, u32[]{:S(2)}, u32[]{:S(2)}) collective-permute-start(bf16[2,768,512]{2,1,0:T(8,128)(2,1)S(1)} %pad_maximum_fusion.1.refs_0_), channel_id=1, source_target_pairs={{0,1},{1,2},{2,3},{4,5},{5,6},{6,7},{8,9},{9,10},{10,11},{12,13},{... | collective-permute-start | bytes 4718600 | tf_op jit(solution)/shard_map/ppermute | solution.py:370
  2033.5 98.9 %collective-permute-start.76 = (bf16[2,768,512]{2,1,0:T(8,128)(2,1)S(1)}, bf16[2,768,512]{2,1,0:T(8,128)(2,1)}, u32[]{:S(2)}, u32[]{:S(2)}) collective-permute-start(bf16[2,768,512]{2,1,0:T(8,128)(2,1)S(1)} %pad_maximum_fusion.1.refs_0_), channel_id=1, source_target_pairs={{1,0},{2,1},{3,2},{5,4},{6,5},{7,6},{9,8},{10,9},{11,10},{13,12},{... | collective-permute-start | bytes 4718600 | tf_op jit(solution)/shard_map/ppermute | solution.py:370
  2042.7 29.5 %collective-permute-start.89 = (f32[2,2048]{1,0:T(2,128)S(1)}, f32[2,2048]{1,0:T(2,128)S(1)}, u32[]{:S(2)}, u32[]{:S(2)}) collective-permute-start(f32[2,2048]{1,0:T(2,128)S(1)} %constant_dynamic-update-slice_fusion.1), channel_id=1, source_target_pairs={{0,1},{1,0},{2,3},{3,2},{4,5},{5,4},{6,7},{7,6},{8,9},{9,8},{10,11... | collective-permute-start | bytes 49160 | tf_op jit(solution)/shard_map/ppermute | solution.py:370
  2046.2 30.7 %collective-permute-start.91 = (f32[2,2048]{1,0:T(2,128)S(1)}, f32[2,2048]{1,0:T(2,128)S(1)}, u32[]{:S(2)}, u32[]{:S(2)}) collective-permute-start(f32[2,2048]{1,0:T(2,128)S(1)} %constant_dynamic-update-slice_fusion.1), channel_id=1, source_target_pairs={{0,3},{1,2},{2,1},{3,0},{4,7},{5,6},{6,5},{7,4},{8,11},{9,10},{10,... | collective-permute-start | bytes 49160 | tf_op jit(solution)/shard_map/ppermute | solution.py:370
  2072.2 28.0 %collective-permute-start.81 = (bf16[256,512]{1,0:T(8,128)(2,1)S(1)}, bf16[256,512]{1,0:T(8,128)(2,1)S(1)}, u32[]{:S(2)}, u32[]{:S(2)}) collective-permute-start(bf16[256,512]{1,0:T(8,128)(2,1)S(1)} %get-tuple-element.157), channel_id=1, source_target_pairs={{0,0},{1,1},{2,4},{3,5},{4,2},{5,3},{6,6},{7,7},{8,8},{9,9},{10,12... | collective-permute-start | bytes 786440 | tf_op jit(solution)/shard_map/ppermute | solution.py:370
  2076.9 27.1 %collective-permute-start.63 = (bf16[768,512]{1,0:T(8,128)(2,1)}, bf16[768,512]{1,0:T(8,128)(2,1)}, u32[]{:S(2)}, u32[]{:S(2)}) collective-permute-start(bf16[768,512]{1,0:T(8,128)(2,1)} %get-tuple-element.146), channel_id=1, source_target_pairs={{0,4},{1,5},{2,0},{3,1},{4,6},{5,7},{6,2},{7,3},{8,12},{9,13},{10,... | collective-permute-start | bytes 2359304 | tf_op jit(solution)/shard_map/ppermute | solution.py:370
  2077.0 47.7 %collective-permute-start.62 = (bf16[768,512]{1,0:T(8,128)(2,1)}, bf16[768,512]{1,0:T(8,128)(2,1)}, u32[]{:S(2)}, u32[]{:S(2)}) collective-permute-start(bf16[768,512]{1,0:T(8,128)(2,1)} %get-tuple-element.145), channel_id=1, source_target_pairs={{0,0},{1,1},{2,4},{3,5},{4,2},{5,3},{6,6},{7,7},{8,8},{9,9},{10,12... | collective-permute-start | bytes 2359304 | tf_op jit(solution)/shard_map/ppermute | solution.py:370
  2101.4 26.6 %collective-permute-start.93 = (f32[2,2048]{1,0:T(2,128)S(1)}, f32[2,2048]{1,0:T(2,128)S(1)}, u32[]{:S(2)}, u32[]{:S(2)}) collective-permute-start(f32[2,2048]{1,0:T(2,128)S(1)} %add.583), channel_id=1, source_target_pairs={{0,8},{1,9},{2,10},{3,11},{4,12},{5,13},{6,14},{7,15},{8,0},{9,1},... | collective-permute-start | bytes 49160 | tf_op jit(solution)/shard_map/ppermute | solution.py:370
  2104.0 38.2 %collective-permute-start.84 = (bf16[256,1376]{0,1:T(8,128)(2,1)}, bf16[256,1376]{0,1:T(8,128)(2,1)}, u32[]{:S(2)}, u32[]{:S(2)}) collective-permute-start(bf16[256,1376]{0,1:T(8,128)(2,1)} %get-tuple-element.152), channel_id=1, source_target_pairs={{0,4},{1,5},{2,0},{3,1},{4,6},{5,7},{6,2},{7,3},{8,12},{9,13},{10,... | collective-permute-start | bytes 2113544 | tf_op jit(solution)/shard_map/ppermute | solution.py:370
  2128.6 42.8 %collective-permute-start.83 = (bf16[256,1376]{0,1:T(8,128)(2,1)}, bf16[256,1376]{0,1:T(8,128)(2,1)}, u32[]{:S(2)}, u32[]{:S(2)}) collective-permute-start(bf16[256,1376]{0,1:T(8,128)(2,1)} %get-tuple-element.151), channel_id=1, source_target_pairs={{0,0},{1,1},{2,4},{3,5},{4,2},{5,3},{6,6},{7,7},{8,8},{9,9},{10,12... | collective-permute-start | bytes 2113544 | tf_op jit(solution)/shard_map/ppermute | solution.py:370
  2130.6 97.3 %collective-permute-start.74 = (bf16[2,768,512]{2,1,0:T(8,128)(2,1)S(1)}, bf16[2,768,512]{2,1,0:T(8,128)(2,1)}, u32[]{:S(2)}, u32[]{:S(2)}) collective-permute-start(bf16[2,768,512]{2,1,0:T(8,128)(2,1)S(1)} %collective-permute-done.73.refs_1_), channel_id=1, source_target_pairs={{1,2},{2,3},{5,6},{6,7},{9,10},{10,11},{13,14},{14,15},{17,18},{18... | collective-permute-start | bytes 4718600 | tf_op jit(solution)/shard_map/ppermute | solution.py:370
  2132.4 97.3 %collective-permute-start.77 = (bf16[2,768,512]{2,1,0:T(8,128)(2,1)}, bf16[2,768,512]{2,1,0:T(8,128)(2,1)}, u32[]{:S(2)}, u32[]{:S(2)}) collective-permute-start(bf16[2,768,512]{2,1,0:T(8,128)(2,1)} %collective-permute-done.76.refs_4_), channel_id=1, source_target_pairs={{1,0},{2,1},{5,4},{6,5},{9,8},{10,9},{13,12},{14,13},{17,16},{18,1... | collective-permute-start | bytes 4718600 | tf_op jit(solution)/shard_map/ppermute | solution.py:370
  2136.2 35.2 %collective-permute-start.86 = (bf16[256,1376]{0,1:T(8,128)(2,1)}, bf16[256,1376]{0,1:T(8,128)(2,1)}, u32[]{:S(2)}, u32[]{:S(2)}) collective-permute-start(bf16[256,1376]{0,1:T(8,128)(2,1)} %get-tuple-element.150), channel_id=1, source_target_pairs={{0,4},{1,5},{2,0},{3,1},{4,6},{5,7},{6,2},{7,3},{8,12},{9,13},{10,... | collective-permute-start | bytes 2113544 | tf_op jit(solution)/shard_map/ppermute | solution.py:370
  2142.3 85.6 %collective-permute-start.85 = (bf16[256,1376]{0,1:T(8,128)(2,1)}, bf16[256,1376]{0,1:T(8,128)(2,1)}, u32[]{:S(2)}, u32[]{:S(2)}) collective-permute-start(bf16[256,1376]{0,1:T(8,128)(2,1)} %get-tuple-element.149), channel_id=1, source_target_pairs={{0,0},{1,1},{2,4},{3,5},{4,2},{5,3},{6,6},{7,7},{8,8},{9,9},{10,12... | collective-permute-start | bytes 2113544 | tf_op jit(solution)/shard_map/ppermute | solution.py:370
  2171.4 62.1 %collective-permute-start.88 = (bf16[1376,256]{1,0:T(8,128)(2,1)}, bf16[1376,256]{1,0:T(8,128)(2,1)S(1)}, u32[]{:S(2)}, u32[]{:S(2)}) collective-permute-start(bf16[1376,256]{1,0:T(8,128)(2,1)} %get-tuple-element.148), channel_id=1, source_target_pairs={{0,4},{1,5},{2,0},{3,1},{4,6},{5,7},{6,2},{7,3},{8,12},{9,13},{10,... | collective-permute-start | bytes 2113544 | tf_op jit(solution)/shard_map/ppermute | solution.py:370
  2171.4 78.6 %collective-permute-start.87 = (bf16[1376,256]{1,0:T(8,128)(2,1)}, bf16[1376,256]{1,0:T(8,128)(2,1)S(1)}, u32[]{:S(2)}, u32[]{:S(2)}) collective-permute-start(bf16[1376,256]{1,0:T(8,128)(2,1)} %get-tuple-element.147), channel_id=1, source_target_pairs={{0,0},{1,1},{2,4},{3,5},{4,2},{5,3},{6,6},{7,7},{8,8},{9,9},{10,12... | collective-permute-start | bytes 2113544 | tf_op jit(solution)/shard_map/ppermute | solution.py:370
  2227.9 23.4 %collective-permute-start.80 = (bf16[256,640]{1,0:T(8,128)(2,1)S(1)}, bf16[256,640]{1,0:T(8,128)(2,1)S(1)}, u32[]{:S(2)}, u32[]{:S(2)}) collective-permute-start(bf16[256,640]{1,0:T(8,128)(2,1)S(1)} %get-tuple-element.156), channel_id=1, source_target_pairs={{0,4},{1,5},{2,0},{3,1},{4,6},{5,7},{6,2},{7,3},{8,12},{9,13},{10,... | collective-permute-start | bytes 983048 | tf_op jit(solution)/shard_map/ppermute | solution.py:370
  2227.9 31.6 %collective-permute-start.75 = (bf16[2,768,512]{2,1,0:T(8,128)(2,1)}, bf16[2,768,512]{2,1,0:T(8,128)(2,1)}, u32[]{:S(2)}, u32[]{:S(2)}) collective-permute-start(bf16[2,768,512]{2,1,0:T(8,128)(2,1)} %collective-permute-done.74.refs_2_), channel_id=1, source_target_pairs={{2,3},{6,7},{10,11},{14,15},{18,19},{22,23},{26,27},{30,31}} | collective-permute-start | bytes 4718600 | tf_op jit(solution)/shard_map/ppermute | solution.py:370
  2229.7 56.9 %collective-permute-start.78 = (bf16[2,768,512]{2,1,0:T(8,128)(2,1)}, bf16[2,768,512]{2,1,0:T(8,128)(2,1)}, u32[]{:S(2)}, u32[]{:S(2)}) collective-permute-start(bf16[2,768,512]{2,1,0:T(8,128)(2,1)} %collective-permute-done.77.refs_5_), channel_id=1, source_target_pairs={{1,0},{5,4},{9,8},{13,12},{17,16},{21,20},{25,24},{29,28}} | collective-permute-start | bytes 4718600 | tf_op jit(solution)/shard_map/ppermute | solution.py:370
  2233.6 23.5 %collective-permute-start.79 = (bf16[256,640]{1,0:T(8,128)(2,1)S(1)}, bf16[256,640]{1,0:T(8,128)(2,1)S(1)}, u32[]{:S(2)}, u32[]{:S(2)}) collective-permute-start(bf16[256,640]{1,0:T(8,128)(2,1)S(1)} %get-tuple-element.155), channel_id=1, source_target_pairs={{0,0},{1,1},{2,4},{3,5},{4,2},{5,3},{6,6},{7,7},{8,8},{9,9},{10,12... | collective-permute-start | bytes 983048 | tf_op jit(solution)/shard_map/ppermute | solution.py:370
  (118 other events, 4834.2 us)
Sparse Core Ops, SparseCore 0:
  1780.6 37.6 reduce-scatter.7
  1821.7 64.6 reduce-scatter.9
  1889.8 65.3 reduce-scatter.11
  1958.4 64.7 reduce-scatter.13
  2026.3 39.5 reduce-scatter.5

commit v3 on v2

--- a/solution.py
+++ b/solution.py
@@ -262,8 +262,8 @@
     return lax.dot_general(a, b, (((ca,), (cb,)), ((), ())), preferred_element_type=F32)
 
 
-def after(value, *others):
-    return lax.optimization_barrier((value, *others))[0]
+def tie(*values):
+    return lax.optimization_barrier(values)
 
 
 def place_kernel(offsets, *refs, axis):
@@ -289,10 +289,11 @@
         grid_spec=pltpu.PrefetchScalarGridSpec(
             num_scalar_prefetch=1,
             grid=(),
-            in_specs=[pl.BlockSpec(memory_space=pl.ANY)] * len(pieces),
+            in_specs=[pl.BlockSpec(memory_space=pltpu.VMEM)] * len(pieces),
             out_specs=pl.BlockSpec(memory_space=pl.ANY),
             scratch_shapes=[pltpu.SemaphoreType.DMA((len(pieces),))],
         ),
+        compiler_params=pltpu.CompilerParams(vmem_limit_bytes=32 * 2**20),
         out_shape=jax.ShapeDtypeStruct(tuple(shape), pieces[0].dtype),
         cost_estimate=pl.CostEstimate(flops=0, bytes_accessed=2 * size, transcendentals=0),
     )(jnp.stack(offsets).astype(jnp.int32), *pieces)
@@ -400,11 +401,12 @@
             jnp.concatenate([second_if_zero, first_if_zero], axis),
         )
 
-    def gather_chips(value, axis=0, needs=()):
-        size = value.shape[axis]
+    chip_groups = [[c * CORES + k for c in range(chips)] for k in range(CORES)]
+
+    def gather_chips(owns, axis):
+        size = owns[0].shape[axis]
         bits = [1 << i for i in range(chips.bit_length() - 1)]
         pieces, offsets = [], []
-        owns = spread(after(value, *needs) if needs else value)
         for own, order, k in zip(owns, (bits, bits[::-1]), (batch, 1 - batch)):
             held = {0: own}
             for bit in order:
@@ -413,43 +415,52 @@
             for mask, got in held.items():
                 pieces.append(got)
                 offsets.append(((chip ^ mask) * CORES + k) * size)
-        return place(pieces, offsets, axis), owns
-
-    chip_groups = [[c * CORES + k for c in range(chips)] for k in range(CORES)]
-
-    def scatter_chips(value, axis):
-        mine = lax.psum_scatter(
-            value.astype(BF),
-            "seq",
-            scatter_dimension=axis,
-            tiled=True,
-            axis_index_groups=chip_groups,
+        return place(pieces, offsets, axis)
+
+    def gather_chips_bulk(owns, axis):
+        size = owns[0].shape[axis]
+        both = place(list(owns), [batch * size, (1 - batch) * size], axis)
+        return lax.all_gather(
+            both, "seq", axis=axis, tiled=True, axis_index_groups=chip_groups
         )
+
+    def sum_chips(value, axis):
+        return lax.psum_scatter(
+            value, "seq", scatter_dimension=axis, tiled=True, axis_index_groups=chip_groups
+        )
+
+    def send_halves(mine, axis):
         size = mine.shape[axis] // CORES
         same = lax.dynamic_slice_in_dim(mine, batch * size, size, axis)
         other = lax.dynamic_slice_in_dim(mine, (1 - batch) * size, size, axis)
-        a, b = unspread(same, other)
-        return a.astype(F32) + b.astype(F32)
-
-    def gather_ranks(own):
+        return unspread(same, other)
+
+    def add(halves):
+        return halves[0].astype(F32) + halves[1].astype(F32)
+
+    def send_parts(own):
+        return [to_part(own, d) for d in range(1, group)]
+
+    def gather_ranks(own, arrived):
         found = []
-        for d in range(group):
-            here = own if d == 0 else to_part(own, d)
+        for d, here in enumerate([own, *arrived]):
             found.append((core * group + (part ^ d), here))
             found.append(((1 - core) * group + (part ^ d), to_core(here)))
         return found
 
-    def reduce_ranks(partial, needs=()):
-        arrived = []
+    def reduce_begin(partial):
+        totals = []
         for d in range(group - 1, -1, -1):
             away = to_core(partial((1 - core) * group + (part ^ d)).astype(BF))
             total = partial(core * group + (part ^ d)) + away.astype(F32)
-            if d:
-                total = total.astype(BF)
-                total = after(total, *needs) if needs else total
-                total = to_part(total, d).astype(F32)
-            arrived.append(total)
-        return sum(arrived[:-1], arrived[-1])
+            totals.append(total.astype(BF) if d else total)
+        return totals[-1], totals[-2::-1]
+
+    def reduce_send(totals):
+        return [to_part(total, d + 1) for d, total in enumerate(totals)]
+
+    def reduce_end(own, arrived):
+        return sum((got.astype(F32) for got in arrived), own)
 
     def sum_ranks(value):
         for d in [1 << i for i in range(group.bit_length() - 1)]:
@@ -469,15 +480,17 @@
     tokens_c = chip_tokens(tokens)
     grad_out = chip_tokens(cotangent)
 
+    def half(value, k):
+        return lax.dynamic_slice_in_dim(value, k * block, block, 0)
+
     qk_width, v_width = heads * QK, heads * HEAD_V
-    qkv_full, first = gather_chips(jnp.concatenate([w_query, w_key, w_value], 1))
+    qkv_owns = spread(jnp.concatenate([w_query, w_key, w_value], 1))
     gains = lax.all_gather(jnp.stack([gain_mixer, gain_mlp]), "seq", axis=1, tiled=True)
+    w_output, gains, *qkv_owns = tie(w_output, gains, *qkv_owns)
     gains = gains.astype(F32)
     mixer_gain, mlp_gain = gains[0], gains[1]
-    output_full, first = gather_chips(w_output, 0, first)
-    gate_full, first = gather_chips(w_gate, 0, first)
-    up_full, first = gather_chips(w_up, 0, first)
-    down_full, first = gather_chips(w_down, 1, first)
+    output_owns = spread(w_output)
+    qkv_full = gather_chips(qkv_owns, 0)
 
     bounds = jnp.cumsum(lax.dynamic_index_in_dim(lengths, batch, 0, False))
 
@@ -500,6 +513,9 @@
     inv_one = lax.rsqrt(jnp.mean(tokens_f * tokens_f, axis=-1, keepdims=True) + EPS)
     normed = (tokens_f * inv_one * mixer_gain).astype(BF)
     qkv = dot(normed, qkv_full).astype(BF)
+    w_gate, qkv, *output_owns = tie(w_gate.T, qkv, *output_owns)
+    gate_owns = spread(w_gate)
+    output_full = gather_chips(output_owns, 0)
 
     query, keys = qkv[:, :qk_width], qkv[:, qk_width : 2 * qk_width]
     values = qkv[:, 2 * qk_width :]
@@ -517,7 +533,7 @@
             flat[cut:].reshape(heads, -1)[:, :NFEAT],
         )
 
-    def scan_blocks(both, blocks_order, step):
+    def scan_blocks(both, blocks_order, step, meanwhile):
         state, total = both[..., :HEAD_V], both[..., HEAD_V]
         at_end = (state[blocks_order[0]], total[blocks_order[0]])
         for i in blocks_order[1:]:
@@ -528,8 +544,10 @@
             )
         message = pack(*at_end)
         run = None
+        arrived = [shift_chip(message, step * d) for d in range(1, chips)]
+        *arrived, state, total, meanwhile = tie(*arrived, state, total, meanwhile)
         for d in range(1, chips):
-            got = unpack(shift_chip(message, step * d))
+            got = unpack(arrived[d - 1])
             other = chip - step * d
             if step > 0:
                 same = edges[0] == segment_of((other + 1) * rows - 1)
@@ -545,23 +563,33 @@
         state, total = (jnp.stack([found[i][j] for i in range(CORES)]) for j in range(2))
         total = jnp.broadcast_to(total[..., None], state.shape)
         both = jnp.concatenate([state, total], -1).astype(BF)
-        return jnp.pad(both, ((0, 0), (0, 0), (0, LANES - NFEAT), (0, 0)))
+        both = jnp.pad(both, ((0, 0), (0, 0), (0, LANES - NFEAT), (0, 0)))
+        return both, meanwhile
 
     (local,) = local_states(marks, keys, values)
-    states = scan_blocks(local, list(range(CORES)), 1)
+    states, gate_owns = scan_blocks(local, list(range(CORES)), 1, gate_owns)
+    up_owns = spread(tie(w_up.T, states)[0])
+    gate_full = gather_chips_bulk(gate_owns, 1)
     mixer_own, denom = mixer(marks, query, keys, values, states)
 
-    mixer_parts = gather_ranks(mixer_own)
+    arrived = send_parts(mixer_own)
+    w_down, *up_owns = tie(w_down, *up_owns)
+    down_owns = spread(w_down)
+    up_full = gather_chips_bulk(up_owns, 1)
+    mixer_parts = gather_ranks(mixer_own, arrived)
     branch_own = sum(dot(got, row_piece(output_full, r)) for r, got in mixer_parts).astype(BF)
-    branch_parts = gather_ranks(branch_own)
+    arrived = send_parts(branch_own)
+    *arrived, gate_full, down_owns = tie(*arrived, gate_full, down_owns)
+    down_full = gather_chips(down_owns, 1)
+    branch_parts = gather_ranks(branch_own, arrived)
     branch = place([got for _, got in branch_parts], [r * piece for r, _ in branch_parts], 1)
     hidden_state = tokens_f + branch.astype(F32)
     inv_two = lax.rsqrt(jnp.mean(hidden_state * hidden_state, axis=-1, keepdims=True) + EPS)
     normed_two = (hidden_state * inv_two * mlp_gain).astype(BF)
 
     grad_hidden = dot(grad_out, down_full, 1, 1).astype(BF).astype(F32)
-    gate = dot(normed_two, gate_full).astype(BF).astype(F32)
-    upward = dot(normed_two, up_full).astype(BF).astype(F32)
+    gate = dot(normed_two, gate_full, 1, 1).astype(BF).astype(F32)
+    upward = dot(normed_two, up_full, 1, 1).astype(BF).astype(F32)
     logistic = jax.nn.sigmoid(gate)
     activated = gate * logistic
     hidden = (activated * upward).astype(BF)
@@ -569,11 +597,18 @@
     grad_up_f = grad_hidden * activated
     grad_gate_b, grad_up_b = grad_gate_f.astype(BF), grad_up_f.astype(BF)
     inner_two = sum_ranks(jnp.sum(grad_gate_f * gate + grad_up_f * upward, axis=1)) / width
-    normed_grad = reduce_ranks(
-        lambda r: dot(grad_gate_b, row_piece(gate_full, r), 1, 1)
-        + dot(grad_up_b, row_piece(up_full, r), 1, 1),
-        (inner_two,),
-    )
+    own, totals = reduce_begin(
+        lambda r: dot(grad_gate_b, column_piece(gate_full, r))
+        + dot(grad_up_b, column_piece(up_full, r))
+    )
+    inner_two, *totals = tie(inner_two, *totals)
+    arrived = reduce_send(totals)
+    up_sum = sum_chips(dot(grad_up_b, normed_two, 0, 0).astype(BF), 1)
+    gate_sum = dot(grad_gate_b, normed_two, 0, 0).astype(BF)
+    up_sum, gate_sum, *arrived = tie(up_sum, gate_sum, *arrived)
+    normed_grad = reduce_end(own, arrived)
+    gate_sum = sum_chips(gate_sum, 1)
+    up_halves = send_halves(up_sum, 1)
     tokens_own = column_piece(tokens_c, rank).astype(F32)
     hidden_own = tokens_own + branch_own.astype(F32)
     scaled_two = hidden_own * inv_two
@@ -584,9 +619,27 @@
     grad_gain_mlp = jnp.sum(normed_grad * scaled_two, axis=0)
     branch_grad = hidden_grad.astype(BF)
 
-    mixer_grad = reduce_ranks(lambda r: dot(branch_grad, row_piece(output_full, r), 1, 1))
+    own, totals = reduce_begin(lambda r: dot(branch_grad, row_piece(output_full, r), 1, 1))
+    arrived = reduce_send(totals)
+    mlp_own, mlp_totals = reduce_begin(lambda r: dot(hidden, column_piece(down_full, r)))
+    down_sum = dot(hidden, grad_out, 0, 0).astype(BF)
+    arrived, mlp_own, mlp_totals, down_sum, gate_sum, up_halves = tie(
+        arrived, mlp_own, mlp_totals, down_sum, gate_sum, up_halves
+    )
+    mixer_grad = reduce_end(own, arrived)
+    mlp_arrived = reduce_send(mlp_totals)
+    down_sum = sum_chips(down_sum, 1)
+    gate_halves = send_halves(gate_sum, 1)
+    output_sum = place(
+        [dot(got, branch_grad, 0, 0).astype(BF) for _, got in mixer_parts],
+        [r * piece for r, _ in mixer_parts],
+        0,
+    )
+    output_sum = sum_chips(output_sum, 0)
     (grad_local,) = grad_states(marks, query, mixer_grad, mixer_own, denom)
-    carried = scan_blocks(grad_local, list(range(CORES))[::-1], -1)
+    carried, gate_halves = scan_blocks(
+        grad_local, list(range(CORES))[::-1], -1, gate_halves
+    )
     grad_qkv = jnp.concatenate(
         mixer_back(
             marks, query, keys, values, mixer_grad, mixer_own, denom, states, carried
@@ -595,9 +648,20 @@
     )
     inner_one = jnp.sum(grad_qkv.astype(F32) * qkv.astype(F32), axis=1)
     inner_one = sum_ranks(inner_one) / width
-    input_normed = reduce_ranks(
-        lambda r: dot(grad_qkv, row_piece(qkv_full, r), 1, 1), (inner_one,)
-    )
+    grad_qkv, mlp_arrived, down_sum = tie(grad_qkv, mlp_arrived, down_sum)
+    mixed_own = (hidden_own + reduce_end(mlp_own, mlp_arrived)).astype(BF)
+    mixed_halves = unspread(half(mixed_own, batch), half(mixed_own, 1 - batch))
+    own, totals = reduce_begin(lambda r: dot(grad_qkv, row_piece(qkv_full, r), 1, 1))
+    inner_one, *totals = tie(inner_one, *totals)
+    arrived = reduce_send(totals)
+    down_halves = send_halves(down_sum, 1)
+    qkv_sum = dot(normed, grad_qkv, 0, 0).astype(BF)
+    arrived, mixed_halves, down_halves, qkv_sum, output_sum = tie(
+        arrived, mixed_halves, down_halves, qkv_sum, output_sum
+    )
+    input_normed = reduce_end(own, arrived)
+    qkv_sum = sum_chips(qkv_sum, 0)
+    mixed = ordered(mixed_halves[0][None], mixed_halves[1][None], core, 0)
     scaled_one = tokens_own * inv_one
     mixer_gain_own = lax.dynamic_slice_in_dim(mixer_gain, rank * piece, piece, 0)
     grad_gain_mixer = jnp.sum(input_normed * scaled_one, axis=0)
@@ -606,9 +670,6 @@
         + inv_one * (input_normed * mixer_gain_own - scaled_one * inner_one[:, None])
     ).astype(BF)
 
-    def half(value, k):
-        return lax.dynamic_slice_in_dim(value, k * block, block, 0)
-
     gain_grads = lax.dynamic_update_slice_in_dim(
         jnp.zeros((2, width), F32), jnp.stack([grad_gain_mixer, grad_gain_mlp]), rank * piece, 1
     )
@@ -616,8 +677,9 @@
         move(gain_grads, lambda c, k, m, l: (c, k, *divmod((m * group + l) ^ d, group)))
         for d in range(1, feat_count)
     ]
-    input_own = after(input_own, gain_grads)
-    input_pair = jnp.stack([half(input_own, core), to_core(half(input_own, 1 - core))])
+    other_half = to_core(half(input_own, 1 - core))
+    input_own, other_half, *planes = tie(input_own, other_half, *planes)
+    input_pair = jnp.stack([half(input_own, core), other_half])
 
     def step_plane(value, step, first):
         def target(c, k, m, l):
@@ -629,45 +691,41 @@
 
         return move(value, target)
 
+    gain_grads = sum(planes, gain_grads)
+    output_halves = send_halves(output_sum, 0)
+    hops = [to_core] + [
+        functools.partial(to_chip, mask=1 << i) for i in range(chips.bit_length() - 1)
+    ]
     ups, downs = [input_pair], [input_pair]
     for d in range(feat_count - 1):
-        ups.append(step_plane(ups[-1], 1, d))
-        downs.append(step_plane(downs[-1], -1, d))
+        up, down = step_plane(ups[-1], 1, d), step_plane(downs[-1], -1, d)
+        if hops:
+            up, down, gain_grads, got = tie(up, down, gain_grads, hops[0](gain_grads))
+            gain_grads, hops = gain_grads + got, hops[1:]
+        if d == 0:
+            up, down, qkv_sum = tie(up, down, qkv_sum)
+            qkv_halves = send_halves(qkv_sum, 0)
+        if d == 1:
+            up, down, output_halves = tie(up, down, output_halves)
+        ups.append(up), downs.append(down)
+    for hop in hops:
+        gain_grads = gain_grads + hop(gain_grads)
     input_grad = widen(ups + downs[1:], feat_rank, core, micro, group, width)
 
-    gain_grads = sum(planes, gain_grads)
-    gain_grads = gain_grads + to_core(gain_grads)
-    for bit in [1 << i for i in range(chips.bit_length() - 1)]:
-        gain_grads = gain_grads + to_chip(gain_grads, bit)
     shard = width // seq_count
     gain_grads = lax.dynamic_slice_in_dim(gain_grads, seq_rank * shard, shard, 1)
 
-    mlp_own = reduce_ranks(lambda r: dot(hidden, column_piece(down_full, r)), (mixer_grad,))
-    mixed_own = (hidden_own + mlp_own).astype(BF)
-    same, other = unspread(half(mixed_own, batch), half(mixed_own, 1 - batch))
-    mixed = ordered(same[None], other[None], core, 0)
-
-    grad_gate = scatter_chips(dot(normed_two, grad_gate_b, 0, 0), 0)
-    grad_up = scatter_chips(dot(normed_two, grad_up_b, 0, 0), 0)
-    grad_down = scatter_chips(dot(hidden, grad_out, 0, 0), 1)
-    grad_output = place(
-        [dot(got, branch_grad, 0, 0).astype(BF) for _, got in mixer_parts],
-        [r * piece for r, _ in mixer_parts],
-        0,
-    )
-    grad_output = scatter_chips(grad_output, 0)
-    grad_qkv_w = scatter_chips(dot(normed, grad_qkv, 0, 0), 0)
-
+    grad_qkv_w = add(qkv_halves)
     return (
         mixed,
         input_grad,
         grad_qkv_w[:, :qk_width],
         grad_qkv_w[:, qk_width : 2 * qk_width],
         grad_qkv_w[:, 2 * qk_width :],
-        grad_output,
-        grad_gate,
-        grad_up,
-        grad_down,
+        add(output_halves),
+        add(gate_halves).T,
+        add(up_halves).T,
+        add(down_halves),
         gain_grads[0],
         gain_grads[1],
     )

time: 2320 us -> 926 us (0.40)
  Pallas kernels: 1370 us -> 77.1 us
  starting transfers between devices: 179 us -> 131 us
  waiting for transfers between devices: 397 us -> 361 us
    pallas_call x9, Pallas kernels: 1310 us -> 20.4 us  [place(): pl.pallas_call(functools.partial(place_kernel, axis=axis), grid_spec=pltp...]
    ppermute x95 -> x83, starting transfers between devices: 179 us -> 130 us  [move(): return lax.ppermute(value, ('seq', 'feat'), pairs)]
    ppermute x95 -> x83, waiting for transfers between devices: 397 us -> 357 us  [move(): return lax.ppermute(value, ('seq', 'feat'), pairs)]
    ppermute x16 -> x0, local copies, waits for them, and re-layouts: 36 us -> none  [move(): return lax.ppermute(value, ('seq', 'feat'), pairs)]
  transfers between devices with their start and end apart: 100 -> 90, of which waited for: 31 -> 40; matrix products, arithmetic and copies ran while one was open for 10% -> 26% of each run, Pallas kernels for 48% -> 7%
where the time goes in v3:
time: 926 us; the launch traced here: 913 us
  waiting for transfers between devices  361 us (39%)
  matrix products  212 us (23%)
  starting transfers between devices  131 us (14%)
  Pallas kernels  77.1 us (8%)
  local copies, waits for them, and re-layouts  52.3 us (6%)
  other arithmetic  47.2 us (5%)
  between operations  24 us (3%)
  blocking collectives  9.53 us (1%)
    ppermute x83, waiting for transfers between devices, move(): return lax.ppermute(value, ('seq', 'feat'), pairs)  357 us
    dot_general x36, matrix products, dot(): lax.dot_general(a, b, (((ca,), (cb,)), ((), ())), preferred_element_type=...  212 us
    ppermute x83, starting transfers between devices, move(): return lax.ppermute(value, ('seq', 'feat'), pairs)  130 us
    pallas_call x4, Pallas kernels, run(): pl.pallas_call(functools.partial(kernel, heads=heads, block=block), grid_...  47.3 us
    unnamed x226, local copies, waits for them, and re-layouts  27.9 us
    pallas_call x9, Pallas kernels, place(): pl.pallas_call(functools.partial(place_kernel, axis=axis), grid_spec=pltp...  20.4 us
  transfers between devices with their start and end apart: 90, of which 40 were waited for; matrix products, arithmetic and copies ran while one was open for 26% of the time, Pallas kernels for 7%

profile of v3, /device:TPU:7, one launch (start us, length us, event | category | flops | bytes accessed | tf_op | source)
XLA Modules:
  0.0 913.3 jit_solution(11854411611642461341)
XLA Ops:
  12.1 4.6 collective-permute-start.1
  18.9 9.5 %all_gather.9 = bf16[2,2048]{1,0:T(2,128)(2,1)S(1)} all-gather(bf16[2,256]{1,0:T(2,128)(2,1)S(1)} %pad_maximum_fusion.6), channel_id=1, replica_groups=mesh['seq'=8,'feat'=4] {'seq'}, dimensions={1}, use_global_device_ids=true | all-gather | bytes 9216 | tf_op jit(solution)/shard_map/all_gather | solution.py:488
  33.4 6.3 collective-permute-done.3.refs_1_
  40.9 4.9 collective-permute-done.4.refs_2_
  61.8 5.3 convolution_convert_fusion.7
  71.1 4.3 shard_map.242
  86.0 14.4 %collective-permute-done.16.refs_1_ = bf16[1376,256]{1,0:T(8,128)(2,1)} collective-permute-done((bf16[1376,256]{1,0:T(8,128)(2,1)}, bf16[1376,256]{1,0:T(8,128)(2,1)}, u32[]{:S(2)}, u32[]{:S(2)}) %collective-permute-start.16) | collective-permute-done | bytes 704544 | tf_op jit(solution)/shard_map/ppermute | solution.py:371
  119.6 9.5 %shard_map.243 = (bf16[1536,512]{1,0:T(8,128)(2,1)}, f32[1536,512]{1,0:T(8,128)}) custom-call(s32[2,5]{1,0:T(2,128)S(1)} %pad_add_fusion.marks, bf16[1536,64]{1,0:T(8,128)(2,1)S(1)} %copy-done.21, bf16[1536,64]{1,0:T(8,128)(2,1)S(1)} %get-tuple-element.235.k_ref, bf16[1536,512]{1,0:T(8,128)(2,1)S(1)} %slice.184.v_ref, ...), custom_call_target="tpu_custom_call" | custom-call | flops 6144000000 | bytes 9216000 | tf_op jit(solution)/shard_map/pallas_call | solution.py:220
  130.8 6.0 collective-permute-done.18.refs_2_
  140.2 6.7 collective-permute-done.21.refs_6_
  146.8 9.1 collective-permute-start.28
  158.1 20.3 %collective-permute-done.24 = bf16[1536,512]{1,0:T(8,128)(2,1)} collective-permute-done((bf16[1536,512]{1,0:T(8,128)(2,1)}, bf16[1536,512]{1,0:T(8,128)(2,1)}, u32[]{:S(2)}, u32[]{:S(2)}) %collective-permute-start.24) | collective-permute-done | bytes 1572896 | tf_op jit(solution)/shard_map/ppermute | solution.py:371
  180.5 4.0 dynamic-slice_bitcast_fusion.refs_0_
  204.6 4.0 collective-permute-start.30
  208.7 11.8 %collective-permute-done.31.refs_4_ = bf16[1376,256]{1,0:T(8,128)(2,1)S(1)} collective-permute-done((bf16[1376,256]{1,0:T(8,128)(2,1)S(1)}, bf16[1376,256]{1,0:T(8,128)(2,1)S(1)}, u32[]{:S(2)}, u32[]{:S(2)}) %collective-permute-start.31) | collective-permute-done | bytes 704544 | tf_op jit(solution)/shard_map/ppermute | solution.py:371
  221.5 32.1 %collective-permute-done.30.refs_0_ = bf16[1376,256]{1,0:T(8,128)(2,1)S(1)} collective-permute-done((bf16[1376,256]{1,0:T(8,128)(2,1)S(1)}, bf16[1376,256]{1,0:T(8,128)(2,1)S(1)}, u32[]{:S(2)}, u32[]{:S(2)}) %collective-permute-start.30) | collective-permute-done | bytes 704544 | tf_op jit(solution)/shard_map/ppermute | solution.py:371
  259.3 14.7 %collective-permute-done.34.refs_2_ = bf16[1376,256]{1,0:T(8,128)(2,1)S(1)} collective-permute-done((bf16[1376,256]{1,0:T(8,128)(2,1)}, bf16[1376,256]{1,0:T(8,128)(2,1)S(1)}, u32[]{:S(2)}, u32[]{:S(2)}) %collective-permute-start.34) | collective-permute-done | bytes 704544 | tf_op jit(solution)/shard_map/ppermute | solution.py:371
  275.7 13.4 %collective-permute-done.36.refs_5_ = bf16[1376,256]{1,0:T(8,128)(2,1)S(1)} collective-permute-done((bf16[1376,256]{1,0:T(8,128)(2,1)}, bf16[1376,256]{1,0:T(8,128)(2,1)S(1)}, u32[]{:S(2)}, u32[]{:S(2)}) %collective-permute-start.36) | collective-permute-done | bytes 704544 | tf_op jit(solution)/shard_map/ppermute | solution.py:371
  290.7 4.2 shard_map.241
  297.6 6.6 collective-permute-done.35.refs_3_
  314.6 4.1 multiply_convert_fusion
  321.4 12.3 %convolution_convert_fusion.3 = bf16[1536,1376]{0,1:T(8,128)(2,1)} fusion(bf16[1536,2048]{1,0:T(8,128)(2,1)S(1)} %multiply_convert_fusion, bf16[1376,2048]{1,0:T(8,128)(2,1)} %all-gather.3.cloned.1.call-done), kind=kOutput, calls=%fused_computation.30 | convolution fusion | flops 8659156992 | bytes 16154624 | tf_op jit(solution)/shard_map/dot_general | solution.py:262
  333.8 14.3 %convolution_convert_fusion.4 = bf16[1536,1376]{0,1:T(8,128)(2,1)} fusion(bf16[1536,2048]{1,0:T(8,128)(2,1)} %copy-done.59, bf16[1376,2048]{1,0:T(8,128)(2,1)} %all-gather.5.cloned.1.call-done), kind=kOutput, calls=%fused_computation.31 | convolution fusion | flops 8659156992 | bytes 16154624 | tf_op jit(solution)/shard_map/dot_general | solution.py:262
  348.0 21.1 %fusion.21 = (bf16[1536,1376]{0,1:T(8,128)(2,1)}, f32[1536]{0:T(1024)S(1)}, bf16[1536,1376]{0,1:T(8,128)(2,1)}, bf16[1536,1376]{0,1:T(8,128)(2,1)S(1)}) fusion(bf16[1536,1376]{0,1:T(8,128)(2,1)} %convolution_convert_fusion.3, bf16[1536,1376]{0,1:T(8,128)(2,1)} %convolution_convert_fusion.4, bf16[1536,2048]{1,0:T(8,128)(2,1)} %copy-done.5, ...), kind=kOutput, calls=%fused_computation.59 | convolution fusion | flops 8705652736 | bytes 33069056 | tf_op jit(solution)/shard_map/dot_general | solution.py:262
  371.2 10.6 %convolution_convert_fusion.2 = bf16[1376,2048]{1,0:T(8,128)(2,1)} fusion(bf16[1536,1376]{0,1:T(8,128)(2,1)S(1)} %get-tuple-element.234, bf16[1536,2048]{1,0:T(8,128)(2,1)S(1)} %bitcast.133), kind=kOutput, calls=%fused_computation.29 | convolution fusion | flops 8659861504 | bytes 16154624 | tf_op jit(solution)/shard_map/dot_general | solution.py:262
  381.9 5.2 fusion.47
  387.1 5.4 fusion.28
  398.4 4.4 fusion.50
  402.9 5.3 fusion.29
  409.1 10.6 %convolution_convert_fusion.1 = bf16[1376,2048]{1,0:T(8,128)(2,1)} fusion(bf16[1536,1376]{0,1:T(8,128)(2,1)S(1)} %bitcast.160, bf16[1536,2048]{1,0:T(8,128)(2,1)S(1)} %bitcast.135), kind=kOutput, calls=%fused_computation.28 | convolution fusion | flops 8659861504 | bytes 16154624 | tf_op jit(solution)/shard_map/dot_general | solution.py:262
  419.6 25.0 %collective-permute-done.43 = bf16[1536,512]{1,0:T(8,128)(2,1)S(1)} collective-permute-done((bf16[1536,512]{1,0:T(8,128)(2,1)}, bf16[1536,512]{1,0:T(8,128)(2,1)S(1)}, u32[]{:S(2)}, u32[]{:S(2)}) %collective-permute-start.43) | collective-permute-done | bytes 1572896 | tf_op jit(solution)/shard_map/ppermute | solution.py:371
  447.9 5.5 fusion.53
  453.4 5.5 fusion.27
  459.7 3.8 convolution_convert_fusion.13
  463.6 3.8 convolution_convert_fusion.12
  468.0 4.6 fusion.56
  472.7 7.6 fusion.134
  483.8 10.8 %convolution_convert_fusion = bf16[1376,2048]{1,0:T(8,128)(2,1)} fusion(bf16[1536,1376]{0,1:T(8,128)(2,1)S(1)} %bitcast.164, bf16[1536,2048]{1,0:T(8,128)(2,1)S(1)} %bitcast.129), kind=kOutput, calls=%fused_computation.27 | convolution fusion | flops 8659861504 | bytes 16154624 | tf_op jit(solution)/shard_map/dot_general | solution.py:262
  504.3 7.4 convolution_add_fusion.7
  511.7 5.4 fusion.31
  517.1 23.3 %collective-permute-done.50 = bf16[1376,256]{1,0:T(8,128)(2,1)S(1)} collective-permute-done((bf16[1376,256]{1,0:T(8,128)(2,1)S(1)}, bf16[1376,256]{1,0:T(8,128)(2,1)S(1)}, u32[]{:S(2)}, u32[]{:S(2)}) %collective-permute-start.50) | collective-permute-done | bytes 704544 | tf_op jit(solution)/shard_map/ppermute | solution.py:371
  540.4 7.5 collective-permute-done.49
  566.6 5.0 fusion.15.do_ref
  571.6 6.8 shard_map.249
  603.1 13.9 %collective-permute-done.54 = bf16[1376,256]{1,0:T(8,128)(2,1)} collective-permute-done((bf16[1376,256]{1,0:T(8,128)(2,1)}, bf16[1376,256]{1,0:T(8,128)(2,1)}, u32[]{:S(2)}, u32[]{:S(2)}) %collective-permute-start.54) | collective-permute-done | bytes 704544 | tf_op jit(solution)/shard_map/ppermute | solution.py:371
  628.1 26.7 %shard_map.250 = (bf16[1536,64]{1,0:T(8,128)(2,1)S(1)}, bf16[1536,64]{1,0:T(8,128)(2,1)S(1)}, bf16[1536,512]{1,0:T(8,128)(2,1)S(1)}) custom-call(s32[2,5]{1,0:T(2,128)S(1)} %copy-done.43, bf16[1536,64]{1,0:T(8,128)(2,1)S(1)} %copy-done.23, bf16[1536,64]{1,0:T(8,128)(2,1)S(1)} %copy-done.20, bf16[1536,512]{1,0:T(8,128)(2,1)} %copy-done.12, ...), custom_call_target="tpu_custom_call" | custom-call | flops 15360000000 | bytes 9216000 | tf_op jit(solution)/shard_map/pallas_call | solution.py:220
  655.9 3.7 convolution_convert_fusion.11
  669.8 4.6 fusion.33
  682.3 4.1 collective-permute-start.63
  686.4 3.7 convolution_convert_fusion.10
  691.0 7.9 collective-permute-start.65
  698.9 7.1 convolution_convert_fusion.6
  706.0 30.1 %collective-permute-done.63 = bf16[1376,256]{1,0:T(8,128)(2,1)} collective-permute-done((bf16[1376,256]{1,0:T(8,128)(2,1)}, bf16[1376,256]{1,0:T(8,128)(2,1)}, u32[]{:S(2)}, u32[]{:S(2)}) %collective-permute-start.63) | collective-permute-done | bytes 704544 | tf_op jit(solution)/shard_map/ppermute | solution.py:371
  736.1 6.4 collective-permute-done.60
  743.3 6.0 fusion.26
  759.2 4.3 collective-permute-start.70
  766.4 27.8 %collective-permute-done.71.refs_4_ = bf16[2,768,512]{2,1,0:T(8,128)(2,1)S(1)} collective-permute-done((bf16[2,768,512]{2,1,0:T(8,128)(2,1)S(1)}, bf16[2,768,512]{2,1,0:T(8,128)(2,1)S(1)}, u32[]{:S(2)}, u32[]{:S(2)}) %collective-permute-start.71) | collective-permute-done | bytes 1572896 | tf_op jit(solution)/shard_map/ppermute | solution.py:371
  801.3 7.2 collective-permute-start.77
  808.5 5.1 collective-permute-start.76
  816.7 18.7 %collective-permute-done.74.refs_5_ = bf16[2,768,512]{2,1,0:T(8,128)(2,1)} collective-permute-done((bf16[2,768,512]{2,1,0:T(8,128)(2,1)}, bf16[2,768,512]{2,1,0:T(8,128)(2,1)}, u32[]{:S(2)}, u32[]{:S(2)}) %collective-permute-start.74) | collective-permute-done | bytes 1572896 | tf_op jit(solution)/shard_map/ppermute | solution.py:371
  835.5 15.2 %collective-permute-done.76 = bf16[256,512]{1,0:T(8,128)(2,1)S(1)} collective-permute-done((bf16[256,512]{1,0:T(8,128)(2,1)S(1)}, bf16[256,512]{1,0:T(8,128)(2,1)S(1)}, u32[]{:S(2)}, u32[]{:S(2)}) %collective-permute-start.76) | collective-permute-done | bytes 262176 | tf_op jit(solution)/shard_map/ppermute | solution.py:371
  862.6 7.8 collective-permute-done.81
  875.9 20.3 %collective-permute-done.79.refs_6_ = bf16[2,768,512]{2,1,0:T(8,128)(2,1)} collective-permute-done((bf16[2,768,512]{2,1,0:T(8,128)(2,1)}, bf16[2,768,512]{2,1,0:T(8,128)(2,1)}, u32[]{:S(2)}, u32[]{:S(2)}) %collective-permute-start.79) | collective-permute-done | bytes 1572896 | tf_op jit(solution)/shard_map/ppermute | solution.py:371
  896.8 9.4 %shard_map.252 = f32[2,768,2048]{2,1,0:T(8,128)} custom-call(s32[2]{0:T(128)S(1)} %pad_add_fusion.5.where, bf16[2,768,512]{2,1,0:T(8,128)(2,1)S(1)} %pad_maximum_fusion.1.refs_0_, bf16[2,768,512]{2,1,0:T(8,128)(2,1)S(1)} %collective-permute-done.70.refs_1_, bf16[2,768,512]{2,1,0:T(8,128)(2,1)} %collective-permute-done.73.refs_2_, ...), custom_call_target="tpu_custom_call" | custom-call | tf_op jit(solution)/shard_map/pallas_call | solution.py:321
  (531 shorter events, 252.0 us)
Async XLA Ops:
  7.2 248.5 %all-gather.3.cloned.1.call-start = ((), (), s32[]{:S(2)}) async-start(), calls=%async_computation.5 | async-start | bytes 7045120 | tf_op jit(solution)/shard_map/all_gather | solution.py:423
  9.5 46.4 %collective-permute-start = (bf16[768,2048]{1,0:T(8,128)(2,1)S(1)}, bf16[768,2048]{1,0:T(8,128)(2,1)}, u32[]{:S(2)}, u32[]{:S(2)}) collective-permute-start(bf16[768,2048]{1,0:T(8,128)(2,1)S(1)} %dynamic-slice_bitcast_fusion.1.refs_0_), channel_id=1, source_target_pairs={{0,4},{1,5},{2,6},{3,7},{4,0},{5,1},{6,2},{7,3},{8,12},{9,13},{10,... | collective-permute-start | bytes 9437192 | tf_op jit(solution)/shard_map/ppermute | solution.py:371
  12.0 16.6 %collective-permute-start.2 = (bf16[256,640]{1,0:T(8,128)(2,1)}, bf16[256,640]{1,0:T(8,128)(2,1)S(1)}, u32[]{:S(2)}, u32[]{:S(2)}) collective-permute-start(bf16[256,640]{1,0:T(8,128)(2,1)} %pad_maximum_fusion.2), channel_id=1, source_target_pairs={{0,2},{1,3},{2,6},{3,7},{4,0},{5,1},{6,4},{7,5},{8,10},{9,11},{10,... | collective-permute-start | bytes 983048 | tf_op jit(solution)/shard_map/ppermute | solution.py:371
  12.1 17.6 %collective-permute-start.1 = (bf16[256,640]{1,0:T(8,128)(2,1)}, bf16[256,640]{1,0:T(8,128)(2,1)}, u32[]{:S(2)}, u32[]{:S(2)}) collective-permute-start(bf16[256,640]{1,0:T(8,128)(2,1)} %pad_maximum_fusion.2), channel_id=1, source_target_pairs={{0,0},{1,1},{2,4},{3,5},{4,2},{5,3},{6,6},{7,7},{8,8},{9,9},{10,12... | collective-permute-start | bytes 983048 | tf_op jit(solution)/shard_map/ppermute | solution.py:371
  31.0 14.8 %collective-permute-start.4 = (bf16[256,640]{1,0:T(8,128)(2,1)}, bf16[256,640]{1,0:T(8,128)(2,1)S(1)}, u32[]{:S(2)}, u32[]{:S(2)}) collective-permute-start(bf16[256,640]{1,0:T(8,128)(2,1)} %collective-permute-done.1.refs_0_), channel_id=1, source_target_pairs={{0,16},{1,17},{2,18},{3,19},{4,20},{5,21},{6,22},{7,23},{8,24},{9,... | collective-permute-start | bytes 983048 | tf_op jit(solution)/shard_map/ppermute | solution.py:371
  32.2 15.9 %collective-permute-start.7 = (bf16[256,640]{1,0:T(8,128)(2,1)S(1)}, bf16[256,640]{1,0:T(8,128)(2,1)S(1)}, u32[]{:S(2)}, u32[]{:S(2)}) collective-permute-start(bf16[256,640]{1,0:T(8,128)(2,1)S(1)} %collective-permute-done.2.refs_4_), channel_id=1, source_target_pairs={{0,8},{1,9},{2,10},{3,11},{4,12},{5,13},{6,14},{7,15},{8,0},{9,1},... | collective-permute-start | bytes 983048 | tf_op jit(solution)/shard_map/ppermute | solution.py:371
  39.7 13.7 %collective-permute-start.8 = (bf16[256,640]{1,0:T(8,128)(2,1)S(1)}, bf16[256,640]{1,0:T(8,128)(2,1)S(1)}, u32[]{:S(2)}, u32[]{:S(2)}) collective-permute-start(bf16[256,640]{1,0:T(8,128)(2,1)S(1)} %collective-permute-done.6.refs_5_), channel_id=1, source_target_pairs={{0,8},{1,9},{2,10},{3,11},{4,12},{5,13},{6,14},{7,15},{8,0},{9,1},... | collective-permute-start | bytes 983048 | tf_op jit(solution)/shard_map/ppermute | solution.py:371
  45.8 21.4 %collective-permute-start.10 = (bf16[256,512]{1,0:T(8,128)(2,1)}, bf16[256,512]{1,0:T(8,128)(2,1)S(1)}, u32[]{:S(2)}, u32[]{:S(2)}) collective-permute-start(bf16[256,512]{1,0:T(8,128)(2,1)} %param.22), channel_id=1, source_target_pairs={{0,2},{1,3},{2,6},{3,7},{4,0},{5,1},{6,4},{7,5},{8,10},{9,11},{10,... | collective-permute-start | bytes 786440 | tf_op jit(solution)/shard_map/ppermute | solution.py:371
  48.0 19.2 %collective-permute-start.9 = (bf16[256,512]{1,0:T(8,128)(2,1)}, bf16[256,512]{1,0:T(8,128)(2,1)S(1)}, u32[]{:S(2)}, u32[]{:S(2)}) collective-permute-start(bf16[256,512]{1,0:T(8,128)(2,1)} %param.22), channel_id=1, source_target_pairs={{0,0},{1,1},{2,4},{3,5},{4,2},{5,3},{6,6},{7,7},{8,8},{9,9},{10,12... | collective-permute-start | bytes 786440 | tf_op jit(solution)/shard_map/ppermute | solution.py:371
  67.2 33.2 %collective-permute-start.16 = (bf16[1376,256]{1,0:T(8,128)(2,1)}, bf16[1376,256]{1,0:T(8,128)(2,1)}, u32[]{:S(2)}, u32[]{:S(2)}) collective-permute-start(bf16[1376,256]{1,0:T(8,128)(2,1)} %bitcast.4), channel_id=1, source_target_pairs={{0,2},{1,3},{2,6},{3,7},{4,0},{5,1},{6,4},{7,5},{8,10},{9,11},{10,... | collective-permute-start | bytes 2113544 | tf_op jit(solution)/shard_map/ppermute | solution.py:371
  68.0 33.1 %collective-permute-start.15 = (bf16[1376,256]{1,0:T(8,128)(2,1)}, bf16[1376,256]{1,0:T(8,128)(2,1)}, u32[]{:S(2)}, u32[]{:S(2)}) collective-permute-start(bf16[1376,256]{1,0:T(8,128)(2,1)} %bitcast.4), channel_id=1, source_target_pairs={{0,0},{1,1},{2,4},{3,5},{4,2},{5,3},{6,6},{7,7},{8,8},{9,9},{10,12... | collective-permute-start | bytes 2113544 | tf_op jit(solution)/shard_map/ppermute | solution.py:371
  104.1 229.7 %all-gather.5.cloned.1.call-start = ((), (), s32[]{:S(2)}) async-start(), calls=%async_computation.6 | async-start | bytes 7045120 | tf_op jit(solution)/shard_map/all_gather | solution.py:423
  129.1 49.4 %collective-permute-start.24 = (bf16[1536,512]{1,0:T(8,128)(2,1)}, bf16[1536,512]{1,0:T(8,128)(2,1)}, u32[]{:S(2)}, u32[]{:S(2)}) collective-permute-start(bf16[1536,512]{1,0:T(8,128)(2,1)} %get-tuple-element.105.o_ref), channel_id=1, source_target_pairs={{0,1},{1,0},{2,3},{3,2},{4,5},{5,4},{6,7},{7,6},{8,9},{9,8},{10,11... | collective-permute-start | bytes 4718600 | tf_op jit(solution)/shard_map/ppermute | solution.py:371
  129.1 67.6 %collective-permute-start.23 = (bf16[1536,512]{1,0:T(8,128)(2,1)}, bf16[1536,512]{1,0:T(8,128)(2,1)}, u32[]{:S(2)}, u32[]{:S(2)}) collective-permute-start(bf16[1536,512]{1,0:T(8,128)(2,1)} %get-tuple-element.105.o_ref), channel_id=1, source_target_pairs={{0,4},{1,5},{2,6},{3,7},{4,0},{5,1},{6,2},{7,3},{8,12},{9,13},{10,... | collective-permute-start | bytes 4718600 | tf_op jit(solution)/shard_map/ppermute | solution.py:371
  130.7 16.1 %collective-permute-start.21 = (bf16[256,512]{1,0:T(8,128)(2,1)S(1)}, bf16[256,512]{1,0:T(8,128)(2,1)S(1)}, u32[]{:S(2)}, u32[]{:S(2)}) collective-permute-start(bf16[256,512]{1,0:T(8,128)(2,1)S(1)} %copy-done.25), channel_id=1, source_target_pairs={{0,8},{1,9},{2,10},{3,11},{4,12},{5,13},{6,14},{7,15},{8,0},{9,1},... | collective-permute-start | bytes 786440 | tf_op jit(solution)/shard_map/ppermute | solution.py:371
  137.5 18.4 %collective-permute-start.20 = (bf16[256,512]{1,0:T(8,128)(2,1)S(1)}, bf16[256,512]{1,0:T(8,128)(2,1)S(1)}, u32[]{:S(2)}, u32[]{:S(2)}) collective-permute-start(bf16[256,512]{1,0:T(8,128)(2,1)S(1)} %copy-done.25), channel_id=1, source_target_pairs={{0,16},{1,17},{2,18},{3,19},{4,20},{5,21},{6,22},{7,23},{8,24},{9,... | collective-permute-start | bytes 786440 | tf_op jit(solution)/shard_map/ppermute | solution.py:371
  137.5 54.8 %collective-permute-start.29 = (bf16[1376,256]{1,0:T(8,128)(2,1)}, bf16[1376,256]{1,0:T(8,128)(2,1)S(1)}, u32[]{:S(2)}, u32[]{:S(2)}) collective-permute-start(bf16[1376,256]{1,0:T(8,128)(2,1)} %bitcast.33), channel_id=1, source_target_pairs={{0,2},{1,3},{2,6},{3,7},{4,0},{5,1},{6,4},{7,5},{8,10},{9,11},{10,... | collective-permute-start | bytes 2113544 | tf_op jit(solution)/shard_map/ppermute | solution.py:371
  146.8 45.5 %collective-permute-start.28 = (bf16[1376,256]{1,0:T(8,128)(2,1)}, bf16[1376,256]{1,0:T(8,128)(2,1)S(1)}, u32[]{:S(2)}, u32[]{:S(2)}) collective-permute-start(bf16[1376,256]{1,0:T(8,128)(2,1)} %bitcast.33), channel_id=1, source_target_pairs={{0,0},{1,1},{2,4},{3,5},{4,2},{5,3},{6,6},{7,7},{8,8},{9,9},{10,12... | collective-permute-start | bytes 2113544 | tf_op jit(solution)/shard_map/ppermute | solution.py:371
  155.9 22.5 %collective-permute-start.19 = (bf16[256,512]{1,0:T(8,128)(2,1)S(1)}, bf16[256,512]{1,0:T(8,128)(2,1)S(1)}, u32[]{:S(2)}, u32[]{:S(2)}) collective-permute-start(bf16[256,512]{1,0:T(8,128)(2,1)S(1)} %collective-permute-done.17.refs_1_), channel_id=1, source_target_pairs={{0,16},{1,17},{2,18},{3,19},{4,20},{5,21},{6,22},{7,23},{8,24},{9,... | collective-permute-start | bytes 786440 | tf_op jit(solution)/shard_map/ppermute | solution.py:371
  178.4 23.1 %collective-permute-start.25 = (bf16[1536,512]{1,0:T(8,128)(2,1)}, bf16[1536,512]{1,0:T(8,128)(2,1)}, u32[]{:S(2)}, u32[]{:S(2)}) collective-permute-start(bf16[1536,512]{1,0:T(8,128)(2,1)} %collective-permute-done.24), channel_id=1, source_target_pairs={{0,4},{1,5},{2,6},{3,7},{4,0},{5,1},{6,2},{7,3},{8,12},{9,13},{10,... | collective-permute-start | bytes 4718600 | tf_op jit(solution)/shard_map/ppermute | solution.py:371
  186.7 71.2 %collective-permute-start.11 = (bf16[768,2048]{1,0:T(8,128)(2,1)}, bf16[768,2048]{1,0:T(8,128)(2,1)}, u32[]{:S(2)}, u32[]{:S(2)}) collective-permute-start(bf16[768,2048]{1,0:T(8,128)(2,1)} %dynamic-slice_bitcast_fusion.refs_0_), channel_id=1, source_target_pairs={{0,4},{1,5},{2,6},{3,7},{4,0},{5,1},{6,2},{7,3},{8,12},{9,13},{10,... | collective-permute-start | bytes 9437192 | tf_op jit(solution)/shard_map/ppermute | solution.py:371
  194.2 253.6 %reduce-scatter.6.cloned.1.call-start = ((), (), s32[]{:S(2)}) async-start(), calls=%async_computation.7 | async-start | bytes 7045120 | tf_op jit(solution)/shard_map/reduce_scatter | solution.py:428
  204.4 51.2 %collective-permute-start.27 = (bf16[1536,512]{1,0:T(8,128)(2,1)S(1)}, bf16[1536,512]{1,0:T(8,128)(2,1)S(1)}, u32[]{:S(2)}, u32[]{:S(2)}) collective-permute-start(bf16[1536,512]{1,0:T(8,128)(2,1)S(1)} %fusion.30.refs_0_), channel_id=1, source_target_pairs={{0,1},{1,0},{2,3},{3,2},{4,5},{5,4},{6,7},{7,6},{8,9},{9,8},{10,11... | collective-permute-start | bytes 4718600 | tf_op jit(solution)/shard_map/ppermute | solution.py:371
  204.5 16.0 %collective-permute-start.31 = (bf16[1376,256]{1,0:T(8,128)(2,1)S(1)}, bf16[1376,256]{1,0:T(8,128)(2,1)S(1)}, u32[]{:S(2)}, u32[]{:S(2)}) collective-permute-start(bf16[1376,256]{1,0:T(8,128)(2,1)S(1)} %copy-done.83), channel_id=1, source_target_pairs={{0,2},{1,3},{2,6},{3,7},{4,0},{5,1},{6,4},{7,5},{8,10},{9,11},{10,... | collective-permute-start | bytes 2113544 | tf_op jit(solution)/shard_map/ppermute | solution.py:371
  204.6 48.9 %collective-permute-start.30 = (bf16[1376,256]{1,0:T(8,128)(2,1)S(1)}, bf16[1376,256]{1,0:T(8,128)(2,1)S(1)}, u32[]{:S(2)}, u32[]{:S(2)}) collective-permute-start(bf16[1376,256]{1,0:T(8,128)(2,1)S(1)} %copy-done.83), channel_id=1, source_target_pairs={{0,0},{1,1},{2,4},{3,5},{4,2},{5,3},{6,6},{7,7},{8,8},{9,9},{10,12... | collective-permute-start | bytes 2113544 | tf_op jit(solution)/shard_map/ppermute | solution.py:371
  208.6 100.9 %collective-permute-start.26 = (bf16[1536,512]{1,0:T(8,128)(2,1)S(1)}, bf16[1536,512]{1,0:T(8,128)(2,1)}, u32[]{:S(2)}, u32[]{:S(2)}) collective-permute-start(bf16[1536,512]{1,0:T(8,128)(2,1)S(1)} %fusion.30.refs_0_), channel_id=1, source_target_pairs={{0,4},{1,5},{2,6},{3,7},{4,0},{5,1},{6,2},{7,3},{8,12},{9,13},{10,... | collective-permute-start | bytes 4718600 | tf_op jit(solution)/shard_map/ppermute | solution.py:371
  255.7 53.9 %collective-permute-start.32 = (bf16[1536,512]{1,0:T(8,128)(2,1)S(1)}, bf16[1536,512]{1,0:T(8,128)(2,1)S(1)}, u32[]{:S(2)}, u32[]{:S(2)}) collective-permute-start(bf16[1536,512]{1,0:T(8,128)(2,1)S(1)} %collective-permute-done.27.refs_2_), channel_id=1, source_target_pairs={{0,4},{1,5},{2,6},{3,7},{4,0},{5,1},{6,2},{7,3},{8,12},{9,13},{10,... | collective-permute-start | bytes 4718600 | tf_op jit(solution)/shard_map/ppermute | solution.py:371
  256.4 17.6 %collective-permute-start.34 = (bf16[1376,256]{1,0:T(8,128)(2,1)}, bf16[1376,256]{1,0:T(8,128)(2,1)S(1)}, u32[]{:S(2)}, u32[]{:S(2)}) collective-permute-start(bf16[1376,256]{1,0:T(8,128)(2,1)} %copy-done.17), channel_id=1, source_target_pairs={{0,16},{1,17},{2,18},{3,19},{4,20},{5,21},{6,22},{7,23},{8,24},{9,... | collective-permute-start | bytes 2113544 | tf_op jit(solution)/shard_map/ppermute | solution.py:371
  256.4 19.1 %collective-permute-start.33 = (bf16[1376,256]{1,0:T(8,128)(2,1)}, bf16[1376,256]{1,0:T(8,128)(2,1)S(1)}, u32[]{:S(2)}, u32[]{:S(2)}) collective-permute-start(bf16[1376,256]{1,0:T(8,128)(2,1)} %copy-done.17), channel_id=1, source_target_pairs={{0,8},{1,9},{2,10},{3,11},{4,12},{5,13},{6,14},{7,15},{8,0},{9,1},... | collective-permute-start | bytes 2113544 | tf_op jit(solution)/shard_map/ppermute | solution.py:371
  257.9 31.3 %collective-permute-start.36 = (bf16[1376,256]{1,0:T(8,128)(2,1)}, bf16[1376,256]{1,0:T(8,128)(2,1)S(1)}, u32[]{:S(2)}, u32[]{:S(2)}) collective-permute-start(bf16[1376,256]{1,0:T(8,128)(2,1)} %copy-done.15), channel_id=1, source_target_pairs={{0,16},{1,17},{2,18},{3,19},{4,20},{5,21},{6,22},{7,23},{8,24},{9,... | collective-permute-start | bytes 2113544 | tf_op jit(solution)/shard_map/ppermute | solution.py:371
  274.0 23.6 %collective-permute-start.37 = (bf16[1376,256]{1,0:T(8,128)(2,1)}, bf16[1376,256]{1,0:T(8,128)(2,1)S(1)}, u32[]{:S(2)}, u32[]{:S(2)}) collective-permute-start(bf16[1376,256]{1,0:T(8,128)(2,1)} %copy-done.15), channel_id=1, source_target_pairs={{0,8},{1,9},{2,10},{3,11},{4,12},{5,13},{6,14},{7,15},{8,0},{9,1},... | collective-permute-start | bytes 2113544 | tf_op jit(solution)/shard_map/ppermute | solution.py:371
  275.5 28.7 %collective-permute-start.35 = (bf16[1376,256]{1,0:T(8,128)(2,1)S(1)}, bf16[1376,256]{1,0:T(8,128)(2,1)S(1)}, u32[]{:S(2)}, u32[]{:S(2)}) collective-permute-start(bf16[1376,256]{1,0:T(8,128)(2,1)S(1)} %collective-permute-done.33.refs_1_), channel_id=1, source_target_pairs={{0,16},{1,17},{2,18},{3,19},{4,20},{5,21},{6,22},{7,23},{8,24},{9,... | collective-permute-start | bytes 2113544 | tf_op jit(solution)/shard_map/ppermute | solution.py:371
  289.1 16.5 %collective-permute-start.38 = (bf16[1376,256]{1,0:T(8,128)(2,1)S(1)}, bf16[1376,256]{1,0:T(8,128)(2,1)S(1)}, u32[]{:S(2)}, u32[]{:S(2)}) collective-permute-start(bf16[1376,256]{1,0:T(8,128)(2,1)S(1)} %collective-permute-done.36.refs_5_), channel_id=1, source_target_pairs={{0,8},{1,9},{2,10},{3,11},{4,12},{5,13},{6,14},{7,15},{8,0},{9,1},... | collective-permute-start | bytes 2113544 | tf_op jit(solution)/shard_map/ppermute | solution.py:371
  381.8 167.0 %reduce-scatter.8.cloned.1.call-start = ((), (), s32[]{:S(2)}) async-start(), calls=%async_computation.8 | async-start | bytes 7045120 | tf_op jit(solution)/shard_map/reduce_scatter | solution.py:428
  408.2 36.5 %collective-permute-start.43 = (bf16[1536,512]{1,0:T(8,128)(2,1)}, bf16[1536,512]{1,0:T(8,128)(2,1)S(1)}, u32[]{:S(2)}, u32[]{:S(2)}) collective-permute-start(bf16[1536,512]{1,0:T(8,128)(2,1)} %fusion.29), channel_id=1, source_target_pairs={{0,1},{1,0},{2,3},{3,2},{4,5},{5,4},{6,7},{7,6},{8,9},{9,8},{10,11... | collective-permute-start | bytes 4718600 | tf_op jit(solution)/shard_map/ppermute | solution.py:371
  447.8 208.0 %reduce-scatter.10.cloned.1.call-start = ((), (), s32[]{:S(2)}) async-start(), calls=%async_computation.9 | async-start | bytes 7045120 | tf_op jit(solution)/shard_map/reduce_scatter | solution.py:428
  458.9 13.7 %collective-permute-start.39 = (bf16[1536,512]{1,0:T(8,128)(2,1)S(1)}, bf16[1536,512]{1,0:T(8,128)(2,1)S(1)}, u32[]{:S(2)}, u32[]{:S(2)}) collective-permute-start(bf16[1536,512]{1,0:T(8,128)(2,1)S(1)} %fusion.27), channel_id=1, source_target_pairs={{0,4},{1,5},{2,6},{3,7},{4,0},{5,1},{6,2},{7,3},{8,12},{9,13},{10,... | collective-permute-start | bytes 4718600 | tf_op jit(solution)/shard_map/ppermute | solution.py:371
  463.5 40.7 %collective-permute-start.47 = (bf16[1536,512]{1,0:T(8,128)(2,1)}, bf16[1536,512]{1,0:T(8,128)(2,1)}, u32[]{:S(2)}, u32[]{:S(2)}) collective-permute-start(bf16[1536,512]{1,0:T(8,128)(2,1)} %convolution_convert_fusion.13), channel_id=1, source_target_pairs={{0,4},{1,5},{2,6},{3,7},{4,0},{5,1},{6,2},{7,3},{8,12},{9,13},{10,... | collective-permute-start | bytes 4718600 | tf_op jit(solution)/shard_map/ppermute | solution.py:371
  467.4 44.2 %collective-permute-start.48 = (bf16[1536,512]{1,0:T(8,128)(2,1)}, bf16[1536,512]{1,0:T(8,128)(2,1)}, u32[]{:S(2)}, u32[]{:S(2)}) collective-permute-start(bf16[1536,512]{1,0:T(8,128)(2,1)} %convolution_convert_fusion.12), channel_id=1, source_target_pairs={{0,4},{1,5},{2,6},{3,7},{4,0},{5,1},{6,2},{7,3},{8,12},{9,13},{10,... | collective-permute-start | bytes 4718600 | tf_op jit(solution)/shard_map/ppermute | solution.py:371
  497.4 51.4 %collective-permute-start.46 = (bf16[1536,512]{1,0:T(8,128)(2,1)S(1)}, bf16[1536,512]{1,0:T(8,128)(2,1)}, u32[]{:S(2)}, u32[]{:S(2)}) collective-permute-start(bf16[1536,512]{1,0:T(8,128)(2,1)S(1)} %fusion.32), channel_id=1, source_target_pairs={{0,1},{1,0},{2,3},{3,2},{4,5},{5,4},{6,7},{7,6},{8,9},{9,8},{10,11... | collective-permute-start | bytes 4718600 | tf_op jit(solution)/shard_map/ppermute | solution.py:371
  498.7 41.7 %collective-permute-start.50 = (bf16[1376,256]{1,0:T(8,128)(2,1)S(1)}, bf16[1376,256]{1,0:T(8,128)(2,1)S(1)}, u32[]{:S(2)}, u32[]{:S(2)}) collective-permute-start(bf16[1376,256]{1,0:T(8,128)(2,1)S(1)} %get-tuple-element.243), channel_id=1, source_target_pairs={{0,4},{1,5},{2,0},{3,1},{4,6},{5,7},{6,2},{7,3},{8,12},{9,13},{10,... | collective-permute-start | bytes 2113544 | tf_op jit(solution)/shard_map/ppermute | solution.py:371
  500.9 47.0 %collective-permute-start.49 = (bf16[1376,256]{1,0:T(8,128)(2,1)S(1)}, bf16[1376,256]{1,0:T(8,128)(2,1)S(1)}, u32[]{:S(2)}, u32[]{:S(2)}) collective-permute-start(bf16[1376,256]{1,0:T(8,128)(2,1)S(1)} %get-tuple-element.244), channel_id=1, source_target_pairs={{0,0},{1,1},{2,4},{3,5},{4,2},{5,3},{6,6},{7,7},{8,8},{9,9},{10,12... | collective-permute-start | bytes 2113544 | tf_op jit(solution)/shard_map/ppermute | solution.py:371
  548.8 157.2 %reduce-scatter.12.cloned.1.call-start = ((), (), s32[]{:S(2)}) async-start(), calls=%async_computation.10 | async-start | bytes 2621440 | tf_op jit(solution)/shard_map/reduce_scatter | solution.py:428
  552.1 14.5 %collective-permute-start.44 = (bf16[1536,512]{1,0:T(8,128)(2,1)}, bf16[1536,512]{1,0:T(8,128)(2,1)}, u32[]{:S(2)}, u32[]{:S(2)}) collective-permute-start(bf16[1536,512]{1,0:T(8,128)(2,1)} %convolution_convert_fusion.9), channel_id=1, source_target_pairs={{0,4},{1,5},{2,6},{3,7},{4,0},{5,1},{6,2},{7,3},{8,12},{9,13},{10,... | collective-permute-start | bytes 4718600 | tf_op jit(solution)/shard_map/ppermute | solution.py:371
  582.1 21.0 %collective-permute-start.55 = (bf16[1376,256]{1,0:T(8,128)(2,1)}, bf16[1376,256]{1,0:T(8,128)(2,1)}, u32[]{:S(2)}, u32[]{:S(2)}) collective-permute-start(bf16[1376,256]{1,0:T(8,128)(2,1)} %get-tuple-element.241), channel_id=1, source_target_pairs={{0,4},{1,5},{2,0},{3,1},{4,6},{5,7},{6,2},{7,3},{8,12},{9,13},{10,... | collective-permute-start | bytes 2113544 | tf_op jit(solution)/shard_map/ppermute | solution.py:371
  584.4 32.6 %collective-permute-start.54 = (bf16[1376,256]{1,0:T(8,128)(2,1)}, bf16[1376,256]{1,0:T(8,128)(2,1)}, u32[]{:S(2)}, u32[]{:S(2)}) collective-permute-start(bf16[1376,256]{1,0:T(8,128)(2,1)} %get-tuple-element.242), channel_id=1, source_target_pairs={{0,0},{1,1},{2,4},{3,5},{4,2},{5,3},{6,6},{7,7},{8,8},{9,9},{10,12... | collective-permute-start | bytes 2113544 | tf_op jit(solution)/shard_map/ppermute | solution.py:371
  600.8 194.6 %reduce-scatter.14.cloned.1.call-start = ((), (), s32[]{:S(2)}) async-start(), calls=%async_computation.11 | async-start | bytes 3276800 | tf_op jit(solution)/shard_map/reduce_scatter | solution.py:428
  601.3 54.5 %collective-permute-start.58 = (bf16[1536,512]{1,0:T(8,128)(2,1)}, bf16[1536,512]{1,0:T(8,128)(2,1)}, u32[]{:S(2)}, u32[]{:S(2)}) collective-permute-start(bf16[1536,512]{1,0:T(8,128)(2,1)} %fusion.31), channel_id=1, source_target_pairs={{0,1},{1,0},{2,3},{3,2},{4,5},{5,4},{6,7},{7,6},{8,9},{9,8},{10,11... | collective-permute-start | bytes 4718600 | tf_op jit(solution)/shard_map/ppermute | solution.py:371
  668.9 21.2 %collective-permute-start.64 = (bf16[1376,256]{1,0:T(8,128)(2,1)S(1)}, bf16[1376,256]{1,0:T(8,128)(2,1)S(1)}, u32[]{:S(2)}, u32[]{:S(2)}) collective-permute-start(bf16[1376,256]{1,0:T(8,128)(2,1)S(1)} %get-tuple-element.239), channel_id=1, source_target_pairs={{0,4},{1,5},{2,0},{3,1},{4,6},{5,7},{6,2},{7,3},{8,12},{9,13},{10,... | collective-permute-start | bytes 2113544 | tf_op jit(solution)/shard_map/ppermute | solution.py:371
  674.5 68.1 %collective-permute-start.60 = (bf16[1536,512]{1,0:T(8,128)(2,1)}, bf16[1536,512]{1,0:T(8,128)(2,1)}, u32[]{:S(2)}, u32[]{:S(2)}) collective-permute-start(bf16[1536,512]{1,0:T(8,128)(2,1)} %fusion.33), channel_id=1, source_target_pairs={{0,1},{1,0},{2,3},{3,2},{4,5},{5,4},{6,7},{7,6},{8,9},{9,8},{10,11... | collective-permute-start | bytes 4718600 | tf_op jit(solution)/shard_map/ppermute | solution.py:371
  679.4 56.8 %collective-permute-start.62 = (bf16[768,512]{1,0:T(8,128)(2,1)}, bf16[768,512]{1,0:T(8,128)(2,1)}, u32[]{:S(2)}, u32[]{:S(2)}) collective-permute-start(bf16[768,512]{1,0:T(8,128)(2,1)} %get-tuple-element.237), channel_id=1, source_target_pairs={{0,4},{1,5},{2,0},{3,1},{4,6},{5,7},{6,2},{7,3},{8,12},{9,13},{10,... | collective-permute-start | bytes 2359304 | tf_op jit(solution)/shard_map/ppermute | solution.py:371
  679.9 56.3 %collective-permute-start.61 = (bf16[768,512]{1,0:T(8,128)(2,1)}, bf16[768,512]{1,0:T(8,128)(2,1)}, u32[]{:S(2)}, u32[]{:S(2)}) collective-permute-start(bf16[768,512]{1,0:T(8,128)(2,1)} %get-tuple-element.238), channel_id=1, source_target_pairs={{0,0},{1,1},{2,4},{3,5},{4,2},{5,3},{6,6},{7,7},{8,8},{9,9},{10,12... | collective-permute-start | bytes 2359304 | tf_op jit(solution)/shard_map/ppermute | solution.py:371
  682.3 53.8 %collective-permute-start.63 = (bf16[1376,256]{1,0:T(8,128)(2,1)}, bf16[1376,256]{1,0:T(8,128)(2,1)}, u32[]{:S(2)}, u32[]{:S(2)}) collective-permute-start(bf16[1376,256]{1,0:T(8,128)(2,1)} %get-tuple-element.240), channel_id=1, source_target_pairs={{0,0},{1,1},{2,4},{3,5},{4,2},{5,3},{6,6},{7,7},{8,8},{9,9},{10,12... | collective-permute-start | bytes 2113544 | tf_op jit(solution)/shard_map/ppermute | solution.py:371
  691.0 52.3 %collective-permute-start.65 = (bf16[1536,512]{1,0:T(8,128)(2,1)}, bf16[1536,512]{1,0:T(8,128)(2,1)}, u32[]{:S(2)}, u32[]{:S(2)}) collective-permute-start(bf16[1536,512]{1,0:T(8,128)(2,1)} %convolution_convert_fusion.10), channel_id=1, source_target_pairs={{0,4},{1,5},{2,6},{3,7},{4,0},{5,1},{6,2},{7,3},{8,12},{9,13},{10,... | collective-permute-start | bytes 4718600 | tf_op jit(solution)/shard_map/ppermute | solution.py:371
  757.9 36.4 %collective-permute-start.71 = (bf16[2,768,512]{2,1,0:T(8,128)(2,1)S(1)}, bf16[2,768,512]{2,1,0:T(8,128)(2,1)S(1)}, u32[]{:S(2)}, u32[]{:S(2)}) collective-permute-start(bf16[2,768,512]{2,1,0:T(8,128)(2,1)S(1)} %pad_maximum_fusion.1.refs_0_), channel_id=1, source_target_pairs={{1,0},{2,1},{3,2},{5,4},{6,5},{7,6},{9,8},{10,9},{11,10},{13,12},{... | collective-permute-start | bytes 4718600 | tf_op jit(solution)/shard_map/ppermute | solution.py:371
  759.2 36.2 %collective-permute-start.70 = (bf16[2,768,512]{2,1,0:T(8,128)(2,1)S(1)}, bf16[2,768,512]{2,1,0:T(8,128)(2,1)S(1)}, u32[]{:S(2)}, u32[]{:S(2)}) collective-permute-start(bf16[2,768,512]{2,1,0:T(8,128)(2,1)S(1)} %pad_maximum_fusion.1.refs_0_), channel_id=1, source_target_pairs={{0,1},{1,2},{2,3},{4,5},{5,6},{6,7},{8,9},{9,10},{10,11},{12,13},{... | collective-permute-start | bytes 4718600 | tf_op jit(solution)/shard_map/ppermute | solution.py:371
  795.5 21.3 %collective-permute-start.73 = (bf16[2,768,512]{2,1,0:T(8,128)(2,1)S(1)}, bf16[2,768,512]{2,1,0:T(8,128)(2,1)}, u32[]{:S(2)}, u32[]{:S(2)}) collective-permute-start(bf16[2,768,512]{2,1,0:T(8,128)(2,1)S(1)} %collective-permute-done.70.refs_1_), channel_id=1, source_target_pairs={{1,2},{2,3},{5,6},{6,7},{9,10},{10,11},{13,14},{14,15},{17,18},{18... | collective-permute-start | bytes 4718600 | tf_op jit(solution)/shard_map/ppermute | solution.py:371
  797.3 38.2 %collective-permute-start.74 = (bf16[2,768,512]{2,1,0:T(8,128)(2,1)}, bf16[2,768,512]{2,1,0:T(8,128)(2,1)}, u32[]{:S(2)}, u32[]{:S(2)}) collective-permute-start(bf16[2,768,512]{2,1,0:T(8,128)(2,1)} %copy-done.61), channel_id=1, source_target_pairs={{1,0},{2,1},{5,4},{6,5},{9,8},{10,9},{13,12},{14,13},{17,16},{18,1... | collective-permute-start | bytes 4718600 | tf_op jit(solution)/shard_map/ppermute | solution.py:371
  801.3 34.1 %collective-permute-start.77 = (bf16[256,512]{1,0:T(8,128)(2,1)S(1)}, bf16[256,512]{1,0:T(8,128)(2,1)S(1)}, u32[]{:S(2)}, u32[]{:S(2)}) collective-permute-start(bf16[256,512]{1,0:T(8,128)(2,1)S(1)} %get-tuple-element.249), channel_id=1, source_target_pairs={{0,4},{1,5},{2,0},{3,1},{4,6},{5,7},{6,2},{7,3},{8,12},{9,13},{10,... | collective-permute-start | bytes 786440 | tf_op jit(solution)/shard_map/ppermute | solution.py:371
  808.5 42.1 %collective-permute-start.76 = (bf16[256,512]{1,0:T(8,128)(2,1)S(1)}, bf16[256,512]{1,0:T(8,128)(2,1)S(1)}, u32[]{:S(2)}, u32[]{:S(2)}) collective-permute-start(bf16[256,512]{1,0:T(8,128)(2,1)S(1)} %get-tuple-element.250), channel_id=1, source_target_pairs={{0,0},{1,1},{2,4},{3,5},{4,2},{5,3},{6,6},{7,7},{8,8},{9,9},{10,12... | collective-permute-start | bytes 786440 | tf_op jit(solution)/shard_map/ppermute | solution.py:371
  850.6 25.3 %collective-permute-start.78 = (bf16[2,768,512]{2,1,0:T(8,128)(2,1)}, bf16[2,768,512]{2,1,0:T(8,128)(2,1)}, u32[]{:S(2)}, u32[]{:S(2)}) collective-permute-start(bf16[2,768,512]{2,1,0:T(8,128)(2,1)} %collective-permute-done.73.refs_2_), channel_id=1, source_target_pairs={{2,3},{6,7},{10,11},{14,15},{18,19},{22,23},{26,27},{30,31}} | collective-permute-start | bytes 4718600 | tf_op jit(solution)/shard_map/ppermute | solution.py:371
  852.5 43.7 %collective-permute-start.79 = (bf16[2,768,512]{2,1,0:T(8,128)(2,1)}, bf16[2,768,512]{2,1,0:T(8,128)(2,1)}, u32[]{:S(2)}, u32[]{:S(2)}) collective-permute-start(bf16[2,768,512]{2,1,0:T(8,128)(2,1)} %collective-permute-done.74.refs_5_), channel_id=1, source_target_pairs={{1,0},{5,4},{9,8},{13,12},{17,16},{21,20},{25,24},{29,28}} | collective-permute-start | bytes 4718600 | tf_op jit(solution)/shard_map/ppermute | solution.py:371
  853.9 16.5 %collective-permute-start.81 = (bf16[256,640]{1,0:T(8,128)(2,1)S(1)}, bf16[256,640]{1,0:T(8,128)(2,1)S(1)}, u32[]{:S(2)}, u32[]{:S(2)}) collective-permute-start(bf16[256,640]{1,0:T(8,128)(2,1)S(1)} %get-tuple-element.247), channel_id=1, source_target_pairs={{0,0},{1,1},{2,4},{3,5},{4,2},{5,3},{6,6},{7,7},{8,8},{9,9},{10,12... | collective-permute-start | bytes 983048 | tf_op jit(solution)/shard_map/ppermute | solution.py:371
  856.8 13.6 %collective-permute-start.82 = (bf16[256,640]{1,0:T(8,128)(2,1)S(1)}, bf16[256,640]{1,0:T(8,128)(2,1)S(1)}, u32[]{:S(2)}, u32[]{:S(2)}) collective-permute-start(bf16[256,640]{1,0:T(8,128)(2,1)S(1)} %get-tuple-element.248), channel_id=1, source_target_pairs={{0,4},{1,5},{2,0},{3,1},{4,6},{5,7},{6,2},{7,3},{8,12},{9,13},{10,... | collective-permute-start | bytes 983048 | tf_op jit(solution)/shard_map/ppermute | solution.py:371
  (139 other events, 1600.8 us)
Sparse Core Ops, SparseCore 0:
  104.2 74.7 all-gather.2
  194.3 62.8 all-gather.4
  381.9 65.7 reduce-scatter.5
  450.7 64.6 reduce-scatter.7
  548.9 67.7 reduce-scatter.9
  619.5 37.2 reduce-scatter.11
  742.7 38.2 reduce-scatter.13

commit v4 on v3

--- a/solution.py
+++ b/solution.py
@@ -362,8 +362,9 @@
         pairs = []
         for s in range(seq_count):
             for f in range(feat_count):
-                there = target(s // CORES, s % CORES, f // group, f % group)
-                if there is not None:
+                here = (s // CORES, s % CORES, f // group, f % group)
+                there = target(*here)
+                if there is not None and there != here:
                     c2, k2, m2, l2 = there
                     pairs.append(
                         (s * feat_count + f, (c2 * CORES + k2) * feat_count + m2 * group + l2)
@@ -383,16 +384,14 @@
         return move(value, lambda c, k, m, l: (c + d, k, m, l) if 0 <= c + d < chips else None)
 
     def spread(value):
-        return (
-            move(value, lambda c, k, m, l: (c, m, k, l)),
-            move(value, lambda c, k, m, l: (c, m, 1 - k, l)),
-        )
+        moved = move(value, lambda c, k, m, l: (c, m, k, l))
+        other = move(value, lambda c, k, m, l: (c, m, 1 - k, l))
+        return jnp.where(core == batch, value, moved), other
 
     def unspread(same, other):
-        return (
-            move(same, lambda c, k, m, l: (c, m, k, l)),
-            move(other, lambda c, k, m, l: (c, 1 - m, k, l)),
-        )
+        moved = move(same, lambda c, k, m, l: (c, m, k, l))
+        other = move(other, lambda c, k, m, l: (c, 1 - m, k, l))
+        return jnp.where(core == batch, same, moved), other
 
     def ordered(first_if_zero, second_if_zero, bit, axis):
         return jnp.where(
@@ -403,15 +402,26 @@
 
     chip_groups = [[c * CORES + k for c in range(chips)] for k in range(CORES)]
 
-    def gather_chips(owns, axis):
-        size = owns[0].shape[axis]
-        bits = [1 << i for i in range(chips.bit_length() - 1)]
-        pieces, offsets = [], []
-        for own, order, k in zip(owns, (bits, bits[::-1]), (batch, 1 - batch)):
-            held = {0: own}
+    bits = [1 << i for i in range(chips.bit_length() - 1)]
+    orders = (bits, bits[::-1])
+
+    def all_hops(owns):
+        helds = [{0: own} for own in owns]
+        for held, order in zip(helds, orders):
             for bit in order:
                 for mask in list(held):
                     held[mask | bit] = to_chip(held[mask], bit)
+        return helds
+
+    def straight(owns):
+        return [
+            {mask: to_chip(own, mask) if mask else own for mask in range(chips)} for own in owns
+        ]
+
+    def place_chips(helds, axis):
+        size = helds[0][0].shape[axis]
+        pieces, offsets = [], []
+        for held, k in zip(helds, (batch, 1 - batch)):
             for mask, got in held.items():
                 pieces.append(got)
                 offsets.append(((chip ^ mask) * CORES + k) * size)
@@ -448,13 +458,12 @@
             found.append(((1 - core) * group + (part ^ d), to_core(here)))
         return found
 
-    def reduce_begin(partial):
-        totals = []
-        for d in range(group - 1, -1, -1):
-            away = to_core(partial((1 - core) * group + (part ^ d)).astype(BF))
-            total = partial(core * group + (part ^ d)) + away.astype(F32)
-            totals.append(total.astype(BF) if d else total)
-        return totals[-1], totals[-2::-1]
+    def reduce_part(partial, d):
+        away = to_core(partial((1 - core) * group + (part ^ d)).astype(BF))
+        return partial(core * group + (part ^ d)) + away.astype(F32)
+
+    def reduce_away(partial):
+        return [reduce_part(partial, d).astype(BF) for d in range(1, group)]
 
     def reduce_send(totals):
         return [to_part(total, d + 1) for d, total in enumerate(totals)]
@@ -486,11 +495,11 @@
     qk_width, v_width = heads * QK, heads * HEAD_V
     qkv_owns = spread(jnp.concatenate([w_query, w_key, w_value], 1))
     gains = lax.all_gather(jnp.stack([gain_mixer, gain_mlp]), "seq", axis=1, tiled=True)
-    w_output, gains, *qkv_owns = tie(w_output, gains, *qkv_owns)
+    w_gate, gains, *qkv_owns = tie(w_gate.T, gains, *qkv_owns)
     gains = gains.astype(F32)
     mixer_gain, mlp_gain = gains[0], gains[1]
-    output_owns = spread(w_output)
-    qkv_full = gather_chips(qkv_owns, 0)
+    gate_owns = spread(w_gate)
+    qkv_full = place_chips(all_hops(qkv_owns), 0)
 
     bounds = jnp.cumsum(lax.dynamic_index_in_dim(lengths, batch, 0, False))
 
@@ -513,9 +522,6 @@
     inv_one = lax.rsqrt(jnp.mean(tokens_f * tokens_f, axis=-1, keepdims=True) + EPS)
     normed = (tokens_f * inv_one * mixer_gain).astype(BF)
     qkv = dot(normed, qkv_full).astype(BF)
-    w_gate, qkv, *output_owns = tie(w_gate.T, qkv, *output_owns)
-    gate_owns = spread(w_gate)
-    output_full = gather_chips(output_owns, 0)
 
     query, keys = qkv[:, :qk_width], qkv[:, qk_width : 2 * qk_width]
     values = qkv[:, 2 * qk_width :]
@@ -568,28 +574,37 @@
 
     (local,) = local_states(marks, keys, values)
     states, gate_owns = scan_blocks(local, list(range(CORES)), 1, gate_owns)
-    up_owns = spread(tie(w_up.T, states)[0])
+    w_output, gate_owns = tie(w_output, gate_owns)
+    output_owns = spread(w_output)
     gate_full = gather_chips_bulk(gate_owns, 1)
+    w_up, states = tie(w_up.T, states)
+    up_owns = spread(w_up)
     mixer_own, denom = mixer(marks, query, keys, values, states)
+    mixer_own, output_owns, up_owns = tie(mixer_own, output_owns, up_owns)
 
     arrived = send_parts(mixer_own)
-    w_down, *up_owns = tie(w_down, *up_owns)
+    up_full = gather_chips_bulk(up_owns, 1)
+    output_full = place_chips(all_hops(output_owns), 0)
+    w_down, mixer_own = tie(w_down, mixer_own)
     down_owns = spread(w_down)
-    up_full = gather_chips_bulk(up_owns, 1)
     mixer_parts = gather_ranks(mixer_own, arrived)
     branch_own = sum(dot(got, row_piece(output_full, r)) for r, got in mixer_parts).astype(BF)
+    branch_own, down_owns = tie(branch_own, down_owns)
     arrived = send_parts(branch_own)
-    *arrived, gate_full, down_owns = tie(*arrived, gate_full, down_owns)
-    down_full = gather_chips(down_owns, 1)
+    downs = straight(down_owns)
+    *arrived, gate_full = tie(*arrived, gate_full)
     branch_parts = gather_ranks(branch_own, arrived)
     branch = place([got for _, got in branch_parts], [r * piece for r, _ in branch_parts], 1)
     hidden_state = tokens_f + branch.astype(F32)
     inv_two = lax.rsqrt(jnp.mean(hidden_state * hidden_state, axis=-1, keepdims=True) + EPS)
     normed_two = (hidden_state * inv_two * mlp_gain).astype(BF)
 
+    gate = dot(normed_two, gate_full, 1, 1).astype(BF)
+    upward = dot(normed_two, up_full, 1, 1).astype(BF)
+    downs, gate, upward = tie(downs, gate, upward)
+    down_full = place_chips(downs, 1)
+    gate, upward = gate.astype(F32), upward.astype(F32)
     grad_hidden = dot(grad_out, down_full, 1, 1).astype(BF).astype(F32)
-    gate = dot(normed_two, gate_full, 1, 1).astype(BF).astype(F32)
-    upward = dot(normed_two, up_full, 1, 1).astype(BF).astype(F32)
     logistic = jax.nn.sigmoid(gate)
     activated = gate * logistic
     hidden = (activated * upward).astype(BF)
@@ -597,18 +612,19 @@
     grad_up_f = grad_hidden * activated
     grad_gate_b, grad_up_b = grad_gate_f.astype(BF), grad_up_f.astype(BF)
     inner_two = sum_ranks(jnp.sum(grad_gate_f * gate + grad_up_f * upward, axis=1)) / width
-    own, totals = reduce_begin(
-        lambda r: dot(grad_gate_b, column_piece(gate_full, r))
-        + dot(grad_up_b, column_piece(up_full, r))
-    )
-    inner_two, *totals = tie(inner_two, *totals)
+    def hidden_part(grads, r):
+        return dot(grads[0], column_piece(gate_full, r)) + dot(grads[1], column_piece(up_full, r))
+
+    grads = (grad_gate_b, grad_up_b)
+    totals = reduce_away(functools.partial(hidden_part, grads))
+    inner_two, totals, grads = tie(inner_two, totals, grads)
     arrived = reduce_send(totals)
-    up_sum = sum_chips(dot(grad_up_b, normed_two, 0, 0).astype(BF), 1)
-    gate_sum = dot(grad_gate_b, normed_two, 0, 0).astype(BF)
-    up_sum, gate_sum, *arrived = tie(up_sum, gate_sum, *arrived)
+    own = reduce_part(functools.partial(hidden_part, grads), 0)
+    up_sum = sum_chips(dot(grads[1], normed_two, 0, 0).astype(BF), 1)
+    gate_sum = dot(grads[0], normed_two, 0, 0).astype(BF)
+    own, gate_sum, arrived = tie(own, gate_sum, arrived)
     normed_grad = reduce_end(own, arrived)
     gate_sum = sum_chips(gate_sum, 1)
-    up_halves = send_halves(up_sum, 1)
     tokens_own = column_piece(tokens_c, rank).astype(F32)
     hidden_own = tokens_own + branch_own.astype(F32)
     scaled_two = hidden_own * inv_two
@@ -619,27 +635,42 @@
     grad_gain_mlp = jnp.sum(normed_grad * scaled_two, axis=0)
     branch_grad = hidden_grad.astype(BF)
 
-    own, totals = reduce_begin(lambda r: dot(branch_grad, row_piece(output_full, r), 1, 1))
+    def output_part(grad, r):
+        return dot(grad, row_piece(output_full, r), 1, 1)
+
+    totals = reduce_away(functools.partial(output_part, branch_grad))
+    totals, branch_grad, hidden, up_sum = tie(totals, branch_grad, hidden, up_sum)
     arrived = reduce_send(totals)
-    mlp_own, mlp_totals = reduce_begin(lambda r: dot(hidden, column_piece(down_full, r)))
+    own = reduce_part(functools.partial(output_part, branch_grad), 0)
+
+    def down_part(r):
+        return dot(hidden, column_piece(down_full, r))
+
+    mlp_totals, mlp_own = reduce_away(down_part), reduce_part(down_part, 0)
     down_sum = dot(hidden, grad_out, 0, 0).astype(BF)
-    arrived, mlp_own, mlp_totals, down_sum, gate_sum, up_halves = tie(
-        arrived, mlp_own, mlp_totals, down_sum, gate_sum, up_halves
+    up_sum, down_sum = tie(up_sum, down_sum)
+    up_halves = send_halves(up_sum, 1)
+    arrived, own, mlp_own, mlp_totals, down_sum, gate_sum = tie(
+        arrived, own, mlp_own, mlp_totals, down_sum, gate_sum
     )
     mixer_grad = reduce_end(own, arrived)
     mlp_arrived = reduce_send(mlp_totals)
     down_sum = sum_chips(down_sum, 1)
     gate_halves = send_halves(gate_sum, 1)
+    (grad_local,) = grad_states(marks, query, mixer_grad, mixer_own, denom)
+    grad_local, branch_grad = tie(grad_local, branch_grad)
     output_sum = place(
         [dot(got, branch_grad, 0, 0).astype(BF) for _, got in mixer_parts],
         [r * piece for r, _ in mixer_parts],
         0,
     )
+    carried, (up_halves, output_sum) = scan_blocks(
+        grad_local, list(range(CORES))[::-1], -1, (up_halves, output_sum)
+    )
+    carried, mlp_arrived, down_sum, output_sum = tie(
+        carried, mlp_arrived, down_sum, output_sum
+    )
     output_sum = sum_chips(output_sum, 0)
-    (grad_local,) = grad_states(marks, query, mixer_grad, mixer_own, denom)
-    carried, gate_halves = scan_blocks(
-        grad_local, list(range(CORES))[::-1], -1, gate_halves
-    )
     grad_qkv = jnp.concatenate(
         mixer_back(
             marks, query, keys, values, mixer_grad, mixer_own, denom, states, carried
@@ -648,16 +679,20 @@
     )
     inner_one = jnp.sum(grad_qkv.astype(F32) * qkv.astype(F32), axis=1)
     inner_one = sum_ranks(inner_one) / width
-    grad_qkv, mlp_arrived, down_sum = tie(grad_qkv, mlp_arrived, down_sum)
+
+    def input_part(grad, r):
+        return dot(grad, row_piece(qkv_full, r), 1, 1)
+
+    totals = reduce_away(functools.partial(input_part, grad_qkv))
+    totals, grad_qkv, inner_one, gate_halves = tie(totals, grad_qkv, inner_one, gate_halves)
+    arrived = reduce_send(totals)
     mixed_own = (hidden_own + reduce_end(mlp_own, mlp_arrived)).astype(BF)
     mixed_halves = unspread(half(mixed_own, batch), half(mixed_own, 1 - batch))
-    own, totals = reduce_begin(lambda r: dot(grad_qkv, row_piece(qkv_full, r), 1, 1))
-    inner_one, *totals = tie(inner_one, *totals)
-    arrived = reduce_send(totals)
     down_halves = send_halves(down_sum, 1)
+    own = reduce_part(functools.partial(input_part, grad_qkv), 0)
     qkv_sum = dot(normed, grad_qkv, 0, 0).astype(BF)
-    arrived, mixed_halves, down_halves, qkv_sum, output_sum = tie(
-        arrived, mixed_halves, down_halves, qkv_sum, output_sum
+    arrived, own, mixed_halves, down_halves, qkv_sum, output_sum = tie(
+        arrived, own, mixed_halves, down_halves, qkv_sum, output_sum
     )
     input_normed = reduce_end(own, arrived)
     qkv_sum = sum_chips(qkv_sum, 0)
@@ -705,8 +740,6 @@
         if d == 0:
             up, down, qkv_sum = tie(up, down, qkv_sum)
             qkv_halves = send_halves(qkv_sum, 0)
-        if d == 1:
-            up, down, output_halves = tie(up, down, output_halves)
         ups.append(up), downs.append(down)
     for hop in hops:
         gain_grads = gain_grads + hop(gain_grads)

time: 926 us -> 907 us (0.979)
  waiting for transfers between devices: 361 us -> 318 us
  other arithmetic: 47.2 us -> 86.7 us
  matrix products: 212 us -> 196 us
    ppermute x83, waiting for transfers between devices: 357 us -> 314 us  [move(): return lax.ppermute(value, ('seq', 'feat'), pairs)]
    dot_general x36, matrix products: 212 us -> 196 us  [dot(): lax.dot_general(a, b, (((ca,), (cb,)), ((), ())), preferred_element_type=...]
    convert_element_type x0 -> x2, other arithmetic: none -> 13.1 us  [the longest x1 7.49 us: on_device(): grad_gate_b, grad_up_b = (grad_gate_f.astype(BF), grad_up_f.astype(BF))]
    select_n x0 -> x9, other arithmetic: none -> 9.52 us  [the longest x4 4.91 us: unspread(): return (jnp.where(core == batch, same, moved), other)]
    unnamed x226 -> x208, local copies, waits for them, and re-layouts: 27.9 us -> 20.8 us
  transfers between devices with their start and end apart: 90 -> 90, of which waited for: 40 -> 33; matrix products, arithmetic and copies ran while one was open for 26% -> 30% of each run, Pallas kernels for 7% -> 7%
where the time goes in v4:
time: 907 us; the launch traced here: 890 us
  waiting for transfers between devices  318 us (35%)
  matrix products  196 us (22%)
  starting transfers between devices  123 us (14%)
  other arithmetic  86.7 us (10%)
  Pallas kernels  79.4 us (9%)
  local copies, waits for them, and re-layouts  53.8 us (6%)
  between operations  23.8 us (3%)
    ppermute x83, waiting for transfers between devices, move(): return lax.ppermute(value, ('seq', 'feat'), pairs)  314 us
    dot_general x36, matrix products, dot(): lax.dot_general(a, b, (((ca,), (cb,)), ((), ())), preferred_element_type=...  196 us
    ppermute x83, starting transfers between devices, move(): return lax.ppermute(value, ('seq', 'feat'), pairs)  123 us
    pallas_call x4, Pallas kernels, run(): pl.pallas_call(functools.partial(kernel, heads=heads, block=block), grid_...  46.6 us
    pallas_call x9, Pallas kernels, place(): pl.pallas_call(functools.partial(place_kernel, axis=axis), grid_spec=pltp...  23.5 us
    unnamed x208, local copies, waits for them, and re-layouts  20.8 us
  transfers between devices with their start and end apart: 90, of which 33 were waited for; matrix products, arithmetic and copies ran while one was open for 30% of the time, Pallas kernels for 7%

profile of v4, /device:TPU:7, one launch (start us, length us, event | category | flops | bytes accessed | tf_op | source)
XLA Modules:
  0.0 890.0 jit_solution(194182759469683646)
XLA Ops:
  12.1 4.1 collective-permute-start.1
  23.7 8.5 all_gather.9
  39.5 4.9 collective-permute-done.3.refs_1_
  46.5 5.8 collective-permute-done.4.refs_2_
  52.3 4.4 collective-permute-start.13
  66.8 5.3 convolution_convert_fusion.7
  73.6 4.3 shard_map.242
  102.9 4.8 collective-permute-start.15
  117.1 9.2 %shard_map.243 = (bf16[1536,512]{1,0:T(8,128)(2,1)S(1)}, f32[1536,512]{1,0:T(8,128)}) custom-call(s32[2,5]{1,0:T(2,128)S(1)} %copy-done.33, bf16[1536,64]{1,0:T(8,128)(2,1)S(1)} %copy-done.23, bf16[1536,64]{1,0:T(8,128)(2,1)S(1)} %get-tuple-element.287.k_ref, bf16[1536,512]{1,0:T(8,128)(2,1)S(1)} %slice.236.v_ref, ...), custom_call_target="tpu_custom_call" | custom-call | flops 6144000000 | bytes 9216000 | tf_op jit(solution)/shard_map/pallas_call | solution.py:220
  126.3 8.1 collective-permute-done.15
  135.4 14.1 %collective-permute-done.17 = bf16[1376,256]{1,0:T(8,128)(2,1)S(1)} collective-permute-done((bf16[1376,256]{1,0:T(8,128)(2,1)S(1)}, bf16[1376,256]{1,0:T(8,128)(2,1)S(1)}, u32[]{:S(2)}, u32[]{:S(2)}) %collective-permute-start.17) | collective-permute-done | bytes 704544 | tf_op jit(solution)/shard_map/ppermute | solution.py:372
  152.5 5.1 collective-permute-start.28
  157.6 6.3 collective-permute-done.19.refs_1_
  165.5 6.0 collective-permute-done.22.refs_5_
  184.9 12.9 %collective-permute-done.26 = bf16[1536,512]{1,0:T(8,128)(2,1)} collective-permute-done((bf16[1536,512]{1,0:T(8,128)(2,1)S(1)}, bf16[1536,512]{1,0:T(8,128)(2,1)}, u32[]{:S(2)}, u32[]{:S(2)}) %collective-permute-start.26) | collective-permute-done | bytes 1572896 | tf_op jit(solution)/shard_map/ppermute | solution.py:372
  210.7 32.8 %collective-permute-done.31.refs_2_ = bf16[1536,512]{1,0:T(8,128)(2,1)} collective-permute-done((bf16[1536,512]{1,0:T(8,128)(2,1)S(1)}, bf16[1536,512]{1,0:T(8,128)(2,1)}, u32[]{:S(2)}, u32[]{:S(2)}) %collective-permute-start.31) | collective-permute-done | bytes 1572896 | tf_op jit(solution)/shard_map/ppermute | solution.py:372
  243.6 4.1 shard_map.241
  260.4 4.1 multiply_convert_fusion
  264.6 14.4 %convolution_convert_fusion.5 = bf16[1536,1376]{0,1:T(8,128)(2,1)} fusion(bf16[1536,2048]{1,0:T(8,128)(2,1)S(1)} %multiply_convert_fusion, bf16[1376,2048]{1,0:T(8,128)(2,1)} %all-gather.3.cloned.1.call-done), kind=kOutput, calls=%fused_computation.32 | convolution fusion | flops 8659156992 | bytes 16154624 | tf_op jit(solution)/shard_map/dot_general | solution.py:262
  280.2 12.9 %convolution_convert_fusion.4 = bf16[1536,1376]{0,1:T(8,128)(2,1)S(1)} fusion(bf16[1536,2048]{1,0:T(8,128)(2,1)} %copy-done.52, bf16[1376,2048]{1,0:T(8,128)(2,1)} %all-gather.5.cloned.1.call-done), kind=kOutput, calls=%fused_computation.31 | convolution fusion | flops 8659156992 | bytes 16154624 | tf_op jit(solution)/shard_map/dot_general | solution.py:262
  293.2 4.4 collective-permute-done.36.refs_5_
  297.6 14.8 %collective-permute-done.38.refs_7_ = bf16[1376,256]{1,0:T(8,128)(2,1)} collective-permute-done((bf16[1376,256]{1,0:T(8,128)(2,1)S(1)}, bf16[1376,256]{1,0:T(8,128)(2,1)}, u32[]{:S(2)}, u32[]{:S(2)}) %collective-permute-start.38) | collective-permute-done | bytes 704544 | tf_op jit(solution)/shard_map/ppermute | solution.py:372
  316.3 13.2 %convolution_convert_fusion.3 = bf16[1536,1376]{0,1:T(8,128)(2,1)S(1)} fusion(bf16[1536,2048]{1,0:T(8,128)(2,1)} %copy-done.5, bf16[1376,2048]{1,0:T(8,128)(2,1)S(1)} %shard_map.248), kind=kOutput, calls=%fused_computation.30 | convolution fusion | flops 8659156992 | bytes 16154624 | tf_op jit(solution)/shard_map/dot_general | solution.py:262
  329.6 7.5 fusion.18
  337.1 5.1 fusion.55
  342.2 4.1 fusion.24
  356.0 5.3 fusion.26
  361.3 10.7 %convolution_convert_fusion.1 = bf16[1376,2048]{1,0:T(8,128)(2,1)} fusion(bf16[1536,1376]{0,1:T(8,128)(2,1)S(1)} %get-tuple-element.160, bf16[1536,2048]{1,0:T(8,128)(2,1)S(1)} %bitcast.131), kind=kOutput, calls=%fused_computation.28 | convolution fusion | flops 8659861504 | bytes 16154624 | tf_op jit(solution)/shard_map/dot_general | solution.py:262
  372.0 5.5 fusion.49
  377.5 7.6 fusion.25
  386.8 10.6 %convolution_convert_fusion.2 = bf16[1376,2048]{1,0:T(8,128)(2,1)} fusion(bf16[1536,1376]{0,1:T(8,128)(2,1)S(1)} %bitcast.139, bf16[1536,2048]{1,0:T(8,128)(2,1)S(1)} %bitcast.133), kind=kOutput, calls=%fused_computation.29 | convolution fusion | flops 8659861504 | bytes 16154624 | tf_op jit(solution)/shard_map/dot_general | solution.py:262
  397.4 4.8 fusion.52
  402.3 7.6 fusion.17
  409.9 11.4 %collective-permute-done.43 = bf16[1536,512]{1,0:T(8,128)(2,1)S(1)} collective-permute-done((bf16[1536,512]{1,0:T(8,128)(2,1)}, bf16[1536,512]{1,0:T(8,128)(2,1)S(1)}, u32[]{:S(2)}, u32[]{:S(2)}) %collective-permute-start.43) | collective-permute-done | bytes 1572896 | tf_op jit(solution)/shard_map/ppermute | solution.py:372
  422.5 5.6 fusion.132
  439.3 6.6 convolution_convert_fusion.13
  446.0 5.7 convolution_convert_fusion.12
  452.5 10.6 %convolution_convert_fusion = bf16[1376,2048]{1,0:T(8,128)(2,1)} fusion(bf16[1536,1376]{0,1:T(8,128)(2,1)S(1)} %bitcast.135, bf16[1536,2048]{1,0:T(8,128)(2,1)S(1)} %bitcast.129), kind=kOutput, calls=%fused_computation.27 | convolution fusion | flops 8659861504 | bytes 16154624 | tf_op jit(solution)/shard_map/dot_general | solution.py:262
  464.4 4.4 convolution_add_fusion.2
  468.8 7.5 convert_add_fusion.4
  476.3 5.6 add_convert_fusion.1
  481.9 17.5 %collective-permute-done.45 = bf16[1536,512]{1,0:T(8,128)(2,1)} collective-permute-done((bf16[1536,512]{1,0:T(8,128)(2,1)}, bf16[1536,512]{1,0:T(8,128)(2,1)}, u32[]{:S(2)}, u32[]{:S(2)}) %collective-permute-start.45) | collective-permute-done | bytes 1572896 | tf_op jit(solution)/shard_map/ppermute | solution.py:372
  505.3 4.6 collective-permute-start.52
  513.6 20.2 %collective-permute-done.52 = bf16[1376,256]{1,0:T(8,128)(2,1)S(1)} collective-permute-done((bf16[1376,256]{1,0:T(8,128)(2,1)S(1)}, bf16[1376,256]{1,0:T(8,128)(2,1)S(1)}, u32[]{:S(2)}, u32[]{:S(2)}) %collective-permute-start.52) | collective-permute-done | bytes 704544 | tf_op jit(solution)/shard_map/ppermute | solution.py:372
  534.8 4.7 convert_add_fusion.3.do_ref
  539.5 6.6 shard_map.249
  571.8 6.4 collective-permute-start.58
  598.9 26.4 %shard_map.251 = (bf16[1536,64]{1,0:T(8,128)(2,1)S(1)}, bf16[1536,64]{1,0:T(8,128)(2,1)S(1)}, bf16[1536,512]{1,0:T(8,128)(2,1)S(1)}) custom-call(s32[2,5]{1,0:T(2,128)S(1)} %copy-done.34, bf16[1536,64]{1,0:T(8,128)(2,1)S(1)} %copy-done.25, bf16[1536,64]{1,0:T(8,128)(2,1)S(1)} %copy-done.22, bf16[1536,512]{1,0:T(8,128)(2,1)} %copy-done.15, ...), custom_call_target="tpu_custom_call" | custom-call | flops 15360000000 | bytes 9216000 | tf_op jit(solution)/shard_map/pallas_call | solution.py:220
  642.0 4.5 collective-permute-start.64
  647.2 4.2 fusion.29
  654.5 45.4 %collective-permute-done.64 = bf16[1376,256]{1,0:T(8,128)(2,1)S(1)} collective-permute-done((bf16[1376,256]{1,0:T(8,128)(2,1)S(1)}, bf16[1376,256]{1,0:T(8,128)(2,1)S(1)}, u32[]{:S(2)}, u32[]{:S(2)}) %collective-permute-start.64) | collective-permute-done | bytes 704544 | tf_op jit(solution)/shard_map/ppermute | solution.py:372
  701.8 7.4 convolution_convert_fusion.6
  709.3 4.8 convolution_add_fusion
  714.0 10.3 %collective-permute-done.60 = bf16[1536,512]{1,0:T(8,128)(2,1)} collective-permute-done((bf16[1536,512]{1,0:T(8,128)(2,1)}, bf16[1536,512]{1,0:T(8,128)(2,1)}, u32[]{:S(2)}, u32[]{:S(2)}) %collective-permute-start.60) | collective-permute-done | bytes 1572896 | tf_op jit(solution)/shard_map/ppermute | solution.py:372
  725.1 6.3 fusion.23
  745.2 27.7 %collective-permute-done.70.refs_1_ = bf16[2,768,512]{2,1,0:T(8,128)(2,1)S(1)} collective-permute-done((bf16[2,768,512]{2,1,0:T(8,128)(2,1)S(1)}, bf16[2,768,512]{2,1,0:T(8,128)(2,1)S(1)}, u32[]{:S(2)}, u32[]{:S(2)}) %collective-permute-start.70) | collective-permute-done | bytes 1572896 | tf_op jit(solution)/shard_map/ppermute | solution.py:372
  785.4 6.9 collective-permute-start.82
  792.3 5.8 collective-permute-start.81
  798.1 17.8 %collective-permute-done.74.refs_5_ = bf16[2,768,512]{2,1,0:T(8,128)(2,1)} collective-permute-done((bf16[2,768,512]{2,1,0:T(8,128)(2,1)}, bf16[2,768,512]{2,1,0:T(8,128)(2,1)}, u32[]{:S(2)}, u32[]{:S(2)}) %collective-permute-start.74) | collective-permute-done | bytes 1572896 | tf_op jit(solution)/shard_map/ppermute | solution.py:372
  821.5 7.0 collective-permute-start.80
  828.5 7.8 collective-permute-start.79
  840.0 9.8 %collective-permute-done.79 = bf16[256,640]{1,0:T(8,128)(2,1)S(1)} collective-permute-done((bf16[256,640]{1,0:T(8,128)(2,1)S(1)}, bf16[256,640]{1,0:T(8,128)(2,1)S(1)}, u32[]{:S(2)}, u32[]{:S(2)}) %collective-permute-start.79) | collective-permute-done | bytes 327712 | tf_op jit(solution)/shard_map/ppermute | solution.py:372
  853.0 19.9 %collective-permute-done.77.refs_6_ = bf16[2,768,512]{2,1,0:T(8,128)(2,1)} collective-permute-done((bf16[2,768,512]{2,1,0:T(8,128)(2,1)}, bf16[2,768,512]{2,1,0:T(8,128)(2,1)}, u32[]{:S(2)}, u32[]{:S(2)}) %collective-permute-start.77) | collective-permute-done | bytes 1572896 | tf_op jit(solution)/shard_map/ppermute | solution.py:372
  873.5 9.4 %shard_map.252 = f32[2,768,2048]{2,1,0:T(8,128)} custom-call(s32[2]{0:T(128)S(1)} %pad_add_fusion.5.where, bf16[2,768,512]{2,1,0:T(8,128)(2,1)S(1)} %pad_maximum_fusion.1.refs_0_, bf16[2,768,512]{2,1,0:T(8,128)(2,1)S(1)} %collective-permute-done.70.refs_1_, bf16[2,768,512]{2,1,0:T(8,128)(2,1)} %collective-permute-done.73.refs_2_, ...), custom_call_target="tpu_custom_call" | custom-call | tf_op jit(solution)/shard_map/pallas_call | solution.py:321
  (524 shorter events, 253.9 us)
Async XLA Ops:
  7.2 236.3 %all-gather.3.cloned.1.call-start = ((), (), s32[]{:S(2)}) async-start(), calls=%async_computation.5 | async-start | bytes 7045120 | tf_op jit(solution)/shard_map/all_gather | solution.py:433
  9.5 51.4 %collective-permute-start = (bf16[768,2048]{1,0:T(8,128)(2,1)S(1)}, bf16[768,2048]{1,0:T(8,128)(2,1)}, u32[]{:S(2)}, u32[]{:S(2)}) collective-permute-start(bf16[768,2048]{1,0:T(8,128)(2,1)S(1)} %dynamic-slice_bitcast_fusion.1.refs_0_), channel_id=1, source_target_pairs={{0,4},{1,5},{2,6},{3,7},{4,0},{5,1},{6,2},{7,3},{8,12},{9,13},{10,... | collective-permute-start | bytes 9437192 | tf_op jit(solution)/shard_map/ppermute | solution.py:372
  12.1 21.8 %collective-permute-start.1 = (bf16[256,640]{1,0:T(8,128)(2,1)}, bf16[256,640]{1,0:T(8,128)(2,1)}, u32[]{:S(2)}, u32[]{:S(2)}) collective-permute-start(bf16[256,640]{1,0:T(8,128)(2,1)} %pad_maximum_fusion.2), channel_id=1, source_target_pairs={{2,4},{3,5},{4,2},{5,3},{10,12},{11,13},{12,10},{13,11},{18,20},{1... | collective-permute-start | bytes 983048 | tf_op jit(solution)/shard_map/ppermute | solution.py:372
  16.2 18.9 %collective-permute-start.2 = (bf16[256,640]{1,0:T(8,128)(2,1)}, bf16[256,640]{1,0:T(8,128)(2,1)S(1)}, u32[]{:S(2)}, u32[]{:S(2)}) collective-permute-start(bf16[256,640]{1,0:T(8,128)(2,1)} %pad_maximum_fusion.2), channel_id=1, source_target_pairs={{0,2},{1,3},{2,6},{3,7},{4,0},{5,1},{6,4},{7,5},{8,10},{9,11},{10,... | collective-permute-start | bytes 983048 | tf_op jit(solution)/shard_map/ppermute | solution.py:372
  38.1 14.2 %collective-permute-start.4 = (bf16[256,640]{1,0:T(8,128)(2,1)S(1)}, bf16[256,640]{1,0:T(8,128)(2,1)S(1)}, u32[]{:S(2)}, u32[]{:S(2)}) collective-permute-start(bf16[256,640]{1,0:T(8,128)(2,1)S(1)} %broadcast_select_fusion.7.refs_0_), channel_id=1, source_target_pairs={{0,16},{1,17},{2,18},{3,19},{4,20},{5,21},{6,22},{7,23},{8,24},{9,... | collective-permute-start | bytes 983048 | tf_op jit(solution)/shard_map/ppermute | solution.py:372
  39.3 17.4 %collective-permute-start.7 = (bf16[256,640]{1,0:T(8,128)(2,1)S(1)}, bf16[256,640]{1,0:T(8,128)(2,1)S(1)}, u32[]{:S(2)}, u32[]{:S(2)}) collective-permute-start(bf16[256,640]{1,0:T(8,128)(2,1)S(1)} %collective-permute-done.2.refs_4_), channel_id=1, source_target_pairs={{0,8},{1,9},{2,10},{3,11},{4,12},{5,13},{6,14},{7,15},{8,0},{9,1},... | collective-permute-start | bytes 983048 | tf_op jit(solution)/shard_map/ppermute | solution.py:372
  44.4 14.9 %collective-permute-start.5 = (bf16[256,640]{1,0:T(8,128)(2,1)S(1)}, bf16[256,640]{1,0:T(8,128)(2,1)S(1)}, u32[]{:S(2)}, u32[]{:S(2)}) collective-permute-start(bf16[256,640]{1,0:T(8,128)(2,1)S(1)} %collective-permute-done.3.refs_1_), channel_id=1, source_target_pairs={{0,16},{1,17},{2,18},{3,19},{4,20},{5,21},{6,22},{7,23},{8,24},{9,... | collective-permute-start | bytes 983048 | tf_op jit(solution)/shard_map/ppermute | solution.py:372
  45.6 13.7 %collective-permute-start.8 = (bf16[256,640]{1,0:T(8,128)(2,1)S(1)}, bf16[256,640]{1,0:T(8,128)(2,1)S(1)}, u32[]{:S(2)}, u32[]{:S(2)}) collective-permute-start(bf16[256,640]{1,0:T(8,128)(2,1)S(1)} %collective-permute-done.6.refs_5_), channel_id=1, source_target_pairs={{0,8},{1,9},{2,10},{3,11},{4,12},{5,13},{6,14},{7,15},{8,0},{9,1},... | collective-permute-start | bytes 983048 | tf_op jit(solution)/shard_map/ppermute | solution.py:372
  52.3 35.1 %collective-permute-start.13 = (bf16[1376,256]{1,0:T(8,128)(2,1)}, bf16[1376,256]{1,0:T(8,128)(2,1)}, u32[]{:S(2)}, u32[]{:S(2)}) collective-permute-start(bf16[1376,256]{1,0:T(8,128)(2,1)} %bitcast.146), channel_id=1, source_target_pairs={{2,4},{3,5},{4,2},{5,3},{10,12},{11,13},{12,10},{13,11},{18,20},{1... | collective-permute-start | bytes 2113544 | tf_op jit(solution)/shard_map/ppermute | solution.py:372
  56.7 32.3 %collective-permute-start.14 = (bf16[1376,256]{1,0:T(8,128)(2,1)}, bf16[1376,256]{1,0:T(8,128)(2,1)}, u32[]{:S(2)}, u32[]{:S(2)}) collective-permute-start(bf16[1376,256]{1,0:T(8,128)(2,1)} %bitcast.147), channel_id=1, source_target_pairs={{0,2},{1,3},{2,6},{3,7},{4,0},{5,1},{6,4},{7,5},{8,10},{9,11},{10,... | collective-permute-start | bytes 2113544 | tf_op jit(solution)/shard_map/ppermute | solution.py:372
  93.6 186.7 %all-gather.5.cloned.1.call-start = ((), (), s32[]{:S(2)}) async-start(), calls=%async_computation.6 | async-start | bytes 7045120 | tf_op jit(solution)/shard_map/all_gather | solution.py:433
  102.9 31.5 %collective-permute-start.15 = (bf16[256,512]{1,0:T(8,128)(2,1)}, bf16[256,512]{1,0:T(8,128)(2,1)}, u32[]{:S(2)}, u32[]{:S(2)}) collective-permute-start(bf16[256,512]{1,0:T(8,128)(2,1)} %param.22), channel_id=1, source_target_pairs={{2,4},{3,5},{4,2},{5,3},{10,12},{11,13},{12,10},{13,11},{18,20},{1... | collective-permute-start | bytes 786440 | tf_op jit(solution)/shard_map/ppermute | solution.py:372
  107.7 41.8 %collective-permute-start.16 = (bf16[256,512]{1,0:T(8,128)(2,1)}, bf16[256,512]{1,0:T(8,128)(2,1)}, u32[]{:S(2)}, u32[]{:S(2)}) collective-permute-start(bf16[256,512]{1,0:T(8,128)(2,1)} %param.22), channel_id=1, source_target_pairs={{0,2},{1,3},{2,6},{3,7},{4,0},{5,1},{6,4},{7,5},{8,10},{9,11},{10,... | collective-permute-start | bytes 786440 | tf_op jit(solution)/shard_map/ppermute | solution.py:372
  111.1 38.4 %collective-permute-start.17 = (bf16[1376,256]{1,0:T(8,128)(2,1)S(1)}, bf16[1376,256]{1,0:T(8,128)(2,1)S(1)}, u32[]{:S(2)}, u32[]{:S(2)}) collective-permute-start(bf16[1376,256]{1,0:T(8,128)(2,1)S(1)} %bitcast.149), channel_id=1, source_target_pairs={{2,4},{3,5},{4,2},{5,3},{10,12},{11,13},{12,10},{13,11},{18,20},{1... | collective-permute-start | bytes 2113544 | tf_op jit(solution)/shard_map/ppermute | solution.py:372
  113.0 37.6 %collective-permute-start.18 = (bf16[1376,256]{1,0:T(8,128)(2,1)S(1)}, bf16[1376,256]{1,0:T(8,128)(2,1)S(1)}, u32[]{:S(2)}, u32[]{:S(2)}) collective-permute-start(bf16[1376,256]{1,0:T(8,128)(2,1)S(1)} %bitcast.150), channel_id=1, source_target_pairs={{0,2},{1,3},{2,6},{3,7},{4,0},{5,1},{6,4},{7,5},{8,10},{9,11},{10,... | collective-permute-start | bytes 2113544 | tf_op jit(solution)/shard_map/ppermute | solution.py:372
  151.5 46.3 %collective-permute-start.26 = (bf16[1536,512]{1,0:T(8,128)(2,1)S(1)}, bf16[1536,512]{1,0:T(8,128)(2,1)}, u32[]{:S(2)}, u32[]{:S(2)}) collective-permute-start(bf16[1536,512]{1,0:T(8,128)(2,1)S(1)} %get-tuple-element.136.o_ref), channel_id=1, source_target_pairs={{0,1},{1,0},{2,3},{3,2},{4,5},{5,4},{6,7},{7,6},{8,9},{9,8},{10,11... | collective-permute-start | bytes 4718600 | tf_op jit(solution)/shard_map/ppermute | solution.py:372
  152.5 48.1 %collective-permute-start.28 = (bf16[1376,256]{1,0:T(8,128)(2,1)}, bf16[1376,256]{1,0:T(8,128)(2,1)}, u32[]{:S(2)}, u32[]{:S(2)}) collective-permute-start(bf16[1376,256]{1,0:T(8,128)(2,1)} %param.25), channel_id=1, source_target_pairs={{2,4},{3,5},{4,2},{5,3},{10,12},{11,13},{12,10},{13,11},{18,20},{1... | collective-permute-start | bytes 2113544 | tf_op jit(solution)/shard_map/ppermute | solution.py:372
  157.5 46.6 %collective-permute-start.25 = (bf16[1536,512]{1,0:T(8,128)(2,1)S(1)}, bf16[1536,512]{1,0:T(8,128)(2,1)}, u32[]{:S(2)}, u32[]{:S(2)}) collective-permute-start(bf16[1536,512]{1,0:T(8,128)(2,1)S(1)} %get-tuple-element.136.o_ref), channel_id=1, source_target_pairs={{0,4},{1,5},{2,6},{3,7},{4,0},{5,1},{6,2},{7,3},{8,12},{9,13},{10,... | collective-permute-start | bytes 4718600 | tf_op jit(solution)/shard_map/ppermute | solution.py:372
  179.0 256.5 %reduce-scatter.6.cloned.1.call-start = ((), (), s32[]{:S(2)}) async-start(), calls=%async_computation.7 | async-start | bytes 7045120 | tf_op jit(solution)/shard_map/reduce_scatter | solution.py:438
  179.0 64.6 %collective-permute-start.9 = (bf16[768,2048]{1,0:T(8,128)(2,1)}, bf16[768,2048]{1,0:T(8,128)(2,1)}, u32[]{:S(2)}, u32[]{:S(2)}) collective-permute-start(bf16[768,2048]{1,0:T(8,128)(2,1)} %dynamic-slice_bitcast_fusion.refs_0_), channel_id=1, source_target_pairs={{0,4},{1,5},{2,6},{3,7},{4,0},{5,1},{6,2},{7,3},{8,12},{9,13},{10,... | collective-permute-start | bytes 9437192 | tf_op jit(solution)/shard_map/ppermute | solution.py:372
  180.7 28.0 %collective-permute-start.29 = (bf16[1376,256]{1,0:T(8,128)(2,1)}, bf16[1376,256]{1,0:T(8,128)(2,1)S(1)}, u32[]{:S(2)}, u32[]{:S(2)}) collective-permute-start(bf16[1376,256]{1,0:T(8,128)(2,1)} %param.25), channel_id=1, source_target_pairs={{0,2},{1,3},{2,6},{3,7},{4,0},{5,1},{6,4},{7,5},{8,10},{9,11},{10,... | collective-permute-start | bytes 2113544 | tf_op jit(solution)/shard_map/ppermute | solution.py:372
  208.7 34.7 %collective-permute-start.31 = (bf16[1536,512]{1,0:T(8,128)(2,1)S(1)}, bf16[1536,512]{1,0:T(8,128)(2,1)}, u32[]{:S(2)}, u32[]{:S(2)}) collective-permute-start(bf16[1536,512]{1,0:T(8,128)(2,1)S(1)} %fusion.27.refs_0_), channel_id=1, source_target_pairs={{0,1},{1,0},{2,3},{3,2},{4,5},{5,4},{6,7},{7,6},{8,9},{9,8},{10,11... | collective-permute-start | bytes 4718600 | tf_op jit(solution)/shard_map/ppermute | solution.py:372
  210.6 42.4 %collective-permute-start.30 = (bf16[1536,512]{1,0:T(8,128)(2,1)S(1)}, bf16[1536,512]{1,0:T(8,128)(2,1)}, u32[]{:S(2)}, u32[]{:S(2)}) collective-permute-start(bf16[1536,512]{1,0:T(8,128)(2,1)S(1)} %fusion.27.refs_0_), channel_id=1, source_target_pairs={{0,4},{1,5},{2,6},{3,7},{4,0},{5,1},{6,2},{7,3},{8,12},{9,13},{10,... | collective-permute-start | bytes 4718600 | tf_op jit(solution)/shard_map/ppermute | solution.py:372
  250.4 28.6 %collective-permute-start.33 = (bf16[1376,256]{1,0:T(8,128)(2,1)S(1)}, bf16[1376,256]{1,0:T(8,128)(2,1)}, u32[]{:S(2)}, u32[]{:S(2)}) collective-permute-start(bf16[1376,256]{1,0:T(8,128)(2,1)S(1)} %broadcast_select_fusion.4.refs_0_), channel_id=1, source_target_pairs={{0,8},{1,9},{2,10},{3,11},{4,12},{5,13},{6,14},{7,15},{8,0},{9,1},... | collective-permute-start | bytes 2113544 | tf_op jit(solution)/shard_map/ppermute | solution.py:372
  250.5 42.7 %collective-permute-start.34 = (bf16[1376,256]{1,0:T(8,128)(2,1)S(1)}, bf16[1376,256]{1,0:T(8,128)(2,1)}, u32[]{:S(2)}, u32[]{:S(2)}) collective-permute-start(bf16[1376,256]{1,0:T(8,128)(2,1)S(1)} %broadcast_select_fusion.4.refs_0_), channel_id=1, source_target_pairs={{0,16},{1,17},{2,18},{3,19},{4,20},{5,21},{6,22},{7,23},{8,24},{9,... | collective-permute-start | bytes 2113544 | tf_op jit(solution)/shard_map/ppermute | solution.py:372
  251.8 41.4 %collective-permute-start.35 = (bf16[1376,256]{1,0:T(8,128)(2,1)S(1)}, bf16[1376,256]{1,0:T(8,128)(2,1)}, u32[]{:S(2)}, u32[]{:S(2)}) collective-permute-start(bf16[1376,256]{1,0:T(8,128)(2,1)S(1)} %broadcast_select_fusion.4.refs_0_), channel_id=1, source_target_pairs={{0,24},{1,25},{2,26},{3,27},{4,28},{5,29},{6,30},{7,31},{8,16},{9,... | collective-permute-start | bytes 2113544 | tf_op jit(solution)/shard_map/ppermute | solution.py:372
  253.1 44.5 %collective-permute-start.36 = (bf16[1376,256]{1,0:T(8,128)(2,1)S(1)}, bf16[1376,256]{1,0:T(8,128)(2,1)}, u32[]{:S(2)}, u32[]{:S(2)}) collective-permute-start(bf16[1376,256]{1,0:T(8,128)(2,1)S(1)} %collective-permute-done.29.refs_4_), channel_id=1, source_target_pairs={{0,8},{1,9},{2,10},{3,11},{4,12},{5,13},{6,14},{7,15},{8,0},{9,1},... | collective-permute-start | bytes 2113544 | tf_op jit(solution)/shard_map/ppermute | solution.py:372
  253.1 44.5 %collective-permute-start.37 = (bf16[1376,256]{1,0:T(8,128)(2,1)S(1)}, bf16[1376,256]{1,0:T(8,128)(2,1)}, u32[]{:S(2)}, u32[]{:S(2)}) collective-permute-start(bf16[1376,256]{1,0:T(8,128)(2,1)S(1)} %collective-permute-done.29.refs_4_), channel_id=1, source_target_pairs={{0,16},{1,17},{2,18},{3,19},{4,20},{5,21},{6,22},{7,23},{8,24},{9,... | collective-permute-start | bytes 2113544 | tf_op jit(solution)/shard_map/ppermute | solution.py:372
  279.0 33.4 %collective-permute-start.38 = (bf16[1376,256]{1,0:T(8,128)(2,1)S(1)}, bf16[1376,256]{1,0:T(8,128)(2,1)}, u32[]{:S(2)}, u32[]{:S(2)}) collective-permute-start(bf16[1376,256]{1,0:T(8,128)(2,1)S(1)} %collective-permute-done.29.refs_4_), channel_id=1, source_target_pairs={{0,24},{1,25},{2,26},{3,27},{4,28},{5,29},{6,30},{7,31},{8,16},{9,... | collective-permute-start | bytes 2113544 | tf_op jit(solution)/shard_map/ppermute | solution.py:372
  372.0 131.0 %reduce-scatter.8.cloned.1.call-start = ((), (), s32[]{:S(2)}) async-start(), calls=%async_computation.8 | async-start | bytes 7045120 | tf_op jit(solution)/shard_map/reduce_scatter | solution.py:438
  385.1 17.2 %collective-permute-start.42 = (bf16[1536,512]{1,0:T(8,128)(2,1)}, bf16[1536,512]{1,0:T(8,128)(2,1)}, u32[]{:S(2)}, u32[]{:S(2)}) collective-permute-start(bf16[1536,512]{1,0:T(8,128)(2,1)} %fusion.25), channel_id=1, source_target_pairs={{0,4},{1,5},{2,6},{3,7},{4,0},{5,1},{6,2},{7,3},{8,12},{9,13},{10,... | collective-permute-start | bytes 4718600 | tf_op jit(solution)/shard_map/ppermute | solution.py:372
  385.1 36.2 %collective-permute-start.43 = (bf16[1536,512]{1,0:T(8,128)(2,1)}, bf16[1536,512]{1,0:T(8,128)(2,1)S(1)}, u32[]{:S(2)}, u32[]{:S(2)}) collective-permute-start(bf16[1536,512]{1,0:T(8,128)(2,1)} %fusion.26), channel_id=1, source_target_pairs={{0,1},{1,0},{2,3},{3,2},{4,5},{5,4},{6,7},{7,6},{8,9},{9,8},{10,11... | collective-permute-start | bytes 4718600 | tf_op jit(solution)/shard_map/ppermute | solution.py:372
  421.4 174.2 %reduce-scatter.10.cloned.1.call-start = ((), (), s32[]{:S(2)}) async-start(), calls=%async_computation.9 | async-start | bytes 7045120 | tf_op jit(solution)/shard_map/reduce_scatter | solution.py:438
  438.9 25.5 %collective-permute-start.46 = (bf16[1536,512]{1,0:T(8,128)(2,1)}, bf16[1536,512]{1,0:T(8,128)(2,1)}, u32[]{:S(2)}, u32[]{:S(2)}) collective-permute-start(bf16[1536,512]{1,0:T(8,128)(2,1)} %convolution_convert_fusion.8), channel_id=1, source_target_pairs={{0,4},{1,5},{2,6},{3,7},{4,0},{5,1},{6,2},{7,3},{8,12},{9,13},{10,... | collective-permute-start | bytes 4718600 | tf_op jit(solution)/shard_map/ppermute | solution.py:372
  445.9 22.9 %collective-permute-start.47 = (bf16[1536,512]{1,0:T(8,128)(2,1)}, bf16[1536,512]{1,0:T(8,128)(2,1)}, u32[]{:S(2)}, u32[]{:S(2)}) collective-permute-start(bf16[1536,512]{1,0:T(8,128)(2,1)} %convolution_convert_fusion.13), channel_id=1, source_target_pairs={{0,4},{1,5},{2,6},{3,7},{4,0},{5,1},{6,2},{7,3},{8,12},{9,13},{10,... | collective-permute-start | bytes 4718600 | tf_op jit(solution)/shard_map/ppermute | solution.py:372
  451.7 24.6 %collective-permute-start.48 = (bf16[1536,512]{1,0:T(8,128)(2,1)}, bf16[1536,512]{1,0:T(8,128)(2,1)}, u32[]{:S(2)}, u32[]{:S(2)}) collective-permute-start(bf16[1536,512]{1,0:T(8,128)(2,1)} %convolution_convert_fusion.12), channel_id=1, source_target_pairs={{0,4},{1,5},{2,6},{3,7},{4,0},{5,1},{6,2},{7,3},{8,12},{9,13},{10,... | collective-permute-start | bytes 4718600 | tf_op jit(solution)/shard_map/ppermute | solution.py:372
  463.1 36.3 %collective-permute-start.45 = (bf16[1536,512]{1,0:T(8,128)(2,1)}, bf16[1536,512]{1,0:T(8,128)(2,1)}, u32[]{:S(2)}, u32[]{:S(2)}) collective-permute-start(bf16[1536,512]{1,0:T(8,128)(2,1)} %fusion.28), channel_id=1, source_target_pairs={{0,1},{1,0},{2,3},{3,2},{4,5},{5,4},{6,7},{7,6},{8,9},{9,8},{10,11... | collective-permute-start | bytes 4718600 | tf_op jit(solution)/shard_map/ppermute | solution.py:372
  503.0 221.4 %reduce-scatter.12.cloned.1.call-start = ((), (), s32[]{:S(2)}) async-start(), calls=%async_computation.10 | async-start | bytes 2621440 | tf_op jit(solution)/shard_map/reduce_scatter | solution.py:438
  505.3 28.5 %collective-permute-start.52 = (bf16[1376,256]{1,0:T(8,128)(2,1)S(1)}, bf16[1376,256]{1,0:T(8,128)(2,1)S(1)}, u32[]{:S(2)}, u32[]{:S(2)}) collective-permute-start(bf16[1376,256]{1,0:T(8,128)(2,1)S(1)} %get-tuple-element.296), channel_id=1, source_target_pairs={{2,4},{3,5},{4,2},{5,3},{10,12},{11,13},{12,10},{13,11},{18,20},{1... | collective-permute-start | bytes 2113544 | tf_op jit(solution)/shard_map/ppermute | solution.py:372
  513.5 58.3 %collective-permute-start.53 = (bf16[1376,256]{1,0:T(8,128)(2,1)}, bf16[1376,256]{1,0:T(8,128)(2,1)}, u32[]{:S(2)}, u32[]{:S(2)}) collective-permute-start(bf16[1376,256]{1,0:T(8,128)(2,1)} %get-tuple-element.295), channel_id=1, source_target_pairs={{0,4},{1,5},{2,0},{3,1},{4,6},{5,7},{6,2},{7,3},{8,12},{9,13},{10,... | collective-permute-start | bytes 2113544 | tf_op jit(solution)/shard_map/ppermute | solution.py:372
  550.6 27.6 %collective-permute-start.49 = (bf16[648,128]{1,0:T(8,128)(2,1)}, bf16[648,128]{1,0:T(8,128)(2,1)}, u32[]{:S(2)}, u32[]{:S(2)}) collective-permute-start(bf16[648,128]{1,0:T(8,128)(2,1)} %pad_maximum_fusion.4), channel_id=1, source_target_pairs={{8,0},{9,1},{10,2},{11,3},{12,4},{13,5},{14,6},{15,7},{16,8},{17,9... | collective-permute-start | bytes 497672 | tf_op jit(solution)/shard_map/ppermute | solution.py:372
  554.2 24.1 %collective-permute-start.50 = (bf16[648,128]{1,0:T(8,128)(2,1)}, bf16[648,128]{1,0:T(8,128)(2,1)}, u32[]{:S(2)}, u32[]{:S(2)}) collective-permute-start(bf16[648,128]{1,0:T(8,128)(2,1)} %pad_maximum_fusion.4), channel_id=1, source_target_pairs={{16,0},{17,1},{18,2},{19,3},{20,4},{21,5},{22,6},{23,7},{24,8},{25... | collective-permute-start | bytes 497672 | tf_op jit(solution)/shard_map/ppermute | solution.py:372
  556.5 21.8 %collective-permute-start.51 = (bf16[648,128]{1,0:T(8,128)(2,1)}, bf16[648,128]{1,0:T(8,128)(2,1)}, u32[]{:S(2)}, u32[]{:S(2)}) collective-permute-start(bf16[648,128]{1,0:T(8,128)(2,1)} %pad_maximum_fusion.4), channel_id=1, source_target_pairs={{24,0},{25,1},{26,2},{27,3},{28,4},{29,5},{30,6},{31,7}} | collective-permute-start | bytes 497672 | tf_op jit(solution)/shard_map/ppermute | solution.py:372
  558.5 37.1 %collective-permute-start.54 = (bf16[1536,512]{1,0:T(8,128)(2,1)}, bf16[1536,512]{1,0:T(8,128)(2,1)}, u32[]{:S(2)}, u32[]{:S(2)}) collective-permute-start(bf16[1536,512]{1,0:T(8,128)(2,1)} %add_convert_fusion.1), channel_id=1, source_target_pairs={{0,1},{1,0},{2,3},{3,2},{4,5},{5,4},{6,7},{7,6},{8,9},{9,8},{10,11... | collective-permute-start | bytes 4718600 | tf_op jit(solution)/shard_map/ppermute | solution.py:372
  571.8 58.8 %collective-permute-start.58 = (bf16[1376,256]{1,0:T(8,128)(2,1)}, bf16[1376,256]{1,0:T(8,128)(2,1)}, u32[]{:S(2)}, u32[]{:S(2)}) collective-permute-start(bf16[1376,256]{1,0:T(8,128)(2,1)} %get-tuple-element.294), channel_id=1, source_target_pairs={{2,4},{3,5},{4,2},{5,3},{10,12},{11,13},{12,10},{13,11},{18,20},{1... | collective-permute-start | bytes 2113544 | tf_op jit(solution)/shard_map/ppermute | solution.py:372
  578.2 73.2 %collective-permute-start.59 = (bf16[1376,256]{1,0:T(8,128)(2,1)}, bf16[1376,256]{1,0:T(8,128)(2,1)}, u32[]{:S(2)}, u32[]{:S(2)}) collective-permute-start(bf16[1376,256]{1,0:T(8,128)(2,1)} %get-tuple-element.293), channel_id=1, source_target_pairs={{0,4},{1,5},{2,0},{3,1},{4,6},{5,7},{6,2},{7,3},{8,12},{9,13},{10,... | collective-permute-start | bytes 2113544 | tf_op jit(solution)/shard_map/ppermute | solution.py:372
  630.1 17.0 %collective-permute-start.55 = (bf16[1536,512]{1,0:T(8,128)(2,1)}, bf16[1536,512]{1,0:T(8,128)(2,1)}, u32[]{:S(2)}, u32[]{:S(2)}) collective-permute-start(bf16[1536,512]{1,0:T(8,128)(2,1)} %convolution_convert_fusion.11), channel_id=1, source_target_pairs={{0,4},{1,5},{2,6},{3,7},{4,0},{5,1},{6,2},{7,3},{8,12},{9,13},{10,... | collective-permute-start | bytes 4718600 | tf_op jit(solution)/shard_map/ppermute | solution.py:372
  632.7 144.3 %reduce-scatter.14.cloned.1.call-start = ((), (), s32[]{:S(2)}) async-start(), calls=%async_computation.11 | async-start | bytes 3276800 | tf_op jit(solution)/shard_map/reduce_scatter | solution.py:438
  637.6 63.2 %collective-permute-start.62 = (bf16[768,512]{1,0:T(8,128)(2,1)S(1)}, bf16[768,512]{1,0:T(8,128)(2,1)S(1)}, u32[]{:S(2)}, u32[]{:S(2)}) collective-permute-start(bf16[768,512]{1,0:T(8,128)(2,1)S(1)} %get-tuple-element.290), channel_id=1, source_target_pairs={{2,4},{3,5},{4,2},{5,3},{10,12},{11,13},{12,10},{13,11},{18,20},{1... | collective-permute-start | bytes 2359304 | tf_op jit(solution)/shard_map/ppermute | solution.py:372
  639.6 74.4 %collective-permute-start.63 = (bf16[768,512]{1,0:T(8,128)(2,1)}, bf16[768,512]{1,0:T(8,128)(2,1)}, u32[]{:S(2)}, u32[]{:S(2)}) collective-permute-start(bf16[768,512]{1,0:T(8,128)(2,1)} %get-tuple-element.289), channel_id=1, source_target_pairs={{0,4},{1,5},{2,0},{3,1},{4,6},{5,7},{6,2},{7,3},{8,12},{9,13},{10,... | collective-permute-start | bytes 2359304 | tf_op jit(solution)/shard_map/ppermute | solution.py:372
  642.0 57.8 %collective-permute-start.64 = (bf16[1376,256]{1,0:T(8,128)(2,1)S(1)}, bf16[1376,256]{1,0:T(8,128)(2,1)S(1)}, u32[]{:S(2)}, u32[]{:S(2)}) collective-permute-start(bf16[1376,256]{1,0:T(8,128)(2,1)S(1)} %get-tuple-element.292), channel_id=1, source_target_pairs={{2,4},{3,5},{4,2},{5,3},{10,12},{11,13},{12,10},{13,11},{18,20},{1... | collective-permute-start | bytes 2113544 | tf_op jit(solution)/shard_map/ppermute | solution.py:372
  647.1 66.9 %collective-permute-start.65 = (bf16[1376,256]{1,0:T(8,128)(2,1)}, bf16[1376,256]{1,0:T(8,128)(2,1)}, u32[]{:S(2)}, u32[]{:S(2)}) collective-permute-start(bf16[1376,256]{1,0:T(8,128)(2,1)} %get-tuple-element.291), channel_id=1, source_target_pairs={{0,4},{1,5},{2,0},{3,1},{4,6},{5,7},{6,2},{7,3},{8,12},{9,13},{10,... | collective-permute-start | bytes 2113544 | tf_op jit(solution)/shard_map/ppermute | solution.py:372
  653.9 55.3 %collective-permute-start.61 = (bf16[1536,512]{1,0:T(8,128)(2,1)}, bf16[1536,512]{1,0:T(8,128)(2,1)}, u32[]{:S(2)}, u32[]{:S(2)}) collective-permute-start(bf16[1536,512]{1,0:T(8,128)(2,1)} %convolution_convert_fusion.10), channel_id=1, source_target_pairs={{0,4},{1,5},{2,6},{3,7},{4,0},{5,1},{6,2},{7,3},{8,12},{9,13},{10,... | collective-permute-start | bytes 4718600 | tf_op jit(solution)/shard_map/ppermute | solution.py:372
  700.8 23.6 %collective-permute-start.60 = (bf16[1536,512]{1,0:T(8,128)(2,1)}, bf16[1536,512]{1,0:T(8,128)(2,1)}, u32[]{:S(2)}, u32[]{:S(2)}) collective-permute-start(bf16[1536,512]{1,0:T(8,128)(2,1)} %fusion.29), channel_id=1, source_target_pairs={{0,1},{1,0},{2,3},{3,2},{4,5},{5,4},{6,7},{7,6},{8,9},{9,8},{10,11... | collective-permute-start | bytes 4718600 | tf_op jit(solution)/shard_map/ppermute | solution.py:372
  739.7 33.3 %collective-permute-start.70 = (bf16[2,768,512]{2,1,0:T(8,128)(2,1)S(1)}, bf16[2,768,512]{2,1,0:T(8,128)(2,1)S(1)}, u32[]{:S(2)}, u32[]{:S(2)}) collective-permute-start(bf16[2,768,512]{2,1,0:T(8,128)(2,1)S(1)} %pad_maximum_fusion.1.refs_0_), channel_id=1, source_target_pairs={{0,1},{1,2},{2,3},{4,5},{5,6},{6,7},{8,9},{9,10},{10,11},{12,13},{... | collective-permute-start | bytes 4718600 | tf_op jit(solution)/shard_map/ppermute | solution.py:372
  741.1 35.9 %collective-permute-start.71 = (bf16[2,768,512]{2,1,0:T(8,128)(2,1)S(1)}, bf16[2,768,512]{2,1,0:T(8,128)(2,1)}, u32[]{:S(2)}, u32[]{:S(2)}) collective-permute-start(bf16[2,768,512]{2,1,0:T(8,128)(2,1)S(1)} %pad_maximum_fusion.1.refs_0_), channel_id=1, source_target_pairs={{1,0},{2,1},{3,2},{5,4},{6,5},{7,6},{9,8},{10,9},{11,10},{13,12},{... | collective-permute-start | bytes 4718600 | tf_op jit(solution)/shard_map/ppermute | solution.py:372
  777.0 21.1 %collective-permute-start.73 = (bf16[2,768,512]{2,1,0:T(8,128)(2,1)S(1)}, bf16[2,768,512]{2,1,0:T(8,128)(2,1)}, u32[]{:S(2)}, u32[]{:S(2)}) collective-permute-start(bf16[2,768,512]{2,1,0:T(8,128)(2,1)S(1)} %collective-permute-done.70.refs_1_), channel_id=1, source_target_pairs={{1,2},{2,3},{5,6},{6,7},{9,10},{10,11},{13,14},{14,15},{17,18},{18... | collective-permute-start | bytes 4718600 | tf_op jit(solution)/shard_map/ppermute | solution.py:372
  778.8 37.1 %collective-permute-start.74 = (bf16[2,768,512]{2,1,0:T(8,128)(2,1)}, bf16[2,768,512]{2,1,0:T(8,128)(2,1)}, u32[]{:S(2)}, u32[]{:S(2)}) collective-permute-start(bf16[2,768,512]{2,1,0:T(8,128)(2,1)} %collective-permute-done.71.refs_4_), channel_id=1, source_target_pairs={{1,0},{2,1},{5,4},{6,5},{9,8},{10,9},{13,12},{14,13},{17,16},{18,1... | collective-permute-start | bytes 4718600 | tf_op jit(solution)/shard_map/ppermute | solution.py:372
  785.4 43.1 %collective-permute-start.82 = (bf16[256,512]{1,0:T(8,128)(2,1)S(1)}, bf16[256,512]{1,0:T(8,128)(2,1)S(1)}, u32[]{:S(2)}, u32[]{:S(2)}) collective-permute-start(bf16[256,512]{1,0:T(8,128)(2,1)S(1)} %get-tuple-element.302), channel_id=1, source_target_pairs={{0,4},{1,5},{2,0},{3,1},{4,6},{5,7},{6,2},{7,3},{8,12},{9,13},{10,... | collective-permute-start | bytes 786440 | tf_op jit(solution)/shard_map/ppermute | solution.py:372
  792.3 46.8 %collective-permute-start.81 = (bf16[256,512]{1,0:T(8,128)(2,1)S(1)}, bf16[256,512]{1,0:T(8,128)(2,1)S(1)}, u32[]{:S(2)}, u32[]{:S(2)}) collective-permute-start(bf16[256,512]{1,0:T(8,128)(2,1)S(1)} %get-tuple-element.301), channel_id=1, source_target_pairs={{2,4},{3,5},{4,2},{5,3},{10,12},{11,13},{12,10},{13,11},{18,20},{1... | collective-permute-start | bytes 786440 | tf_op jit(solution)/shard_map/ppermute | solution.py:372
  816.0 37.1 %collective-permute-start.76 = (bf16[2,768,512]{2,1,0:T(8,128)(2,1)}, bf16[2,768,512]{2,1,0:T(8,128)(2,1)}, u32[]{:S(2)}, u32[]{:S(2)}) collective-permute-start(bf16[2,768,512]{2,1,0:T(8,128)(2,1)} %collective-permute-done.73.refs_2_), channel_id=1, source_target_pairs={{2,3},{6,7},{10,11},{14,15},{18,19},{22,23},{26,27},{30,31}} | collective-permute-start | bytes 4718600 | tf_op jit(solution)/shard_map/ppermute | solution.py:372
  817.8 55.1 %collective-permute-start.77 = (bf16[2,768,512]{2,1,0:T(8,128)(2,1)}, bf16[2,768,512]{2,1,0:T(8,128)(2,1)}, u32[]{:S(2)}, u32[]{:S(2)}) collective-permute-start(bf16[2,768,512]{2,1,0:T(8,128)(2,1)} %collective-permute-done.74.refs_5_), channel_id=1, source_target_pairs={{1,0},{5,4},{9,8},{13,12},{17,16},{21,20},{25,24},{29,28}} | collective-permute-start | bytes 4718600 | tf_op jit(solution)/shard_map/ppermute | solution.py:372
  821.5 18.4 %collective-permute-start.80 = (bf16[256,640]{1,0:T(8,128)(2,1)S(1)}, bf16[256,640]{1,0:T(8,128)(2,1)S(1)}, u32[]{:S(2)}, u32[]{:S(2)}) collective-permute-start(bf16[256,640]{1,0:T(8,128)(2,1)S(1)} %get-tuple-element.300), channel_id=1, source_target_pairs={{0,4},{1,5},{2,0},{3,1},{4,6},{5,7},{6,2},{7,3},{8,12},{9,13},{10,... | collective-permute-start | bytes 983048 | tf_op jit(solution)/shard_map/ppermute | solution.py:372
  828.5 21.3 %collective-permute-start.79 = (bf16[256,640]{1,0:T(8,128)(2,1)S(1)}, bf16[256,640]{1,0:T(8,128)(2,1)S(1)}, u32[]{:S(2)}, u32[]{:S(2)}) collective-permute-start(bf16[256,640]{1,0:T(8,128)(2,1)S(1)} %get-tuple-element.299), channel_id=1, source_target_pairs={{2,4},{3,5},{4,2},{5,3},{10,12},{11,13},{12,10},{13,11},{18,20},{1... | collective-permute-start | bytes 983048 | tf_op jit(solution)/shard_map/ppermute | solution.py:372
  (130 other events, 1492.1 us)
Sparse Core Ops, SparseCore 0:
  93.7 68.2 all-gather.2
  179.1 64.1 all-gather.4
  372.1 63.1 reduce-scatter.5
  438.2 64.6 reduce-scatter.7
  505.9 68.6 reduce-scatter.9
  632.8 33.0 reduce-scatter.11
  724.5 36.9 reduce-scatter.13

commit v5 on v4

--- a/solution.py
+++ b/solution.py
@@ -573,9 +573,9 @@
         return both, meanwhile
 
     (local,) = local_states(marks, keys, values)
-    states, gate_owns = scan_blocks(local, list(range(CORES)), 1, gate_owns)
-    w_output, gate_owns = tie(w_output, gate_owns)
+    w_output, gate_owns, local = tie(w_output, gate_owns, local)
     output_owns = spread(w_output)
+    states, output_owns = scan_blocks(local, list(range(CORES)), 1, output_owns)
     gate_full = gather_chips_bulk(gate_owns, 1)
     w_up, states = tie(w_up.T, states)
     up_owns = spread(w_up)
@@ -601,13 +601,16 @@
 
     gate = dot(normed_two, gate_full, 1, 1).astype(BF)
     upward = dot(normed_two, up_full, 1, 1).astype(BF)
-    downs, gate, upward = tie(downs, gate, upward)
+    hidden = jax.nn.silu(gate.astype(F32)) * upward.astype(F32)
+    hidden = hidden.astype(BF)
+    down_sum = dot(hidden, grad_out, 0, 0).astype(BF)
+    downs, gate, upward, hidden, down_sum = tie(downs, gate, upward, hidden, down_sum)
+    down_sum = sum_chips(down_sum, 1)
     down_full = place_chips(downs, 1)
     gate, upward = gate.astype(F32), upward.astype(F32)
     grad_hidden = dot(grad_out, down_full, 1, 1).astype(BF).astype(F32)
     logistic = jax.nn.sigmoid(gate)
     activated = gate * logistic
-    hidden = (activated * upward).astype(BF)
     grad_gate_f = grad_hidden * upward * logistic * (1.0 + gate * (1.0 - logistic))
     grad_up_f = grad_hidden * activated
     grad_gate_b, grad_up_b = grad_gate_f.astype(BF), grad_up_f.astype(BF)
@@ -622,8 +625,9 @@
     own = reduce_part(functools.partial(hidden_part, grads), 0)
     up_sum = sum_chips(dot(grads[1], normed_two, 0, 0).astype(BF), 1)
     gate_sum = dot(grads[0], normed_two, 0, 0).astype(BF)
-    own, gate_sum, arrived = tie(own, gate_sum, arrived)
+    own, gate_sum, arrived, down_sum = tie(own, gate_sum, arrived, down_sum)
     normed_grad = reduce_end(own, arrived)
+    down_halves = send_halves(down_sum, 1)
     gate_sum = sum_chips(gate_sum, 1)
     tokens_own = column_piece(tokens_c, rank).astype(F32)
     hidden_own = tokens_own + branch_own.astype(F32)
@@ -639,7 +643,7 @@
         return dot(grad, row_piece(output_full, r), 1, 1)
 
     totals = reduce_away(functools.partial(output_part, branch_grad))
-    totals, branch_grad, hidden, up_sum = tie(totals, branch_grad, hidden, up_sum)
+    totals, branch_grad, hidden = tie(totals, branch_grad, hidden)
     arrived = reduce_send(totals)
     own = reduce_part(functools.partial(output_part, branch_grad), 0)
 
@@ -647,16 +651,11 @@
         return dot(hidden, column_piece(down_full, r))
 
     mlp_totals, mlp_own = reduce_away(down_part), reduce_part(down_part, 0)
-    down_sum = dot(hidden, grad_out, 0, 0).astype(BF)
-    up_sum, down_sum = tie(up_sum, down_sum)
-    up_halves = send_halves(up_sum, 1)
-    arrived, own, mlp_own, mlp_totals, down_sum, gate_sum = tie(
-        arrived, own, mlp_own, mlp_totals, down_sum, gate_sum
+    arrived, own, mlp_own, mlp_totals, down_halves, up_sum = tie(
+        arrived, own, mlp_own, mlp_totals, down_halves, up_sum
     )
     mixer_grad = reduce_end(own, arrived)
     mlp_arrived = reduce_send(mlp_totals)
-    down_sum = sum_chips(down_sum, 1)
-    gate_halves = send_halves(gate_sum, 1)
     (grad_local,) = grad_states(marks, query, mixer_grad, mixer_own, denom)
     grad_local, branch_grad = tie(grad_local, branch_grad)
     output_sum = place(
@@ -664,19 +663,18 @@
         [r * piece for r, _ in mixer_parts],
         0,
     )
-    carried, (up_halves, output_sum) = scan_blocks(
-        grad_local, list(range(CORES))[::-1], -1, (up_halves, output_sum)
-    )
-    carried, mlp_arrived, down_sum, output_sum = tie(
-        carried, mlp_arrived, down_sum, output_sum
-    )
+    carried, (mlp_arrived, output_sum) = scan_blocks(
+        grad_local, list(range(CORES))[::-1], -1, (mlp_arrived, output_sum)
+    )
+    carried, output_sum, gate_sum, up_sum = tie(carried, output_sum, gate_sum, up_sum)
+    up_halves = send_halves(up_sum, 1)
     output_sum = sum_chips(output_sum, 0)
-    grad_qkv = jnp.concatenate(
-        mixer_back(
-            marks, query, keys, values, mixer_grad, mixer_own, denom, states, carried
-        ),
-        1,
-    )
+    grad_qkv = mixer_back(
+        marks, query, keys, values, mixer_grad, mixer_own, denom, states, carried
+    )
+    grad_qkv, up_halves, gate_sum = tie(grad_qkv, up_halves, gate_sum)
+    gate_halves = send_halves(gate_sum, 1)
+    grad_qkv = jnp.concatenate(grad_qkv, 1)
     inner_one = jnp.sum(grad_qkv.astype(F32) * qkv.astype(F32), axis=1)
     inner_one = sum_ranks(inner_one) / width
 
@@ -688,11 +686,10 @@
     arrived = reduce_send(totals)
     mixed_own = (hidden_own + reduce_end(mlp_own, mlp_arrived)).astype(BF)
     mixed_halves = unspread(half(mixed_own, batch), half(mixed_own, 1 - batch))
-    down_halves = send_halves(down_sum, 1)
     own = reduce_part(functools.partial(input_part, grad_qkv), 0)
     qkv_sum = dot(normed, grad_qkv, 0, 0).astype(BF)
-    arrived, own, mixed_halves, down_halves, qkv_sum, output_sum = tie(
-        arrived, own, mixed_halves, down_halves, qkv_sum, output_sum
+    arrived, own, mixed_halves, qkv_sum, output_sum = tie(
+        arrived, own, mixed_halves, qkv_sum, output_sum
     )
     input_normed = reduce_end(own, arrived)
     qkv_sum = sum_chips(qkv_sum, 0)

time: 907 us -> 872 us (0.961)
  waiting for transfers between devices: 318 us -> 288 us
  starting transfers between devices: 123 us -> 137 us
  other arithmetic: 86.7 us -> 76 us
    ppermute x83, waiting for transfers between devices: 314 us -> 288 us  [move(): return lax.ppermute(value, ('seq', 'feat'), pairs)]
    ppermute x83, starting transfers between devices: 123 us -> 137 us  [move(): return lax.ppermute(value, ('seq', 'feat'), pairs)]
    unnamed x208 -> x216, local copies, waits for them, and re-layouts: 20.8 us -> 30.4 us
  transfers between devices with their start and end apart: 90 -> 90, of which waited for: 33 -> 35; matrix products, arithmetic and copies ran while one was open for 30% -> 33% of each run, Pallas kernels for 7% -> 8%
where the time goes in v5:
time: 872 us; the launch traced here: 858 us
  waiting for transfers between devices  288 us (33%)
  matrix products  193 us (22%)
  starting transfers between devices  137 us (16%)
  Pallas kernels  78.7 us (9%)
  other arithmetic  76 us (9%)
  local copies, waits for them, and re-layouts  51.8 us (6%)
  between operations  24.2 us (3%)
    ppermute x83, waiting for transfers between devices, move(): return lax.ppermute(value, ('seq', 'feat'), pairs)  288 us
    dot_general x36, matrix products, dot(): lax.dot_general(a, b, (((ca,), (cb,)), ((), ())), preferred_element_type=...  193 us
    ppermute x83, starting transfers between devices, move(): return lax.ppermute(value, ('seq', 'feat'), pairs)  137 us
    pallas_call x4, Pallas kernels, run(): pl.pallas_call(functools.partial(kernel, heads=heads, block=block), grid_...  46.5 us
    unnamed x216, local copies, waits for them, and re-layouts  30.4 us
    pallas_call x9, Pallas kernels, place(): pl.pallas_call(functools.partial(place_kernel, axis=axis), grid_spec=pltp...  22.9 us
  transfers between devices with their start and end apart: 90, of which 35 were waited for; matrix products, arithmetic and copies ran while one was open for 33% of the time, Pallas kernels for 8%

profile of v5, /device:TPU:7, one launch (start us, length us, event | category | flops | bytes accessed | tf_op | source)
XLA Modules:
  0.0 857.7 jit_solution(1424746378156001399)
XLA Ops:
  11.5 4.1 collective-permute-start.1
  21.0 8.2 all_gather.9
  41.3 5.5 collective-permute-done.6.refs_5_
  50.2 3.6 collective-permute-done.5.refs_3_
  57.7 6.6 collective-permute-done.10
  71.1 5.3 convolution_convert_fusion.7
  77.9 4.3 shard_map.242
  98.3 5.6 collective-permute-done.15
  105.6 4.2 collective-permute-done.13
  113.5 5.6 collective-permute-start.17
  122.2 9.2 %shard_map.243 = (bf16[1536,512]{1,0:T(8,128)(2,1)S(1)}, f32[1536,512]{1,0:T(8,128)}) custom-call(s32[2,5]{1,0:T(2,128)S(1)} %pad_add_fusion.marks, bf16[1536,64]{1,0:T(8,128)(2,1)S(1)} %copy-done.25, bf16[1536,64]{1,0:T(8,128)(2,1)S(1)} %copy-done.23, bf16[1536,512]{1,0:T(8,128)(2,1)S(1)} %slice.236.v_ref, bf16[2,4,256,256]{3,2,1,0:T(8,128)(2,1)S(1)} %fusion.66.s_ref, ...), custom_call_target="tpu_custom_call" | custom-call | flops 6144000000 | bytes 9216000 | tf_op jit(solution)/shard_map/pallas_call | solution.py:220
  131.5 18.6 %collective-permute-done.17 = bf16[1376,256]{1,0:T(8,128)(2,1)S(1)} collective-permute-done((bf16[1376,256]{1,0:T(8,128)(2,1)S(1)}, bf16[1376,256]{1,0:T(8,128)(2,1)S(1)}, u32[]{:S(2)}, u32[]{:S(2)}) %collective-permute-start.17) | collective-permute-done | bytes 704544 | tf_op jit(solution)/shard_map/ppermute | solution.py:372
  151.0 3.4 collective-permute-start.20
  162.4 5.7 collective-permute-done.23.refs_6_
  170.1 4.0 dynamic-slice_bitcast_fusion.refs_0_
  183.1 13.6 %collective-permute-done.26 = bf16[1536,512]{1,0:T(8,128)(2,1)} collective-permute-done((bf16[1536,512]{1,0:T(8,128)(2,1)S(1)}, bf16[1536,512]{1,0:T(8,128)(2,1)}, u32[]{:S(2)}, u32[]{:S(2)}) %collective-permute-start.26) | collective-permute-done | bytes 1572896 | tf_op jit(solution)/shard_map/ppermute | solution.py:372
  210.2 31.8 %collective-permute-done.31.refs_2_ = bf16[1536,512]{1,0:T(8,128)(2,1)} collective-permute-done((bf16[1536,512]{1,0:T(8,128)(2,1)S(1)}, bf16[1536,512]{1,0:T(8,128)(2,1)}, u32[]{:S(2)}, u32[]{:S(2)}) %collective-permute-start.31) | collective-permute-done | bytes 1572896 | tf_op jit(solution)/shard_map/ppermute | solution.py:372
  242.1 4.1 shard_map.241
  252.0 3.4 collective-permute-start.34
  263.5 4.1 multiply_convert_fusion
  270.3 12.3 %convolution_convert_fusion.5 = bf16[1536,1376]{0,1:T(8,128)(2,1)} fusion(bf16[1536,2048]{1,0:T(8,128)(2,1)S(1)} %multiply_convert_fusion, bf16[1376,2048]{1,0:T(8,128)(2,1)} %all-gather.3.cloned.1.call-done), kind=kOutput, calls=%fused_computation.37 | convolution fusion | flops 8659156992 | bytes 16154624 | tf_op jit(solution)/shard_map/dot_general | solution.py:262
  282.6 25.4 %fusion.15 = (bf16[1536,1376]{0,1:T(8,128)(2,1)S(1)}, bf16[1536,1376]{0,1:T(8,128)(2,1)}) fusion(bf16[1536,1376]{0,1:T(8,128)(2,1)} %convolution_convert_fusion.5, bf16[1536,2048]{1,0:T(8,128)(2,1)} %copy-done.52, bf16[1376,2048]{1,0:T(8,128)(2,1)} %all-gather.5.cloned.1.call-done), kind=kOutput, calls=%fused_computation.31 | convolution fusion | flops 8676065280 | bytes 24608768 | tf_op jit(solution)/shard_map/dot_general | solution.py:262
  310.1 12.6 %convolution_convert_fusion.2 = bf16[1376,2048]{1,0:T(8,128)(2,1)} fusion(bf16[1536,1376]{0,1:T(8,128)(2,1)S(1)} %get-tuple-element.175, bf16[1536,2048]{1,0:T(8,128)(2,1)} %copy-done.5), kind=kOutput, calls=%fused_computation.34 | convolution fusion | flops 8659861504 | bytes 16154624 | tf_op jit(solution)/shard_map/dot_general | solution.py:262
  324.4 3.9 shard_map.248
  328.3 13.2 %convolution_convert_fusion.3 = bf16[1536,1376]{0,1:T(8,128)(2,1)S(1)} fusion(bf16[1536,2048]{1,0:T(8,128)(2,1)} %copy-done.5, bf16[1376,2048]{1,0:T(8,128)(2,1)S(1)} %shard_map.248), kind=kOutput, calls=%fused_computation.35 | convolution fusion | flops 8659156992 | bytes 16154624 | tf_op jit(solution)/shard_map/dot_general | solution.py:262
  341.6 6.3 fusion.64
  347.9 5.2 fusion.58
  362.2 4.0 fusion.61
  366.3 4.1 fusion.29
  370.3 10.6 %convolution_convert_fusion = bf16[1376,2048]{1,0:T(8,128)(2,1)} fusion(bf16[1536,1376]{0,1:T(8,128)(2,1)S(1)} %get-tuple-element.166, bf16[1536,2048]{1,0:T(8,128)(2,1)S(1)} %bitcast.131), kind=kOutput, calls=%fused_computation.32 | convolution fusion | flops 8659861504 | bytes 16154624 | tf_op jit(solution)/shard_map/dot_general | solution.py:262
  381.2 5.5 fusion.52
  386.7 6.8 fusion.28
  393.5 10.6 %convolution_convert_fusion.1 = bf16[1376,2048]{1,0:T(8,128)(2,1)} fusion(bf16[1536,1376]{0,1:T(8,128)(2,1)S(1)} %bitcast.135, bf16[1536,2048]{1,0:T(8,128)(2,1)S(1)} %bitcast.133), kind=kOutput, calls=%fused_computation.33 | convolution fusion | flops 8659861504 | bytes 16154624 | tf_op jit(solution)/shard_map/dot_general | solution.py:262
  404.1 4.8 fusion.55
  408.9 8.0 fusion.20
  418.6 5.5 fusion.132
  424.1 3.6 convolution_convert_fusion.9
  432.2 3.9 fusion.31
  436.1 5.4 convolution_convert_fusion.13
  442.6 4.4 collective-permute-start.49
  451.3 25.0 %collective-permute-done.49 = bf16[1376,256]{1,0:T(8,128)(2,1)S(1)} collective-permute-done((bf16[1376,256]{1,0:T(8,128)(2,1)S(1)}, bf16[1376,256]{1,0:T(8,128)(2,1)S(1)}, u32[]{:S(2)}, u32[]{:S(2)}) %collective-permute-start.49) | collective-permute-done | bytes 704544 | tf_op jit(solution)/shard_map/ppermute | solution.py:372
  477.3 4.4 convert_add_fusion.4
  484.5 4.0 add_convert_fusion.1
  488.6 15.0 %collective-permute-done.45 = bf16[1536,512]{1,0:T(8,128)(2,1)} collective-permute-done((bf16[1536,512]{1,0:T(8,128)(2,1)}, bf16[1536,512]{1,0:T(8,128)(2,1)}, u32[]{:S(2)}, u32[]{:S(2)}) %collective-permute-start.45) | collective-permute-done | bytes 1572896 | tf_op jit(solution)/shard_map/ppermute | solution.py:372
  503.6 4.8 convert_add_fusion.3.do_ref
  508.4 6.6 shard_map.249
  519.7 6.2 collective-permute-start.53
  562.4 26.3 %shard_map.251 = (bf16[1536,64]{1,0:T(8,128)(2,1)S(1)}, bf16[1536,64]{1,0:T(8,128)(2,1)S(1)}, bf16[1536,512]{1,0:T(8,128)(2,1)S(1)}) custom-call(s32[2,5]{1,0:T(2,128)S(1)} %copy-done.35, bf16[1536,64]{1,0:T(8,128)(2,1)S(1)} %copy-done.27, bf16[1536,64]{1,0:T(8,128)(2,1)S(1)} %copy-done.24, bf16[1536,512]{1,0:T(8,128)(2,1)} %copy-done.15, ...), custom_call_target="tpu_custom_call" | custom-call | flops 15360000000 | bytes 9216000 | tf_op jit(solution)/shard_map/pallas_call | solution.py:220
  594.3 4.8 collective-permute-start.60
  606.8 24.6 %collective-permute-done.60 = bf16[1376,256]{1,0:T(8,128)(2,1)S(1)} collective-permute-done((bf16[1376,256]{1,0:T(8,128)(2,1)S(1)}, bf16[1376,256]{1,0:T(8,128)(2,1)S(1)}, u32[]{:S(2)}, u32[]{:S(2)}) %collective-permute-start.60) | collective-permute-done | bytes 704544 | tf_op jit(solution)/shard_map/ppermute | solution.py:372
  637.6 13.1 %collective-permute-start.63 = (bf16[1536,512]{1,0:T(8,128)(2,1)}, bf16[1536,512]{1,0:T(8,128)(2,1)}, u32[]{:S(2)}, u32[]{:S(2)}) collective-permute-start(bf16[1536,512]{1,0:T(8,128)(2,1)} %convolution_convert_fusion.10), channel_id=1, source_target_pairs={{0,4},{1,5},{2,6},{3,7},{4,0},{5,1},{6,2},{7,3},{8,12},{9,13},{10,... | collective-permute-start | bytes 4718600 | tf_op jit(solution)/shard_map/ppermute | solution.py:372
  654.4 7.0 convolution_convert_fusion.6
  661.4 5.3 convolution_add_fusion
  667.8 29.0 %collective-permute-done.62 = bf16[1536,512]{1,0:T(8,128)(2,1)S(1)} collective-permute-done((bf16[1536,512]{1,0:T(8,128)(2,1)}, bf16[1536,512]{1,0:T(8,128)(2,1)S(1)}, u32[]{:S(2)}, u32[]{:S(2)}) %collective-permute-start.62) | collective-permute-done | bytes 1572896 | tf_op jit(solution)/shard_map/ppermute | solution.py:372
  697.9 6.3 fusion.25
  713.8 4.1 collective-permute-start.70
  720.7 28.2 %collective-permute-done.71.refs_4_ = bf16[2,768,512]{2,1,0:T(8,128)(2,1)S(1)} collective-permute-done((bf16[2,768,512]{2,1,0:T(8,128)(2,1)S(1)}, bf16[2,768,512]{2,1,0:T(8,128)(2,1)S(1)}, u32[]{:S(2)}, u32[]{:S(2)}) %collective-permute-start.71) | collective-permute-done | bytes 1572896 | tf_op jit(solution)/shard_map/ppermute | solution.py:372
  760.1 7.3 collective-permute-start.82
  767.3 22.7 %collective-permute-done.74.refs_5_ = bf16[2,768,512]{2,1,0:T(8,128)(2,1)} collective-permute-done((bf16[2,768,512]{2,1,0:T(8,128)(2,1)}, bf16[2,768,512]{2,1,0:T(8,128)(2,1)}, u32[]{:S(2)}, u32[]{:S(2)}) %collective-permute-start.74) | collective-permute-done | bytes 1572896 | tf_op jit(solution)/shard_map/ppermute | solution.py:372
  794.4 10.0 %collective-permute-start.81 = (bf16[256,512]{1,0:T(8,128)(2,1)S(1)}, bf16[256,512]{1,0:T(8,128)(2,1)S(1)}, u32[]{:S(2)}, u32[]{:S(2)}) collective-permute-start(bf16[256,512]{1,0:T(8,128)(2,1)S(1)} %get-tuple-element.310), channel_id=1, source_target_pairs={{2,4},{3,5},{4,2},{5,3},{10,12},{11,13},{12,10},{13,11},{18,20},{1... | collective-permute-start | bytes 786440 | tf_op jit(solution)/shard_map/ppermute | solution.py:372
  809.3 8.5 collective-permute-done.81
  818.7 6.1 collective-permute-done.79
  829.2 11.5 %collective-permute-done.77.refs_6_ = bf16[2,768,512]{2,1,0:T(8,128)(2,1)} collective-permute-done((bf16[2,768,512]{2,1,0:T(8,128)(2,1)}, bf16[2,768,512]{2,1,0:T(8,128)(2,1)}, u32[]{:S(2)}, u32[]{:S(2)}) %collective-permute-start.77) | collective-permute-done | bytes 1572896 | tf_op jit(solution)/shard_map/ppermute | solution.py:372
  841.2 9.4 %shard_map.252 = f32[2,768,2048]{2,1,0:T(8,128)} custom-call(s32[2]{0:T(128)S(1)} %pad_add_fusion.5.where, bf16[2,768,512]{2,1,0:T(8,128)(2,1)S(1)} %pad_maximum_fusion.1.refs_0_, bf16[2,768,512]{2,1,0:T(8,128)(2,1)S(1)} %collective-permute-done.70.refs_1_, bf16[2,768,512]{2,1,0:T(8,128)(2,1)} %collective-permute-done.73.refs_2_, ...), custom_call_target="tpu_custom_call" | custom-call | tf_op jit(solution)/shard_map/pallas_call | solution.py:321
  (533 shorter events, 236.4 us)
Async XLA Ops:
  7.2 234.8 %all-gather.3.cloned.1.call-start = ((), (), s32[]{:S(2)}) async-start(), calls=%async_computation.5 | async-start | bytes 7045120 | tf_op jit(solution)/shard_map/all_gather | solution.py:433
  10.8 19.6 %collective-permute-start.2 = (bf16[256,640]{1,0:T(8,128)(2,1)}, bf16[256,640]{1,0:T(8,128)(2,1)}, u32[]{:S(2)}, u32[]{:S(2)}) collective-permute-start(bf16[256,640]{1,0:T(8,128)(2,1)} %pad_maximum_fusion.2), channel_id=1, source_target_pairs={{0,2},{1,3},{2,6},{3,7},{4,0},{5,1},{6,4},{7,5},{8,10},{9,11},{10,... | collective-permute-start | bytes 983048 | tf_op jit(solution)/shard_map/ppermute | solution.py:372
  11.5 17.7 %collective-permute-start.1 = (bf16[256,640]{1,0:T(8,128)(2,1)}, bf16[256,640]{1,0:T(8,128)(2,1)}, u32[]{:S(2)}, u32[]{:S(2)}) collective-permute-start(bf16[256,640]{1,0:T(8,128)(2,1)} %pad_maximum_fusion.2), channel_id=1, source_target_pairs={{2,4},{3,5},{4,2},{5,3},{10,12},{11,13},{12,10},{13,11},{18,20},{1... | collective-permute-start | bytes 983048 | tf_op jit(solution)/shard_map/ppermute | solution.py:372
  17.8 47.8 %collective-permute-start = (bf16[768,2048]{1,0:T(8,128)(2,1)S(1)}, bf16[768,2048]{1,0:T(8,128)(2,1)}, u32[]{:S(2)}, u32[]{:S(2)}) collective-permute-start(bf16[768,2048]{1,0:T(8,128)(2,1)S(1)} %dynamic-slice_bitcast_fusion.1.refs_0_), channel_id=1, source_target_pairs={{0,4},{1,5},{2,6},{3,7},{4,0},{5,1},{6,2},{7,3},{8,12},{9,13},{10,... | collective-permute-start | bytes 9437192 | tf_op jit(solution)/shard_map/ppermute | solution.py:372
  31.9 14.9 %collective-permute-start.6 = (bf16[256,640]{1,0:T(8,128)(2,1)}, bf16[256,640]{1,0:T(8,128)(2,1)}, u32[]{:S(2)}, u32[]{:S(2)}) collective-permute-start(bf16[256,640]{1,0:T(8,128)(2,1)} %collective-permute-done.2.refs_4_), channel_id=1, source_target_pairs={{0,16},{1,17},{2,18},{3,19},{4,20},{5,21},{6,22},{7,23},{8,24},{9,... | collective-permute-start | bytes 983048 | tf_op jit(solution)/shard_map/ppermute | solution.py:372
  33.2 31.2 %collective-permute-start.10 = (bf16[1376,256]{1,0:T(8,128)(2,1)}, bf16[1376,256]{1,0:T(8,128)(2,1)}, u32[]{:S(2)}, u32[]{:S(2)}) collective-permute-start(bf16[1376,256]{1,0:T(8,128)(2,1)} %bitcast.144), channel_id=1, source_target_pairs={{2,4},{3,5},{4,2},{5,3},{10,12},{11,13},{12,10},{13,11},{18,20},{1... | collective-permute-start | bytes 2113544 | tf_op jit(solution)/shard_map/ppermute | solution.py:372
  48.1 34.1 %collective-permute-start.11 = (bf16[1376,256]{1,0:T(8,128)(2,1)}, bf16[1376,256]{1,0:T(8,128)(2,1)S(1)}, u32[]{:S(2)}, u32[]{:S(2)}) collective-permute-start(bf16[1376,256]{1,0:T(8,128)(2,1)} %bitcast.145), channel_id=1, source_target_pairs={{0,2},{1,3},{2,6},{3,7},{4,0},{5,1},{6,4},{7,5},{8,10},{9,11},{10,... | collective-permute-start | bytes 2113544 | tf_op jit(solution)/shard_map/ppermute | solution.py:372
  84.0 198.7 %all-gather.5.cloned.1.call-start = ((), (), s32[]{:S(2)}) async-start(), calls=%async_computation.6 | async-start | bytes 7045120 | tf_op jit(solution)/shard_map/all_gather | solution.py:433
  90.0 13.9 %collective-permute-start.15 = (bf16[256,512]{1,0:T(8,128)(2,1)}, bf16[256,512]{1,0:T(8,128)(2,1)}, u32[]{:S(2)}, u32[]{:S(2)}) collective-permute-start(bf16[256,512]{1,0:T(8,128)(2,1)} %param.22), channel_id=1, source_target_pairs={{2,4},{3,5},{4,2},{5,3},{10,12},{11,13},{12,10},{13,11},{18,20},{1... | collective-permute-start | bytes 786440 | tf_op jit(solution)/shard_map/ppermute | solution.py:372
  93.5 16.3 %collective-permute-start.16 = (bf16[256,512]{1,0:T(8,128)(2,1)}, bf16[256,512]{1,0:T(8,128)(2,1)}, u32[]{:S(2)}, u32[]{:S(2)}) collective-permute-start(bf16[256,512]{1,0:T(8,128)(2,1)} %param.22), channel_id=1, source_target_pairs={{0,2},{1,3},{2,6},{3,7},{4,0},{5,1},{6,4},{7,5},{8,10},{9,11},{10,... | collective-permute-start | bytes 786440 | tf_op jit(solution)/shard_map/ppermute | solution.py:372
  95.4 14.3 %collective-permute-start.13 = (bf16[648,128]{1,0:T(8,128)(2,1)S(1)}, bf16[648,128]{1,0:T(8,128)(2,1)S(1)}, u32[]{:S(2)}, u32[]{:S(2)}) collective-permute-start(bf16[648,128]{1,0:T(8,128)(2,1)S(1)} %pad_maximum_fusion.3), channel_id=1, source_target_pairs={{0,16},{1,17},{2,18},{3,19},{4,20},{5,21},{6,22},{7,23},{8,24},{9,... | collective-permute-start | bytes 497672 | tf_op jit(solution)/shard_map/ppermute | solution.py:372
  96.7 13.0 %collective-permute-start.12 = (bf16[648,128]{1,0:T(8,128)(2,1)S(1)}, bf16[648,128]{1,0:T(8,128)(2,1)S(1)}, u32[]{:S(2)}, u32[]{:S(2)}) collective-permute-start(bf16[648,128]{1,0:T(8,128)(2,1)S(1)} %pad_maximum_fusion.3), channel_id=1, source_target_pairs={{0,8},{1,9},{2,10},{3,11},{4,12},{5,13},{6,14},{7,15},{8,16},{9,17... | collective-permute-start | bytes 497672 | tf_op jit(solution)/shard_map/ppermute | solution.py:372
  113.5 36.6 %collective-permute-start.17 = (bf16[1376,256]{1,0:T(8,128)(2,1)S(1)}, bf16[1376,256]{1,0:T(8,128)(2,1)S(1)}, u32[]{:S(2)}, u32[]{:S(2)}) collective-permute-start(bf16[1376,256]{1,0:T(8,128)(2,1)S(1)} %bitcast.147), channel_id=1, source_target_pairs={{2,4},{3,5},{4,2},{5,3},{10,12},{11,13},{12,10},{13,11},{18,20},{1... | collective-permute-start | bytes 2113544 | tf_op jit(solution)/shard_map/ppermute | solution.py:372
  119.2 31.0 %collective-permute-start.18 = (bf16[1376,256]{1,0:T(8,128)(2,1)S(1)}, bf16[1376,256]{1,0:T(8,128)(2,1)S(1)}, u32[]{:S(2)}, u32[]{:S(2)}) collective-permute-start(bf16[1376,256]{1,0:T(8,128)(2,1)S(1)} %bitcast.148), channel_id=1, source_target_pairs={{0,2},{1,3},{2,6},{3,7},{4,0},{5,1},{6,4},{7,5},{8,10},{9,11},{10,... | collective-permute-start | bytes 2113544 | tf_op jit(solution)/shard_map/ppermute | solution.py:372
  151.0 45.6 %collective-permute-start.26 = (bf16[1536,512]{1,0:T(8,128)(2,1)S(1)}, bf16[1536,512]{1,0:T(8,128)(2,1)}, u32[]{:S(2)}, u32[]{:S(2)}) collective-permute-start(bf16[1536,512]{1,0:T(8,128)(2,1)S(1)} %get-tuple-element.142.o_ref), channel_id=1, source_target_pairs={{0,1},{1,0},{2,3},{3,2},{4,5},{5,4},{6,7},{7,6},{8,9},{9,8},{10,11... | collective-permute-start | bytes 4718600 | tf_op jit(solution)/shard_map/ppermute | solution.py:372
  154.4 44.3 %collective-permute-start.28 = (bf16[1376,256]{1,0:T(8,128)(2,1)}, bf16[1376,256]{1,0:T(8,128)(2,1)}, u32[]{:S(2)}, u32[]{:S(2)}) collective-permute-start(bf16[1376,256]{1,0:T(8,128)(2,1)} %param.25), channel_id=1, source_target_pairs={{2,4},{3,5},{4,2},{5,3},{10,12},{11,13},{12,10},{13,11},{18,20},{1... | collective-permute-start | bytes 2113544 | tf_op jit(solution)/shard_map/ppermute | solution.py:372
  157.7 44.7 %collective-permute-start.25 = (bf16[1536,512]{1,0:T(8,128)(2,1)S(1)}, bf16[1536,512]{1,0:T(8,128)(2,1)}, u32[]{:S(2)}, u32[]{:S(2)}) collective-permute-start(bf16[1536,512]{1,0:T(8,128)(2,1)S(1)} %get-tuple-element.142.o_ref), channel_id=1, source_target_pairs={{0,4},{1,5},{2,6},{3,7},{4,0},{5,1},{6,2},{7,3},{8,12},{9,13},{10,... | collective-permute-start | bytes 4718600 | tf_op jit(solution)/shard_map/ppermute | solution.py:372
  175.8 241.7 %reduce-scatter.6.cloned.1.call-start = ((), (), s32[]{:S(2)}) async-start(), calls=%async_computation.7 | async-start | bytes 7045120 | tf_op jit(solution)/shard_map/reduce_scatter | solution.py:438
  176.9 65.2 %collective-permute-start.9 = (bf16[768,2048]{1,0:T(8,128)(2,1)}, bf16[768,2048]{1,0:T(8,128)(2,1)}, u32[]{:S(2)}, u32[]{:S(2)}) collective-permute-start(bf16[768,2048]{1,0:T(8,128)(2,1)} %dynamic-slice_bitcast_fusion.refs_0_), channel_id=1, source_target_pairs={{0,4},{1,5},{2,6},{3,7},{4,0},{5,1},{6,2},{7,3},{8,12},{9,13},{10,... | collective-permute-start | bytes 9437192 | tf_op jit(solution)/shard_map/ppermute | solution.py:372
  178.1 28.8 %collective-permute-start.29 = (bf16[1376,256]{1,0:T(8,128)(2,1)}, bf16[1376,256]{1,0:T(8,128)(2,1)S(1)}, u32[]{:S(2)}, u32[]{:S(2)}) collective-permute-start(bf16[1376,256]{1,0:T(8,128)(2,1)} %param.25), channel_id=1, source_target_pairs={{0,2},{1,3},{2,6},{3,7},{4,0},{5,1},{6,4},{7,5},{8,10},{9,11},{10,... | collective-permute-start | bytes 2113544 | tf_op jit(solution)/shard_map/ppermute | solution.py:372
  206.9 35.1 %collective-permute-start.31 = (bf16[1536,512]{1,0:T(8,128)(2,1)S(1)}, bf16[1536,512]{1,0:T(8,128)(2,1)}, u32[]{:S(2)}, u32[]{:S(2)}) collective-permute-start(bf16[1536,512]{1,0:T(8,128)(2,1)S(1)} %fusion.30.refs_0_), channel_id=1, source_target_pairs={{0,1},{1,0},{2,3},{3,2},{4,5},{5,4},{6,7},{7,6},{8,9},{9,8},{10,11... | collective-permute-start | bytes 4718600 | tf_op jit(solution)/shard_map/ppermute | solution.py:372
  210.2 46.3 %collective-permute-start.30 = (bf16[1536,512]{1,0:T(8,128)(2,1)S(1)}, bf16[1536,512]{1,0:T(8,128)(2,1)}, u32[]{:S(2)}, u32[]{:S(2)}) collective-permute-start(bf16[1536,512]{1,0:T(8,128)(2,1)S(1)} %fusion.30.refs_0_), channel_id=1, source_target_pairs={{0,4},{1,5},{2,6},{3,7},{4,0},{5,1},{6,2},{7,3},{8,12},{9,13},{10,... | collective-permute-start | bytes 4718600 | tf_op jit(solution)/shard_map/ppermute | solution.py:372
  242.0 15.7 %collective-permute-start.32 = (bf16[1536,512]{1,0:T(8,128)(2,1)}, bf16[1536,512]{1,0:T(8,128)(2,1)S(1)}, u32[]{:S(2)}, u32[]{:S(2)}) collective-permute-start(bf16[1536,512]{1,0:T(8,128)(2,1)} %collective-permute-done.31.refs_2_), channel_id=1, source_target_pairs={{0,4},{1,5},{2,6},{3,7},{4,0},{5,1},{6,2},{7,3},{8,12},{9,13},{10,... | collective-permute-start | bytes 4718600 | tf_op jit(solution)/shard_map/ppermute | solution.py:372
  248.9 59.1 %collective-permute-start.35 = (bf16[1376,256]{1,0:T(8,128)(2,1)S(1)}, bf16[1376,256]{1,0:T(8,128)(2,1)}, u32[]{:S(2)}, u32[]{:S(2)}) collective-permute-start(bf16[1376,256]{1,0:T(8,128)(2,1)S(1)} %broadcast_select_fusion.4.refs_0_), channel_id=1, source_target_pairs={{0,24},{1,25},{2,26},{3,27},{4,28},{5,29},{6,30},{7,31},{8,16},{9,... | collective-permute-start | bytes 2113544 | tf_op jit(solution)/shard_map/ppermute | solution.py:372
  252.0 70.7 %collective-permute-start.34 = (bf16[1376,256]{1,0:T(8,128)(2,1)S(1)}, bf16[1376,256]{1,0:T(8,128)(2,1)}, u32[]{:S(2)}, u32[]{:S(2)}) collective-permute-start(bf16[1376,256]{1,0:T(8,128)(2,1)S(1)} %broadcast_select_fusion.4.refs_0_), channel_id=1, source_target_pairs={{0,16},{1,17},{2,18},{3,19},{4,20},{5,21},{6,22},{7,23},{8,24},{9,... | collective-permute-start | bytes 2113544 | tf_op jit(solution)/shard_map/ppermute | solution.py:372
  255.3 67.3 %collective-permute-start.33 = (bf16[1376,256]{1,0:T(8,128)(2,1)S(1)}, bf16[1376,256]{1,0:T(8,128)(2,1)}, u32[]{:S(2)}, u32[]{:S(2)}) collective-permute-start(bf16[1376,256]{1,0:T(8,128)(2,1)S(1)} %broadcast_select_fusion.4.refs_0_), channel_id=1, source_target_pairs={{0,8},{1,9},{2,10},{3,11},{4,12},{5,13},{6,14},{7,15},{8,0},{9,1},... | collective-permute-start | bytes 2113544 | tf_op jit(solution)/shard_map/ppermute | solution.py:372
  256.5 66.1 %collective-permute-start.38 = (bf16[1376,256]{1,0:T(8,128)(2,1)S(1)}, bf16[1376,256]{1,0:T(8,128)(2,1)}, u32[]{:S(2)}, u32[]{:S(2)}) collective-permute-start(bf16[1376,256]{1,0:T(8,128)(2,1)S(1)} %collective-permute-done.29.refs_4_), channel_id=1, source_target_pairs={{0,24},{1,25},{2,26},{3,27},{4,28},{5,29},{6,30},{7,31},{8,16},{9,... | collective-permute-start | bytes 2113544 | tf_op jit(solution)/shard_map/ppermute | solution.py:372
  257.7 64.9 %collective-permute-start.37 = (bf16[1376,256]{1,0:T(8,128)(2,1)S(1)}, bf16[1376,256]{1,0:T(8,128)(2,1)}, u32[]{:S(2)}, u32[]{:S(2)}) collective-permute-start(bf16[1376,256]{1,0:T(8,128)(2,1)S(1)} %collective-permute-done.29.refs_4_), channel_id=1, source_target_pairs={{0,16},{1,17},{2,18},{3,19},{4,20},{5,21},{6,22},{7,23},{8,24},{9,... | collective-permute-start | bytes 2113544 | tf_op jit(solution)/shard_map/ppermute | solution.py:372
  308.0 16.2 %collective-permute-start.36 = (bf16[1376,256]{1,0:T(8,128)(2,1)S(1)}, bf16[1376,256]{1,0:T(8,128)(2,1)}, u32[]{:S(2)}, u32[]{:S(2)}) collective-permute-start(bf16[1376,256]{1,0:T(8,128)(2,1)S(1)} %collective-permute-done.29.refs_4_), channel_id=1, source_target_pairs={{0,8},{1,9},{2,10},{3,11},{4,12},{5,13},{6,14},{7,15},{8,0},{9,1},... | collective-permute-start | bytes 2113544 | tf_op jit(solution)/shard_map/ppermute | solution.py:372
  324.2 164.3 %reduce-scatter.8.cloned.1.call-start = ((), (), s32[]{:S(2)}) async-start(), calls=%async_computation.8 | async-start | bytes 7045120 | tf_op jit(solution)/shard_map/reduce_scatter | solution.py:438
  381.0 171.6 %reduce-scatter.10.cloned.1.call-start = ((), (), s32[]{:S(2)}) async-start(), calls=%async_computation.9 | async-start | bytes 7045120 | tf_op jit(solution)/shard_map/reduce_scatter | solution.py:438
  381.1 36.4 %collective-permute-start.43 = (bf16[1536,512]{1,0:T(8,128)(2,1)}, bf16[1536,512]{1,0:T(8,128)(2,1)S(1)}, u32[]{:S(2)}, u32[]{:S(2)}) collective-permute-start(bf16[1536,512]{1,0:T(8,128)(2,1)} %fusion.29), channel_id=1, source_target_pairs={{0,1},{1,0},{2,3},{3,2},{4,5},{5,4},{6,7},{7,6},{8,9},{9,8},{10,11... | collective-permute-start | bytes 4718600 | tf_op jit(solution)/shard_map/ppermute | solution.py:372
  393.5 15.5 %collective-permute-start.42 = (bf16[1536,512]{1,0:T(8,128)(2,1)}, bf16[1536,512]{1,0:T(8,128)(2,1)}, u32[]{:S(2)}, u32[]{:S(2)}) collective-permute-start(bf16[1536,512]{1,0:T(8,128)(2,1)} %fusion.28), channel_id=1, source_target_pairs={{0,4},{1,5},{2,6},{3,7},{4,0},{5,1},{6,2},{7,3},{8,12},{9,13},{10,... | collective-permute-start | bytes 4718600 | tf_op jit(solution)/shard_map/ppermute | solution.py:372
  417.5 279.2 %reduce-scatter.12.cloned.1.call-start = ((), (), s32[]{:S(2)}) async-start(), calls=%async_computation.10 | async-start | bytes 2621440 | tf_op jit(solution)/shard_map/reduce_scatter | solution.py:438
  441.5 35.8 %collective-permute-start.47 = (bf16[1536,512]{1,0:T(8,128)(2,1)S(1)}, bf16[1536,512]{1,0:T(8,128)(2,1)S(1)}, u32[]{:S(2)}, u32[]{:S(2)}) collective-permute-start(bf16[1536,512]{1,0:T(8,128)(2,1)S(1)} %convolution_convert_fusion.13), channel_id=1, source_target_pairs={{0,4},{1,5},{2,6},{3,7},{4,0},{5,1},{6,2},{7,3},{8,12},{9,13},{10,... | collective-permute-start | bytes 4718600 | tf_op jit(solution)/shard_map/ppermute | solution.py:372
  441.8 46.7 %collective-permute-start.50 = (bf16[1376,256]{1,0:T(8,128)(2,1)S(1)}, bf16[1376,256]{1,0:T(8,128)(2,1)}, u32[]{:S(2)}, u32[]{:S(2)}) collective-permute-start(bf16[1376,256]{1,0:T(8,128)(2,1)S(1)} %get-tuple-element.304), channel_id=1, source_target_pairs={{0,4},{1,5},{2,0},{3,1},{4,6},{5,7},{6,2},{7,3},{8,12},{9,13},{10,... | collective-permute-start | bytes 2113544 | tf_op jit(solution)/shard_map/ppermute | solution.py:372
  442.6 33.8 %collective-permute-start.49 = (bf16[1376,256]{1,0:T(8,128)(2,1)S(1)}, bf16[1376,256]{1,0:T(8,128)(2,1)S(1)}, u32[]{:S(2)}, u32[]{:S(2)}) collective-permute-start(bf16[1376,256]{1,0:T(8,128)(2,1)S(1)} %get-tuple-element.305), channel_id=1, source_target_pairs={{2,4},{3,5},{4,2},{5,3},{10,12},{11,13},{12,10},{13,11},{18,20},{1... | collective-permute-start | bytes 2113544 | tf_op jit(solution)/shard_map/ppermute | solution.py:372
  448.0 33.7 %collective-permute-start.46 = (bf16[1536,512]{1,0:T(8,128)(2,1)S(1)}, bf16[1536,512]{1,0:T(8,128)(2,1)S(1)}, u32[]{:S(2)}, u32[]{:S(2)}) collective-permute-start(bf16[1536,512]{1,0:T(8,128)(2,1)S(1)} %convolution_convert_fusion.8), channel_id=1, source_target_pairs={{0,4},{1,5},{2,6},{3,7},{4,0},{5,1},{6,2},{7,3},{8,12},{9,13},{10,... | collective-permute-start | bytes 4718600 | tf_op jit(solution)/shard_map/ppermute | solution.py:372
  450.8 33.7 %collective-permute-start.48 = (bf16[1536,512]{1,0:T(8,128)(2,1)S(1)}, bf16[1536,512]{1,0:T(8,128)(2,1)S(1)}, u32[]{:S(2)}, u32[]{:S(2)}) collective-permute-start(bf16[1536,512]{1,0:T(8,128)(2,1)S(1)} %convolution_convert_fusion.12), channel_id=1, source_target_pairs={{0,4},{1,5},{2,6},{3,7},{4,0},{5,1},{6,2},{7,3},{8,12},{9,13},{10,... | collective-permute-start | bytes 4718600 | tf_op jit(solution)/shard_map/ppermute | solution.py:372
  477.3 26.3 %collective-permute-start.45 = (bf16[1536,512]{1,0:T(8,128)(2,1)}, bf16[1536,512]{1,0:T(8,128)(2,1)}, u32[]{:S(2)}, u32[]{:S(2)}) collective-permute-start(bf16[1536,512]{1,0:T(8,128)(2,1)} %fusion.31), channel_id=1, source_target_pairs={{0,1},{1,0},{2,3},{3,2},{4,5},{5,4},{6,7},{7,6},{8,9},{9,8},{10,11... | collective-permute-start | bytes 4718600 | tf_op jit(solution)/shard_map/ppermute | solution.py:372
  516.9 27.3 %collective-permute-start.54 = (bf16[1536,512]{1,0:T(8,128)(2,1)}, bf16[1536,512]{1,0:T(8,128)(2,1)}, u32[]{:S(2)}, u32[]{:S(2)}) collective-permute-start(bf16[1536,512]{1,0:T(8,128)(2,1)} %add_convert_fusion.1), channel_id=1, source_target_pairs={{0,1},{1,0},{2,3},{3,2},{4,5},{5,4},{6,7},{7,6},{8,9},{9,8},{10,11... | collective-permute-start | bytes 4718600 | tf_op jit(solution)/shard_map/ppermute | solution.py:372
  519.7 21.7 %collective-permute-start.53 = (bf16[648,128]{1,0:T(8,128)(2,1)}, bf16[648,128]{1,0:T(8,128)(2,1)}, u32[]{:S(2)}, u32[]{:S(2)}) collective-permute-start(bf16[648,128]{1,0:T(8,128)(2,1)} %pad_maximum_fusion.4), channel_id=1, source_target_pairs={{24,0},{25,1},{26,2},{27,3},{28,4},{29,5},{30,6},{31,7}} | collective-permute-start | bytes 497672 | tf_op jit(solution)/shard_map/ppermute | solution.py:372
  525.9 15.5 %collective-permute-start.52 = (bf16[648,128]{1,0:T(8,128)(2,1)}, bf16[648,128]{1,0:T(8,128)(2,1)}, u32[]{:S(2)}, u32[]{:S(2)}) collective-permute-start(bf16[648,128]{1,0:T(8,128)(2,1)} %pad_maximum_fusion.4), channel_id=1, source_target_pairs={{16,0},{17,1},{18,2},{19,3},{20,4},{21,5},{22,6},{23,7},{24,8},{25... | collective-permute-start | bytes 497672 | tf_op jit(solution)/shard_map/ppermute | solution.py:372
  527.8 13.6 %collective-permute-start.51 = (bf16[648,128]{1,0:T(8,128)(2,1)}, bf16[648,128]{1,0:T(8,128)(2,1)}, u32[]{:S(2)}, u32[]{:S(2)}) collective-permute-start(bf16[648,128]{1,0:T(8,128)(2,1)} %pad_maximum_fusion.4), channel_id=1, source_target_pairs={{8,0},{9,1},{10,2},{11,3},{12,4},{13,5},{14,6},{15,7},{16,8},{17,9... | collective-permute-start | bytes 497672 | tf_op jit(solution)/shard_map/ppermute | solution.py:372
  555.1 36.8 %collective-permute-start.56 = (bf16[1376,256]{1,0:T(8,128)(2,1)}, bf16[1376,256]{1,0:T(8,128)(2,1)}, u32[]{:S(2)}, u32[]{:S(2)}) collective-permute-start(bf16[1376,256]{1,0:T(8,128)(2,1)} %get-tuple-element.302), channel_id=1, source_target_pairs={{0,4},{1,5},{2,0},{3,1},{4,6},{5,7},{6,2},{7,3},{8,12},{9,13},{10,... | collective-permute-start | bytes 2113544 | tf_op jit(solution)/shard_map/ppermute | solution.py:372
  555.1 34.6 %collective-permute-start.55 = (bf16[1376,256]{1,0:T(8,128)(2,1)}, bf16[1376,256]{1,0:T(8,128)(2,1)}, u32[]{:S(2)}, u32[]{:S(2)}) collective-permute-start(bf16[1376,256]{1,0:T(8,128)(2,1)} %get-tuple-element.303), channel_id=1, source_target_pairs={{2,4},{3,5},{4,2},{5,3},{10,12},{11,13},{12,10},{13,11},{18,20},{1... | collective-permute-start | bytes 2113544 | tf_op jit(solution)/shard_map/ppermute | solution.py:372
  589.4 160.6 %reduce-scatter.14.cloned.1.call-start = ((), (), s32[]{:S(2)}) async-start(), calls=%async_computation.11 | async-start | bytes 3276800 | tf_op jit(solution)/shard_map/reduce_scatter | solution.py:438
  594.3 37.1 %collective-permute-start.60 = (bf16[1376,256]{1,0:T(8,128)(2,1)S(1)}, bf16[1376,256]{1,0:T(8,128)(2,1)S(1)}, u32[]{:S(2)}, u32[]{:S(2)}) collective-permute-start(bf16[1376,256]{1,0:T(8,128)(2,1)S(1)} %get-tuple-element.301), channel_id=1, source_target_pairs={{2,4},{3,5},{4,2},{5,3},{10,12},{11,13},{12,10},{13,11},{18,20},{1... | collective-permute-start | bytes 2113544 | tf_op jit(solution)/shard_map/ppermute | solution.py:372
  600.6 31.8 %collective-permute-start.57 = (bf16[1536,512]{1,0:T(8,128)(2,1)S(1)}, bf16[1536,512]{1,0:T(8,128)(2,1)S(1)}, u32[]{:S(2)}, u32[]{:S(2)}) collective-permute-start(bf16[1536,512]{1,0:T(8,128)(2,1)S(1)} %convolution_convert_fusion.11), channel_id=1, source_target_pairs={{0,4},{1,5},{2,6},{3,7},{4,0},{5,1},{6,2},{7,3},{8,12},{9,13},{10,... | collective-permute-start | bytes 4718600 | tf_op jit(solution)/shard_map/ppermute | solution.py:372
  604.7 48.7 %collective-permute-start.64 = (bf16[768,512]{1,0:T(8,128)(2,1)S(1)}, bf16[768,512]{1,0:T(8,128)(2,1)S(1)}, u32[]{:S(2)}, u32[]{:S(2)}) collective-permute-start(bf16[768,512]{1,0:T(8,128)(2,1)S(1)} %get-tuple-element.299), channel_id=1, source_target_pairs={{2,4},{3,5},{4,2},{5,3},{10,12},{11,13},{12,10},{13,11},{18,20},{1... | collective-permute-start | bytes 2359304 | tf_op jit(solution)/shard_map/ppermute | solution.py:372
  606.7 28.3 %collective-permute-start.61 = (bf16[1376,256]{1,0:T(8,128)(2,1)S(1)}, bf16[1376,256]{1,0:T(8,128)(2,1)S(1)}, u32[]{:S(2)}, u32[]{:S(2)}) collective-permute-start(bf16[1376,256]{1,0:T(8,128)(2,1)S(1)} %get-tuple-element.300), channel_id=1, source_target_pairs={{0,4},{1,5},{2,0},{3,1},{4,6},{5,7},{6,2},{7,3},{8,12},{9,13},{10,... | collective-permute-start | bytes 2113544 | tf_op jit(solution)/shard_map/ppermute | solution.py:372
  637.6 23.8 %collective-permute-start.63 = (bf16[1536,512]{1,0:T(8,128)(2,1)}, bf16[1536,512]{1,0:T(8,128)(2,1)}, u32[]{:S(2)}, u32[]{:S(2)}) collective-permute-start(bf16[1536,512]{1,0:T(8,128)(2,1)} %convolution_convert_fusion.10), channel_id=1, source_target_pairs={{0,4},{1,5},{2,6},{3,7},{4,0},{5,1},{6,2},{7,3},{8,12},{9,13},{10,... | collective-permute-start | bytes 4718600 | tf_op jit(solution)/shard_map/ppermute | solution.py:372
  650.6 17.1 %collective-permute-start.65 = (bf16[768,512]{1,0:T(8,128)(2,1)}, bf16[768,512]{1,0:T(8,128)(2,1)}, u32[]{:S(2)}, u32[]{:S(2)}) collective-permute-start(bf16[768,512]{1,0:T(8,128)(2,1)} %get-tuple-element.298), channel_id=1, source_target_pairs={{0,4},{1,5},{2,0},{3,1},{4,6},{5,7},{6,2},{7,3},{8,12},{9,13},{10,... | collective-permute-start | bytes 2359304 | tf_op jit(solution)/shard_map/ppermute | solution.py:372
  650.8 45.9 %collective-permute-start.62 = (bf16[1536,512]{1,0:T(8,128)(2,1)}, bf16[1536,512]{1,0:T(8,128)(2,1)S(1)}, u32[]{:S(2)}, u32[]{:S(2)}) collective-permute-start(bf16[1536,512]{1,0:T(8,128)(2,1)} %fusion.32), channel_id=1, source_target_pairs={{0,1},{1,0},{2,3},{3,2},{4,5},{5,4},{6,7},{7,6},{8,9},{9,8},{10,11... | collective-permute-start | bytes 4718600 | tf_op jit(solution)/shard_map/ppermute | solution.py:372
  712.5 36.4 %collective-permute-start.71 = (bf16[2,768,512]{2,1,0:T(8,128)(2,1)S(1)}, bf16[2,768,512]{2,1,0:T(8,128)(2,1)S(1)}, u32[]{:S(2)}, u32[]{:S(2)}) collective-permute-start(bf16[2,768,512]{2,1,0:T(8,128)(2,1)S(1)} %pad_maximum_fusion.1.refs_0_), channel_id=1, source_target_pairs={{1,0},{2,1},{3,2},{5,4},{6,5},{7,6},{9,8},{10,9},{11,10},{13,12},{... | collective-permute-start | bytes 4718600 | tf_op jit(solution)/shard_map/ppermute | solution.py:372
  713.8 36.3 %collective-permute-start.70 = (bf16[2,768,512]{2,1,0:T(8,128)(2,1)S(1)}, bf16[2,768,512]{2,1,0:T(8,128)(2,1)S(1)}, u32[]{:S(2)}, u32[]{:S(2)}) collective-permute-start(bf16[2,768,512]{2,1,0:T(8,128)(2,1)S(1)} %pad_maximum_fusion.1.refs_0_), channel_id=1, source_target_pairs={{0,1},{1,2},{2,3},{4,5},{5,6},{6,7},{8,9},{9,10},{10,11},{12,13},{... | collective-permute-start | bytes 4718600 | tf_op jit(solution)/shard_map/ppermute | solution.py:372
  750.1 17.3 %collective-permute-start.73 = (bf16[2,768,512]{2,1,0:T(8,128)(2,1)S(1)}, bf16[2,768,512]{2,1,0:T(8,128)(2,1)}, u32[]{:S(2)}, u32[]{:S(2)}) collective-permute-start(bf16[2,768,512]{2,1,0:T(8,128)(2,1)S(1)} %collective-permute-done.70.refs_1_), channel_id=1, source_target_pairs={{1,2},{2,3},{5,6},{6,7},{9,10},{10,11},{13,14},{14,15},{17,18},{18... | collective-permute-start | bytes 4718600 | tf_op jit(solution)/shard_map/ppermute | solution.py:372
  751.9 38.1 %collective-permute-start.74 = (bf16[2,768,512]{2,1,0:T(8,128)(2,1)}, bf16[2,768,512]{2,1,0:T(8,128)(2,1)}, u32[]{:S(2)}, u32[]{:S(2)}) collective-permute-start(bf16[2,768,512]{2,1,0:T(8,128)(2,1)} %copy-done.61), channel_id=1, source_target_pairs={{1,0},{2,1},{5,4},{6,5},{9,8},{10,9},{13,12},{14,13},{17,16},{18,1... | collective-permute-start | bytes 4718600 | tf_op jit(solution)/shard_map/ppermute | solution.py:372
  760.1 44.5 %collective-permute-start.82 = (bf16[256,512]{1,0:T(8,128)(2,1)S(1)}, bf16[256,512]{1,0:T(8,128)(2,1)S(1)}, u32[]{:S(2)}, u32[]{:S(2)}) collective-permute-start(bf16[256,512]{1,0:T(8,128)(2,1)S(1)} %get-tuple-element.311), channel_id=1, source_target_pairs={{0,4},{1,5},{2,0},{3,1},{4,6},{5,7},{6,2},{7,3},{8,12},{9,13},{10,... | collective-permute-start | bytes 786440 | tf_op jit(solution)/shard_map/ppermute | solution.py:372
  790.0 39.2 %collective-permute-start.76 = (bf16[2,768,512]{2,1,0:T(8,128)(2,1)}, bf16[2,768,512]{2,1,0:T(8,128)(2,1)}, u32[]{:S(2)}, u32[]{:S(2)}) collective-permute-start(bf16[2,768,512]{2,1,0:T(8,128)(2,1)} %collective-permute-done.73.refs_2_), channel_id=1, source_target_pairs={{2,3},{6,7},{10,11},{14,15},{18,19},{22,23},{26,27},{30,31}} | collective-permute-start | bytes 4718600 | tf_op jit(solution)/shard_map/ppermute | solution.py:372
  791.9 48.8 %collective-permute-start.77 = (bf16[2,768,512]{2,1,0:T(8,128)(2,1)}, bf16[2,768,512]{2,1,0:T(8,128)(2,1)}, u32[]{:S(2)}, u32[]{:S(2)}) collective-permute-start(bf16[2,768,512]{2,1,0:T(8,128)(2,1)} %collective-permute-done.74.refs_5_), channel_id=1, source_target_pairs={{1,0},{5,4},{9,8},{13,12},{17,16},{21,20},{25,24},{29,28}} | collective-permute-start | bytes 4718600 | tf_op jit(solution)/shard_map/ppermute | solution.py:372
  794.4 23.4 %collective-permute-start.81 = (bf16[256,512]{1,0:T(8,128)(2,1)S(1)}, bf16[256,512]{1,0:T(8,128)(2,1)S(1)}, u32[]{:S(2)}, u32[]{:S(2)}) collective-permute-start(bf16[256,512]{1,0:T(8,128)(2,1)S(1)} %get-tuple-element.310), channel_id=1, source_target_pairs={{2,4},{3,5},{4,2},{5,3},{10,12},{11,13},{12,10},{13,11},{18,20},{1... | collective-permute-start | bytes 786440 | tf_op jit(solution)/shard_map/ppermute | solution.py:372
  804.5 14.1 %collective-permute-start.80 = (bf16[256,640]{1,0:T(8,128)(2,1)S(1)}, bf16[256,640]{1,0:T(8,128)(2,1)S(1)}, u32[]{:S(2)}, u32[]{:S(2)}) collective-permute-start(bf16[256,640]{1,0:T(8,128)(2,1)S(1)} %get-tuple-element.309), channel_id=1, source_target_pairs={{0,4},{1,5},{2,0},{3,1},{4,6},{5,7},{6,2},{7,3},{8,12},{9,13},{10,... | collective-permute-start | bytes 983048 | tf_op jit(solution)/shard_map/ppermute | solution.py:372
  804.6 20.2 %collective-permute-start.79 = (bf16[256,640]{1,0:T(8,128)(2,1)S(1)}, bf16[256,640]{1,0:T(8,128)(2,1)S(1)}, u32[]{:S(2)}, u32[]{:S(2)}) collective-permute-start(bf16[256,640]{1,0:T(8,128)(2,1)S(1)} %get-tuple-element.308), channel_id=1, source_target_pairs={{2,4},{3,5},{4,2},{5,3},{10,12},{11,13},{12,10},{13,11},{18,20},{1... | collective-permute-start | bytes 983048 | tf_op jit(solution)/shard_map/ppermute | solution.py:372
  (134 other events, 1757.7 us)
Sparse Core Ops, SparseCore 0:
  84.1 68.3 all-gather.2
  175.9 63.9 all-gather.4
  324.3 64.8 reduce-scatter.5
  392.2 64.6 reduce-scatter.7
  459.8 65.6 reduce-scatter.9
  589.6 35.3 reduce-scatter.11
  696.9 39.2 reduce-scatter.13

commit v6 on v5

--- a/solution.py
+++ b/solution.py
@@ -495,11 +495,13 @@
     qk_width, v_width = heads * QK, heads * HEAD_V
     qkv_owns = spread(jnp.concatenate([w_query, w_key, w_value], 1))
     gains = lax.all_gather(jnp.stack([gain_mixer, gain_mlp]), "seq", axis=1, tiled=True)
-    w_gate, gains, *qkv_owns = tie(w_gate.T, gains, *qkv_owns)
+    w_output, gains, *qkv_owns = tie(w_output, gains, *qkv_owns)
     gains = gains.astype(F32)
     mixer_gain, mlp_gain = gains[0], gains[1]
+    output_owns = spread(w_output)
+    qkv_full = place_chips(all_hops(qkv_owns), 0)
+    w_gate, qkv_full, output_owns = tie(w_gate.T, qkv_full, output_owns)
     gate_owns = spread(w_gate)
-    qkv_full = place_chips(all_hops(qkv_owns), 0)
 
     bounds = jnp.cumsum(lax.dynamic_index_in_dim(lengths, batch, 0, False))
 
@@ -532,11 +534,10 @@
         return jnp.concatenate([state.reshape(-1, HEAD_V), total], 0).astype(BF)
 
     def unpack(flat):
-        flat = flat.astype(F32)
         cut = heads * NFEAT
         return (
-            flat[:cut].reshape(heads, NFEAT, HEAD_V),
-            flat[cut:].reshape(heads, -1)[:, :NFEAT],
+            flat[:cut].reshape(heads, NFEAT, HEAD_V).astype(F32),
+            flat[cut:].reshape(heads, -1)[:, :NFEAT].astype(F32),
         )
 
     def scan_blocks(both, blocks_order, step, meanwhile):
@@ -573,14 +574,12 @@
         return both, meanwhile
 
     (local,) = local_states(marks, keys, values)
-    w_output, gate_owns, local = tie(w_output, gate_owns, local)
-    output_owns = spread(w_output)
-    states, output_owns = scan_blocks(local, list(range(CORES)), 1, output_owns)
+    states, gate_owns = scan_blocks(local, list(range(CORES)), 1, gate_owns)
+    w_up, states, output_owns = tie(w_up.T, states, output_owns)
+    up_owns = spread(w_up)
     gate_full = gather_chips_bulk(gate_owns, 1)
-    w_up, states = tie(w_up.T, states)
-    up_owns = spread(w_up)
     mixer_own, denom = mixer(marks, query, keys, values, states)
-    mixer_own, output_owns, up_owns = tie(mixer_own, output_owns, up_owns)
+    mixer_own, up_owns = tie(mixer_own, up_owns)
 
     arrived = send_parts(mixer_own)
     up_full = gather_chips_bulk(up_owns, 1)
@@ -672,8 +671,7 @@
     grad_qkv = mixer_back(
         marks, query, keys, values, mixer_grad, mixer_own, denom, states, carried
     )
-    grad_qkv, up_halves, gate_sum = tie(grad_qkv, up_halves, gate_sum)
-    gate_halves = send_halves(gate_sum, 1)
+    grad_qkv, up_halves = tie(grad_qkv, up_halves)
     grad_qkv = jnp.concatenate(grad_qkv, 1)
     inner_one = jnp.sum(grad_qkv.astype(F32) * qkv.astype(F32), axis=1)
     inner_one = sum_ranks(inner_one) / width
@@ -682,7 +680,7 @@
         return dot(grad, row_piece(qkv_full, r), 1, 1)
 
     totals = reduce_away(functools.partial(input_part, grad_qkv))
-    totals, grad_qkv, inner_one, gate_halves = tie(totals, grad_qkv, inner_one, gate_halves)
+    totals, grad_qkv, inner_one = tie(totals, grad_qkv, inner_one)
     arrived = reduce_send(totals)
     mixed_own = (hidden_own + reduce_end(mlp_own, mlp_arrived)).astype(BF)
     mixed_halves = unspread(half(mixed_own, batch), half(mixed_own, 1 - batch))
@@ -705,13 +703,14 @@
     gain_grads = lax.dynamic_update_slice_in_dim(
         jnp.zeros((2, width), F32), jnp.stack([grad_gain_mixer, grad_gain_mlp]), rank * piece, 1
     )
+    other_half = to_core(half(input_own, 1 - core))
+    input_own, other_half = tie(input_own, other_half)
+    input_pair = jnp.stack([half(input_own, core), other_half])
+    input_pair, gain_grads = tie(input_pair, gain_grads)
     planes = [
         move(gain_grads, lambda c, k, m, l: (c, k, *divmod((m * group + l) ^ d, group)))
         for d in range(1, feat_count)
     ]
-    other_half = to_core(half(input_own, 1 - core))
-    input_own, other_half, *planes = tie(input_own, other_half, *planes)
-    input_pair = jnp.stack([half(input_own, core), other_half])
 
     def step_plane(value, step, first):
         def target(c, k, m, l):
@@ -723,20 +722,22 @@
 
         return move(value, target)
 
-    gain_grads = sum(planes, gain_grads)
-    output_halves = send_halves(output_sum, 0)
     hops = [to_core] + [
         functools.partial(to_chip, mask=1 << i) for i in range(chips.bit_length() - 1)
     ]
     ups, downs = [input_pair], [input_pair]
     for d in range(feat_count - 1):
         up, down = step_plane(ups[-1], 1, d), step_plane(downs[-1], -1, d)
-        if hops:
+        if d == 0:
+            up, down, planes, output_sum = tie(up, down, planes, output_sum)
+            output_halves = send_halves(output_sum, 0)
+            gain_grads = sum(planes, gain_grads)
+        elif hops:
             up, down, gain_grads, got = tie(up, down, gain_grads, hops[0](gain_grads))
             gain_grads, hops = gain_grads + got, hops[1:]
-        if d == 0:
-            up, down, qkv_sum = tie(up, down, qkv_sum)
-            qkv_halves = send_halves(qkv_sum, 0)
+        if d == feat_count - 3:
+            up, down, gate_sum, qkv_sum = tie(up, down, gate_sum, qkv_sum)
+            gate_halves, qkv_halves = send_halves(gate_sum, 1), send_halves(qkv_sum, 0)
         ups.append(up), downs.append(down)
     for hop in hops:
         gain_grads = gain_grads + hop(gain_grads)

time: 872 us -> 845 us (0.969)
  starting transfers between devices: 137 us -> 103 us
  waiting for transfers between devices: 288 us -> 300 us
    ppermute x83, starting transfers between devices: 137 us -> 102 us  [move(): return lax.ppermute(value, ('seq', 'feat'), pairs)]
    ppermute x83, waiting for transfers between devices: 288 us -> 300 us  [move(): return lax.ppermute(value, ('seq', 'feat'), pairs)]
    unnamed x216 -> x206, local copies, waits for them, and re-layouts: 30.4 us -> 23.2 us
  transfers between devices with their start and end apart: 90 -> 90, of which waited for: 35 -> 30; matrix products, arithmetic and copies ran while one was open for 33% -> 34% of each run, Pallas kernels for 8% -> 9%
where the time goes in v6:
time: 845 us; the launch traced here: 832 us
  waiting for transfers between devices  300 us (36%)
  matrix products  194 us (23%)
  starting transfers between devices  103 us (12%)
  Pallas kernels  79.6 us (9%)
  other arithmetic  73.4 us (9%)
  local copies, waits for them, and re-layouts  48.6 us (6%)
  between operations  24.2 us (3%)
  blocking collectives  9.09 us (1%)
    ppermute x83, waiting for transfers between devices, move(): return lax.ppermute(value, ('seq', 'feat'), pairs)  300 us
    dot_general x36, matrix products, dot(): lax.dot_general(a, b, (((ca,), (cb,)), ((), ())), preferred_element_type=...  194 us
    ppermute x83, starting transfers between devices, move(): return lax.ppermute(value, ('seq', 'feat'), pairs)  102 us
    pallas_call x4, Pallas kernels, run(): pl.pallas_call(functools.partial(kernel, heads=heads, block=block), grid_...  47.1 us
    unnamed x206, local copies, waits for them, and re-layouts  23.2 us
    pallas_call x9, Pallas kernels, place(): pl.pallas_call(functools.partial(place_kernel, axis=axis), grid_spec=pltp...  23.1 us
  transfers between devices with their start and end apart: 90, of which 30 were waited for; matrix products, arithmetic and copies ran while one was open for 34% of the time, Pallas kernels for 9%

profile of v6, /device:TPU:7, one launch (start us, length us, event | category | flops | bytes accessed | tf_op | source)
XLA Modules:
  0.0 831.6 jit_solution(6596871288661138022)
XLA Ops:
  11.5 4.1 collective-permute-start.1
  19.8 9.1 %all_gather.9 = bf16[2,2048]{1,0:T(2,128)(2,1)} all-gather(bf16[2,256]{1,0:T(2,128)(2,1)S(1)} %pad_maximum_fusion.5), channel_id=1, replica_groups=mesh['seq'=8,'feat'=4] {'seq'}, dimensions={1}, use_global_device_ids=true | all-gather | bytes 9216 | tf_op jit(solution)/shard_map/all_gather | solution.py:497
  39.2 5.5 collective-permute-done.9
  54.8 6.2 collective-permute-done.8.refs_7_
  72.5 5.3 convolution_convert_fusion.7
  79.3 4.3 shard_map.242
  89.0 6.5 collective-permute-done.15
  114.6 9.5 %shard_map.243 = (bf16[1536,512]{1,0:T(8,128)(2,1)}, f32[1536,512]{1,0:T(8,128)}) custom-call(s32[2,5]{1,0:T(2,128)S(1)} %copy-done.33, bf16[1536,64]{1,0:T(8,128)(2,1)S(1)} %copy-done.19, bf16[1536,64]{1,0:T(8,128)(2,1)S(1)} %get-tuple-element.286.k_ref, bf16[1536,512]{1,0:T(8,128)(2,1)S(1)} %slice.236.v_ref, bf16[2,4,256,256]{3,2,1,0:T(8,128)(2,1)S(1)} %fusion.66.s_ref, ...), custom_call_target="tpu_custom_call" | custom-call | flops 6144000000 | bytes 9216000 | tf_op jit(solution)/shard_map/pallas_call | solution.py:220
  124.1 23.7 %collective-permute-done.17 = bf16[1376,256]{1,0:T(8,128)(2,1)S(1)} collective-permute-done((bf16[1376,256]{1,0:T(8,128)(2,1)}, bf16[1376,256]{1,0:T(8,128)(2,1)S(1)}, u32[]{:S(2)}, u32[]{:S(2)}) %collective-permute-start.17) | collective-permute-done | bytes 704544 | tf_op jit(solution)/shard_map/ppermute | solution.py:372
  150.5 4.5 collective-permute-start.28
  155.1 7.7 collective-permute-done.20.refs_2_
  164.5 12.4 %collective-permute-done.23.refs_6_ = bf16[256,512]{1,0:T(8,128)(2,1)S(1)} collective-permute-done((bf16[256,512]{1,0:T(8,128)(2,1)S(1)}, bf16[256,512]{1,0:T(8,128)(2,1)S(1)}, u32[]{:S(2)}, u32[]{:S(2)}) %collective-permute-start.23) | collective-permute-done | bytes 262176 | tf_op jit(solution)/shard_map/ppermute | solution.py:372
  178.3 4.0 dynamic-slice_bitcast_fusion.refs_0_
  204.5 3.5 collective-permute-done.29.refs_4_
  208.9 35.0 %collective-permute-done.31.refs_2_ = bf16[1536,512]{1,0:T(8,128)(2,1)} collective-permute-done((bf16[1536,512]{1,0:T(8,128)(2,1)S(1)}, bf16[1536,512]{1,0:T(8,128)(2,1)}, u32[]{:S(2)}, u32[]{:S(2)}) %collective-permute-start.31) | collective-permute-done | bytes 1572896 | tf_op jit(solution)/shard_map/ppermute | solution.py:372
  243.9 4.5 shard_map.241
  261.5 4.1 multiply_convert_fusion
  268.4 12.3 %convolution_convert_fusion.5 = bf16[1536,1376]{0,1:T(8,128)(2,1)} fusion(bf16[1536,2048]{1,0:T(8,128)(2,1)S(1)} %multiply_convert_fusion, bf16[1376,2048]{1,0:T(8,128)(2,1)} %all-gather.3.cloned.1.call-done), kind=kOutput, calls=%fused_computation.37 | convolution fusion | flops 8659156992 | bytes 16154624 | tf_op jit(solution)/shard_map/dot_general | solution.py:262
  280.7 15.7 %fusion.15 = (bf16[1536,1376]{0,1:T(8,128)(2,1)S(1)}, bf16[1536,1376]{0,1:T(8,128)(2,1)}) fusion(bf16[1536,1376]{0,1:T(8,128)(2,1)} %convolution_convert_fusion.5, bf16[1536,2048]{1,0:T(8,128)(2,1)} %copy-done.52, bf16[1376,2048]{1,0:T(8,128)(2,1)} %all-gather.5.cloned.1.call-done), kind=kOutput, calls=%fused_computation.31 | convolution fusion | flops 8676065280 | bytes 24608768 | tf_op jit(solution)/shard_map/dot_general | solution.py:262
  298.5 12.6 %convolution_convert_fusion.2 = bf16[1376,2048]{1,0:T(8,128)(2,1)} fusion(bf16[1536,1376]{0,1:T(8,128)(2,1)S(1)} %get-tuple-element.174, bf16[1536,2048]{1,0:T(8,128)(2,1)} %copy-done.5), kind=kOutput, calls=%fused_computation.34 | convolution fusion | flops 8659861504 | bytes 16154624 | tf_op jit(solution)/shard_map/dot_general | solution.py:262
  311.1 5.1 collective-permute-done.37.refs_6_
  316.5 3.9 shard_map.248
  320.4 13.2 %convolution_convert_fusion.3 = bf16[1536,1376]{0,1:T(8,128)(2,1)S(1)} fusion(bf16[1536,2048]{1,0:T(8,128)(2,1)} %copy-done.5, bf16[1376,2048]{1,0:T(8,128)(2,1)S(1)} %shard_map.248), kind=kOutput, calls=%fused_computation.35 | convolution fusion | flops 8659156992 | bytes 16154624 | tf_op jit(solution)/shard_map/dot_general | solution.py:262
  333.7 6.3 fusion.64
  340.0 5.2 fusion.58
  352.6 4.1 fusion.61
  356.8 4.0 fusion.29
  360.8 10.6 %convolution_convert_fusion = bf16[1376,2048]{1,0:T(8,128)(2,1)} fusion(bf16[1536,1376]{0,1:T(8,128)(2,1)S(1)} %get-tuple-element.165, bf16[1536,2048]{1,0:T(8,128)(2,1)S(1)} %bitcast.131), kind=kOutput, calls=%fused_computation.32 | convolution fusion | flops 8659861504 | bytes 16154624 | tf_op jit(solution)/shard_map/dot_general | solution.py:262
  372.8 5.5 fusion.52
  378.3 6.7 fusion.28
  385.4 10.6 %convolution_convert_fusion.1 = bf16[1376,2048]{1,0:T(8,128)(2,1)} fusion(bf16[1536,1376]{0,1:T(8,128)(2,1)S(1)} %bitcast.135, bf16[1536,2048]{1,0:T(8,128)(2,1)S(1)} %bitcast.133), kind=kOutput, calls=%fused_computation.33 | convolution fusion | flops 8659861504 | bytes 16154624 | tf_op jit(solution)/shard_map/dot_general | solution.py:262
  396.0 4.8 fusion.55
  400.8 8.0 fusion.20
  410.0 5.4 fusion.129
  415.4 3.6 convolution_convert_fusion.9
  423.1 4.0 fusion.31
  427.0 5.4 convolution_convert_fusion.13
  442.2 25.0 %collective-permute-done.49 = bf16[1376,256]{1,0:T(8,128)(2,1)S(1)} collective-permute-done((bf16[1376,256]{1,0:T(8,128)(2,1)S(1)}, bf16[1376,256]{1,0:T(8,128)(2,1)S(1)}, u32[]{:S(2)}, u32[]{:S(2)}) %collective-permute-start.49) | collective-permute-done | bytes 704544 | tf_op jit(solution)/shard_map/ppermute | solution.py:372
  468.2 4.4 convert_add_fusion.4
  475.4 4.1 add_convert_fusion.1
  479.5 15.0 %collective-permute-done.45 = bf16[1536,512]{1,0:T(8,128)(2,1)} collective-permute-done((bf16[1536,512]{1,0:T(8,128)(2,1)}, bf16[1536,512]{1,0:T(8,128)(2,1)}, u32[]{:S(2)}, u32[]{:S(2)}) %collective-permute-start.45) | collective-permute-done | bytes 1572896 | tf_op jit(solution)/shard_map/ppermute | solution.py:372
  494.5 4.5 convert_add_fusion.3.do_ref
  500.1 6.8 shard_map.249
  509.5 3.9 collective-permute-start.53
  529.7 5.7 collective-permute-done.54
  547.9 26.4 %shard_map.251 = (bf16[1536,64]{1,0:T(8,128)(2,1)S(1)}, bf16[1536,64]{1,0:T(8,128)(2,1)S(1)}, bf16[1536,512]{1,0:T(8,128)(2,1)S(1)}) custom-call(s32[2,5]{1,0:T(2,128)S(1)} %copy-done.34, bf16[1536,64]{1,0:T(8,128)(2,1)S(1)} %copy-done.20, bf16[1536,64]{1,0:T(8,128)(2,1)S(1)} %copy-done.18, bf16[1536,512]{1,0:T(8,128)(2,1)} %copy-done.10, ...), custom_call_target="tpu_custom_call" | custom-call | flops 15360000000 | bytes 9216000 | tf_op jit(solution)/shard_map/pallas_call | solution.py:220
  577.2 4.2 convolution_convert_fusion.11
  581.7 3.9 add_convert_fusion
  587.5 4.7 collective-permute-start.62
  592.8 4.1 fusion.32
  600.8 15.2 %collective-permute-done.62 = bf16[768,512]{1,0:T(8,128)(2,1)S(1)} collective-permute-done((bf16[768,512]{1,0:T(8,128)(2,1)S(1)}, bf16[768,512]{1,0:T(8,128)(2,1)S(1)}, u32[]{:S(2)}, u32[]{:S(2)}) %collective-permute-start.62) | collective-permute-done | bytes 786464 | tf_op jit(solution)/shard_map/ppermute | solution.py:372
  617.0 10.1 %convolution_convert_fusion.6 = bf16[2048,640]{1,0:T(8,128)(2,1)} fusion(bf16[1536,640]{1,0:T(8,128)(2,1)} %copy-done.57, bf16[1536,2048]{1,0:T(8,128)(2,1)} %copy-done.2, f32[2048]{0:T(1024)} %bitcast.153, f32[1536]{0:T(1024)} %copy-done.74), kind=kOutput, calls=%fused_computation.56 | convolution fusion | flops 4040425472 | bytes 10893312 | tf_op jit(solution)/shard_map/dot_general | solution.py:262
  627.1 4.8 convolution_add_fusion
  631.9 19.8 %collective-permute-done.60 = bf16[1536,512]{1,0:T(8,128)(2,1)} collective-permute-done((bf16[1536,512]{1,0:T(8,128)(2,1)}, bf16[1536,512]{1,0:T(8,128)(2,1)}, u32[]{:S(2)}, u32[]{:S(2)}) %collective-permute-start.60) | collective-permute-done | bytes 1572896 | tf_op jit(solution)/shard_map/ppermute | solution.py:372
  652.4 6.3 fusion.25
  665.0 4.3 collective-permute-start.65
  672.9 29.5 %collective-permute-done.69 = f32[2,2048]{1,0:T(2,128)S(1)} collective-permute-done((f32[2,2048]{1,0:T(2,128)S(1)}, f32[2,2048]{1,0:T(2,128)S(1)}, u32[]{:S(2)}, u32[]{:S(2)}) %collective-permute-start.69) | collective-permute-done | bytes 16416 | tf_op jit(solution)/shard_map/ppermute | solution.py:372
  710.5 33.0 %collective-permute-done.71.refs_5_ = bf16[2,768,512]{2,1,0:T(8,128)(2,1)} collective-permute-done((bf16[2,768,512]{2,1,0:T(8,128)(2,1)}, bf16[2,768,512]{2,1,0:T(8,128)(2,1)}, u32[]{:S(2)}, u32[]{:S(2)}) %collective-permute-start.71) | collective-permute-done | bytes 1572896 | tf_op jit(solution)/shard_map/ppermute | solution.py:372
  750.8 3.3 collective-permute-start.77
  759.8 3.6 collective-permute-start.76
  764.6 13.6 %collective-permute-done.78 = bf16[256,512]{1,0:T(8,128)(2,1)S(1)} collective-permute-done((bf16[256,512]{1,0:T(8,128)(2,1)S(1)}, bf16[256,512]{1,0:T(8,128)(2,1)S(1)}, u32[]{:S(2)}, u32[]{:S(2)}) %collective-permute-start.78) | collective-permute-done | bytes 262176 | tf_op jit(solution)/shard_map/ppermute | solution.py:372
  780.9 15.7 %collective-permute-done.76 = bf16[256,640]{1,0:T(8,128)(2,1)S(1)} collective-permute-done((bf16[256,640]{1,0:T(8,128)(2,1)S(1)}, bf16[256,640]{1,0:T(8,128)(2,1)S(1)}, u32[]{:S(2)}, u32[]{:S(2)}) %collective-permute-start.76) | collective-permute-done | bytes 327712 | tf_op jit(solution)/shard_map/ppermute | solution.py:372
  801.3 10.6 %collective-permute-done.80 = bf16[1376,256]{1,0:T(8,128)(2,1)} collective-permute-done((bf16[1376,256]{1,0:T(8,128)(2,1)}, bf16[1376,256]{1,0:T(8,128)(2,1)}, u32[]{:S(2)}, u32[]{:S(2)}) %collective-permute-start.80) | collective-permute-done | bytes 704544 | tf_op jit(solution)/shard_map/ppermute | solution.py:372
  814.5 9.4 %shard_map.252 = f32[2,768,2048]{2,1,0:T(8,128)} custom-call(s32[2]{0:T(128)S(1)} %pad_add_fusion.5.where, bf16[2,768,512]{2,1,0:T(8,128)(2,1)S(1)} %pad_maximum_fusion.1.refs_0_, bf16[2,768,512]{2,1,0:T(8,128)(2,1)S(1)} %collective-permute-done.65.refs_1_, bf16[2,768,512]{2,1,0:T(8,128)(2,1)} %collective-permute-done.70.refs_2_, ...), custom_call_target="tpu_custom_call" | custom-call | tf_op jit(solution)/shard_map/pallas_call | solution.py:321
  (512 shorter events, 218.6 us)
Async XLA Ops:
  7.2 236.6 %all-gather.3.cloned.1.call-start = ((), (), s32[]{:S(2)}) async-start(), calls=%async_computation.5 | async-start | bytes 7045120 | tf_op jit(solution)/shard_map/all_gather | solution.py:433
  10.8 20.5 %collective-permute-start.2 = (bf16[256,640]{1,0:T(8,128)(2,1)}, bf16[256,640]{1,0:T(8,128)(2,1)}, u32[]{:S(2)}, u32[]{:S(2)}) collective-permute-start(bf16[256,640]{1,0:T(8,128)(2,1)} %pad_maximum_fusion.2), channel_id=1, source_target_pairs={{0,2},{1,3},{2,6},{3,7},{4,0},{5,1},{6,4},{7,5},{8,10},{9,11},{10,... | collective-permute-start | bytes 983048 | tf_op jit(solution)/shard_map/ppermute | solution.py:372
  11.5 18.6 %collective-permute-start.1 = (bf16[256,640]{1,0:T(8,128)(2,1)}, bf16[256,640]{1,0:T(8,128)(2,1)}, u32[]{:S(2)}, u32[]{:S(2)}) collective-permute-start(bf16[256,640]{1,0:T(8,128)(2,1)} %pad_maximum_fusion.2), channel_id=1, source_target_pairs={{2,4},{3,5},{4,2},{5,3},{10,12},{11,13},{12,10},{13,11},{18,20},{1... | collective-permute-start | bytes 983048 | tf_op jit(solution)/shard_map/ppermute | solution.py:372
  17.8 49.1 %collective-permute-start = (bf16[768,2048]{1,0:T(8,128)(2,1)S(1)}, bf16[768,2048]{1,0:T(8,128)(2,1)}, u32[]{:S(2)}, u32[]{:S(2)}) collective-permute-start(bf16[768,2048]{1,0:T(8,128)(2,1)S(1)} %dynamic-slice_bitcast_fusion.1.refs_0_), channel_id=1, source_target_pairs={{0,4},{1,5},{2,6},{3,7},{4,0},{5,1},{6,2},{7,3},{8,12},{9,13},{10,... | collective-permute-start | bytes 9437192 | tf_op jit(solution)/shard_map/ppermute | solution.py:372
  44.7 19.1 %collective-permute-start.10 = (bf16[256,512]{1,0:T(8,128)(2,1)}, bf16[256,512]{1,0:T(8,128)(2,1)S(1)}, u32[]{:S(2)}, u32[]{:S(2)}) collective-permute-start(bf16[256,512]{1,0:T(8,128)(2,1)} %param.22), channel_id=1, source_target_pairs={{0,2},{1,3},{2,6},{3,7},{4,0},{5,1},{6,4},{7,5},{8,10},{9,11},{10,... | collective-permute-start | bytes 786440 | tf_op jit(solution)/shard_map/ppermute | solution.py:372
  63.8 34.1 %collective-permute-start.16 = (bf16[1376,256]{1,0:T(8,128)(2,1)}, bf16[1376,256]{1,0:T(8,128)(2,1)}, u32[]{:S(2)}, u32[]{:S(2)}) collective-permute-start(bf16[1376,256]{1,0:T(8,128)(2,1)} %bitcast.8), channel_id=1, source_target_pairs={{0,2},{1,3},{2,6},{3,7},{4,0},{5,1},{6,4},{7,5},{8,10},{9,11},{10,... | collective-permute-start | bytes 2113544 | tf_op jit(solution)/shard_map/ppermute | solution.py:372
  64.9 30.6 %collective-permute-start.15 = (bf16[1376,256]{1,0:T(8,128)(2,1)}, bf16[1376,256]{1,0:T(8,128)(2,1)}, u32[]{:S(2)}, u32[]{:S(2)}) collective-permute-start(bf16[1376,256]{1,0:T(8,128)(2,1)} %bitcast.8), channel_id=1, source_target_pairs={{2,4},{3,5},{4,2},{5,3},{10,12},{11,13},{12,10},{13,11},{18,20},{1... | collective-permute-start | bytes 2113544 | tf_op jit(solution)/shard_map/ppermute | solution.py:372
  101.5 179.2 %all-gather.5.cloned.1.call-start = ((), (), s32[]{:S(2)}) async-start(), calls=%async_computation.6 | async-start | bytes 7045120 | tf_op jit(solution)/shard_map/all_gather | solution.py:433
  111.8 36.0 %collective-permute-start.17 = (bf16[1376,256]{1,0:T(8,128)(2,1)}, bf16[1376,256]{1,0:T(8,128)(2,1)S(1)}, u32[]{:S(2)}, u32[]{:S(2)}) collective-permute-start(bf16[1376,256]{1,0:T(8,128)(2,1)} %bitcast.144), channel_id=1, source_target_pairs={{2,4},{3,5},{4,2},{5,3},{10,12},{11,13},{12,10},{13,11},{18,20},{1... | collective-permute-start | bytes 2113544 | tf_op jit(solution)/shard_map/ppermute | solution.py:372
  114.4 33.6 %collective-permute-start.18 = (bf16[1376,256]{1,0:T(8,128)(2,1)}, bf16[1376,256]{1,0:T(8,128)(2,1)S(1)}, u32[]{:S(2)}, u32[]{:S(2)}) collective-permute-start(bf16[1376,256]{1,0:T(8,128)(2,1)} %bitcast.145), channel_id=1, source_target_pairs={{0,2},{1,3},{2,6},{3,7},{4,0},{5,1},{6,4},{7,5},{8,10},{9,11},{10,... | collective-permute-start | bytes 2113544 | tf_op jit(solution)/shard_map/ppermute | solution.py:372
  148.9 43.5 %collective-permute-start.26 = (bf16[1536,512]{1,0:T(8,128)(2,1)}, bf16[1536,512]{1,0:T(8,128)(2,1)}, u32[]{:S(2)}, u32[]{:S(2)}) collective-permute-start(bf16[1536,512]{1,0:T(8,128)(2,1)} %get-tuple-element.141.o_ref), channel_id=1, source_target_pairs={{0,1},{1,0},{2,3},{3,2},{4,5},{5,4},{6,7},{7,6},{8,9},{9,8},{10,11... | collective-permute-start | bytes 4718600 | tf_op jit(solution)/shard_map/ppermute | solution.py:372
  148.9 13.9 %collective-permute-start.20 = (bf16[256,512]{1,0:T(8,128)(2,1)S(1)}, bf16[256,512]{1,0:T(8,128)(2,1)S(1)}, u32[]{:S(2)}, u32[]{:S(2)}) collective-permute-start(bf16[256,512]{1,0:T(8,128)(2,1)S(1)} %copy-done.11), channel_id=1, source_target_pairs={{0,16},{1,17},{2,18},{3,19},{4,20},{5,21},{6,22},{7,23},{8,24},{9,... | collective-permute-start | bytes 786440 | tf_op jit(solution)/shard_map/ppermute | solution.py:372
  149.8 14.7 %collective-permute-start.19 = (bf16[256,512]{1,0:T(8,128)(2,1)S(1)}, bf16[256,512]{1,0:T(8,128)(2,1)S(1)}, u32[]{:S(2)}, u32[]{:S(2)}) collective-permute-start(bf16[256,512]{1,0:T(8,128)(2,1)S(1)} %copy-done.11), channel_id=1, source_target_pairs={{0,8},{1,9},{2,10},{3,11},{4,12},{5,13},{6,14},{7,15},{8,0},{9,1},... | collective-permute-start | bytes 786440 | tf_op jit(solution)/shard_map/ppermute | solution.py:372
  150.5 42.8 %collective-permute-start.28 = (bf16[1376,256]{1,0:T(8,128)(2,1)}, bf16[1376,256]{1,0:T(8,128)(2,1)}, u32[]{:S(2)}, u32[]{:S(2)}) collective-permute-start(bf16[1376,256]{1,0:T(8,128)(2,1)} %param.25), channel_id=1, source_target_pairs={{2,4},{3,5},{4,2},{5,3},{10,12},{11,13},{12,10},{13,11},{18,20},{1... | collective-permute-start | bytes 2113544 | tf_op jit(solution)/shard_map/ppermute | solution.py:372
  155.0 41.9 %collective-permute-start.25 = (bf16[1536,512]{1,0:T(8,128)(2,1)}, bf16[1536,512]{1,0:T(8,128)(2,1)}, u32[]{:S(2)}, u32[]{:S(2)}) collective-permute-start(bf16[1536,512]{1,0:T(8,128)(2,1)} %get-tuple-element.141.o_ref), channel_id=1, source_target_pairs={{0,4},{1,5},{2,6},{3,7},{4,0},{5,1},{6,2},{7,3},{8,12},{9,13},{10,... | collective-permute-start | bytes 4718600 | tf_op jit(solution)/shard_map/ppermute | solution.py:372
  162.8 14.1 %collective-permute-start.23 = (bf16[256,512]{1,0:T(8,128)(2,1)S(1)}, bf16[256,512]{1,0:T(8,128)(2,1)S(1)}, u32[]{:S(2)}, u32[]{:S(2)}) collective-permute-start(bf16[256,512]{1,0:T(8,128)(2,1)S(1)} %copy-done.22), channel_id=1, source_target_pairs={{0,8},{1,9},{2,10},{3,11},{4,12},{5,13},{6,14},{7,15},{8,0},{9,1},... | collective-permute-start | bytes 786440 | tf_op jit(solution)/shard_map/ppermute | solution.py:372
  164.5 13.7 %collective-permute-start.22 = (bf16[256,512]{1,0:T(8,128)(2,1)S(1)}, bf16[256,512]{1,0:T(8,128)(2,1)S(1)}, u32[]{:S(2)}, u32[]{:S(2)}) collective-permute-start(bf16[256,512]{1,0:T(8,128)(2,1)S(1)} %copy-done.22), channel_id=1, source_target_pairs={{0,16},{1,17},{2,18},{3,19},{4,20},{5,21},{6,22},{7,23},{8,24},{9,... | collective-permute-start | bytes 786440 | tf_op jit(solution)/shard_map/ppermute | solution.py:372
  184.2 59.8 %collective-permute-start.11 = (bf16[768,2048]{1,0:T(8,128)(2,1)}, bf16[768,2048]{1,0:T(8,128)(2,1)}, u32[]{:S(2)}, u32[]{:S(2)}) collective-permute-start(bf16[768,2048]{1,0:T(8,128)(2,1)} %dynamic-slice_bitcast_fusion.refs_0_), channel_id=1, source_target_pairs={{0,4},{1,5},{2,6},{3,7},{4,0},{5,1},{6,2},{7,3},{8,12},{9,13},{10,... | collective-permute-start | bytes 9437192 | tf_op jit(solution)/shard_map/ppermute | solution.py:372
  189.3 18.7 %collective-permute-start.29 = (bf16[1376,256]{1,0:T(8,128)(2,1)}, bf16[1376,256]{1,0:T(8,128)(2,1)S(1)}, u32[]{:S(2)}, u32[]{:S(2)}) collective-permute-start(bf16[1376,256]{1,0:T(8,128)(2,1)} %param.25), channel_id=1, source_target_pairs={{0,2},{1,3},{2,6},{3,7},{4,0},{5,1},{6,4},{7,5},{8,10},{9,11},{10,... | collective-permute-start | bytes 2113544 | tf_op jit(solution)/shard_map/ppermute | solution.py:372
  192.3 216.6 %reduce-scatter.6.cloned.1.call-start = ((), (), s32[]{:S(2)}) async-start(), calls=%async_computation.7 | async-start | bytes 7045120 | tf_op jit(solution)/shard_map/reduce_scatter | solution.py:438
  208.0 35.8 %collective-permute-start.31 = (bf16[1536,512]{1,0:T(8,128)(2,1)S(1)}, bf16[1536,512]{1,0:T(8,128)(2,1)}, u32[]{:S(2)}, u32[]{:S(2)}) collective-permute-start(bf16[1536,512]{1,0:T(8,128)(2,1)S(1)} %fusion.30.refs_0_), channel_id=1, source_target_pairs={{0,1},{1,0},{2,3},{3,2},{4,5},{5,4},{6,7},{7,6},{8,9},{9,8},{10,11... | collective-permute-start | bytes 4718600 | tf_op jit(solution)/shard_map/ppermute | solution.py:372
  208.0 45.8 %collective-permute-start.30 = (bf16[1536,512]{1,0:T(8,128)(2,1)S(1)}, bf16[1536,512]{1,0:T(8,128)(2,1)}, u32[]{:S(2)}, u32[]{:S(2)}) collective-permute-start(bf16[1536,512]{1,0:T(8,128)(2,1)S(1)} %fusion.30.refs_0_), channel_id=1, source_target_pairs={{0,4},{1,5},{2,6},{3,7},{4,0},{5,1},{6,2},{7,3},{8,12},{9,13},{10,... | collective-permute-start | bytes 4718600 | tf_op jit(solution)/shard_map/ppermute | solution.py:372
  251.1 45.3 %collective-permute-start.35 = (bf16[1376,256]{1,0:T(8,128)(2,1)S(1)}, bf16[1376,256]{1,0:T(8,128)(2,1)}, u32[]{:S(2)}, u32[]{:S(2)}) collective-permute-start(bf16[1376,256]{1,0:T(8,128)(2,1)S(1)} %broadcast_select_fusion.3.refs_0_), channel_id=1, source_target_pairs={{0,24},{1,25},{2,26},{3,27},{4,28},{5,29},{6,30},{7,31},{8,16},{9,... | collective-permute-start | bytes 2113544 | tf_op jit(solution)/shard_map/ppermute | solution.py:372
  252.3 58.9 %collective-permute-start.34 = (bf16[1376,256]{1,0:T(8,128)(2,1)S(1)}, bf16[1376,256]{1,0:T(8,128)(2,1)}, u32[]{:S(2)}, u32[]{:S(2)}) collective-permute-start(bf16[1376,256]{1,0:T(8,128)(2,1)S(1)} %broadcast_select_fusion.3.refs_0_), channel_id=1, source_target_pairs={{0,16},{1,17},{2,18},{3,19},{4,20},{5,21},{6,22},{7,23},{8,24},{9,... | collective-permute-start | bytes 2113544 | tf_op jit(solution)/shard_map/ppermute | solution.py:372
  253.4 57.7 %collective-permute-start.33 = (bf16[1376,256]{1,0:T(8,128)(2,1)S(1)}, bf16[1376,256]{1,0:T(8,128)(2,1)}, u32[]{:S(2)}, u32[]{:S(2)}) collective-permute-start(bf16[1376,256]{1,0:T(8,128)(2,1)S(1)} %broadcast_select_fusion.3.refs_0_), channel_id=1, source_target_pairs={{0,8},{1,9},{2,10},{3,11},{4,12},{5,13},{6,14},{7,15},{8,0},{9,1},... | collective-permute-start | bytes 2113544 | tf_op jit(solution)/shard_map/ppermute | solution.py:372
  253.7 57.4 %collective-permute-start.38 = (bf16[1376,256]{1,0:T(8,128)(2,1)S(1)}, bf16[1376,256]{1,0:T(8,128)(2,1)}, u32[]{:S(2)}, u32[]{:S(2)}) collective-permute-start(bf16[1376,256]{1,0:T(8,128)(2,1)S(1)} %collective-permute-done.29.refs_4_), channel_id=1, source_target_pairs={{0,24},{1,25},{2,26},{3,27},{4,28},{5,29},{6,30},{7,31},{8,16},{9,... | collective-permute-start | bytes 2113544 | tf_op jit(solution)/shard_map/ppermute | solution.py:372
  254.9 61.3 %collective-permute-start.37 = (bf16[1376,256]{1,0:T(8,128)(2,1)S(1)}, bf16[1376,256]{1,0:T(8,128)(2,1)}, u32[]{:S(2)}, u32[]{:S(2)}) collective-permute-start(bf16[1376,256]{1,0:T(8,128)(2,1)S(1)} %collective-permute-done.29.refs_4_), channel_id=1, source_target_pairs={{0,16},{1,17},{2,18},{3,19},{4,20},{5,21},{6,22},{7,23},{8,24},{9,... | collective-permute-start | bytes 2113544 | tf_op jit(solution)/shard_map/ppermute | solution.py:372
  296.4 19.9 %collective-permute-start.36 = (bf16[1376,256]{1,0:T(8,128)(2,1)S(1)}, bf16[1376,256]{1,0:T(8,128)(2,1)}, u32[]{:S(2)}, u32[]{:S(2)}) collective-permute-start(bf16[1376,256]{1,0:T(8,128)(2,1)S(1)} %collective-permute-done.29.refs_4_), channel_id=1, source_target_pairs={{0,8},{1,9},{2,10},{3,11},{4,12},{5,13},{6,14},{7,15},{8,0},{9,1},... | collective-permute-start | bytes 2113544 | tf_op jit(solution)/shard_map/ppermute | solution.py:372
  316.3 163.2 %reduce-scatter.8.cloned.1.call-start = ((), (), s32[]{:S(2)}) async-start(), calls=%async_computation.8 | async-start | bytes 7045120 | tf_op jit(solution)/shard_map/reduce_scatter | solution.py:438
  371.5 170.8 %reduce-scatter.10.cloned.1.call-start = ((), (), s32[]{:S(2)}) async-start(), calls=%async_computation.9 | async-start | bytes 7045120 | tf_op jit(solution)/shard_map/reduce_scatter | solution.py:438
  371.5 37.3 %collective-permute-start.43 = (bf16[1536,512]{1,0:T(8,128)(2,1)}, bf16[1536,512]{1,0:T(8,128)(2,1)S(1)}, u32[]{:S(2)}, u32[]{:S(2)}) collective-permute-start(bf16[1536,512]{1,0:T(8,128)(2,1)} %fusion.29), channel_id=1, source_target_pairs={{0,1},{1,0},{2,3},{3,2},{4,5},{5,4},{6,7},{7,6},{8,9},{9,8},{10,11... | collective-permute-start | bytes 4718600 | tf_op jit(solution)/shard_map/ppermute | solution.py:372
  385.1 15.8 %collective-permute-start.42 = (bf16[1536,512]{1,0:T(8,128)(2,1)}, bf16[1536,512]{1,0:T(8,128)(2,1)}, u32[]{:S(2)}, u32[]{:S(2)}) collective-permute-start(bf16[1536,512]{1,0:T(8,128)(2,1)} %fusion.28), channel_id=1, source_target_pairs={{0,4},{1,5},{2,6},{3,7},{4,0},{5,1},{6,2},{7,3},{8,12},{9,13},{10,... | collective-permute-start | bytes 4718600 | tf_op jit(solution)/shard_map/ppermute | solution.py:372
  408.9 242.8 %reduce-scatter.12.cloned.1.call-start = ((), (), s32[]{:S(2)}) async-start(), calls=%async_computation.10 | async-start | bytes 2621440 | tf_op jit(solution)/shard_map/reduce_scatter | solution.py:438
  432.4 35.7 %collective-permute-start.47 = (bf16[1536,512]{1,0:T(8,128)(2,1)S(1)}, bf16[1536,512]{1,0:T(8,128)(2,1)S(1)}, u32[]{:S(2)}, u32[]{:S(2)}) collective-permute-start(bf16[1536,512]{1,0:T(8,128)(2,1)S(1)} %convolution_convert_fusion.13), channel_id=1, source_target_pairs={{0,4},{1,5},{2,6},{3,7},{4,0},{5,1},{6,2},{7,3},{8,12},{9,13},{10,... | collective-permute-start | bytes 4718600 | tf_op jit(solution)/shard_map/ppermute | solution.py:372
  432.9 46.6 %collective-permute-start.50 = (bf16[1376,256]{1,0:T(8,128)(2,1)S(1)}, bf16[1376,256]{1,0:T(8,128)(2,1)}, u32[]{:S(2)}, u32[]{:S(2)}) collective-permute-start(bf16[1376,256]{1,0:T(8,128)(2,1)S(1)} %get-tuple-element.294), channel_id=1, source_target_pairs={{0,4},{1,5},{2,0},{3,1},{4,6},{5,7},{6,2},{7,3},{8,12},{9,13},{10,... | collective-permute-start | bytes 2113544 | tf_op jit(solution)/shard_map/ppermute | solution.py:372
  435.1 32.2 %collective-permute-start.49 = (bf16[1376,256]{1,0:T(8,128)(2,1)S(1)}, bf16[1376,256]{1,0:T(8,128)(2,1)S(1)}, u32[]{:S(2)}, u32[]{:S(2)}) collective-permute-start(bf16[1376,256]{1,0:T(8,128)(2,1)S(1)} %get-tuple-element.295), channel_id=1, source_target_pairs={{2,4},{3,5},{4,2},{5,3},{10,12},{11,13},{12,10},{13,11},{18,20},{1... | collective-permute-start | bytes 2113544 | tf_op jit(solution)/shard_map/ppermute | solution.py:372
  438.9 33.7 %collective-permute-start.46 = (bf16[1536,512]{1,0:T(8,128)(2,1)S(1)}, bf16[1536,512]{1,0:T(8,128)(2,1)S(1)}, u32[]{:S(2)}, u32[]{:S(2)}) collective-permute-start(bf16[1536,512]{1,0:T(8,128)(2,1)S(1)} %convolution_convert_fusion.8), channel_id=1, source_target_pairs={{0,4},{1,5},{2,6},{3,7},{4,0},{5,1},{6,2},{7,3},{8,12},{9,13},{10,... | collective-permute-start | bytes 4718600 | tf_op jit(solution)/shard_map/ppermute | solution.py:372
  441.7 33.7 %collective-permute-start.48 = (bf16[1536,512]{1,0:T(8,128)(2,1)S(1)}, bf16[1536,512]{1,0:T(8,128)(2,1)S(1)}, u32[]{:S(2)}, u32[]{:S(2)}) collective-permute-start(bf16[1536,512]{1,0:T(8,128)(2,1)S(1)} %convolution_convert_fusion.12), channel_id=1, source_target_pairs={{0,4},{1,5},{2,6},{3,7},{4,0},{5,1},{6,2},{7,3},{8,12},{9,13},{10,... | collective-permute-start | bytes 4718600 | tf_op jit(solution)/shard_map/ppermute | solution.py:372
  468.2 26.3 %collective-permute-start.45 = (bf16[1536,512]{1,0:T(8,128)(2,1)}, bf16[1536,512]{1,0:T(8,128)(2,1)}, u32[]{:S(2)}, u32[]{:S(2)}) collective-permute-start(bf16[1536,512]{1,0:T(8,128)(2,1)} %fusion.31), channel_id=1, source_target_pairs={{0,1},{1,0},{2,3},{3,2},{4,5},{5,4},{6,7},{7,6},{8,9},{9,8},{10,11... | collective-permute-start | bytes 4718600 | tf_op jit(solution)/shard_map/ppermute | solution.py:372
  507.9 27.5 %collective-permute-start.54 = (bf16[1536,512]{1,0:T(8,128)(2,1)}, bf16[1536,512]{1,0:T(8,128)(2,1)}, u32[]{:S(2)}, u32[]{:S(2)}) collective-permute-start(bf16[1536,512]{1,0:T(8,128)(2,1)} %add_convert_fusion.1), channel_id=1, source_target_pairs={{0,1},{1,0},{2,3},{3,2},{4,5},{5,4},{6,7},{7,6},{8,9},{9,8},{10,11... | collective-permute-start | bytes 4718600 | tf_op jit(solution)/shard_map/ppermute | solution.py:372
  509.5 20.1 %collective-permute-start.53 = (bf16[648,128]{1,0:T(8,128)(2,1)}, bf16[648,128]{1,0:T(8,128)(2,1)}, u32[]{:S(2)}, u32[]{:S(2)}) collective-permute-start(bf16[648,128]{1,0:T(8,128)(2,1)} %pad_maximum_fusion.4), channel_id=1, source_target_pairs={{24,0},{25,1},{26,2},{27,3},{28,4},{29,5},{30,6},{31,7}} | collective-permute-start | bytes 497672 | tf_op jit(solution)/shard_map/ppermute | solution.py:372
  513.4 16.3 %collective-permute-start.52 = (bf16[648,128]{1,0:T(8,128)(2,1)}, bf16[648,128]{1,0:T(8,128)(2,1)}, u32[]{:S(2)}, u32[]{:S(2)}) collective-permute-start(bf16[648,128]{1,0:T(8,128)(2,1)} %pad_maximum_fusion.4), channel_id=1, source_target_pairs={{16,0},{17,1},{18,2},{19,3},{20,4},{21,5},{22,6},{23,7},{24,8},{25... | collective-permute-start | bytes 497672 | tf_op jit(solution)/shard_map/ppermute | solution.py:372
  515.4 14.3 %collective-permute-start.51 = (bf16[648,128]{1,0:T(8,128)(2,1)}, bf16[648,128]{1,0:T(8,128)(2,1)}, u32[]{:S(2)}, u32[]{:S(2)}) collective-permute-start(bf16[648,128]{1,0:T(8,128)(2,1)} %pad_maximum_fusion.4), channel_id=1, source_target_pairs={{8,0},{9,1},{10,2},{11,3},{12,4},{13,5},{14,6},{15,7},{16,8},{17,9... | collective-permute-start | bytes 497672 | tf_op jit(solution)/shard_map/ppermute | solution.py:372
  543.7 31.6 %collective-permute-start.56 = (bf16[1376,256]{1,0:T(8,128)(2,1)S(1)}, bf16[1376,256]{1,0:T(8,128)(2,1)S(1)}, u32[]{:S(2)}, u32[]{:S(2)}) collective-permute-start(bf16[1376,256]{1,0:T(8,128)(2,1)S(1)} %get-tuple-element.292), channel_id=1, source_target_pairs={{0,4},{1,5},{2,0},{3,1},{4,6},{5,7},{6,2},{7,3},{8,12},{9,13},{10,... | collective-permute-start | bytes 2113544 | tf_op jit(solution)/shard_map/ppermute | solution.py:372
  543.8 30.6 %collective-permute-start.55 = (bf16[1376,256]{1,0:T(8,128)(2,1)S(1)}, bf16[1376,256]{1,0:T(8,128)(2,1)S(1)}, u32[]{:S(2)}, u32[]{:S(2)}) collective-permute-start(bf16[1376,256]{1,0:T(8,128)(2,1)S(1)} %get-tuple-element.293), channel_id=1, source_target_pairs={{2,4},{3,5},{4,2},{5,3},{10,12},{11,13},{12,10},{13,11},{18,20},{1... | collective-permute-start | bytes 2113544 | tf_op jit(solution)/shard_map/ppermute | solution.py:372
  581.5 162.1 %reduce-scatter.14.cloned.1.call-start = ((), (), s32[]{:S(2)}) async-start(), calls=%async_computation.11 | async-start | bytes 3276800 | tf_op jit(solution)/shard_map/reduce_scatter | solution.py:438
  587.5 28.5 %collective-permute-start.62 = (bf16[768,512]{1,0:T(8,128)(2,1)S(1)}, bf16[768,512]{1,0:T(8,128)(2,1)S(1)}, u32[]{:S(2)}, u32[]{:S(2)}) collective-permute-start(bf16[768,512]{1,0:T(8,128)(2,1)S(1)} %get-tuple-element.289), channel_id=1, source_target_pairs={{2,4},{3,5},{4,2},{5,3},{10,12},{11,13},{12,10},{13,11},{18,20},{1... | collective-permute-start | bytes 2359304 | tf_op jit(solution)/shard_map/ppermute | solution.py:372
  599.5 27.7 %collective-permute-start.61 = (bf16[1536,512]{1,0:T(8,128)(2,1)}, bf16[1536,512]{1,0:T(8,128)(2,1)}, u32[]{:S(2)}, u32[]{:S(2)}) collective-permute-start(bf16[1536,512]{1,0:T(8,128)(2,1)} %convolution_convert_fusion.10), channel_id=1, source_target_pairs={{0,4},{1,5},{2,6},{3,7},{4,0},{5,1},{6,2},{7,3},{8,12},{9,13},{10,... | collective-permute-start | bytes 4718600 | tf_op jit(solution)/shard_map/ppermute | solution.py:372
  599.5 32.4 %collective-permute-start.63 = (bf16[768,512]{1,0:T(8,128)(2,1)}, bf16[768,512]{1,0:T(8,128)(2,1)}, u32[]{:S(2)}, u32[]{:S(2)}) collective-permute-start(bf16[768,512]{1,0:T(8,128)(2,1)} %get-tuple-element.288), channel_id=1, source_target_pairs={{0,4},{1,5},{2,0},{3,1},{4,6},{5,7},{6,2},{7,3},{8,12},{9,13},{10,... | collective-permute-start | bytes 2359304 | tf_op jit(solution)/shard_map/ppermute | solution.py:372
  599.6 52.1 %collective-permute-start.60 = (bf16[1536,512]{1,0:T(8,128)(2,1)}, bf16[1536,512]{1,0:T(8,128)(2,1)}, u32[]{:S(2)}, u32[]{:S(2)}) collective-permute-start(bf16[1536,512]{1,0:T(8,128)(2,1)} %fusion.32), channel_id=1, source_target_pairs={{0,1},{1,0},{2,3},{3,2},{4,5},{5,4},{6,7},{7,6},{8,9},{9,8},{10,11... | collective-permute-start | bytes 4718600 | tf_op jit(solution)/shard_map/ppermute | solution.py:372
  663.7 39.4 %collective-permute-start.66 = (bf16[2,768,512]{2,1,0:T(8,128)(2,1)S(1)}, bf16[2,768,512]{2,1,0:T(8,128)(2,1)}, u32[]{:S(2)}, u32[]{:S(2)}) collective-permute-start(bf16[2,768,512]{2,1,0:T(8,128)(2,1)S(1)} %pad_maximum_fusion.1.refs_0_), channel_id=1, source_target_pairs={{1,0},{2,1},{3,2},{5,4},{6,5},{7,6},{9,8},{10,9},{11,10},{13,12},{... | collective-permute-start | bytes 4718600 | tf_op jit(solution)/shard_map/ppermute | solution.py:372
  665.0 38.1 %collective-permute-start.65 = (bf16[2,768,512]{2,1,0:T(8,128)(2,1)S(1)}, bf16[2,768,512]{2,1,0:T(8,128)(2,1)S(1)}, u32[]{:S(2)}, u32[]{:S(2)}) collective-permute-start(bf16[2,768,512]{2,1,0:T(8,128)(2,1)S(1)} %pad_maximum_fusion.1.refs_0_), channel_id=1, source_target_pairs={{0,1},{1,2},{2,3},{4,5},{5,6},{6,7},{8,9},{9,10},{10,11},{12,13},{... | collective-permute-start | bytes 4718600 | tf_op jit(solution)/shard_map/ppermute | solution.py:372
  669.3 33.1 %collective-permute-start.69 = (f32[2,2048]{1,0:T(2,128)S(1)}, f32[2,2048]{1,0:T(2,128)S(1)}, u32[]{:S(2)}, u32[]{:S(2)}) collective-permute-start(f32[2,2048]{1,0:T(2,128)S(1)} %constant_dynamic-update-slice_fusion), channel_id=1, source_target_pairs={{0,3},{1,2},{2,1},{3,0},{4,7},{5,6},{6,5},{7,4},{8,11},{9,10},{10,... | collective-permute-start | bytes 49160 | tf_op jit(solution)/shard_map/ppermute | solution.py:372
  669.4 33.3 %collective-permute-start.68 = (f32[2,2048]{1,0:T(2,128)S(1)}, f32[2,2048]{1,0:T(2,128)S(1)}, u32[]{:S(2)}, u32[]{:S(2)}) collective-permute-start(f32[2,2048]{1,0:T(2,128)S(1)} %constant_dynamic-update-slice_fusion), channel_id=1, source_target_pairs={{0,2},{1,3},{2,0},{3,1},{4,6},{5,7},{6,4},{7,5},{8,10},{9,11},{10,... | collective-permute-start | bytes 49160 | tf_op jit(solution)/shard_map/ppermute | solution.py:372
  670.5 32.6 %collective-permute-start.67 = (f32[2,2048]{1,0:T(2,128)S(1)}, f32[2,2048]{1,0:T(2,128)S(1)}, u32[]{:S(2)}, u32[]{:S(2)}) collective-permute-start(f32[2,2048]{1,0:T(2,128)S(1)} %constant_dynamic-update-slice_fusion), channel_id=1, source_target_pairs={{0,1},{1,0},{2,3},{3,2},{4,5},{5,4},{6,7},{7,6},{8,9},{9,8},{10,11... | collective-permute-start | bytes 49160 | tf_op jit(solution)/shard_map/ppermute | solution.py:372
  704.9 38.6 %collective-permute-start.71 = (bf16[2,768,512]{2,1,0:T(8,128)(2,1)}, bf16[2,768,512]{2,1,0:T(8,128)(2,1)}, u32[]{:S(2)}, u32[]{:S(2)}) collective-permute-start(bf16[2,768,512]{2,1,0:T(8,128)(2,1)} %collective-permute-done.66.refs_4_), channel_id=1, source_target_pairs={{1,0},{2,1},{5,4},{6,5},{9,8},{10,9},{13,12},{14,13},{17,16},{18,1... | collective-permute-start | bytes 4718600 | tf_op jit(solution)/shard_map/ppermute | solution.py:372
  743.5 57.5 %collective-permute-start.73 = (bf16[2,768,512]{2,1,0:T(8,128)(2,1)}, bf16[2,768,512]{2,1,0:T(8,128)(2,1)}, u32[]{:S(2)}, u32[]{:S(2)}) collective-permute-start(bf16[2,768,512]{2,1,0:T(8,128)(2,1)} %collective-permute-done.70.refs_2_), channel_id=1, source_target_pairs={{2,3},{6,7},{10,11},{14,15},{18,19},{22,23},{26,27},{30,31}} | collective-permute-start | bytes 4718600 | tf_op jit(solution)/shard_map/ppermute | solution.py:372
  745.5 55.5 %collective-permute-start.74 = (bf16[2,768,512]{2,1,0:T(8,128)(2,1)}, bf16[2,768,512]{2,1,0:T(8,128)(2,1)}, u32[]{:S(2)}, u32[]{:S(2)}) collective-permute-start(bf16[2,768,512]{2,1,0:T(8,128)(2,1)} %collective-permute-done.71.refs_5_), channel_id=1, source_target_pairs={{1,0},{5,4},{9,8},{13,12},{17,16},{21,20},{25,24},{29,28}} | collective-permute-start | bytes 4718600 | tf_op jit(solution)/shard_map/ppermute | solution.py:372
  750.8 27.3 %collective-permute-start.77 = (bf16[256,640]{1,0:T(8,128)(2,1)S(1)}, bf16[256,640]{1,0:T(8,128)(2,1)S(1)}, u32[]{:S(2)}, u32[]{:S(2)}) collective-permute-start(bf16[256,640]{1,0:T(8,128)(2,1)S(1)} %get-tuple-element.299), channel_id=1, source_target_pairs={{0,4},{1,5},{2,0},{3,1},{4,6},{5,7},{6,2},{7,3},{8,12},{9,13},{10,... | collective-permute-start | bytes 983048 | tf_op jit(solution)/shard_map/ppermute | solution.py:372
  756.9 21.2 %collective-permute-start.78 = (bf16[256,512]{1,0:T(8,128)(2,1)S(1)}, bf16[256,512]{1,0:T(8,128)(2,1)S(1)}, u32[]{:S(2)}, u32[]{:S(2)}) collective-permute-start(bf16[256,512]{1,0:T(8,128)(2,1)S(1)} %get-tuple-element.300), channel_id=1, source_target_pairs={{2,4},{3,5},{4,2},{5,3},{10,12},{11,13},{12,10},{13,11},{18,20},{1... | collective-permute-start | bytes 786440 | tf_op jit(solution)/shard_map/ppermute | solution.py:372
  759.8 36.9 %collective-permute-start.76 = (bf16[256,640]{1,0:T(8,128)(2,1)S(1)}, bf16[256,640]{1,0:T(8,128)(2,1)S(1)}, u32[]{:S(2)}, u32[]{:S(2)}) collective-permute-start(bf16[256,640]{1,0:T(8,128)(2,1)S(1)} %get-tuple-element.298), channel_id=1, source_target_pairs={{2,4},{3,5},{4,2},{5,3},{10,12},{11,13},{12,10},{13,11},{18,20},{1... | collective-permute-start | bytes 983048 | tf_op jit(solution)/shard_map/ppermute | solution.py:372
  778.1 23.2 %collective-permute-start.81 = (bf16[1376,256]{1,0:T(8,128)(2,1)}, bf16[1376,256]{1,0:T(8,128)(2,1)}, u32[]{:S(2)}, u32[]{:S(2)}) collective-permute-start(bf16[1376,256]{1,0:T(8,128)(2,1)} %get-tuple-element.291), channel_id=1, source_target_pairs={{0,4},{1,5},{2,0},{3,1},{4,6},{5,7},{6,2},{7,3},{8,12},{9,13},{10,... | collective-permute-start | bytes 2113544 | tf_op jit(solution)/shard_map/ppermute | solution.py:372
  778.1 33.7 %collective-permute-start.80 = (bf16[1376,256]{1,0:T(8,128)(2,1)}, bf16[1376,256]{1,0:T(8,128)(2,1)}, u32[]{:S(2)}, u32[]{:S(2)}) collective-permute-start(bf16[1376,256]{1,0:T(8,128)(2,1)} %get-tuple-element.290), channel_id=1, source_target_pairs={{2,4},{3,5},{4,2},{5,3},{10,12},{11,13},{12,10},{13,11},{18,20},{1... | collective-permute-start | bytes 2113544 | tf_op jit(solution)/shard_map/ppermute | solution.py:372
  801.0 22.9 %collective-permute-start.82 = (f32[2,2048]{1,0:T(2,128)S(1)}, f32[2,2048]{1,0:T(2,128)S(1)}, u32[]{:S(2)}, u32[]{:S(2)}) collective-permute-start(f32[2,2048]{1,0:T(2,128)S(1)} %add.580), channel_id=1, source_target_pairs={{0,16},{1,17},{2,18},{3,19},{4,20},{5,21},{6,22},{7,23},{8,24},{9,... | collective-permute-start | bytes 49160 | tf_op jit(solution)/shard_map/ppermute | solution.py:372
  (128 other events, 1329.9 us)
Sparse Core Ops, SparseCore 0:
  101.6 77.0 all-gather.2
  192.4 79.2 all-gather.4
  316.4 64.6 reduce-scatter.5
  384.1 64.6 reduce-scatter.7
  451.7 68.1 reduce-scatter.9
  581.6 35.1 reduce-scatter.11
  651.9 38.6 reduce-scatter.13

commit v7 on v6

--- a/solution.py
+++ b/solution.py
@@ -662,10 +662,12 @@
         [r * piece for r, _ in mixer_parts],
         0,
     )
-    carried, (mlp_arrived, output_sum) = scan_blocks(
-        grad_local, list(range(CORES))[::-1], -1, (mlp_arrived, output_sum)
-    )
-    carried, output_sum, gate_sum, up_sum = tie(carried, output_sum, gate_sum, up_sum)
+    carried, output_sum = scan_blocks(
+        grad_local, list(range(CORES))[::-1], -1, output_sum
+    )
+    carried, output_sum, gate_sum, up_sum, mlp_arrived = tie(
+        carried, output_sum, gate_sum, up_sum, mlp_arrived
+    )
     up_halves = send_halves(up_sum, 1)
     output_sum = sum_chips(output_sum, 0)
     grad_qkv = mixer_back(
@@ -742,6 +744,7 @@
     for hop in hops:
         gain_grads = gain_grads + hop(gain_grads)
     input_grad = widen(ups + downs[1:], feat_rank, core, micro, group, width)
+    input_grad, gate_halves = tie(input_grad, gate_halves)
 
     shard = width // seq_count
     gain_grads = lax.dynamic_slice_in_dim(gain_grads, seq_rank * shard, shard, 1)

time: 845 us -> 848 us (level)
  waiting for transfers between devices: 300 us -> 290 us
  starting transfers between devices: 103 us -> 112 us
    ppermute x83, waiting for transfers between devices: 300 us -> 290 us  [move(): return lax.ppermute(value, ('seq', 'feat'), pairs)]
    ppermute x83, starting transfers between devices: 102 us -> 112 us  [move(): return lax.ppermute(value, ('seq', 'feat'), pairs)]
    unnamed x206 -> x210, local copies, waits for them, and re-layouts: 23.2 us -> 24.4 us
  transfers between devices with their start and end apart: 90 -> 90, of which waited for: 30 -> 29; matrix products, arithmetic and copies ran while one was open for 34% -> 35% of each run, Pallas kernels for 9% -> 9%
where the time goes in v7:
time: 848 us; the launch traced here: 835 us
  waiting for transfers between devices  290 us (34%)
  matrix products  194 us (23%)
  starting transfers between devices  112 us (13%)
  Pallas kernels  79.1 us (9%)
  other arithmetic  74.2 us (9%)
  local copies, waits for them, and re-layouts  52.8 us (6%)
  between operations  24.1 us (3%)
  blocking collectives  9.09 us (1%)
    ppermute x83, waiting for transfers between devices, move(): return lax.ppermute(value, ('seq', 'feat'), pairs)  290 us
    dot_general x36, matrix products, dot(): lax.dot_general(a, b, (((ca,), (cb,)), ((), ())), preferred_element_type=...  194 us
    ppermute x83, starting transfers between devices, move(): return lax.ppermute(value, ('seq', 'feat'), pairs)  112 us
    pallas_call x4, Pallas kernels, run(): pl.pallas_call(functools.partial(kernel, heads=heads, block=block), grid_...  47.1 us
    unnamed x210, local copies, waits for them, and re-layouts  24.4 us
    pallas_call x9, Pallas kernels, place(): pl.pallas_call(functools.partial(place_kernel, axis=axis), grid_spec=pltp...  23.1 us
  transfers between devices with their start and end apart: 90, of which 29 were waited for; matrix products, arithmetic and copies ran while one was open for 35% of the time, Pallas kernels for 9%

profile of v7, /device:TPU:7, one launch (start us, length us, event | category | flops | bytes accessed | tf_op | source)
XLA Modules:
  0.0 835.4 jit_solution(5081821742620070662)
XLA Ops:
  11.5 4.1 collective-permute-start.1
  19.8 9.1 %all_gather.9 = bf16[2,2048]{1,0:T(2,128)(2,1)} all-gather(bf16[2,256]{1,0:T(2,128)(2,1)S(1)} %pad_maximum_fusion.5), channel_id=1, replica_groups=mesh['seq'=8,'feat'=4] {'seq'}, dimensions={1}, use_global_device_ids=true | all-gather | bytes 9216 | tf_op jit(solution)/shard_map/all_gather | solution.py:497
  39.2 5.5 collective-permute-done.9
  54.8 6.2 collective-permute-done.8.refs_7_
  72.5 5.3 convolution_convert_fusion.7
  79.3 4.3 shard_map.242
  89.1 6.4 collective-permute-done.15
  114.6 9.5 %shard_map.243 = (bf16[1536,512]{1,0:T(8,128)(2,1)}, f32[1536,512]{1,0:T(8,128)}) custom-call(s32[2,5]{1,0:T(2,128)S(1)} %copy-done.35, bf16[1536,64]{1,0:T(8,128)(2,1)S(1)} %copy-done.21, bf16[1536,64]{1,0:T(8,128)(2,1)S(1)} %get-tuple-element.292.k_ref, bf16[1536,512]{1,0:T(8,128)(2,1)S(1)} %slice.236.v_ref, bf16[2,4,256,256]{3,2,1,0:T(8,128)(2,1)S(1)} %fusion.66.s_ref, ...), custom_call_target="tpu_custom_call" | custom-call | flops 6144000000 | bytes 9216000 | tf_op jit(solution)/shard_map/pallas_call | solution.py:220
  124.1 23.5 %collective-permute-done.17 = bf16[1376,256]{1,0:T(8,128)(2,1)S(1)} collective-permute-done((bf16[1376,256]{1,0:T(8,128)(2,1)}, bf16[1376,256]{1,0:T(8,128)(2,1)S(1)}, u32[]{:S(2)}, u32[]{:S(2)}) %collective-permute-start.17) | collective-permute-done | bytes 704544 | tf_op jit(solution)/shard_map/ppermute | solution.py:372
  150.5 4.6 collective-permute-start.28
  155.1 7.6 collective-permute-done.20.refs_2_
  164.5 12.3 %collective-permute-done.23.refs_6_ = bf16[256,512]{1,0:T(8,128)(2,1)S(1)} collective-permute-done((bf16[256,512]{1,0:T(8,128)(2,1)S(1)}, bf16[256,512]{1,0:T(8,128)(2,1)S(1)}, u32[]{:S(2)}, u32[]{:S(2)}) %collective-permute-start.23) | collective-permute-done | bytes 262176 | tf_op jit(solution)/shard_map/ppermute | solution.py:372
  178.3 4.0 dynamic-slice_bitcast_fusion.refs_0_
  208.9 35.0 %collective-permute-done.31.refs_2_ = bf16[1536,512]{1,0:T(8,128)(2,1)} collective-permute-done((bf16[1536,512]{1,0:T(8,128)(2,1)S(1)}, bf16[1536,512]{1,0:T(8,128)(2,1)}, u32[]{:S(2)}, u32[]{:S(2)}) %collective-permute-start.31) | collective-permute-done | bytes 1572896 | tf_op jit(solution)/shard_map/ppermute | solution.py:372
  243.9 4.5 shard_map.241
  261.5 4.1 multiply_convert_fusion
  268.4 12.3 %convolution_convert_fusion.5 = bf16[1536,1376]{0,1:T(8,128)(2,1)} fusion(bf16[1536,2048]{1,0:T(8,128)(2,1)S(1)} %multiply_convert_fusion, bf16[1376,2048]{1,0:T(8,128)(2,1)} %all-gather.3.cloned.1.call-done), kind=kOutput, calls=%fused_computation.37 | convolution fusion | flops 8659156992 | bytes 16154624 | tf_op jit(solution)/shard_map/dot_general | solution.py:262
  280.7 15.7 %fusion.15 = (bf16[1536,1376]{0,1:T(8,128)(2,1)S(1)}, bf16[1536,1376]{0,1:T(8,128)(2,1)}) fusion(bf16[1536,1376]{0,1:T(8,128)(2,1)} %convolution_convert_fusion.5, bf16[1536,2048]{1,0:T(8,128)(2,1)} %copy-done.54, bf16[1376,2048]{1,0:T(8,128)(2,1)} %all-gather.5.cloned.1.call-done), kind=kOutput, calls=%fused_computation.31 | convolution fusion | flops 8676065280 | bytes 24608768 | tf_op jit(solution)/shard_map/dot_general | solution.py:262
  298.6 12.6 %convolution_convert_fusion.2 = bf16[1376,2048]{1,0:T(8,128)(2,1)} fusion(bf16[1536,1376]{0,1:T(8,128)(2,1)S(1)} %get-tuple-element.177, bf16[1536,2048]{1,0:T(8,128)(2,1)} %copy-done.5), kind=kOutput, calls=%fused_computation.34 | convolution fusion | flops 8659861504 | bytes 16154624 | tf_op jit(solution)/shard_map/dot_general | solution.py:262
  311.2 5.0 collective-permute-done.37.refs_6_
  316.4 3.9 shard_map.248
  320.3 13.2 %convolution_convert_fusion.3 = bf16[1536,1376]{0,1:T(8,128)(2,1)S(1)} fusion(bf16[1536,2048]{1,0:T(8,128)(2,1)} %copy-done.5, bf16[1376,2048]{1,0:T(8,128)(2,1)S(1)} %shard_map.248), kind=kOutput, calls=%fused_computation.35 | convolution fusion | flops 8659156992 | bytes 16154624 | tf_op jit(solution)/shard_map/dot_general | solution.py:262
  333.6 6.3 fusion.64
  340.0 5.2 fusion.58
  352.6 4.1 fusion.61
  356.8 4.0 fusion.29
  360.8 10.6 %convolution_convert_fusion = bf16[1376,2048]{1,0:T(8,128)(2,1)} fusion(bf16[1536,1376]{0,1:T(8,128)(2,1)S(1)} %get-tuple-element.168, bf16[1536,2048]{1,0:T(8,128)(2,1)S(1)} %bitcast.131), kind=kOutput, calls=%fused_computation.32 | convolution fusion | flops 8659861504 | bytes 16154624 | tf_op jit(solution)/shard_map/dot_general | solution.py:262
  372.7 5.5 fusion.52
  378.3 6.7 fusion.28
  385.3 10.6 %convolution_convert_fusion.1 = bf16[1376,2048]{1,0:T(8,128)(2,1)} fusion(bf16[1536,1376]{0,1:T(8,128)(2,1)S(1)} %bitcast.135, bf16[1536,2048]{1,0:T(8,128)(2,1)S(1)} %bitcast.133), kind=kOutput, calls=%fused_computation.33 | convolution fusion | flops 8659861504 | bytes 16154624 | tf_op jit(solution)/shard_map/dot_general | solution.py:262
  395.9 4.8 fusion.55
  400.7 8.0 fusion.20
  409.9 5.4 fusion.129
  415.3 3.6 convolution_convert_fusion.9
  422.9 3.9 fusion.31
  426.8 5.4 convolution_convert_fusion.13
  442.0 25.0 %collective-permute-done.49 = bf16[1376,256]{1,0:T(8,128)(2,1)S(1)} collective-permute-done((bf16[1376,256]{1,0:T(8,128)(2,1)S(1)}, bf16[1376,256]{1,0:T(8,128)(2,1)S(1)}, u32[]{:S(2)}, u32[]{:S(2)}) %collective-permute-start.49) | collective-permute-done | bytes 704544 | tf_op jit(solution)/shard_map/ppermute | solution.py:372
  468.0 4.4 convert_add_fusion.4
  475.2 4.1 add_convert_fusion.1
  479.3 15.0 %collective-permute-done.45 = bf16[1536,512]{1,0:T(8,128)(2,1)} collective-permute-done((bf16[1536,512]{1,0:T(8,128)(2,1)}, bf16[1536,512]{1,0:T(8,128)(2,1)}, u32[]{:S(2)}, u32[]{:S(2)}) %collective-permute-start.45) | collective-permute-done | bytes 1572896 | tf_op jit(solution)/shard_map/ppermute | solution.py:372
  494.3 4.5 convert_add_fusion.3.do_ref
  499.9 6.8 shard_map.249
  509.2 4.0 collective-permute-start.53
  536.5 8.9 %collective-permute-done.54 = bf16[1536,512]{1,0:T(8,128)(2,1)} collective-permute-done((bf16[1536,512]{1,0:T(8,128)(2,1)}, bf16[1536,512]{1,0:T(8,128)(2,1)}, u32[]{:S(2)}, u32[]{:S(2)}) %collective-permute-start.54) | collective-permute-done | bytes 1572896 | tf_op jit(solution)/shard_map/ppermute | solution.py:372
  551.0 26.4 %shard_map.251 = (bf16[1536,64]{1,0:T(8,128)(2,1)S(1)}, bf16[1536,64]{1,0:T(8,128)(2,1)S(1)}, bf16[1536,512]{1,0:T(8,128)(2,1)S(1)}) custom-call(s32[2,5]{1,0:T(2,128)S(1)} %copy-done.36, bf16[1536,64]{1,0:T(8,128)(2,1)S(1)} %copy-done.22, bf16[1536,64]{1,0:T(8,128)(2,1)S(1)} %copy-done.20, bf16[1536,512]{1,0:T(8,128)(2,1)} %copy-done.12, ...), custom_call_target="tpu_custom_call" | custom-call | flops 15360000000 | bytes 9216000 | tf_op jit(solution)/shard_map/pallas_call | solution.py:220
  580.3 4.2 convolution_convert_fusion.11
  584.7 3.9 add_convert_fusion
  590.2 5.0 collective-permute-start.62
  595.9 4.2 fusion.32
  604.5 13.9 %collective-permute-done.62 = bf16[768,512]{1,0:T(8,128)(2,1)S(1)} collective-permute-done((bf16[768,512]{1,0:T(8,128)(2,1)S(1)}, bf16[768,512]{1,0:T(8,128)(2,1)S(1)}, u32[]{:S(2)}, u32[]{:S(2)}) %collective-permute-start.62) | collective-permute-done | bytes 786464 | tf_op jit(solution)/shard_map/ppermute | solution.py:372
  619.4 10.1 %convolution_convert_fusion.6 = bf16[2048,640]{1,0:T(8,128)(2,1)} fusion(bf16[1536,640]{1,0:T(8,128)(2,1)} %copy-done.60, bf16[1536,2048]{1,0:T(8,128)(2,1)} %copy-done.2, f32[2048]{0:T(1024)} %bitcast.153, f32[1536]{0:T(1024)} %copy-done.76), kind=kOutput, calls=%fused_computation.56 | convolution fusion | flops 4040425472 | bytes 10893312 | tf_op jit(solution)/shard_map/dot_general | solution.py:262
  629.5 4.8 convolution_add_fusion
  634.3 21.5 %collective-permute-done.60 = bf16[1536,512]{1,0:T(8,128)(2,1)} collective-permute-done((bf16[1536,512]{1,0:T(8,128)(2,1)}, bf16[1536,512]{1,0:T(8,128)(2,1)}, u32[]{:S(2)}, u32[]{:S(2)}) %collective-permute-start.60) | collective-permute-done | bytes 1572896 | tf_op jit(solution)/shard_map/ppermute | solution.py:372
  655.8 6.3 fusion.25
  668.1 4.3 collective-permute-start.65
  676.2 29.4 %collective-permute-done.69 = f32[2,2048]{1,0:T(2,128)S(1)} collective-permute-done((f32[2,2048]{1,0:T(2,128)S(1)}, f32[2,2048]{1,0:T(2,128)S(1)}, u32[]{:S(2)}, u32[]{:S(2)}) %collective-permute-start.69) | collective-permute-done | bytes 16416 | tf_op jit(solution)/shard_map/ppermute | solution.py:372
  714.5 8.0 collective-permute-start.81
  728.3 17.4 %collective-permute-done.71.refs_5_ = bf16[2,768,512]{2,1,0:T(8,128)(2,1)} collective-permute-done((bf16[2,768,512]{2,1,0:T(8,128)(2,1)}, bf16[2,768,512]{2,1,0:T(8,128)(2,1)}, u32[]{:S(2)}, u32[]{:S(2)}) %collective-permute-start.71) | collective-permute-done | bytes 1572896 | tf_op jit(solution)/shard_map/ppermute | solution.py:372
  750.0 7.0 collective-permute-start.79
  757.0 7.0 collective-permute-start.78
  770.5 14.6 %collective-permute-done.78 = bf16[256,640]{1,0:T(8,128)(2,1)S(1)} collective-permute-done((bf16[256,640]{1,0:T(8,128)(2,1)S(1)}, bf16[256,640]{1,0:T(8,128)(2,1)S(1)}, u32[]{:S(2)}, u32[]{:S(2)}) %collective-permute-start.78) | collective-permute-done | bytes 327712 | tf_op jit(solution)/shard_map/ppermute | solution.py:372
  787.6 12.7 %collective-permute-done.76 = bf16[1376,256]{1,0:T(8,128)(2,1)} collective-permute-done((bf16[1376,256]{1,0:T(8,128)(2,1)}, bf16[1376,256]{1,0:T(8,128)(2,1)}, u32[]{:S(2)}, u32[]{:S(2)}) %collective-permute-start.76) | collective-permute-done | bytes 704544 | tf_op jit(solution)/shard_map/ppermute | solution.py:372
  801.6 14.8 %collective-permute-done.74.refs_6_ = bf16[2,768,512]{2,1,0:T(8,128)(2,1)} collective-permute-done((bf16[2,768,512]{2,1,0:T(8,128)(2,1)}, bf16[2,768,512]{2,1,0:T(8,128)(2,1)}, u32[]{:S(2)}, u32[]{:S(2)}) %collective-permute-start.74) | collective-permute-done | bytes 1572896 | tf_op jit(solution)/shard_map/ppermute | solution.py:372
  816.5 8.9 %shard_map.252 = f32[2,768,2048]{2,1,0:T(8,128)} custom-call(s32[2]{0:T(128)S(1)} %pad_add_fusion.5.where, bf16[2,768,512]{2,1,0:T(8,128)(2,1)S(1)} %pad_maximum_fusion.1.refs_0_, bf16[2,768,512]{2,1,0:T(8,128)(2,1)S(1)} %collective-permute-done.65.refs_1_, bf16[2,768,512]{2,1,0:T(8,128)(2,1)S(1)} %copy-done.11, ...), custom_call_target="tpu_custom_call" | custom-call | tf_op jit(solution)/shard_map/pallas_call | solution.py:321
  (517 shorter events, 221.0 us)
Async XLA Ops:
  7.2 236.6 %all-gather.3.cloned.1.call-start = ((), (), s32[]{:S(2)}) async-start(), calls=%async_computation.5 | async-start | bytes 7045120 | tf_op jit(solution)/shard_map/all_gather | solution.py:433
  10.8 20.5 %collective-permute-start.2 = (bf16[256,640]{1,0:T(8,128)(2,1)}, bf16[256,640]{1,0:T(8,128)(2,1)}, u32[]{:S(2)}, u32[]{:S(2)}) collective-permute-start(bf16[256,640]{1,0:T(8,128)(2,1)} %pad_maximum_fusion.2), channel_id=1, source_target_pairs={{0,2},{1,3},{2,6},{3,7},{4,0},{5,1},{6,4},{7,5},{8,10},{9,11},{10,... | collective-permute-start | bytes 983048 | tf_op jit(solution)/shard_map/ppermute | solution.py:372
  11.5 18.6 %collective-permute-start.1 = (bf16[256,640]{1,0:T(8,128)(2,1)}, bf16[256,640]{1,0:T(8,128)(2,1)}, u32[]{:S(2)}, u32[]{:S(2)}) collective-permute-start(bf16[256,640]{1,0:T(8,128)(2,1)} %pad_maximum_fusion.2), channel_id=1, source_target_pairs={{2,4},{3,5},{4,2},{5,3},{10,12},{11,13},{12,10},{13,11},{18,20},{1... | collective-permute-start | bytes 983048 | tf_op jit(solution)/shard_map/ppermute | solution.py:372
  17.8 49.1 %collective-permute-start = (bf16[768,2048]{1,0:T(8,128)(2,1)S(1)}, bf16[768,2048]{1,0:T(8,128)(2,1)}, u32[]{:S(2)}, u32[]{:S(2)}) collective-permute-start(bf16[768,2048]{1,0:T(8,128)(2,1)S(1)} %dynamic-slice_bitcast_fusion.1.refs_0_), channel_id=1, source_target_pairs={{0,4},{1,5},{2,6},{3,7},{4,0},{5,1},{6,2},{7,3},{8,12},{9,13},{10,... | collective-permute-start | bytes 9437192 | tf_op jit(solution)/shard_map/ppermute | solution.py:372
  44.7 19.1 %collective-permute-start.10 = (bf16[256,512]{1,0:T(8,128)(2,1)}, bf16[256,512]{1,0:T(8,128)(2,1)S(1)}, u32[]{:S(2)}, u32[]{:S(2)}) collective-permute-start(bf16[256,512]{1,0:T(8,128)(2,1)} %param.22), channel_id=1, source_target_pairs={{0,2},{1,3},{2,6},{3,7},{4,0},{5,1},{6,4},{7,5},{8,10},{9,11},{10,... | collective-permute-start | bytes 786440 | tf_op jit(solution)/shard_map/ppermute | solution.py:372
  63.8 34.1 %collective-permute-start.16 = (bf16[1376,256]{1,0:T(8,128)(2,1)}, bf16[1376,256]{1,0:T(8,128)(2,1)}, u32[]{:S(2)}, u32[]{:S(2)}) collective-permute-start(bf16[1376,256]{1,0:T(8,128)(2,1)} %bitcast.8), channel_id=1, source_target_pairs={{0,2},{1,3},{2,6},{3,7},{4,0},{5,1},{6,4},{7,5},{8,10},{9,11},{10,... | collective-permute-start | bytes 2113544 | tf_op jit(solution)/shard_map/ppermute | solution.py:372
  64.9 30.6 %collective-permute-start.15 = (bf16[1376,256]{1,0:T(8,128)(2,1)}, bf16[1376,256]{1,0:T(8,128)(2,1)}, u32[]{:S(2)}, u32[]{:S(2)}) collective-permute-start(bf16[1376,256]{1,0:T(8,128)(2,1)} %bitcast.8), channel_id=1, source_target_pairs={{2,4},{3,5},{4,2},{5,3},{10,12},{11,13},{12,10},{13,11},{18,20},{1... | collective-permute-start | bytes 2113544 | tf_op jit(solution)/shard_map/ppermute | solution.py:372
  101.5 179.2 %all-gather.5.cloned.1.call-start = ((), (), s32[]{:S(2)}) async-start(), calls=%async_computation.6 | async-start | bytes 7045120 | tf_op jit(solution)/shard_map/all_gather | solution.py:433
  111.7 35.9 %collective-permute-start.17 = (bf16[1376,256]{1,0:T(8,128)(2,1)}, bf16[1376,256]{1,0:T(8,128)(2,1)S(1)}, u32[]{:S(2)}, u32[]{:S(2)}) collective-permute-start(bf16[1376,256]{1,0:T(8,128)(2,1)} %bitcast.144), channel_id=1, source_target_pairs={{2,4},{3,5},{4,2},{5,3},{10,12},{11,13},{12,10},{13,11},{18,20},{1... | collective-permute-start | bytes 2113544 | tf_op jit(solution)/shard_map/ppermute | solution.py:372
  114.5 33.5 %collective-permute-start.18 = (bf16[1376,256]{1,0:T(8,128)(2,1)}, bf16[1376,256]{1,0:T(8,128)(2,1)S(1)}, u32[]{:S(2)}, u32[]{:S(2)}) collective-permute-start(bf16[1376,256]{1,0:T(8,128)(2,1)} %bitcast.145), channel_id=1, source_target_pairs={{0,2},{1,3},{2,6},{3,7},{4,0},{5,1},{6,4},{7,5},{8,10},{9,11},{10,... | collective-permute-start | bytes 2113544 | tf_op jit(solution)/shard_map/ppermute | solution.py:372
  148.8 43.5 %collective-permute-start.26 = (bf16[1536,512]{1,0:T(8,128)(2,1)}, bf16[1536,512]{1,0:T(8,128)(2,1)}, u32[]{:S(2)}, u32[]{:S(2)}) collective-permute-start(bf16[1536,512]{1,0:T(8,128)(2,1)} %get-tuple-element.144.o_ref), channel_id=1, source_target_pairs={{0,1},{1,0},{2,3},{3,2},{4,5},{5,4},{6,7},{7,6},{8,9},{9,8},{10,11... | collective-permute-start | bytes 4718600 | tf_op jit(solution)/shard_map/ppermute | solution.py:372
  149.7 14.7 %collective-permute-start.19 = (bf16[256,512]{1,0:T(8,128)(2,1)S(1)}, bf16[256,512]{1,0:T(8,128)(2,1)S(1)}, u32[]{:S(2)}, u32[]{:S(2)}) collective-permute-start(bf16[256,512]{1,0:T(8,128)(2,1)S(1)} %copy-done.13), channel_id=1, source_target_pairs={{0,8},{1,9},{2,10},{3,11},{4,12},{5,13},{6,14},{7,15},{8,0},{9,1},... | collective-permute-start | bytes 786440 | tf_op jit(solution)/shard_map/ppermute | solution.py:372
  150.5 42.9 %collective-permute-start.28 = (bf16[1376,256]{1,0:T(8,128)(2,1)}, bf16[1376,256]{1,0:T(8,128)(2,1)}, u32[]{:S(2)}, u32[]{:S(2)}) collective-permute-start(bf16[1376,256]{1,0:T(8,128)(2,1)} %param.25), channel_id=1, source_target_pairs={{2,4},{3,5},{4,2},{5,3},{10,12},{11,13},{12,10},{13,11},{18,20},{1... | collective-permute-start | bytes 2113544 | tf_op jit(solution)/shard_map/ppermute | solution.py:372
  155.0 41.9 %collective-permute-start.25 = (bf16[1536,512]{1,0:T(8,128)(2,1)}, bf16[1536,512]{1,0:T(8,128)(2,1)}, u32[]{:S(2)}, u32[]{:S(2)}) collective-permute-start(bf16[1536,512]{1,0:T(8,128)(2,1)} %get-tuple-element.144.o_ref), channel_id=1, source_target_pairs={{0,4},{1,5},{2,6},{3,7},{4,0},{5,1},{6,2},{7,3},{8,12},{9,13},{10,... | collective-permute-start | bytes 4718600 | tf_op jit(solution)/shard_map/ppermute | solution.py:372
  184.0 59.9 %collective-permute-start.11 = (bf16[768,2048]{1,0:T(8,128)(2,1)}, bf16[768,2048]{1,0:T(8,128)(2,1)}, u32[]{:S(2)}, u32[]{:S(2)}) collective-permute-start(bf16[768,2048]{1,0:T(8,128)(2,1)} %dynamic-slice_bitcast_fusion.refs_0_), channel_id=1, source_target_pairs={{0,4},{1,5},{2,6},{3,7},{4,0},{5,1},{6,2},{7,3},{8,12},{9,13},{10,... | collective-permute-start | bytes 9437192 | tf_op jit(solution)/shard_map/ppermute | solution.py:372
  189.2 18.7 %collective-permute-start.29 = (bf16[1376,256]{1,0:T(8,128)(2,1)}, bf16[1376,256]{1,0:T(8,128)(2,1)S(1)}, u32[]{:S(2)}, u32[]{:S(2)}) collective-permute-start(bf16[1376,256]{1,0:T(8,128)(2,1)} %param.25), channel_id=1, source_target_pairs={{0,2},{1,3},{2,6},{3,7},{4,0},{5,1},{6,4},{7,5},{8,10},{9,11},{10,... | collective-permute-start | bytes 2113544 | tf_op jit(solution)/shard_map/ppermute | solution.py:372
  192.2 216.5 %reduce-scatter.6.cloned.1.call-start = ((), (), s32[]{:S(2)}) async-start(), calls=%async_computation.7 | async-start | bytes 7045120 | tf_op jit(solution)/shard_map/reduce_scatter | solution.py:438
  207.9 35.9 %collective-permute-start.31 = (bf16[1536,512]{1,0:T(8,128)(2,1)S(1)}, bf16[1536,512]{1,0:T(8,128)(2,1)}, u32[]{:S(2)}, u32[]{:S(2)}) collective-permute-start(bf16[1536,512]{1,0:T(8,128)(2,1)S(1)} %fusion.30.refs_0_), channel_id=1, source_target_pairs={{0,1},{1,0},{2,3},{3,2},{4,5},{5,4},{6,7},{7,6},{8,9},{9,8},{10,11... | collective-permute-start | bytes 4718600 | tf_op jit(solution)/shard_map/ppermute | solution.py:372
  207.9 45.8 %collective-permute-start.30 = (bf16[1536,512]{1,0:T(8,128)(2,1)S(1)}, bf16[1536,512]{1,0:T(8,128)(2,1)}, u32[]{:S(2)}, u32[]{:S(2)}) collective-permute-start(bf16[1536,512]{1,0:T(8,128)(2,1)S(1)} %fusion.30.refs_0_), channel_id=1, source_target_pairs={{0,4},{1,5},{2,6},{3,7},{4,0},{5,1},{6,2},{7,3},{8,12},{9,13},{10,... | collective-permute-start | bytes 4718600 | tf_op jit(solution)/shard_map/ppermute | solution.py:372
  251.1 45.4 %collective-permute-start.35 = (bf16[1376,256]{1,0:T(8,128)(2,1)S(1)}, bf16[1376,256]{1,0:T(8,128)(2,1)}, u32[]{:S(2)}, u32[]{:S(2)}) collective-permute-start(bf16[1376,256]{1,0:T(8,128)(2,1)S(1)} %broadcast_select_fusion.4.refs_0_), channel_id=1, source_target_pairs={{0,24},{1,25},{2,26},{3,27},{4,28},{5,29},{6,30},{7,31},{8,16},{9,... | collective-permute-start | bytes 2113544 | tf_op jit(solution)/shard_map/ppermute | solution.py:372
  252.3 59.0 %collective-permute-start.34 = (bf16[1376,256]{1,0:T(8,128)(2,1)S(1)}, bf16[1376,256]{1,0:T(8,128)(2,1)}, u32[]{:S(2)}, u32[]{:S(2)}) collective-permute-start(bf16[1376,256]{1,0:T(8,128)(2,1)S(1)} %broadcast_select_fusion.4.refs_0_), channel_id=1, source_target_pairs={{0,16},{1,17},{2,18},{3,19},{4,20},{5,21},{6,22},{7,23},{8,24},{9,... | collective-permute-start | bytes 2113544 | tf_op jit(solution)/shard_map/ppermute | solution.py:372
  253.4 57.8 %collective-permute-start.33 = (bf16[1376,256]{1,0:T(8,128)(2,1)S(1)}, bf16[1376,256]{1,0:T(8,128)(2,1)}, u32[]{:S(2)}, u32[]{:S(2)}) collective-permute-start(bf16[1376,256]{1,0:T(8,128)(2,1)S(1)} %broadcast_select_fusion.4.refs_0_), channel_id=1, source_target_pairs={{0,8},{1,9},{2,10},{3,11},{4,12},{5,13},{6,14},{7,15},{8,0},{9,1},... | collective-permute-start | bytes 2113544 | tf_op jit(solution)/shard_map/ppermute | solution.py:372
  253.7 57.5 %collective-permute-start.38 = (bf16[1376,256]{1,0:T(8,128)(2,1)S(1)}, bf16[1376,256]{1,0:T(8,128)(2,1)}, u32[]{:S(2)}, u32[]{:S(2)}) collective-permute-start(bf16[1376,256]{1,0:T(8,128)(2,1)S(1)} %collective-permute-done.29.refs_4_), channel_id=1, source_target_pairs={{0,24},{1,25},{2,26},{3,27},{4,28},{5,29},{6,30},{7,31},{8,16},{9,... | collective-permute-start | bytes 2113544 | tf_op jit(solution)/shard_map/ppermute | solution.py:372
  254.9 61.3 %collective-permute-start.37 = (bf16[1376,256]{1,0:T(8,128)(2,1)S(1)}, bf16[1376,256]{1,0:T(8,128)(2,1)}, u32[]{:S(2)}, u32[]{:S(2)}) collective-permute-start(bf16[1376,256]{1,0:T(8,128)(2,1)S(1)} %collective-permute-done.29.refs_4_), channel_id=1, source_target_pairs={{0,16},{1,17},{2,18},{3,19},{4,20},{5,21},{6,22},{7,23},{8,24},{9,... | collective-permute-start | bytes 2113544 | tf_op jit(solution)/shard_map/ppermute | solution.py:372
  296.5 19.8 %collective-permute-start.36 = (bf16[1376,256]{1,0:T(8,128)(2,1)S(1)}, bf16[1376,256]{1,0:T(8,128)(2,1)}, u32[]{:S(2)}, u32[]{:S(2)}) collective-permute-start(bf16[1376,256]{1,0:T(8,128)(2,1)S(1)} %collective-permute-done.29.refs_4_), channel_id=1, source_target_pairs={{0,8},{1,9},{2,10},{3,11},{4,12},{5,13},{6,14},{7,15},{8,0},{9,1},... | collective-permute-start | bytes 2113544 | tf_op jit(solution)/shard_map/ppermute | solution.py:372
  316.3 163.0 %reduce-scatter.8.cloned.1.call-start = ((), (), s32[]{:S(2)}) async-start(), calls=%async_computation.8 | async-start | bytes 7045120 | tf_op jit(solution)/shard_map/reduce_scatter | solution.py:438
  371.4 174.0 %reduce-scatter.10.cloned.1.call-start = ((), (), s32[]{:S(2)}) async-start(), calls=%async_computation.9 | async-start | bytes 7045120 | tf_op jit(solution)/shard_map/reduce_scatter | solution.py:438
  371.5 37.3 %collective-permute-start.43 = (bf16[1536,512]{1,0:T(8,128)(2,1)}, bf16[1536,512]{1,0:T(8,128)(2,1)S(1)}, u32[]{:S(2)}, u32[]{:S(2)}) collective-permute-start(bf16[1536,512]{1,0:T(8,128)(2,1)} %fusion.29), channel_id=1, source_target_pairs={{0,1},{1,0},{2,3},{3,2},{4,5},{5,4},{6,7},{7,6},{8,9},{9,8},{10,11... | collective-permute-start | bytes 4718600 | tf_op jit(solution)/shard_map/ppermute | solution.py:372
  385.0 15.8 %collective-permute-start.42 = (bf16[1536,512]{1,0:T(8,128)(2,1)}, bf16[1536,512]{1,0:T(8,128)(2,1)}, u32[]{:S(2)}, u32[]{:S(2)}) collective-permute-start(bf16[1536,512]{1,0:T(8,128)(2,1)} %fusion.28), channel_id=1, source_target_pairs={{0,4},{1,5},{2,6},{3,7},{4,0},{5,1},{6,2},{7,3},{8,12},{9,13},{10,... | collective-permute-start | bytes 4718600 | tf_op jit(solution)/shard_map/ppermute | solution.py:372
  408.8 247.0 %reduce-scatter.12.cloned.1.call-start = ((), (), s32[]{:S(2)}) async-start(), calls=%async_computation.10 | async-start | bytes 2621440 | tf_op jit(solution)/shard_map/reduce_scatter | solution.py:438
  432.2 35.8 %collective-permute-start.47 = (bf16[1536,512]{1,0:T(8,128)(2,1)S(1)}, bf16[1536,512]{1,0:T(8,128)(2,1)S(1)}, u32[]{:S(2)}, u32[]{:S(2)}) collective-permute-start(bf16[1536,512]{1,0:T(8,128)(2,1)S(1)} %convolution_convert_fusion.13), channel_id=1, source_target_pairs={{0,4},{1,5},{2,6},{3,7},{4,0},{5,1},{6,2},{7,3},{8,12},{9,13},{10,... | collective-permute-start | bytes 4718600 | tf_op jit(solution)/shard_map/ppermute | solution.py:372
  432.6 46.6 %collective-permute-start.50 = (bf16[1376,256]{1,0:T(8,128)(2,1)S(1)}, bf16[1376,256]{1,0:T(8,128)(2,1)}, u32[]{:S(2)}, u32[]{:S(2)}) collective-permute-start(bf16[1376,256]{1,0:T(8,128)(2,1)S(1)} %get-tuple-element.300), channel_id=1, source_target_pairs={{0,4},{1,5},{2,0},{3,1},{4,6},{5,7},{6,2},{7,3},{8,12},{9,13},{10,... | collective-permute-start | bytes 2113544 | tf_op jit(solution)/shard_map/ppermute | solution.py:372
  434.9 32.2 %collective-permute-start.49 = (bf16[1376,256]{1,0:T(8,128)(2,1)S(1)}, bf16[1376,256]{1,0:T(8,128)(2,1)S(1)}, u32[]{:S(2)}, u32[]{:S(2)}) collective-permute-start(bf16[1376,256]{1,0:T(8,128)(2,1)S(1)} %get-tuple-element.301), channel_id=1, source_target_pairs={{2,4},{3,5},{4,2},{5,3},{10,12},{11,13},{12,10},{13,11},{18,20},{1... | collective-permute-start | bytes 2113544 | tf_op jit(solution)/shard_map/ppermute | solution.py:372
  438.7 33.7 %collective-permute-start.46 = (bf16[1536,512]{1,0:T(8,128)(2,1)S(1)}, bf16[1536,512]{1,0:T(8,128)(2,1)S(1)}, u32[]{:S(2)}, u32[]{:S(2)}) collective-permute-start(bf16[1536,512]{1,0:T(8,128)(2,1)S(1)} %convolution_convert_fusion.8), channel_id=1, source_target_pairs={{0,4},{1,5},{2,6},{3,7},{4,0},{5,1},{6,2},{7,3},{8,12},{9,13},{10,... | collective-permute-start | bytes 4718600 | tf_op jit(solution)/shard_map/ppermute | solution.py:372
  441.5 33.7 %collective-permute-start.48 = (bf16[1536,512]{1,0:T(8,128)(2,1)S(1)}, bf16[1536,512]{1,0:T(8,128)(2,1)S(1)}, u32[]{:S(2)}, u32[]{:S(2)}) collective-permute-start(bf16[1536,512]{1,0:T(8,128)(2,1)S(1)} %convolution_convert_fusion.12), channel_id=1, source_target_pairs={{0,4},{1,5},{2,6},{3,7},{4,0},{5,1},{6,2},{7,3},{8,12},{9,13},{10,... | collective-permute-start | bytes 4718600 | tf_op jit(solution)/shard_map/ppermute | solution.py:372
  468.0 26.3 %collective-permute-start.45 = (bf16[1536,512]{1,0:T(8,128)(2,1)}, bf16[1536,512]{1,0:T(8,128)(2,1)}, u32[]{:S(2)}, u32[]{:S(2)}) collective-permute-start(bf16[1536,512]{1,0:T(8,128)(2,1)} %fusion.31), channel_id=1, source_target_pairs={{0,1},{1,0},{2,3},{3,2},{4,5},{5,4},{6,7},{7,6},{8,9},{9,8},{10,11... | collective-permute-start | bytes 4718600 | tf_op jit(solution)/shard_map/ppermute | solution.py:372
  509.2 20.3 %collective-permute-start.53 = (bf16[648,128]{1,0:T(8,128)(2,1)}, bf16[648,128]{1,0:T(8,128)(2,1)}, u32[]{:S(2)}, u32[]{:S(2)}) collective-permute-start(bf16[648,128]{1,0:T(8,128)(2,1)} %pad_maximum_fusion.4), channel_id=1, source_target_pairs={{24,0},{25,1},{26,2},{27,3},{28,4},{29,5},{30,6},{31,7}} | collective-permute-start | bytes 497672 | tf_op jit(solution)/shard_map/ppermute | solution.py:372
  513.2 16.3 %collective-permute-start.52 = (bf16[648,128]{1,0:T(8,128)(2,1)}, bf16[648,128]{1,0:T(8,128)(2,1)}, u32[]{:S(2)}, u32[]{:S(2)}) collective-permute-start(bf16[648,128]{1,0:T(8,128)(2,1)} %pad_maximum_fusion.4), channel_id=1, source_target_pairs={{16,0},{17,1},{18,2},{19,3},{20,4},{21,5},{22,6},{23,7},{24,8},{25... | collective-permute-start | bytes 497672 | tf_op jit(solution)/shard_map/ppermute | solution.py:372
  515.2 14.3 %collective-permute-start.51 = (bf16[648,128]{1,0:T(8,128)(2,1)}, bf16[648,128]{1,0:T(8,128)(2,1)}, u32[]{:S(2)}, u32[]{:S(2)}) collective-permute-start(bf16[648,128]{1,0:T(8,128)(2,1)} %pad_maximum_fusion.4), channel_id=1, source_target_pairs={{8,0},{9,1},{10,2},{11,3},{12,4},{13,5},{14,6},{15,7},{16,8},{17,9... | collective-permute-start | bytes 497672 | tf_op jit(solution)/shard_map/ppermute | solution.py:372
  517.4 28.0 %collective-permute-start.54 = (bf16[1536,512]{1,0:T(8,128)(2,1)}, bf16[1536,512]{1,0:T(8,128)(2,1)}, u32[]{:S(2)}, u32[]{:S(2)}) collective-permute-start(bf16[1536,512]{1,0:T(8,128)(2,1)} %add_convert_fusion.1), channel_id=1, source_target_pairs={{0,1},{1,0},{2,3},{3,2},{4,5},{5,4},{6,7},{7,6},{8,9},{9,8},{10,11... | collective-permute-start | bytes 4718600 | tf_op jit(solution)/shard_map/ppermute | solution.py:372
  546.8 31.6 %collective-permute-start.56 = (bf16[1376,256]{1,0:T(8,128)(2,1)S(1)}, bf16[1376,256]{1,0:T(8,128)(2,1)S(1)}, u32[]{:S(2)}, u32[]{:S(2)}) collective-permute-start(bf16[1376,256]{1,0:T(8,128)(2,1)S(1)} %get-tuple-element.298), channel_id=1, source_target_pairs={{0,4},{1,5},{2,0},{3,1},{4,6},{5,7},{6,2},{7,3},{8,12},{9,13},{10,... | collective-permute-start | bytes 2113544 | tf_op jit(solution)/shard_map/ppermute | solution.py:372
  546.9 30.6 %collective-permute-start.55 = (bf16[1376,256]{1,0:T(8,128)(2,1)S(1)}, bf16[1376,256]{1,0:T(8,128)(2,1)S(1)}, u32[]{:S(2)}, u32[]{:S(2)}) collective-permute-start(bf16[1376,256]{1,0:T(8,128)(2,1)S(1)} %get-tuple-element.299), channel_id=1, source_target_pairs={{2,4},{3,5},{4,2},{5,3},{10,12},{11,13},{12,10},{13,11},{18,20},{1... | collective-permute-start | bytes 2113544 | tf_op jit(solution)/shard_map/ppermute | solution.py:372
  584.5 161.2 %reduce-scatter.14.cloned.1.call-start = ((), (), s32[]{:S(2)}) async-start(), calls=%async_computation.11 | async-start | bytes 3276800 | tf_op jit(solution)/shard_map/reduce_scatter | solution.py:438
  590.2 28.2 %collective-permute-start.62 = (bf16[768,512]{1,0:T(8,128)(2,1)S(1)}, bf16[768,512]{1,0:T(8,128)(2,1)S(1)}, u32[]{:S(2)}, u32[]{:S(2)}) collective-permute-start(bf16[768,512]{1,0:T(8,128)(2,1)S(1)} %get-tuple-element.295), channel_id=1, source_target_pairs={{2,4},{3,5},{4,2},{5,3},{10,12},{11,13},{12,10},{13,11},{18,20},{1... | collective-permute-start | bytes 2359304 | tf_op jit(solution)/shard_map/ppermute | solution.py:372
  602.6 26.9 %collective-permute-start.61 = (bf16[1536,512]{1,0:T(8,128)(2,1)}, bf16[1536,512]{1,0:T(8,128)(2,1)}, u32[]{:S(2)}, u32[]{:S(2)}) collective-permute-start(bf16[1536,512]{1,0:T(8,128)(2,1)} %convolution_convert_fusion.10), channel_id=1, source_target_pairs={{0,4},{1,5},{2,6},{3,7},{4,0},{5,1},{6,2},{7,3},{8,12},{9,13},{10,... | collective-permute-start | bytes 4718600 | tf_op jit(solution)/shard_map/ppermute | solution.py:372
  603.3 31.0 %collective-permute-start.63 = (bf16[768,512]{1,0:T(8,128)(2,1)}, bf16[768,512]{1,0:T(8,128)(2,1)}, u32[]{:S(2)}, u32[]{:S(2)}) collective-permute-start(bf16[768,512]{1,0:T(8,128)(2,1)} %get-tuple-element.294), channel_id=1, source_target_pairs={{0,4},{1,5},{2,0},{3,1},{4,6},{5,7},{6,2},{7,3},{8,12},{9,13},{10,... | collective-permute-start | bytes 2359304 | tf_op jit(solution)/shard_map/ppermute | solution.py:372
  603.3 52.4 %collective-permute-start.60 = (bf16[1536,512]{1,0:T(8,128)(2,1)}, bf16[1536,512]{1,0:T(8,128)(2,1)}, u32[]{:S(2)}, u32[]{:S(2)}) collective-permute-start(bf16[1536,512]{1,0:T(8,128)(2,1)} %fusion.32), channel_id=1, source_target_pairs={{0,1},{1,0},{2,3},{3,2},{4,5},{5,4},{6,7},{7,6},{8,9},{9,8},{10,11... | collective-permute-start | bytes 4718600 | tf_op jit(solution)/shard_map/ppermute | solution.py:372
  666.8 39.4 %collective-permute-start.66 = (bf16[2,768,512]{2,1,0:T(8,128)(2,1)S(1)}, bf16[2,768,512]{2,1,0:T(8,128)(2,1)}, u32[]{:S(2)}, u32[]{:S(2)}) collective-permute-start(bf16[2,768,512]{2,1,0:T(8,128)(2,1)S(1)} %pad_maximum_fusion.1.refs_0_), channel_id=1, source_target_pairs={{1,0},{2,1},{3,2},{5,4},{6,5},{7,6},{9,8},{10,9},{11,10},{13,12},{... | collective-permute-start | bytes 4718600 | tf_op jit(solution)/shard_map/ppermute | solution.py:372
  668.1 38.1 %collective-permute-start.65 = (bf16[2,768,512]{2,1,0:T(8,128)(2,1)S(1)}, bf16[2,768,512]{2,1,0:T(8,128)(2,1)S(1)}, u32[]{:S(2)}, u32[]{:S(2)}) collective-permute-start(bf16[2,768,512]{2,1,0:T(8,128)(2,1)S(1)} %pad_maximum_fusion.1.refs_0_), channel_id=1, source_target_pairs={{0,1},{1,2},{2,3},{4,5},{5,6},{6,7},{8,9},{9,10},{10,11},{12,13},{... | collective-permute-start | bytes 4718600 | tf_op jit(solution)/shard_map/ppermute | solution.py:372
  672.5 33.1 %collective-permute-start.69 = (f32[2,2048]{1,0:T(2,128)S(1)}, f32[2,2048]{1,0:T(2,128)S(1)}, u32[]{:S(2)}, u32[]{:S(2)}) collective-permute-start(f32[2,2048]{1,0:T(2,128)S(1)} %constant_dynamic-update-slice_fusion), channel_id=1, source_target_pairs={{0,3},{1,2},{2,1},{3,0},{4,7},{5,6},{6,5},{7,4},{8,11},{9,10},{10,... | collective-permute-start | bytes 49160 | tf_op jit(solution)/shard_map/ppermute | solution.py:372
  672.5 33.4 %collective-permute-start.68 = (f32[2,2048]{1,0:T(2,128)S(1)}, f32[2,2048]{1,0:T(2,128)S(1)}, u32[]{:S(2)}, u32[]{:S(2)}) collective-permute-start(f32[2,2048]{1,0:T(2,128)S(1)} %constant_dynamic-update-slice_fusion), channel_id=1, source_target_pairs={{0,2},{1,3},{2,0},{3,1},{4,6},{5,7},{6,4},{7,5},{8,10},{9,11},{10,... | collective-permute-start | bytes 49160 | tf_op jit(solution)/shard_map/ppermute | solution.py:372
  673.6 32.7 %collective-permute-start.67 = (f32[2,2048]{1,0:T(2,128)S(1)}, f32[2,2048]{1,0:T(2,128)S(1)}, u32[]{:S(2)}, u32[]{:S(2)}) collective-permute-start(f32[2,2048]{1,0:T(2,128)S(1)} %constant_dynamic-update-slice_fusion), channel_id=1, source_target_pairs={{0,1},{1,0},{2,3},{3,2},{4,5},{5,4},{6,7},{7,6},{8,9},{9,8},{10,11... | collective-permute-start | bytes 49160 | tf_op jit(solution)/shard_map/ppermute | solution.py:372
  706.3 20.8 %collective-permute-start.70 = (bf16[2,768,512]{2,1,0:T(8,128)(2,1)S(1)}, bf16[2,768,512]{2,1,0:T(8,128)(2,1)S(1)}, u32[]{:S(2)}, u32[]{:S(2)}) collective-permute-start(bf16[2,768,512]{2,1,0:T(8,128)(2,1)S(1)} %collective-permute-done.65.refs_1_), channel_id=1, source_target_pairs={{1,2},{2,3},{5,6},{6,7},{9,10},{10,11},{13,14},{14,15},{17,18},{18... | collective-permute-start | bytes 4718600 | tf_op jit(solution)/shard_map/ppermute | solution.py:372
  707.0 38.7 %collective-permute-start.71 = (bf16[2,768,512]{2,1,0:T(8,128)(2,1)}, bf16[2,768,512]{2,1,0:T(8,128)(2,1)}, u32[]{:S(2)}, u32[]{:S(2)}) collective-permute-start(bf16[2,768,512]{2,1,0:T(8,128)(2,1)} %collective-permute-done.66.refs_4_), channel_id=1, source_target_pairs={{1,0},{2,1},{5,4},{6,5},{9,8},{10,9},{13,12},{14,13},{17,16},{18,1... | collective-permute-start | bytes 4718600 | tf_op jit(solution)/shard_map/ppermute | solution.py:372
  712.1 15.0 %collective-permute-start.72 = (f32[2,2048]{1,0:T(2,128)S(1)}, f32[2,2048]{1,0:T(2,128)S(1)}, u32[]{:S(2)}, u32[]{:S(2)}) collective-permute-start(f32[2,2048]{1,0:T(2,128)S(1)} %add_add_fusion), channel_id=1, source_target_pairs={{0,4},{1,5},{2,6},{3,7},{4,0},{5,1},{6,2},{7,3},{8,12},{9,13},{10,... | collective-permute-start | bytes 49160 | tf_op jit(solution)/shard_map/ppermute | solution.py:372
  714.5 42.6 %collective-permute-start.81 = (bf16[256,512]{1,0:T(8,128)(2,1)}, bf16[256,512]{1,0:T(8,128)(2,1)}, u32[]{:S(2)}, u32[]{:S(2)}) collective-permute-start(bf16[256,512]{1,0:T(8,128)(2,1)} %get-tuple-element.307), channel_id=1, source_target_pairs={{0,4},{1,5},{2,0},{3,1},{4,6},{5,7},{6,2},{7,3},{8,12},{9,13},{10,... | collective-permute-start | bytes 786440 | tf_op jit(solution)/shard_map/ppermute | solution.py:372
  725.2 41.4 %collective-permute-start.80 = (bf16[256,512]{1,0:T(8,128)(2,1)S(1)}, bf16[256,512]{1,0:T(8,128)(2,1)}, u32[]{:S(2)}, u32[]{:S(2)}) collective-permute-start(bf16[256,512]{1,0:T(8,128)(2,1)S(1)} %get-tuple-element.306), channel_id=1, source_target_pairs={{2,4},{3,5},{4,2},{5,3},{10,12},{11,13},{12,10},{13,11},{18,20},{1... | collective-permute-start | bytes 786440 | tf_op jit(solution)/shard_map/ppermute | solution.py:372
  745.7 55.9 %collective-permute-start.73 = (bf16[2,768,512]{2,1,0:T(8,128)(2,1)}, bf16[2,768,512]{2,1,0:T(8,128)(2,1)}, u32[]{:S(2)}, u32[]{:S(2)}) collective-permute-start(bf16[2,768,512]{2,1,0:T(8,128)(2,1)} %copy-done.10), channel_id=1, source_target_pairs={{2,3},{6,7},{10,11},{14,15},{18,19},{22,23},{26,27},{30,31}} | collective-permute-start | bytes 4718600 | tf_op jit(solution)/shard_map/ppermute | solution.py:372
  747.5 68.8 %collective-permute-start.74 = (bf16[2,768,512]{2,1,0:T(8,128)(2,1)}, bf16[2,768,512]{2,1,0:T(8,128)(2,1)}, u32[]{:S(2)}, u32[]{:S(2)}) collective-permute-start(bf16[2,768,512]{2,1,0:T(8,128)(2,1)} %collective-permute-done.71.refs_5_), channel_id=1, source_target_pairs={{1,0},{5,4},{9,8},{13,12},{17,16},{21,20},{25,24},{29,28}} | collective-permute-start | bytes 4718600 | tf_op jit(solution)/shard_map/ppermute | solution.py:372
  750.0 20.4 %collective-permute-start.79 = (bf16[256,640]{1,0:T(8,128)(2,1)S(1)}, bf16[256,640]{1,0:T(8,128)(2,1)S(1)}, u32[]{:S(2)}, u32[]{:S(2)}) collective-permute-start(bf16[256,640]{1,0:T(8,128)(2,1)S(1)} %get-tuple-element.305), channel_id=1, source_target_pairs={{0,4},{1,5},{2,0},{3,1},{4,6},{5,7},{6,2},{7,3},{8,12},{9,13},{10,... | collective-permute-start | bytes 983048 | tf_op jit(solution)/shard_map/ppermute | solution.py:372
  757.0 28.1 %collective-permute-start.78 = (bf16[256,640]{1,0:T(8,128)(2,1)S(1)}, bf16[256,640]{1,0:T(8,128)(2,1)S(1)}, u32[]{:S(2)}, u32[]{:S(2)}) collective-permute-start(bf16[256,640]{1,0:T(8,128)(2,1)S(1)} %get-tuple-element.304), channel_id=1, source_target_pairs={{2,4},{3,5},{4,2},{5,3},{10,12},{11,13},{12,10},{13,11},{18,20},{1... | collective-permute-start | bytes 983048 | tf_op jit(solution)/shard_map/ppermute | solution.py:372
  766.6 33.8 %collective-permute-start.76 = (bf16[1376,256]{1,0:T(8,128)(2,1)}, bf16[1376,256]{1,0:T(8,128)(2,1)}, u32[]{:S(2)}, u32[]{:S(2)}) collective-permute-start(bf16[1376,256]{1,0:T(8,128)(2,1)} %get-tuple-element.297), channel_id=1, source_target_pairs={{2,4},{3,5},{4,2},{5,3},{10,12},{11,13},{12,10},{13,11},{18,20},{1... | collective-permute-start | bytes 2113544 | tf_op jit(solution)/shard_map/ppermute | solution.py:372
  770.4 31.1 %collective-permute-start.75 = (f32[2,2048]{1,0:T(2,128)S(1)}, f32[2,2048]{1,0:T(2,128)S(1)}, u32[]{:S(2)}, u32[]{:S(2)}) collective-permute-start(f32[2,2048]{1,0:T(2,128)S(1)} %add.574), channel_id=1, source_target_pairs={{0,8},{1,9},{2,10},{3,11},{4,12},{5,13},{6,14},{7,15},{8,0},{9,1},... | collective-permute-start | bytes 49160 | tf_op jit(solution)/shard_map/ppermute | solution.py:372
  785.1 40.2 %collective-permute-start.77 = (bf16[1376,256]{1,0:T(8,128)(2,1)}, bf16[1376,256]{1,0:T(8,128)(2,1)}, u32[]{:S(2)}, u32[]{:S(2)}) collective-permute-start(bf16[1376,256]{1,0:T(8,128)(2,1)} %get-tuple-element.296), channel_id=1, source_target_pairs={{0,4},{1,5},{2,0},{3,1},{4,6},{5,7},{6,2},{7,3},{8,12},{9,13},{10,... | collective-permute-start | bytes 2113544 | tf_op jit(solution)/shard_map/ppermute | solution.py:372
  (130 other events, 1530.2 us)
Sparse Core Ops, SparseCore 0:
  101.6 77.0 all-gather.2
  192.3 79.2 all-gather.4
  316.4 64.7 reduce-scatter.5
  384.1 64.6 reduce-scatter.7
  451.7 68.4 reduce-scatter.9
  584.7 34.6 reduce-scatter.11
  655.9 37.8 reduce-scatter.13

commit v8 on v6

--- a/solution.py
+++ b/solution.py
@@ -327,6 +327,9 @@
             out_specs=pl.BlockSpec((micro, tile, width), lambda i, w: (0, i, 0)),
         ),
         out_shape=jax.ShapeDtypeStruct((micro, block, width), F32),
+        cost_estimate=pl.CostEstimate(
+            flops=0, bytes_accessed=8 * micro * block * width, transcendentals=0
+        ),
         compiler_params=pltpu.CompilerParams(vmem_limit_bytes=48 * 2**20),
     )(jnp.stack([feat_rank, core]).astype(jnp.int32), *shares)
 

time: 845 us -> 845 us (level)
  no operation moved by 1% of the time
where the time goes in v8:
time: 845 us; the launch traced here: 832 us
  waiting for transfers between devices  300 us (36%)
  matrix products  194 us (23%)
  starting transfers between devices  103 us (12%)
  Pallas kernels  79.6 us (9%)
  other arithmetic  73.4 us (9%)
  local copies, waits for them, and re-layouts  48.6 us (6%)
  between operations  24.2 us (3%)
  blocking collectives  9.09 us (1%)
    ppermute x83, waiting for transfers between devices, move(): return lax.ppermute(value, ('seq', 'feat'), pairs)  300 us
    dot_general x36, matrix products, dot(): lax.dot_general(a, b, (((ca,), (cb,)), ((), ())), preferred_element_type=...  194 us
    ppermute x83, starting transfers between devices, move(): return lax.ppermute(value, ('seq', 'feat'), pairs)  102 us
    pallas_call x4, Pallas kernels, run(): pl.pallas_call(functools.partial(kernel, heads=heads, block=block), grid_...  47.1 us
    unnamed x206, local copies, waits for them, and re-layouts  23.2 us
    pallas_call x9, Pallas kernels, place(): pl.pallas_call(functools.partial(place_kernel, axis=axis), grid_spec=pltp...  23.1 us
  transfers between devices with their start and end apart: 90, of which 30 were waited for; matrix products, arithmetic and copies ran while one was open for 34% of the time, Pallas kernels for 9%

profile of v8, /device:TPU:7, one launch (start us, length us, event | category | flops | bytes accessed | tf_op | source)
XLA Modules:
  0.0 831.6 jit_solution(6596871288661138022)
XLA Ops:
  11.5 4.1 collective-permute-start.1
  19.8 9.1 %all_gather.9 = bf16[2,2048]{1,0:T(2,128)(2,1)} all-gather(bf16[2,256]{1,0:T(2,128)(2,1)S(1)} %pad_maximum_fusion.5), channel_id=1, replica_groups=mesh['seq'=8,'feat'=4] {'seq'}, dimensions={1}, use_global_device_ids=true | all-gather | bytes 9216 | tf_op jit(solution)/shard_map/all_gather | solution.py:500
  39.2 5.5 collective-permute-done.9
  54.8 6.2 collective-permute-done.8.refs_7_
  72.5 5.3 convolution_convert_fusion.7
  79.3 4.3 shard_map.242
  89.0 6.5 collective-permute-done.15
  114.6 9.5 %shard_map.243 = (bf16[1536,512]{1,0:T(8,128)(2,1)}, f32[1536,512]{1,0:T(8,128)}) custom-call(s32[2,5]{1,0:T(2,128)S(1)} %copy-done.33, bf16[1536,64]{1,0:T(8,128)(2,1)S(1)} %copy-done.19, bf16[1536,64]{1,0:T(8,128)(2,1)S(1)} %get-tuple-element.286.k_ref, bf16[1536,512]{1,0:T(8,128)(2,1)S(1)} %slice.236.v_ref, bf16[2,4,256,256]{3,2,1,0:T(8,128)(2,1)S(1)} %fusion.66.s_ref, ...), custom_call_target="tpu_custom_call" | custom-call | flops 6144000000 | bytes 9216000 | tf_op jit(solution)/shard_map/pallas_call | solution.py:220
  124.1 23.7 %collective-permute-done.17 = bf16[1376,256]{1,0:T(8,128)(2,1)S(1)} collective-permute-done((bf16[1376,256]{1,0:T(8,128)(2,1)}, bf16[1376,256]{1,0:T(8,128)(2,1)S(1)}, u32[]{:S(2)}, u32[]{:S(2)}) %collective-permute-start.17) | collective-permute-done | bytes 704544 | tf_op jit(solution)/shard_map/ppermute | solution.py:375
  150.5 4.5 collective-permute-start.28
  155.1 7.7 collective-permute-done.20.refs_2_
  164.5 12.4 %collective-permute-done.23.refs_6_ = bf16[256,512]{1,0:T(8,128)(2,1)S(1)} collective-permute-done((bf16[256,512]{1,0:T(8,128)(2,1)S(1)}, bf16[256,512]{1,0:T(8,128)(2,1)S(1)}, u32[]{:S(2)}, u32[]{:S(2)}) %collective-permute-start.23) | collective-permute-done | bytes 262176 | tf_op jit(solution)/shard_map/ppermute | solution.py:375
  178.3 4.0 dynamic-slice_bitcast_fusion.refs_0_
  204.5 3.5 collective-permute-done.29.refs_4_
  208.9 35.0 %collective-permute-done.31.refs_2_ = bf16[1536,512]{1,0:T(8,128)(2,1)} collective-permute-done((bf16[1536,512]{1,0:T(8,128)(2,1)S(1)}, bf16[1536,512]{1,0:T(8,128)(2,1)}, u32[]{:S(2)}, u32[]{:S(2)}) %collective-permute-start.31) | collective-permute-done | bytes 1572896 | tf_op jit(solution)/shard_map/ppermute | solution.py:375
  243.9 4.5 shard_map.241
  261.5 4.1 multiply_convert_fusion
  268.4 12.3 %convolution_convert_fusion.5 = bf16[1536,1376]{0,1:T(8,128)(2,1)} fusion(bf16[1536,2048]{1,0:T(8,128)(2,1)S(1)} %multiply_convert_fusion, bf16[1376,2048]{1,0:T(8,128)(2,1)} %all-gather.3.cloned.1.call-done), kind=kOutput, calls=%fused_computation.37 | convolution fusion | flops 8659156992 | bytes 16154624 | tf_op jit(solution)/shard_map/dot_general | solution.py:262
  280.7 15.7 %fusion.15 = (bf16[1536,1376]{0,1:T(8,128)(2,1)S(1)}, bf16[1536,1376]{0,1:T(8,128)(2,1)}) fusion(bf16[1536,1376]{0,1:T(8,128)(2,1)} %convolution_convert_fusion.5, bf16[1536,2048]{1,0:T(8,128)(2,1)} %copy-done.52, bf16[1376,2048]{1,0:T(8,128)(2,1)} %all-gather.5.cloned.1.call-done), kind=kOutput, calls=%fused_computation.31 | convolution fusion | flops 8676065280 | bytes 24608768 | tf_op jit(solution)/shard_map/dot_general | solution.py:262
  298.5 12.6 %convolution_convert_fusion.2 = bf16[1376,2048]{1,0:T(8,128)(2,1)} fusion(bf16[1536,1376]{0,1:T(8,128)(2,1)S(1)} %get-tuple-element.174, bf16[1536,2048]{1,0:T(8,128)(2,1)} %copy-done.5), kind=kOutput, calls=%fused_computation.34 | convolution fusion | flops 8659861504 | bytes 16154624 | tf_op jit(solution)/shard_map/dot_general | solution.py:262
  311.1 5.1 collective-permute-done.37.refs_6_
  316.5 3.9 shard_map.248
  320.4 13.2 %convolution_convert_fusion.3 = bf16[1536,1376]{0,1:T(8,128)(2,1)S(1)} fusion(bf16[1536,2048]{1,0:T(8,128)(2,1)} %copy-done.5, bf16[1376,2048]{1,0:T(8,128)(2,1)S(1)} %shard_map.248), kind=kOutput, calls=%fused_computation.35 | convolution fusion | flops 8659156992 | bytes 16154624 | tf_op jit(solution)/shard_map/dot_general | solution.py:262
  333.7 6.3 fusion.64
  340.0 5.2 fusion.58
  352.6 4.1 fusion.61
  356.8 4.0 fusion.29
  360.8 10.6 %convolution_convert_fusion = bf16[1376,2048]{1,0:T(8,128)(2,1)} fusion(bf16[1536,1376]{0,1:T(8,128)(2,1)S(1)} %get-tuple-element.165, bf16[1536,2048]{1,0:T(8,128)(2,1)S(1)} %bitcast.131), kind=kOutput, calls=%fused_computation.32 | convolution fusion | flops 8659861504 | bytes 16154624 | tf_op jit(solution)/shard_map/dot_general | solution.py:262
  372.8 5.5 fusion.52
  378.3 6.7 fusion.28
  385.4 10.6 %convolution_convert_fusion.1 = bf16[1376,2048]{1,0:T(8,128)(2,1)} fusion(bf16[1536,1376]{0,1:T(8,128)(2,1)S(1)} %bitcast.135, bf16[1536,2048]{1,0:T(8,128)(2,1)S(1)} %bitcast.133), kind=kOutput, calls=%fused_computation.33 | convolution fusion | flops 8659861504 | bytes 16154624 | tf_op jit(solution)/shard_map/dot_general | solution.py:262
  396.0 4.8 fusion.55
  400.8 8.0 fusion.20
  410.0 5.4 fusion.129
  415.4 3.6 convolution_convert_fusion.9
  423.1 4.0 fusion.31
  427.0 5.4 convolution_convert_fusion.13
  442.2 25.0 %collective-permute-done.49 = bf16[1376,256]{1,0:T(8,128)(2,1)S(1)} collective-permute-done((bf16[1376,256]{1,0:T(8,128)(2,1)S(1)}, bf16[1376,256]{1,0:T(8,128)(2,1)S(1)}, u32[]{:S(2)}, u32[]{:S(2)}) %collective-permute-start.49) | collective-permute-done | bytes 704544 | tf_op jit(solution)/shard_map/ppermute | solution.py:375
  468.2 4.4 convert_add_fusion.4
  475.4 4.1 add_convert_fusion.1
  479.5 15.0 %collective-permute-done.45 = bf16[1536,512]{1,0:T(8,128)(2,1)} collective-permute-done((bf16[1536,512]{1,0:T(8,128)(2,1)}, bf16[1536,512]{1,0:T(8,128)(2,1)}, u32[]{:S(2)}, u32[]{:S(2)}) %collective-permute-start.45) | collective-permute-done | bytes 1572896 | tf_op jit(solution)/shard_map/ppermute | solution.py:375
  494.5 4.5 convert_add_fusion.3.do_ref
  500.1 6.8 shard_map.249
  509.5 3.9 collective-permute-start.53
  529.7 5.7 collective-permute-done.54
  547.9 26.4 %shard_map.251 = (bf16[1536,64]{1,0:T(8,128)(2,1)S(1)}, bf16[1536,64]{1,0:T(8,128)(2,1)S(1)}, bf16[1536,512]{1,0:T(8,128)(2,1)S(1)}) custom-call(s32[2,5]{1,0:T(2,128)S(1)} %copy-done.34, bf16[1536,64]{1,0:T(8,128)(2,1)S(1)} %copy-done.20, bf16[1536,64]{1,0:T(8,128)(2,1)S(1)} %copy-done.18, bf16[1536,512]{1,0:T(8,128)(2,1)} %copy-done.10, ...), custom_call_target="tpu_custom_call" | custom-call | flops 15360000000 | bytes 9216000 | tf_op jit(solution)/shard_map/pallas_call | solution.py:220
  577.2 4.2 convolution_convert_fusion.11
  581.7 3.9 add_convert_fusion
  587.5 4.7 collective-permute-start.62
  592.8 4.1 fusion.32
  600.8 15.2 %collective-permute-done.62 = bf16[768,512]{1,0:T(8,128)(2,1)S(1)} collective-permute-done((bf16[768,512]{1,0:T(8,128)(2,1)S(1)}, bf16[768,512]{1,0:T(8,128)(2,1)S(1)}, u32[]{:S(2)}, u32[]{:S(2)}) %collective-permute-start.62) | collective-permute-done | bytes 786464 | tf_op jit(solution)/shard_map/ppermute | solution.py:375
  617.0 10.1 %convolution_convert_fusion.6 = bf16[2048,640]{1,0:T(8,128)(2,1)} fusion(bf16[1536,640]{1,0:T(8,128)(2,1)} %copy-done.57, bf16[1536,2048]{1,0:T(8,128)(2,1)} %copy-done.2, f32[2048]{0:T(1024)} %bitcast.153, f32[1536]{0:T(1024)} %copy-done.74), kind=kOutput, calls=%fused_computation.56 | convolution fusion | flops 4040425472 | bytes 10893312 | tf_op jit(solution)/shard_map/dot_general | solution.py:262
  627.1 4.8 convolution_add_fusion
  631.9 19.8 %collective-permute-done.60 = bf16[1536,512]{1,0:T(8,128)(2,1)} collective-permute-done((bf16[1536,512]{1,0:T(8,128)(2,1)}, bf16[1536,512]{1,0:T(8,128)(2,1)}, u32[]{:S(2)}, u32[]{:S(2)}) %collective-permute-start.60) | collective-permute-done | bytes 1572896 | tf_op jit(solution)/shard_map/ppermute | solution.py:375
  652.4 6.3 fusion.25
  665.0 4.3 collective-permute-start.65
  672.9 29.5 %collective-permute-done.69 = f32[2,2048]{1,0:T(2,128)S(1)} collective-permute-done((f32[2,2048]{1,0:T(2,128)S(1)}, f32[2,2048]{1,0:T(2,128)S(1)}, u32[]{:S(2)}, u32[]{:S(2)}) %collective-permute-start.69) | collective-permute-done | bytes 16416 | tf_op jit(solution)/shard_map/ppermute | solution.py:375
  710.5 33.0 %collective-permute-done.71.refs_5_ = bf16[2,768,512]{2,1,0:T(8,128)(2,1)} collective-permute-done((bf16[2,768,512]{2,1,0:T(8,128)(2,1)}, bf16[2,768,512]{2,1,0:T(8,128)(2,1)}, u32[]{:S(2)}, u32[]{:S(2)}) %collective-permute-start.71) | collective-permute-done | bytes 1572896 | tf_op jit(solution)/shard_map/ppermute | solution.py:375
  750.8 3.3 collective-permute-start.77
  759.8 3.6 collective-permute-start.76
  764.6 13.6 %collective-permute-done.78 = bf16[256,512]{1,0:T(8,128)(2,1)S(1)} collective-permute-done((bf16[256,512]{1,0:T(8,128)(2,1)S(1)}, bf16[256,512]{1,0:T(8,128)(2,1)S(1)}, u32[]{:S(2)}, u32[]{:S(2)}) %collective-permute-start.78) | collective-permute-done | bytes 262176 | tf_op jit(solution)/shard_map/ppermute | solution.py:375
  780.9 15.7 %collective-permute-done.76 = bf16[256,640]{1,0:T(8,128)(2,1)S(1)} collective-permute-done((bf16[256,640]{1,0:T(8,128)(2,1)S(1)}, bf16[256,640]{1,0:T(8,128)(2,1)S(1)}, u32[]{:S(2)}, u32[]{:S(2)}) %collective-permute-start.76) | collective-permute-done | bytes 327712 | tf_op jit(solution)/shard_map/ppermute | solution.py:375
  801.3 10.6 %collective-permute-done.80 = bf16[1376,256]{1,0:T(8,128)(2,1)} collective-permute-done((bf16[1376,256]{1,0:T(8,128)(2,1)}, bf16[1376,256]{1,0:T(8,128)(2,1)}, u32[]{:S(2)}, u32[]{:S(2)}) %collective-permute-start.80) | collective-permute-done | bytes 704544 | tf_op jit(solution)/shard_map/ppermute | solution.py:375
  814.5 9.4 %shard_map.252 = f32[2,768,2048]{2,1,0:T(8,128)} custom-call(s32[2]{0:T(128)S(1)} %pad_add_fusion.5.where, bf16[2,768,512]{2,1,0:T(8,128)(2,1)S(1)} %pad_maximum_fusion.1.refs_0_, bf16[2,768,512]{2,1,0:T(8,128)(2,1)S(1)} %collective-permute-done.65.refs_1_, bf16[2,768,512]{2,1,0:T(8,128)(2,1)} %collective-permute-done.70.refs_2_, ...), custom_call_target="tpu_custom_call" | custom-call | bytes 25165824 | tf_op jit(solution)/shard_map/pallas_call | solution.py:321
  (512 shorter events, 218.6 us)
Async XLA Ops:
  7.2 236.6 %all-gather.3.cloned.1.call-start = ((), (), s32[]{:S(2)}) async-start(), calls=%async_computation.5 | async-start | bytes 7045120 | tf_op jit(solution)/shard_map/all_gather | solution.py:436
  10.8 20.5 %collective-permute-start.2 = (bf16[256,640]{1,0:T(8,128)(2,1)}, bf16[256,640]{1,0:T(8,128)(2,1)}, u32[]{:S(2)}, u32[]{:S(2)}) collective-permute-start(bf16[256,640]{1,0:T(8,128)(2,1)} %pad_maximum_fusion.2), channel_id=1, source_target_pairs={{0,2},{1,3},{2,6},{3,7},{4,0},{5,1},{6,4},{7,5},{8,10},{9,11},{10,... | collective-permute-start | bytes 983048 | tf_op jit(solution)/shard_map/ppermute | solution.py:375
  11.5 18.6 %collective-permute-start.1 = (bf16[256,640]{1,0:T(8,128)(2,1)}, bf16[256,640]{1,0:T(8,128)(2,1)}, u32[]{:S(2)}, u32[]{:S(2)}) collective-permute-start(bf16[256,640]{1,0:T(8,128)(2,1)} %pad_maximum_fusion.2), channel_id=1, source_target_pairs={{2,4},{3,5},{4,2},{5,3},{10,12},{11,13},{12,10},{13,11},{18,20},{1... | collective-permute-start | bytes 983048 | tf_op jit(solution)/shard_map/ppermute | solution.py:375
  17.8 49.1 %collective-permute-start = (bf16[768,2048]{1,0:T(8,128)(2,1)S(1)}, bf16[768,2048]{1,0:T(8,128)(2,1)}, u32[]{:S(2)}, u32[]{:S(2)}) collective-permute-start(bf16[768,2048]{1,0:T(8,128)(2,1)S(1)} %dynamic-slice_bitcast_fusion.1.refs_0_), channel_id=1, source_target_pairs={{0,4},{1,5},{2,6},{3,7},{4,0},{5,1},{6,2},{7,3},{8,12},{9,13},{10,... | collective-permute-start | bytes 9437192 | tf_op jit(solution)/shard_map/ppermute | solution.py:375
  44.7 19.1 %collective-permute-start.10 = (bf16[256,512]{1,0:T(8,128)(2,1)}, bf16[256,512]{1,0:T(8,128)(2,1)S(1)}, u32[]{:S(2)}, u32[]{:S(2)}) collective-permute-start(bf16[256,512]{1,0:T(8,128)(2,1)} %param.22), channel_id=1, source_target_pairs={{0,2},{1,3},{2,6},{3,7},{4,0},{5,1},{6,4},{7,5},{8,10},{9,11},{10,... | collective-permute-start | bytes 786440 | tf_op jit(solution)/shard_map/ppermute | solution.py:375
  63.8 34.1 %collective-permute-start.16 = (bf16[1376,256]{1,0:T(8,128)(2,1)}, bf16[1376,256]{1,0:T(8,128)(2,1)}, u32[]{:S(2)}, u32[]{:S(2)}) collective-permute-start(bf16[1376,256]{1,0:T(8,128)(2,1)} %bitcast.8), channel_id=1, source_target_pairs={{0,2},{1,3},{2,6},{3,7},{4,0},{5,1},{6,4},{7,5},{8,10},{9,11},{10,... | collective-permute-start | bytes 2113544 | tf_op jit(solution)/shard_map/ppermute | solution.py:375
  64.9 30.6 %collective-permute-start.15 = (bf16[1376,256]{1,0:T(8,128)(2,1)}, bf16[1376,256]{1,0:T(8,128)(2,1)}, u32[]{:S(2)}, u32[]{:S(2)}) collective-permute-start(bf16[1376,256]{1,0:T(8,128)(2,1)} %bitcast.8), channel_id=1, source_target_pairs={{2,4},{3,5},{4,2},{5,3},{10,12},{11,13},{12,10},{13,11},{18,20},{1... | collective-permute-start | bytes 2113544 | tf_op jit(solution)/shard_map/ppermute | solution.py:375
  101.5 179.2 %all-gather.5.cloned.1.call-start = ((), (), s32[]{:S(2)}) async-start(), calls=%async_computation.6 | async-start | bytes 7045120 | tf_op jit(solution)/shard_map/all_gather | solution.py:436
  111.8 36.0 %collective-permute-start.17 = (bf16[1376,256]{1,0:T(8,128)(2,1)}, bf16[1376,256]{1,0:T(8,128)(2,1)S(1)}, u32[]{:S(2)}, u32[]{:S(2)}) collective-permute-start(bf16[1376,256]{1,0:T(8,128)(2,1)} %bitcast.144), channel_id=1, source_target_pairs={{2,4},{3,5},{4,2},{5,3},{10,12},{11,13},{12,10},{13,11},{18,20},{1... | collective-permute-start | bytes 2113544 | tf_op jit(solution)/shard_map/ppermute | solution.py:375
  114.4 33.6 %collective-permute-start.18 = (bf16[1376,256]{1,0:T(8,128)(2,1)}, bf16[1376,256]{1,0:T(8,128)(2,1)S(1)}, u32[]{:S(2)}, u32[]{:S(2)}) collective-permute-start(bf16[1376,256]{1,0:T(8,128)(2,1)} %bitcast.145), channel_id=1, source_target_pairs={{0,2},{1,3},{2,6},{3,7},{4,0},{5,1},{6,4},{7,5},{8,10},{9,11},{10,... | collective-permute-start | bytes 2113544 | tf_op jit(solution)/shard_map/ppermute | solution.py:375
  148.9 43.5 %collective-permute-start.26 = (bf16[1536,512]{1,0:T(8,128)(2,1)}, bf16[1536,512]{1,0:T(8,128)(2,1)}, u32[]{:S(2)}, u32[]{:S(2)}) collective-permute-start(bf16[1536,512]{1,0:T(8,128)(2,1)} %get-tuple-element.141.o_ref), channel_id=1, source_target_pairs={{0,1},{1,0},{2,3},{3,2},{4,5},{5,4},{6,7},{7,6},{8,9},{9,8},{10,11... | collective-permute-start | bytes 4718600 | tf_op jit(solution)/shard_map/ppermute | solution.py:375
  148.9 13.9 %collective-permute-start.20 = (bf16[256,512]{1,0:T(8,128)(2,1)S(1)}, bf16[256,512]{1,0:T(8,128)(2,1)S(1)}, u32[]{:S(2)}, u32[]{:S(2)}) collective-permute-start(bf16[256,512]{1,0:T(8,128)(2,1)S(1)} %copy-done.11), channel_id=1, source_target_pairs={{0,16},{1,17},{2,18},{3,19},{4,20},{5,21},{6,22},{7,23},{8,24},{9,... | collective-permute-start | bytes 786440 | tf_op jit(solution)/shard_map/ppermute | solution.py:375
  149.8 14.7 %collective-permute-start.19 = (bf16[256,512]{1,0:T(8,128)(2,1)S(1)}, bf16[256,512]{1,0:T(8,128)(2,1)S(1)}, u32[]{:S(2)}, u32[]{:S(2)}) collective-permute-start(bf16[256,512]{1,0:T(8,128)(2,1)S(1)} %copy-done.11), channel_id=1, source_target_pairs={{0,8},{1,9},{2,10},{3,11},{4,12},{5,13},{6,14},{7,15},{8,0},{9,1},... | collective-permute-start | bytes 786440 | tf_op jit(solution)/shard_map/ppermute | solution.py:375
  150.5 42.8 %collective-permute-start.28 = (bf16[1376,256]{1,0:T(8,128)(2,1)}, bf16[1376,256]{1,0:T(8,128)(2,1)}, u32[]{:S(2)}, u32[]{:S(2)}) collective-permute-start(bf16[1376,256]{1,0:T(8,128)(2,1)} %param.25), channel_id=1, source_target_pairs={{2,4},{3,5},{4,2},{5,3},{10,12},{11,13},{12,10},{13,11},{18,20},{1... | collective-permute-start | bytes 2113544 | tf_op jit(solution)/shard_map/ppermute | solution.py:375
  155.0 41.9 %collective-permute-start.25 = (bf16[1536,512]{1,0:T(8,128)(2,1)}, bf16[1536,512]{1,0:T(8,128)(2,1)}, u32[]{:S(2)}, u32[]{:S(2)}) collective-permute-start(bf16[1536,512]{1,0:T(8,128)(2,1)} %get-tuple-element.141.o_ref), channel_id=1, source_target_pairs={{0,4},{1,5},{2,6},{3,7},{4,0},{5,1},{6,2},{7,3},{8,12},{9,13},{10,... | collective-permute-start | bytes 4718600 | tf_op jit(solution)/shard_map/ppermute | solution.py:375
  162.8 14.1 %collective-permute-start.23 = (bf16[256,512]{1,0:T(8,128)(2,1)S(1)}, bf16[256,512]{1,0:T(8,128)(2,1)S(1)}, u32[]{:S(2)}, u32[]{:S(2)}) collective-permute-start(bf16[256,512]{1,0:T(8,128)(2,1)S(1)} %copy-done.22), channel_id=1, source_target_pairs={{0,8},{1,9},{2,10},{3,11},{4,12},{5,13},{6,14},{7,15},{8,0},{9,1},... | collective-permute-start | bytes 786440 | tf_op jit(solution)/shard_map/ppermute | solution.py:375
  164.5 13.7 %collective-permute-start.22 = (bf16[256,512]{1,0:T(8,128)(2,1)S(1)}, bf16[256,512]{1,0:T(8,128)(2,1)S(1)}, u32[]{:S(2)}, u32[]{:S(2)}) collective-permute-start(bf16[256,512]{1,0:T(8,128)(2,1)S(1)} %copy-done.22), channel_id=1, source_target_pairs={{0,16},{1,17},{2,18},{3,19},{4,20},{5,21},{6,22},{7,23},{8,24},{9,... | collective-permute-start | bytes 786440 | tf_op jit(solution)/shard_map/ppermute | solution.py:375
  184.2 59.8 %collective-permute-start.11 = (bf16[768,2048]{1,0:T(8,128)(2,1)}, bf16[768,2048]{1,0:T(8,128)(2,1)}, u32[]{:S(2)}, u32[]{:S(2)}) collective-permute-start(bf16[768,2048]{1,0:T(8,128)(2,1)} %dynamic-slice_bitcast_fusion.refs_0_), channel_id=1, source_target_pairs={{0,4},{1,5},{2,6},{3,7},{4,0},{5,1},{6,2},{7,3},{8,12},{9,13},{10,... | collective-permute-start | bytes 9437192 | tf_op jit(solution)/shard_map/ppermute | solution.py:375
  189.3 18.7 %collective-permute-start.29 = (bf16[1376,256]{1,0:T(8,128)(2,1)}, bf16[1376,256]{1,0:T(8,128)(2,1)S(1)}, u32[]{:S(2)}, u32[]{:S(2)}) collective-permute-start(bf16[1376,256]{1,0:T(8,128)(2,1)} %param.25), channel_id=1, source_target_pairs={{0,2},{1,3},{2,6},{3,7},{4,0},{5,1},{6,4},{7,5},{8,10},{9,11},{10,... | collective-permute-start | bytes 2113544 | tf_op jit(solution)/shard_map/ppermute | solution.py:375
  192.3 216.6 %reduce-scatter.6.cloned.1.call-start = ((), (), s32[]{:S(2)}) async-start(), calls=%async_computation.7 | async-start | bytes 7045120 | tf_op jit(solution)/shard_map/reduce_scatter | solution.py:441
  208.0 35.8 %collective-permute-start.31 = (bf16[1536,512]{1,0:T(8,128)(2,1)S(1)}, bf16[1536,512]{1,0:T(8,128)(2,1)}, u32[]{:S(2)}, u32[]{:S(2)}) collective-permute-start(bf16[1536,512]{1,0:T(8,128)(2,1)S(1)} %fusion.30.refs_0_), channel_id=1, source_target_pairs={{0,1},{1,0},{2,3},{3,2},{4,5},{5,4},{6,7},{7,6},{8,9},{9,8},{10,11... | collective-permute-start | bytes 4718600 | tf_op jit(solution)/shard_map/ppermute | solution.py:375
  208.0 45.8 %collective-permute-start.30 = (bf16[1536,512]{1,0:T(8,128)(2,1)S(1)}, bf16[1536,512]{1,0:T(8,128)(2,1)}, u32[]{:S(2)}, u32[]{:S(2)}) collective-permute-start(bf16[1536,512]{1,0:T(8,128)(2,1)S(1)} %fusion.30.refs_0_), channel_id=1, source_target_pairs={{0,4},{1,5},{2,6},{3,7},{4,0},{5,1},{6,2},{7,3},{8,12},{9,13},{10,... | collective-permute-start | bytes 4718600 | tf_op jit(solution)/shard_map/ppermute | solution.py:375
  251.1 45.3 %collective-permute-start.35 = (bf16[1376,256]{1,0:T(8,128)(2,1)S(1)}, bf16[1376,256]{1,0:T(8,128)(2,1)}, u32[]{:S(2)}, u32[]{:S(2)}) collective-permute-start(bf16[1376,256]{1,0:T(8,128)(2,1)S(1)} %broadcast_select_fusion.3.refs_0_), channel_id=1, source_target_pairs={{0,24},{1,25},{2,26},{3,27},{4,28},{5,29},{6,30},{7,31},{8,16},{9,... | collective-permute-start | bytes 2113544 | tf_op jit(solution)/shard_map/ppermute | solution.py:375
  252.3 58.9 %collective-permute-start.34 = (bf16[1376,256]{1,0:T(8,128)(2,1)S(1)}, bf16[1376,256]{1,0:T(8,128)(2,1)}, u32[]{:S(2)}, u32[]{:S(2)}) collective-permute-start(bf16[1376,256]{1,0:T(8,128)(2,1)S(1)} %broadcast_select_fusion.3.refs_0_), channel_id=1, source_target_pairs={{0,16},{1,17},{2,18},{3,19},{4,20},{5,21},{6,22},{7,23},{8,24},{9,... | collective-permute-start | bytes 2113544 | tf_op jit(solution)/shard_map/ppermute | solution.py:375
  253.4 57.7 %collective-permute-start.33 = (bf16[1376,256]{1,0:T(8,128)(2,1)S(1)}, bf16[1376,256]{1,0:T(8,128)(2,1)}, u32[]{:S(2)}, u32[]{:S(2)}) collective-permute-start(bf16[1376,256]{1,0:T(8,128)(2,1)S(1)} %broadcast_select_fusion.3.refs_0_), channel_id=1, source_target_pairs={{0,8},{1,9},{2,10},{3,11},{4,12},{5,13},{6,14},{7,15},{8,0},{9,1},... | collective-permute-start | bytes 2113544 | tf_op jit(solution)/shard_map/ppermute | solution.py:375
  253.7 57.4 %collective-permute-start.38 = (bf16[1376,256]{1,0:T(8,128)(2,1)S(1)}, bf16[1376,256]{1,0:T(8,128)(2,1)}, u32[]{:S(2)}, u32[]{:S(2)}) collective-permute-start(bf16[1376,256]{1,0:T(8,128)(2,1)S(1)} %collective-permute-done.29.refs_4_), channel_id=1, source_target_pairs={{0,24},{1,25},{2,26},{3,27},{4,28},{5,29},{6,30},{7,31},{8,16},{9,... | collective-permute-start | bytes 2113544 | tf_op jit(solution)/shard_map/ppermute | solution.py:375
  254.9 61.3 %collective-permute-start.37 = (bf16[1376,256]{1,0:T(8,128)(2,1)S(1)}, bf16[1376,256]{1,0:T(8,128)(2,1)}, u32[]{:S(2)}, u32[]{:S(2)}) collective-permute-start(bf16[1376,256]{1,0:T(8,128)(2,1)S(1)} %collective-permute-done.29.refs_4_), channel_id=1, source_target_pairs={{0,16},{1,17},{2,18},{3,19},{4,20},{5,21},{6,22},{7,23},{8,24},{9,... | collective-permute-start | bytes 2113544 | tf_op jit(solution)/shard_map/ppermute | solution.py:375
  296.4 19.9 %collective-permute-start.36 = (bf16[1376,256]{1,0:T(8,128)(2,1)S(1)}, bf16[1376,256]{1,0:T(8,128)(2,1)}, u32[]{:S(2)}, u32[]{:S(2)}) collective-permute-start(bf16[1376,256]{1,0:T(8,128)(2,1)S(1)} %collective-permute-done.29.refs_4_), channel_id=1, source_target_pairs={{0,8},{1,9},{2,10},{3,11},{4,12},{5,13},{6,14},{7,15},{8,0},{9,1},... | collective-permute-start | bytes 2113544 | tf_op jit(solution)/shard_map/ppermute | solution.py:375
  316.3 163.2 %reduce-scatter.8.cloned.1.call-start = ((), (), s32[]{:S(2)}) async-start(), calls=%async_computation.8 | async-start | bytes 7045120 | tf_op jit(solution)/shard_map/reduce_scatter | solution.py:441
  371.5 170.8 %reduce-scatter.10.cloned.1.call-start = ((), (), s32[]{:S(2)}) async-start(), calls=%async_computation.9 | async-start | bytes 7045120 | tf_op jit(solution)/shard_map/reduce_scatter | solution.py:441
  371.5 37.3 %collective-permute-start.43 = (bf16[1536,512]{1,0:T(8,128)(2,1)}, bf16[1536,512]{1,0:T(8,128)(2,1)S(1)}, u32[]{:S(2)}, u32[]{:S(2)}) collective-permute-start(bf16[1536,512]{1,0:T(8,128)(2,1)} %fusion.29), channel_id=1, source_target_pairs={{0,1},{1,0},{2,3},{3,2},{4,5},{5,4},{6,7},{7,6},{8,9},{9,8},{10,11... | collective-permute-start | bytes 4718600 | tf_op jit(solution)/shard_map/ppermute | solution.py:375
  385.1 15.8 %collective-permute-start.42 = (bf16[1536,512]{1,0:T(8,128)(2,1)}, bf16[1536,512]{1,0:T(8,128)(2,1)}, u32[]{:S(2)}, u32[]{:S(2)}) collective-permute-start(bf16[1536,512]{1,0:T(8,128)(2,1)} %fusion.28), channel_id=1, source_target_pairs={{0,4},{1,5},{2,6},{3,7},{4,0},{5,1},{6,2},{7,3},{8,12},{9,13},{10,... | collective-permute-start | bytes 4718600 | tf_op jit(solution)/shard_map/ppermute | solution.py:375
  408.9 242.8 %reduce-scatter.12.cloned.1.call-start = ((), (), s32[]{:S(2)}) async-start(), calls=%async_computation.10 | async-start | bytes 2621440 | tf_op jit(solution)/shard_map/reduce_scatter | solution.py:441
  432.4 35.7 %collective-permute-start.47 = (bf16[1536,512]{1,0:T(8,128)(2,1)S(1)}, bf16[1536,512]{1,0:T(8,128)(2,1)S(1)}, u32[]{:S(2)}, u32[]{:S(2)}) collective-permute-start(bf16[1536,512]{1,0:T(8,128)(2,1)S(1)} %convolution_convert_fusion.13), channel_id=1, source_target_pairs={{0,4},{1,5},{2,6},{3,7},{4,0},{5,1},{6,2},{7,3},{8,12},{9,13},{10,... | collective-permute-start | bytes 4718600 | tf_op jit(solution)/shard_map/ppermute | solution.py:375
  432.9 46.6 %collective-permute-start.50 = (bf16[1376,256]{1,0:T(8,128)(2,1)S(1)}, bf16[1376,256]{1,0:T(8,128)(2,1)}, u32[]{:S(2)}, u32[]{:S(2)}) collective-permute-start(bf16[1376,256]{1,0:T(8,128)(2,1)S(1)} %get-tuple-element.294), channel_id=1, source_target_pairs={{0,4},{1,5},{2,0},{3,1},{4,6},{5,7},{6,2},{7,3},{8,12},{9,13},{10,... | collective-permute-start | bytes 2113544 | tf_op jit(solution)/shard_map/ppermute | solution.py:375
  435.1 32.2 %collective-permute-start.49 = (bf16[1376,256]{1,0:T(8,128)(2,1)S(1)}, bf16[1376,256]{1,0:T(8,128)(2,1)S(1)}, u32[]{:S(2)}, u32[]{:S(2)}) collective-permute-start(bf16[1376,256]{1,0:T(8,128)(2,1)S(1)} %get-tuple-element.295), channel_id=1, source_target_pairs={{2,4},{3,5},{4,2},{5,3},{10,12},{11,13},{12,10},{13,11},{18,20},{1... | collective-permute-start | bytes 2113544 | tf_op jit(solution)/shard_map/ppermute | solution.py:375
  438.9 33.7 %collective-permute-start.46 = (bf16[1536,512]{1,0:T(8,128)(2,1)S(1)}, bf16[1536,512]{1,0:T(8,128)(2,1)S(1)}, u32[]{:S(2)}, u32[]{:S(2)}) collective-permute-start(bf16[1536,512]{1,0:T(8,128)(2,1)S(1)} %convolution_convert_fusion.8), channel_id=1, source_target_pairs={{0,4},{1,5},{2,6},{3,7},{4,0},{5,1},{6,2},{7,3},{8,12},{9,13},{10,... | collective-permute-start | bytes 4718600 | tf_op jit(solution)/shard_map/ppermute | solution.py:375
  441.7 33.7 %collective-permute-start.48 = (bf16[1536,512]{1,0:T(8,128)(2,1)S(1)}, bf16[1536,512]{1,0:T(8,128)(2,1)S(1)}, u32[]{:S(2)}, u32[]{:S(2)}) collective-permute-start(bf16[1536,512]{1,0:T(8,128)(2,1)S(1)} %convolution_convert_fusion.12), channel_id=1, source_target_pairs={{0,4},{1,5},{2,6},{3,7},{4,0},{5,1},{6,2},{7,3},{8,12},{9,13},{10,... | collective-permute-start | bytes 4718600 | tf_op jit(solution)/shard_map/ppermute | solution.py:375
  468.2 26.3 %collective-permute-start.45 = (bf16[1536,512]{1,0:T(8,128)(2,1)}, bf16[1536,512]{1,0:T(8,128)(2,1)}, u32[]{:S(2)}, u32[]{:S(2)}) collective-permute-start(bf16[1536,512]{1,0:T(8,128)(2,1)} %fusion.31), channel_id=1, source_target_pairs={{0,1},{1,0},{2,3},{3,2},{4,5},{5,4},{6,7},{7,6},{8,9},{9,8},{10,11... | collective-permute-start | bytes 4718600 | tf_op jit(solution)/shard_map/ppermute | solution.py:375
  507.9 27.5 %collective-permute-start.54 = (bf16[1536,512]{1,0:T(8,128)(2,1)}, bf16[1536,512]{1,0:T(8,128)(2,1)}, u32[]{:S(2)}, u32[]{:S(2)}) collective-permute-start(bf16[1536,512]{1,0:T(8,128)(2,1)} %add_convert_fusion.1), channel_id=1, source_target_pairs={{0,1},{1,0},{2,3},{3,2},{4,5},{5,4},{6,7},{7,6},{8,9},{9,8},{10,11... | collective-permute-start | bytes 4718600 | tf_op jit(solution)/shard_map/ppermute | solution.py:375
  509.5 20.1 %collective-permute-start.53 = (bf16[648,128]{1,0:T(8,128)(2,1)}, bf16[648,128]{1,0:T(8,128)(2,1)}, u32[]{:S(2)}, u32[]{:S(2)}) collective-permute-start(bf16[648,128]{1,0:T(8,128)(2,1)} %pad_maximum_fusion.4), channel_id=1, source_target_pairs={{24,0},{25,1},{26,2},{27,3},{28,4},{29,5},{30,6},{31,7}} | collective-permute-start | bytes 497672 | tf_op jit(solution)/shard_map/ppermute | solution.py:375
  513.4 16.3 %collective-permute-start.52 = (bf16[648,128]{1,0:T(8,128)(2,1)}, bf16[648,128]{1,0:T(8,128)(2,1)}, u32[]{:S(2)}, u32[]{:S(2)}) collective-permute-start(bf16[648,128]{1,0:T(8,128)(2,1)} %pad_maximum_fusion.4), channel_id=1, source_target_pairs={{16,0},{17,1},{18,2},{19,3},{20,4},{21,5},{22,6},{23,7},{24,8},{25... | collective-permute-start | bytes 497672 | tf_op jit(solution)/shard_map/ppermute | solution.py:375
  515.4 14.3 %collective-permute-start.51 = (bf16[648,128]{1,0:T(8,128)(2,1)}, bf16[648,128]{1,0:T(8,128)(2,1)}, u32[]{:S(2)}, u32[]{:S(2)}) collective-permute-start(bf16[648,128]{1,0:T(8,128)(2,1)} %pad_maximum_fusion.4), channel_id=1, source_target_pairs={{8,0},{9,1},{10,2},{11,3},{12,4},{13,5},{14,6},{15,7},{16,8},{17,9... | collective-permute-start | bytes 497672 | tf_op jit(solution)/shard_map/ppermute | solution.py:375
  543.7 31.6 %collective-permute-start.56 = (bf16[1376,256]{1,0:T(8,128)(2,1)S(1)}, bf16[1376,256]{1,0:T(8,128)(2,1)S(1)}, u32[]{:S(2)}, u32[]{:S(2)}) collective-permute-start(bf16[1376,256]{1,0:T(8,128)(2,1)S(1)} %get-tuple-element.292), channel_id=1, source_target_pairs={{0,4},{1,5},{2,0},{3,1},{4,6},{5,7},{6,2},{7,3},{8,12},{9,13},{10,... | collective-permute-start | bytes 2113544 | tf_op jit(solution)/shard_map/ppermute | solution.py:375
  543.8 30.6 %collective-permute-start.55 = (bf16[1376,256]{1,0:T(8,128)(2,1)S(1)}, bf16[1376,256]{1,0:T(8,128)(2,1)S(1)}, u32[]{:S(2)}, u32[]{:S(2)}) collective-permute-start(bf16[1376,256]{1,0:T(8,128)(2,1)S(1)} %get-tuple-element.293), channel_id=1, source_target_pairs={{2,4},{3,5},{4,2},{5,3},{10,12},{11,13},{12,10},{13,11},{18,20},{1... | collective-permute-start | bytes 2113544 | tf_op jit(solution)/shard_map/ppermute | solution.py:375
  581.5 162.1 %reduce-scatter.14.cloned.1.call-start = ((), (), s32[]{:S(2)}) async-start(), calls=%async_computation.11 | async-start | bytes 3276800 | tf_op jit(solution)/shard_map/reduce_scatter | solution.py:441
  587.5 28.5 %collective-permute-start.62 = (bf16[768,512]{1,0:T(8,128)(2,1)S(1)}, bf16[768,512]{1,0:T(8,128)(2,1)S(1)}, u32[]{:S(2)}, u32[]{:S(2)}) collective-permute-start(bf16[768,512]{1,0:T(8,128)(2,1)S(1)} %get-tuple-element.289), channel_id=1, source_target_pairs={{2,4},{3,5},{4,2},{5,3},{10,12},{11,13},{12,10},{13,11},{18,20},{1... | collective-permute-start | bytes 2359304 | tf_op jit(solution)/shard_map/ppermute | solution.py:375
  599.5 27.7 %collective-permute-start.61 = (bf16[1536,512]{1,0:T(8,128)(2,1)}, bf16[1536,512]{1,0:T(8,128)(2,1)}, u32[]{:S(2)}, u32[]{:S(2)}) collective-permute-start(bf16[1536,512]{1,0:T(8,128)(2,1)} %convolution_convert_fusion.10), channel_id=1, source_target_pairs={{0,4},{1,5},{2,6},{3,7},{4,0},{5,1},{6,2},{7,3},{8,12},{9,13},{10,... | collective-permute-start | bytes 4718600 | tf_op jit(solution)/shard_map/ppermute | solution.py:375
  599.5 32.4 %collective-permute-start.63 = (bf16[768,512]{1,0:T(8,128)(2,1)}, bf16[768,512]{1,0:T(8,128)(2,1)}, u32[]{:S(2)}, u32[]{:S(2)}) collective-permute-start(bf16[768,512]{1,0:T(8,128)(2,1)} %get-tuple-element.288), channel_id=1, source_target_pairs={{0,4},{1,5},{2,0},{3,1},{4,6},{5,7},{6,2},{7,3},{8,12},{9,13},{10,... | collective-permute-start | bytes 2359304 | tf_op jit(solution)/shard_map/ppermute | solution.py:375
  599.6 52.1 %collective-permute-start.60 = (bf16[1536,512]{1,0:T(8,128)(2,1)}, bf16[1536,512]{1,0:T(8,128)(2,1)}, u32[]{:S(2)}, u32[]{:S(2)}) collective-permute-start(bf16[1536,512]{1,0:T(8,128)(2,1)} %fusion.32), channel_id=1, source_target_pairs={{0,1},{1,0},{2,3},{3,2},{4,5},{5,4},{6,7},{7,6},{8,9},{9,8},{10,11... | collective-permute-start | bytes 4718600 | tf_op jit(solution)/shard_map/ppermute | solution.py:375
  663.7 39.4 %collective-permute-start.66 = (bf16[2,768,512]{2,1,0:T(8,128)(2,1)S(1)}, bf16[2,768,512]{2,1,0:T(8,128)(2,1)}, u32[]{:S(2)}, u32[]{:S(2)}) collective-permute-start(bf16[2,768,512]{2,1,0:T(8,128)(2,1)S(1)} %pad_maximum_fusion.1.refs_0_), channel_id=1, source_target_pairs={{1,0},{2,1},{3,2},{5,4},{6,5},{7,6},{9,8},{10,9},{11,10},{13,12},{... | collective-permute-start | bytes 4718600 | tf_op jit(solution)/shard_map/ppermute | solution.py:375
  665.0 38.1 %collective-permute-start.65 = (bf16[2,768,512]{2,1,0:T(8,128)(2,1)S(1)}, bf16[2,768,512]{2,1,0:T(8,128)(2,1)S(1)}, u32[]{:S(2)}, u32[]{:S(2)}) collective-permute-start(bf16[2,768,512]{2,1,0:T(8,128)(2,1)S(1)} %pad_maximum_fusion.1.refs_0_), channel_id=1, source_target_pairs={{0,1},{1,2},{2,3},{4,5},{5,6},{6,7},{8,9},{9,10},{10,11},{12,13},{... | collective-permute-start | bytes 4718600 | tf_op jit(solution)/shard_map/ppermute | solution.py:375
  669.3 33.1 %collective-permute-start.69 = (f32[2,2048]{1,0:T(2,128)S(1)}, f32[2,2048]{1,0:T(2,128)S(1)}, u32[]{:S(2)}, u32[]{:S(2)}) collective-permute-start(f32[2,2048]{1,0:T(2,128)S(1)} %constant_dynamic-update-slice_fusion), channel_id=1, source_target_pairs={{0,3},{1,2},{2,1},{3,0},{4,7},{5,6},{6,5},{7,4},{8,11},{9,10},{10,... | collective-permute-start | bytes 49160 | tf_op jit(solution)/shard_map/ppermute | solution.py:375
  669.4 33.3 %collective-permute-start.68 = (f32[2,2048]{1,0:T(2,128)S(1)}, f32[2,2048]{1,0:T(2,128)S(1)}, u32[]{:S(2)}, u32[]{:S(2)}) collective-permute-start(f32[2,2048]{1,0:T(2,128)S(1)} %constant_dynamic-update-slice_fusion), channel_id=1, source_target_pairs={{0,2},{1,3},{2,0},{3,1},{4,6},{5,7},{6,4},{7,5},{8,10},{9,11},{10,... | collective-permute-start | bytes 49160 | tf_op jit(solution)/shard_map/ppermute | solution.py:375
  670.5 32.6 %collective-permute-start.67 = (f32[2,2048]{1,0:T(2,128)S(1)}, f32[2,2048]{1,0:T(2,128)S(1)}, u32[]{:S(2)}, u32[]{:S(2)}) collective-permute-start(f32[2,2048]{1,0:T(2,128)S(1)} %constant_dynamic-update-slice_fusion), channel_id=1, source_target_pairs={{0,1},{1,0},{2,3},{3,2},{4,5},{5,4},{6,7},{7,6},{8,9},{9,8},{10,11... | collective-permute-start | bytes 49160 | tf_op jit(solution)/shard_map/ppermute | solution.py:375
  704.9 38.6 %collective-permute-start.71 = (bf16[2,768,512]{2,1,0:T(8,128)(2,1)}, bf16[2,768,512]{2,1,0:T(8,128)(2,1)}, u32[]{:S(2)}, u32[]{:S(2)}) collective-permute-start(bf16[2,768,512]{2,1,0:T(8,128)(2,1)} %collective-permute-done.66.refs_4_), channel_id=1, source_target_pairs={{1,0},{2,1},{5,4},{6,5},{9,8},{10,9},{13,12},{14,13},{17,16},{18,1... | collective-permute-start | bytes 4718600 | tf_op jit(solution)/shard_map/ppermute | solution.py:375
  743.5 57.5 %collective-permute-start.73 = (bf16[2,768,512]{2,1,0:T(8,128)(2,1)}, bf16[2,768,512]{2,1,0:T(8,128)(2,1)}, u32[]{:S(2)}, u32[]{:S(2)}) collective-permute-start(bf16[2,768,512]{2,1,0:T(8,128)(2,1)} %collective-permute-done.70.refs_2_), channel_id=1, source_target_pairs={{2,3},{6,7},{10,11},{14,15},{18,19},{22,23},{26,27},{30,31}} | collective-permute-start | bytes 4718600 | tf_op jit(solution)/shard_map/ppermute | solution.py:375
  745.5 55.5 %collective-permute-start.74 = (bf16[2,768,512]{2,1,0:T(8,128)(2,1)}, bf16[2,768,512]{2,1,0:T(8,128)(2,1)}, u32[]{:S(2)}, u32[]{:S(2)}) collective-permute-start(bf16[2,768,512]{2,1,0:T(8,128)(2,1)} %collective-permute-done.71.refs_5_), channel_id=1, source_target_pairs={{1,0},{5,4},{9,8},{13,12},{17,16},{21,20},{25,24},{29,28}} | collective-permute-start | bytes 4718600 | tf_op jit(solution)/shard_map/ppermute | solution.py:375
  750.8 27.3 %collective-permute-start.77 = (bf16[256,640]{1,0:T(8,128)(2,1)S(1)}, bf16[256,640]{1,0:T(8,128)(2,1)S(1)}, u32[]{:S(2)}, u32[]{:S(2)}) collective-permute-start(bf16[256,640]{1,0:T(8,128)(2,1)S(1)} %get-tuple-element.299), channel_id=1, source_target_pairs={{0,4},{1,5},{2,0},{3,1},{4,6},{5,7},{6,2},{7,3},{8,12},{9,13},{10,... | collective-permute-start | bytes 983048 | tf_op jit(solution)/shard_map/ppermute | solution.py:375
  756.9 21.2 %collective-permute-start.78 = (bf16[256,512]{1,0:T(8,128)(2,1)S(1)}, bf16[256,512]{1,0:T(8,128)(2,1)S(1)}, u32[]{:S(2)}, u32[]{:S(2)}) collective-permute-start(bf16[256,512]{1,0:T(8,128)(2,1)S(1)} %get-tuple-element.300), channel_id=1, source_target_pairs={{2,4},{3,5},{4,2},{5,3},{10,12},{11,13},{12,10},{13,11},{18,20},{1... | collective-permute-start | bytes 786440 | tf_op jit(solution)/shard_map/ppermute | solution.py:375
  759.8 36.9 %collective-permute-start.76 = (bf16[256,640]{1,0:T(8,128)(2,1)S(1)}, bf16[256,640]{1,0:T(8,128)(2,1)S(1)}, u32[]{:S(2)}, u32[]{:S(2)}) collective-permute-start(bf16[256,640]{1,0:T(8,128)(2,1)S(1)} %get-tuple-element.298), channel_id=1, source_target_pairs={{2,4},{3,5},{4,2},{5,3},{10,12},{11,13},{12,10},{13,11},{18,20},{1... | collective-permute-start | bytes 983048 | tf_op jit(solution)/shard_map/ppermute | solution.py:375
  778.1 23.2 %collective-permute-start.81 = (bf16[1376,256]{1,0:T(8,128)(2,1)}, bf16[1376,256]{1,0:T(8,128)(2,1)}, u32[]{:S(2)}, u32[]{:S(2)}) collective-permute-start(bf16[1376,256]{1,0:T(8,128)(2,1)} %get-tuple-element.291), channel_id=1, source_target_pairs={{0,4},{1,5},{2,0},{3,1},{4,6},{5,7},{6,2},{7,3},{8,12},{9,13},{10,... | collective-permute-start | bytes 2113544 | tf_op jit(solution)/shard_map/ppermute | solution.py:375
  778.1 33.7 %collective-permute-start.80 = (bf16[1376,256]{1,0:T(8,128)(2,1)}, bf16[1376,256]{1,0:T(8,128)(2,1)}, u32[]{:S(2)}, u32[]{:S(2)}) collective-permute-start(bf16[1376,256]{1,0:T(8,128)(2,1)} %get-tuple-element.290), channel_id=1, source_target_pairs={{2,4},{3,5},{4,2},{5,3},{10,12},{11,13},{12,10},{13,11},{18,20},{1... | collective-permute-start | bytes 2113544 | tf_op jit(solution)/shard_map/ppermute | solution.py:375
  801.0 22.9 %collective-permute-start.82 = (f32[2,2048]{1,0:T(2,128)S(1)}, f32[2,2048]{1,0:T(2,128)S(1)}, u32[]{:S(2)}, u32[]{:S(2)}) collective-permute-start(f32[2,2048]{1,0:T(2,128)S(1)} %add.580), channel_id=1, source_target_pairs={{0,16},{1,17},{2,18},{3,19},{4,20},{5,21},{6,22},{7,23},{8,24},{9,... | collective-permute-start | bytes 49160 | tf_op jit(solution)/shard_map/ppermute | solution.py:375
  (128 other events, 1329.9 us)
Sparse Core Ops, SparseCore 0:
  101.6 77.0 all-gather.2
  192.4 79.2 all-gather.4
  316.4 64.6 reduce-scatter.5
  384.1 64.6 reduce-scatter.7
  451.7 68.1 reduce-scatter.9
  581.6 35.1 reduce-scatter.11
  651.9 38.6 reduce-scatter.13
